TPU v7x, 32 devices: a whole 2x2x4 slice. The times are simulated.
32 devices in a mesh: blk: 32 (over z, y, x, core).
Axes of the slice: x: 2, y: 2, z: 4, core: 2. Of those that a mesh axis runs over, the one named last changes fastest.
Arguments:
- right_side: float32 [4096, 128], P('blk')
- kernel_tiles: float32 [32, 17, 128, 128], P('blk'), as said below
- route_pairs: int32 [17, 2], replicated, may hold values from 0 to 10
Outputs:
- solution: float32 [4096, 128], P('blk')
- residual: float32 [4096, 128], P('blk')
Inputs may be any that keep to these rules, and one draw needn't show every extreme that they name: kernel_tiles makes K symmetric with a positive diagonal of about 1 to 16 inside the diagonal tiles; K is positive definite.
All inputs are finite; a program needn't handle non-finite values.
Results may differ from a plain program's by a relative error of at most 0.0003.
Values sent between devices are 32-bit elements; how exact they have to be, the bound alone decides.
No kernel may reach another device: no remote copies, remote signals or barrier semaphores. Data moves between devices by JAX's collectives and lax.ppermute only.
A program may use at most 128 MiB of HBM per device.

v0:
```python
import jax
import jax.numpy as jnp
from jax import lax
from jax.sharding import PartitionSpec as P


def shifted(value, axis, steps):
    count = lax.axis_size(axis)
    pairs = [(source, (source + steps) % count) for source in range(count)]
    return lax.ppermute(value, axis, pairs)


def collect_cover(vector, cover_list):
    pieces = [vector[None]]
    for offset in cover_list[1:]:
        pieces.append(shifted(vector, "blk", -offset)[None])
    return jnp.concatenate(pieces, axis=0)


def fold_partials(partial_value, cover_list):
    summed = partial_value[0]
    for place, offset in enumerate(cover_list[1:]):
        summed = summed + shifted(partial_value[place + 1], "blk", offset)
    return summed


def column_total(values):
    return lax.psum(jnp.sum(values, axis=0), "blk")


def per_device(right_side, kernel_tiles, route_pairs):
    blocks_total = lax.axis_size("blk")
    window_len = max(8, min(16, blocks_total // 8))
    cover_list = [k for k in range(window_len)] + [
        k * window_len for k in range(1, blocks_total // window_len)
    ]
    cover_len = len(cover_list)
    own_tiles = kernel_tiles[0]
    slot_total = own_tiles.shape[0]
    cover_ids = jnp.arange(cover_len, dtype=jnp.int32)
    slot_ids = jnp.arange(slot_total, dtype=jnp.int32)
    mirror = ((slot_ids > 0) & (slot_ids < slot_total - 1)).astype(jnp.float32)
    row_hot = (route_pairs[:, 0:1] == cover_ids[None, :]).astype(jnp.float32)
    col_hot = (route_pairs[:, 1:2] == cover_ids[None, :]).astype(jnp.float32) * mirror[:, None]
    residual = right_side
    norm_now = column_total(residual * residual)
    blocks = collect_cover(right_side, cover_list)
    by_row = jnp.einsum(
        "tij,tjr->tir",
        own_tiles,
        jnp.take(blocks, route_pairs[:, 1], axis=0),
        precision=lax.Precision.HIGHEST,
    )
    by_col = jnp.einsum(
        "tji,tjr->tir",
        own_tiles,
        jnp.take(blocks, route_pairs[:, 0], axis=0),
        precision=lax.Precision.HIGHEST,
    )
    partial_value = jnp.einsum("tc,tbr->cbr", row_hot, by_row, precision=lax.Precision.HIGHEST)
    partial_value = partial_value + jnp.einsum(
        "tc,tbr->cbr", col_hot, by_col, precision=lax.Precision.HIGHEST
    )
    image = fold_partials(partial_value, cover_list)
    step_len = norm_now / column_total(right_side * image)
    solution = step_len * right_side
    residual = residual - step_len * image
    return (solution, residual)


def solution(mesh):
    return jax.shard_map(
        per_device,
        mesh=mesh,
        in_specs=(P("blk", None), P("blk", None, None, None), P()),
        out_specs=(P("blk", None), P("blk", None)),
        check_vma=False,
    )
```

profile of v0, /device:TPU:0, one launch (start us, length us, event | category | flops | bytes accessed | tf_op | source)
XLA Modules:
  0.0 103.8 jit_solution(9353957606857158976)
XLA Ops:
  0.6 0.0 copy-start
  0.6 6.4 %collective-permute-start = (f32[128,128]{1,0:T(8,128)}, f32[128,128]{1,0:T(8,128)S(1)}, u32[]{:S(2)}, u32[]{:S(2)}) collective-permute-start(f32[128,128]{1,0:T(8,128)} %param.5), channel_id=1, source_target_pairs={{0,31},{1,0},{2,1},{3,2},{4,3},{5,4},{6,5},{7,6},{8,7},{9,8},{10,9... | collective-permute-start | bytes 196616 | tf_op jit(solution)/shard_map/ppermute | solution.py:10
  7.1 0.6 collective-permute-start.1
  7.7 0.3 collective-permute-start.2
  8.0 1.4 %collective-permute-start.3 = (f32[128,128]{1,0:T(8,128)}, f32[128,128]{1,0:T(8,128)S(1)}, u32[]{:S(2)}, u32[]{:S(2)}) collective-permute-start(f32[128,128]{1,0:T(8,128)} %param.5), channel_id=1, source_target_pairs={{0,28},{1,29},{2,30},{3,31},{4,0},{5,1},{6,2},{7,3},{8,4},{9,5},{1... | collective-permute-start | bytes 196616 | tf_op jit(solution)/shard_map/ppermute | solution.py:10
  9.4 0.2 collective-permute-start.4
  9.6 0.9 bitcast_dynamic-update-slice_fusion.10
  10.4 0.8 compare_and_fusion.1
  11.2 0.8 slice_bitcast_fusion.12
  12.0 2.2 %collective-permute-start.5 = (f32[128,128]{1,0:T(8,128)}, f32[128,128]{1,0:T(8,128)S(1)}, u32[]{:S(2)}, u32[]{:S(2)}) collective-permute-start(f32[128,128]{1,0:T(8,128)} %param.5), channel_id=1, source_target_pairs={{0,26},{1,27},{2,28},{3,29},{4,30},{5,31},{6,0},{7,1},{8,2},{9,3},... | collective-permute-start | bytes 196616 | tf_op jit(solution)/shard_map/ppermute | solution.py:10
  14.2 0.1 collective-permute-start.6
  14.3 0.0 collective-permute-done.2
  14.3 2.7 %collective-permute-start.7 = (f32[128,128]{1,0:T(8,128)}, f32[128,128]{1,0:T(8,128)S(1)}, u32[]{:S(2)}, u32[]{:S(2)}) collective-permute-start(f32[128,128]{1,0:T(8,128)} %param.5), channel_id=1, source_target_pairs={{0,24},{1,25},{2,26},{3,27},{4,28},{5,29},{6,30},{7,31},{8,0},{9,1... | collective-permute-start | bytes 196616 | tf_op jit(solution)/shard_map/ppermute | solution.py:10
  17.0 0.0 collective-permute-done.3
  17.0 0.5 collective-permute-start.8
  17.5 1.6 %collective-permute-start.9 = (f32[128,128]{1,0:T(8,128)}, f32[128,128]{1,0:T(8,128)S(1)}, u32[]{:S(2)}, u32[]{:S(2)}) collective-permute-start(f32[128,128]{1,0:T(8,128)} %param.5), channel_id=1, source_target_pairs={{0,8},{1,9},{2,10},{3,11},{4,12},{5,13},{6,14},{7,15},{8,16},{9,17... | collective-permute-start | bytes 196616 | tf_op jit(solution)/shard_map/ppermute | solution.py:10
  19.2 0.0 collective-permute-done.5
  19.2 1.8 %collective-permute-done.7 = f32[128,128]{1,0:T(8,128)S(1)} collective-permute-done((f32[128,128]{1,0:T(8,128)}, f32[128,128]{1,0:T(8,128)S(1)}, u32[]{:S(2)}, u32[]{:S(2)}) %collective-permute-start.7) | collective-permute-done | bytes 65568 | tf_op jit(solution)/shard_map/ppermute | solution.py:10
  21.1 5.2 %collective-permute-done.8 = f32[128,128]{1,0:T(8,128)S(1)} collective-permute-done((f32[128,128]{1,0:T(8,128)}, f32[128,128]{1,0:T(8,128)S(1)}, u32[]{:S(2)}, u32[]{:S(2)}) %collective-permute-start.8) | collective-permute-done | bytes 65568 | tf_op jit(solution)/shard_map/ppermute | solution.py:10
  26.3 0.6 gather_fusion
  26.9 3.0 %fusion.6 = f32[17,128,128]{2,1,0:T(8,128)} fusion(f32[1,17,128,128]{3,2,1,0:T(8,128)S(1)} %copy-done, f32[17,128,128]{2,1,0:T(8,128)S(1)} %gather_fusion, pred[17]{0:T(512)(128)(4,1)S(1)} %get-tuple-element.8), kind=kOutput, calls=%fused_computation.8 | convolution fusion | flops 428097536 | bytes 3342353 | tf_op jit(solution)/shard_map/tij,tjr->tir/dot_general | solution.py:48
  30.0 1.8 %copy.17 = f32[17,128,128]{1,0,2:T(8,128)S(1)} copy(f32[17,128,128]{2,1,0:T(8,128)} %fusion.6) | data formatting | bytes 2228224 | tf_op jit(solution)/shard_map/tij,tjr->tir/dot_general | solution.py:48
  31.8 1.6 %gather_fusion.1 = f32[17,128,128]{2,1,0:T(8,128)} fusion(f32[11,128,128]{2,1,0:T(8,128)S(1)} %bitcast_dynamic-update-slice_fusion, s32[1024]{0:T(1024)S(1)} %get-tuple-element.28), kind=kCustom, calls=%fused_computation.1.clone | custom fusion | bytes 2228292 | tf_op jit(solution)/shard_map/jit(_take)/gather | solution.py:57
  33.4 4.3 %fusion.4 = f32[17,128,128]{2,1,0:T(8,128)} fusion(f32[1,17,128,128]{3,2,1,0:T(8,128)S(1)} %copy-done, f32[17,128,128]{2,1,0:T(8,128)} %gather_fusion.1, pred[17]{0:T(512)(128)(4,1)S(1)} %get-tuple-element.26), kind=kOutput, calls=%fused_computation.6 | convolution fusion | flops 428097536 | bytes 3342353 | tf_op jit(solution)/shard_map/tji,tjr->tir/dot_general | solution.py:54
  37.7 2.9 %copy.18 = f32[17,128,128]{1,0,2:T(8,128)} copy(f32[17,128,128]{2,1,0:T(8,128)} %fusion.4) | data formatting | bytes 2228224 | tf_op jit(solution)/shard_map/tji,tjr->tir/dot_general | solution.py:54
  40.6 0.7 fusion.2
  41.3 0.7 copy-done.1
  42.0 1.0 fusion
  43.0 0.4 copy_add_fusion
  43.4 0.0 copy-start.2
  43.5 0.1 collective-permute-start.10
  43.6 0.7 collective-permute-start.11
  44.2 1.7 %collective-permute-start.12 = (f32[128,128]{1,0:T(8,128)S(1)}, f32[128,128]{1,0:T(8,128)S(1)}, u32[]{:S(2)}, u32[]{:S(2)}) collective-permute-start(f32[128,128]{1,0:T(8,128)S(1)} %get-tuple-element.20), channel_id=1, source_target_pairs={{0,3},{1,4},{2,5},{3,6},{4,7},{5,8},{6,9},{7,10},{8,11},{9,12},{10... | collective-permute-start | bytes 196616 | tf_op jit(solution)/shard_map/ppermute | solution.py:10
  45.9 0.2 collective-permute-start.13
  46.1 0.6 collective-permute-start.14
  46.8 4.7 %collective-permute-done.10 = f32[128,128]{1,0:T(8,128)S(1)} collective-permute-done((f32[128,128]{1,0:T(8,128)S(1)}, f32[128,128]{1,0:T(8,128)S(1)}, u32[]{:S(2)}, u32[]{:S(2)}) %collective-permute-start.10) | collective-permute-done | bytes 65568 | tf_op jit(solution)/shard_map/ppermute | solution.py:10
  51.5 0.0 collective-permute-start.15
  51.5 2.2 %collective-permute-done.11 = f32[128,128]{1,0:T(8,128)S(1)} collective-permute-done((f32[128,128]{1,0:T(8,128)S(1)}, f32[128,128]{1,0:T(8,128)S(1)}, u32[]{:S(2)}, u32[]{:S(2)}) %collective-permute-start.11) | collective-permute-done | bytes 65568 | tf_op jit(solution)/shard_map/ppermute | solution.py:10
  53.7 0.9 collective-permute-start.17
  54.6 1.9 %collective-permute-start.18 = (f32[128,128]{1,0:T(8,128)S(1)}, f32[128,128]{1,0:T(8,128)S(1)}, u32[]{:S(2)}, u32[]{:S(2)}) collective-permute-start(f32[128,128]{1,0:T(8,128)S(1)} %get-tuple-element.14), channel_id=1, source_target_pairs={{0,16},{1,17},{2,18},{3,19},{4,20},{5,21},{6,22},{7,23},{8,24},{9,... | collective-permute-start | bytes 196616 | tf_op jit(solution)/shard_map/ppermute | solution.py:10
  56.5 1.1 %collective-permute-start.19 = (f32[128,128]{1,0:T(8,128)S(1)}, f32[128,128]{1,0:T(8,128)S(1)}, u32[]{:S(2)}, u32[]{:S(2)}) collective-permute-start(f32[128,128]{1,0:T(8,128)S(1)} %get-tuple-element.13), channel_id=1, source_target_pairs={{0,24},{1,25},{2,26},{3,27},{4,28},{5,29},{6,30},{7,31},{8,0},{9,1... | collective-permute-start | bytes 196616 | tf_op jit(solution)/shard_map/ppermute | solution.py:10
  57.6 0.8 collective-permute-done.15
  58.5 0.9 collective-permute-done.16
  59.4 0.7 collective-permute-done.17
  60.0 3.4 %collective-permute-done.18 = f32[128,128]{1,0:T(8,128)S(1)} collective-permute-done((f32[128,128]{1,0:T(8,128)S(1)}, f32[128,128]{1,0:T(8,128)S(1)}, u32[]{:S(2)}, u32[]{:S(2)}) %collective-permute-start.18) | collective-permute-done | bytes 65568 | tf_op jit(solution)/shard_map/ppermute | solution.py:10
  63.4 0.1 multiply_reduce_fusion
  63.5 39.7 %all-reduce = (f32[128]{0:T(128)S(1)}, f32[128]{0:T(128)S(1)}) all-reduce(f32[128]{0:T(128)S(1)} %get-tuple-element.4, f32[128]{0:T(128)S(1)} %get-tuple-element.3), channel_id=1, replica_groups=mesh['blk'=32] {'blk'}, use_global_device_ids=true, to_apply=%region_1.0 | all-reduce | flops 256 | bytes 2048 | tf_op jit(solution)/shard_map/psum | solution.py:28
  103.2 0.7 multiply_subtract_fusion
  (27 shorter events, 0.2 us)
Async XLA Ops:
  0.6 26.3 %copy-start = (f32[1,17,128,128]{3,2,1,0:T(8,128)S(1)}, f32[1,17,128,128]{3,2,1,0:T(8,128)}, u32[]{:S(2)}) copy-start(f32[1,17,128,128]{3,2,1,0:T(8,128)} %param.6) | copy-start | bytes 3342340
  0.6 11.3 %collective-permute-start = (f32[128,128]{1,0:T(8,128)}, f32[128,128]{1,0:T(8,128)S(1)}, u32[]{:S(2)}, u32[]{:S(2)}) collective-permute-start(f32[128,128]{1,0:T(8,128)} %param.5), channel_id=1, source_target_pairs={{0,31},{1,0},{2,1},{3,2},{4,3},{5,4},{6,5},{7,6},{8,7},{9,8},{10,9... | collective-permute-start | bytes 196616 | tf_op jit(solution)/shard_map/ppermute | solution.py:10
  7.1 7.2 %collective-permute-start.1 = (f32[128,128]{1,0:T(8,128)}, f32[128,128]{1,0:T(8,128)S(1)}, u32[]{:S(2)}, u32[]{:S(2)}) collective-permute-start(f32[128,128]{1,0:T(8,128)} %param.5), channel_id=1, source_target_pairs={{0,30},{1,31},{2,0},{3,1},{4,2},{5,3},{6,4},{7,5},{8,6},{9,7},{10,... | collective-permute-start | bytes 196616 | tf_op jit(solution)/shard_map/ppermute | solution.py:10
  7.7 6.6 %collective-permute-start.2 = (f32[128,128]{1,0:T(8,128)}, f32[128,128]{1,0:T(8,128)S(1)}, u32[]{:S(2)}, u32[]{:S(2)}) collective-permute-start(f32[128,128]{1,0:T(8,128)} %param.5), channel_id=1, source_target_pairs={{0,29},{1,30},{2,31},{3,0},{4,1},{5,2},{6,3},{7,4},{8,5},{9,6},{10... | collective-permute-start | bytes 196616 | tf_op jit(solution)/shard_map/ppermute | solution.py:10
  8.0 9.0 %collective-permute-start.3 = (f32[128,128]{1,0:T(8,128)}, f32[128,128]{1,0:T(8,128)S(1)}, u32[]{:S(2)}, u32[]{:S(2)}) collective-permute-start(f32[128,128]{1,0:T(8,128)} %param.5), channel_id=1, source_target_pairs={{0,28},{1,29},{2,30},{3,31},{4,0},{5,1},{6,2},{7,3},{8,4},{9,5},{1... | collective-permute-start | bytes 196616 | tf_op jit(solution)/shard_map/ppermute | solution.py:10
  9.4 8.1 %collective-permute-start.4 = (f32[128,128]{1,0:T(8,128)}, f32[128,128]{1,0:T(8,128)S(1)}, u32[]{:S(2)}, u32[]{:S(2)}) collective-permute-start(f32[128,128]{1,0:T(8,128)} %param.5), channel_id=1, source_target_pairs={{0,27},{1,28},{2,29},{3,30},{4,31},{5,0},{6,1},{7,2},{8,3},{9,4},{... | collective-permute-start | bytes 196616 | tf_op jit(solution)/shard_map/ppermute | solution.py:10
  12.0 7.2 %collective-permute-start.5 = (f32[128,128]{1,0:T(8,128)}, f32[128,128]{1,0:T(8,128)S(1)}, u32[]{:S(2)}, u32[]{:S(2)}) collective-permute-start(f32[128,128]{1,0:T(8,128)} %param.5), channel_id=1, source_target_pairs={{0,26},{1,27},{2,28},{3,29},{4,30},{5,31},{6,0},{7,1},{8,2},{9,3},... | collective-permute-start | bytes 196616 | tf_op jit(solution)/shard_map/ppermute | solution.py:10
  14.2 5.0 %collective-permute-start.6 = (f32[128,128]{1,0:T(8,128)}, f32[128,128]{1,0:T(8,128)S(1)}, u32[]{:S(2)}, u32[]{:S(2)}) collective-permute-start(f32[128,128]{1,0:T(8,128)} %param.5), channel_id=1, source_target_pairs={{0,25},{1,26},{2,27},{3,28},{4,29},{5,30},{6,31},{7,0},{8,1},{9,2}... | collective-permute-start | bytes 196616 | tf_op jit(solution)/shard_map/ppermute | solution.py:10
  14.3 6.7 %collective-permute-start.7 = (f32[128,128]{1,0:T(8,128)}, f32[128,128]{1,0:T(8,128)S(1)}, u32[]{:S(2)}, u32[]{:S(2)}) collective-permute-start(f32[128,128]{1,0:T(8,128)} %param.5), channel_id=1, source_target_pairs={{0,24},{1,25},{2,26},{3,27},{4,28},{5,29},{6,30},{7,31},{8,0},{9,1... | collective-permute-start | bytes 196616 | tf_op jit(solution)/shard_map/ppermute | solution.py:10
  17.0 9.3 %collective-permute-start.8 = (f32[128,128]{1,0:T(8,128)}, f32[128,128]{1,0:T(8,128)S(1)}, u32[]{:S(2)}, u32[]{:S(2)}) collective-permute-start(f32[128,128]{1,0:T(8,128)} %param.5), channel_id=1, source_target_pairs={{0,16},{1,17},{2,18},{3,19},{4,20},{5,21},{6,22},{7,23},{8,24},{9,... | collective-permute-start | bytes 196616 | tf_op jit(solution)/shard_map/ppermute | solution.py:10
  17.5 8.8 %collective-permute-start.9 = (f32[128,128]{1,0:T(8,128)}, f32[128,128]{1,0:T(8,128)S(1)}, u32[]{:S(2)}, u32[]{:S(2)}) collective-permute-start(f32[128,128]{1,0:T(8,128)} %param.5), channel_id=1, source_target_pairs={{0,8},{1,9},{2,10},{3,11},{4,12},{5,13},{6,14},{7,15},{8,16},{9,17... | collective-permute-start | bytes 196616 | tf_op jit(solution)/shard_map/ppermute | solution.py:10
  40.6 1.4 %copy-start.1 = (f32[17,128,128]{1,0,2:T(8,128)S(1)}, f32[17,128,128]{1,0,2:T(8,128)}, u32[]{:S(2)}) copy-start(f32[17,128,128]{1,0,2:T(8,128)} %copy.18) | copy-start | bytes 3342340
  43.4 20.0 %copy-start.2 = (f32[128,128]{1,0:T(8,128)S(1)}, f32[128,128]{1,0:T(8,128)}, u32[]{:S(2)}) copy-start(f32[128,128]{1,0:T(8,128)} %param.5) | copy-start | bytes 196612
  43.5 8.0 %collective-permute-start.10 = (f32[128,128]{1,0:T(8,128)S(1)}, f32[128,128]{1,0:T(8,128)S(1)}, u32[]{:S(2)}, u32[]{:S(2)}) collective-permute-start(f32[128,128]{1,0:T(8,128)S(1)} %get-tuple-element.12), channel_id=1, source_target_pairs={{0,1},{1,2},{2,3},{3,4},{4,5},{5,6},{6,7},{7,8},{8,9},{9,10},{10,1... | collective-permute-start | bytes 196616 | tf_op jit(solution)/shard_map/ppermute | solution.py:10
  43.6 10.1 %collective-permute-start.11 = (f32[128,128]{1,0:T(8,128)S(1)}, f32[128,128]{1,0:T(8,128)S(1)}, u32[]{:S(2)}, u32[]{:S(2)}) collective-permute-start(f32[128,128]{1,0:T(8,128)S(1)} %get-tuple-element.21), channel_id=1, source_target_pairs={{0,2},{1,3},{2,4},{3,5},{4,6},{5,7},{6,8},{7,9},{8,10},{9,11},{10,... | collective-permute-start | bytes 196616 | tf_op jit(solution)/shard_map/ppermute | solution.py:10
  44.2 9.5 %collective-permute-start.12 = (f32[128,128]{1,0:T(8,128)S(1)}, f32[128,128]{1,0:T(8,128)S(1)}, u32[]{:S(2)}, u32[]{:S(2)}) collective-permute-start(f32[128,128]{1,0:T(8,128)S(1)} %get-tuple-element.20), channel_id=1, source_target_pairs={{0,3},{1,4},{2,5},{3,6},{4,7},{5,8},{6,9},{7,10},{8,11},{9,12},{10... | collective-permute-start | bytes 196616 | tf_op jit(solution)/shard_map/ppermute | solution.py:10
  45.9 8.7 %collective-permute-start.13 = (f32[128,128]{1,0:T(8,128)S(1)}, f32[128,128]{1,0:T(8,128)S(1)}, u32[]{:S(2)}, u32[]{:S(2)}) collective-permute-start(f32[128,128]{1,0:T(8,128)S(1)} %get-tuple-element.19), channel_id=1, source_target_pairs={{0,4},{1,5},{2,6},{3,7},{4,8},{5,9},{6,10},{7,11},{8,12},{9,13},{1... | collective-permute-start | bytes 196616 | tf_op jit(solution)/shard_map/ppermute | solution.py:10
  46.1 10.4 %collective-permute-start.14 = (f32[128,128]{1,0:T(8,128)S(1)}, f32[128,128]{1,0:T(8,128)S(1)}, u32[]{:S(2)}, u32[]{:S(2)}) collective-permute-start(f32[128,128]{1,0:T(8,128)S(1)} %get-tuple-element.18), channel_id=1, source_target_pairs={{0,5},{1,6},{2,7},{3,8},{4,9},{5,10},{6,11},{7,12},{8,13},{9,14},{... | collective-permute-start | bytes 196616 | tf_op jit(solution)/shard_map/ppermute | solution.py:10
  51.5 7.0 %collective-permute-start.15 = (f32[128,128]{1,0:T(8,128)S(1)}, f32[128,128]{1,0:T(8,128)S(1)}, u32[]{:S(2)}, u32[]{:S(2)}) collective-permute-start(f32[128,128]{1,0:T(8,128)S(1)} %get-tuple-element.17), channel_id=1, source_target_pairs={{0,6},{1,7},{2,8},{3,9},{4,10},{5,11},{6,12},{7,13},{8,14},{9,15},... | collective-permute-start | bytes 196616 | tf_op jit(solution)/shard_map/ppermute | solution.py:10
  53.7 5.7 %collective-permute-start.16 = (f32[128,128]{1,0:T(8,128)S(1)}, f32[128,128]{1,0:T(8,128)S(1)}, u32[]{:S(2)}, u32[]{:S(2)}) collective-permute-start(f32[128,128]{1,0:T(8,128)S(1)} %get-tuple-element.16), channel_id=1, source_target_pairs={{0,7},{1,8},{2,9},{3,10},{4,11},{5,12},{6,13},{7,14},{8,15},{9,16}... | collective-permute-start | bytes 196616 | tf_op jit(solution)/shard_map/ppermute | solution.py:10
  53.7 6.3 %collective-permute-start.17 = (f32[128,128]{1,0:T(8,128)S(1)}, f32[128,128]{1,0:T(8,128)S(1)}, u32[]{:S(2)}, u32[]{:S(2)}) collective-permute-start(f32[128,128]{1,0:T(8,128)S(1)} %get-tuple-element.15), channel_id=1, source_target_pairs={{0,8},{1,9},{2,10},{3,11},{4,12},{5,13},{6,14},{7,15},{8,16},{9,17... | collective-permute-start | bytes 196616 | tf_op jit(solution)/shard_map/ppermute | solution.py:10
  54.6 8.8 %collective-permute-start.18 = (f32[128,128]{1,0:T(8,128)S(1)}, f32[128,128]{1,0:T(8,128)S(1)}, u32[]{:S(2)}, u32[]{:S(2)}) collective-permute-start(f32[128,128]{1,0:T(8,128)S(1)} %get-tuple-element.14), channel_id=1, source_target_pairs={{0,16},{1,17},{2,18},{3,19},{4,20},{5,21},{6,22},{7,23},{8,24},{9,... | collective-permute-start | bytes 196616 | tf_op jit(solution)/shard_map/ppermute | solution.py:10
  56.5 6.9 %collective-permute-start.19 = (f32[128,128]{1,0:T(8,128)S(1)}, f32[128,128]{1,0:T(8,128)S(1)}, u32[]{:S(2)}, u32[]{:S(2)}) collective-permute-start(f32[128,128]{1,0:T(8,128)S(1)} %get-tuple-element.13), channel_id=1, source_target_pairs={{0,24},{1,25},{2,26},{3,27},{4,28},{5,29},{6,30},{7,31},{8,0},{9,1... | collective-permute-start | bytes 196616 | tf_op jit(solution)/shard_map/ppermute | solution.py:10
where the time goes:
time: 104 us
  blocking collectives  39.7 us (38%)
  starting transfers between devices  23.2 us (22%)
  waiting for transfers between devices  19.8 us (19%)
  local copies, waits for them, and re-layouts  9.39 us (9%)
  matrix products  9.03 us (9%)
  other arithmetic  1.93 us (2%)
    psum x1, blocking collectives, column_total(): return lax.psum(jnp.sum(values, axis=0), 'blk')  39.7 us
    ppermute x20, starting transfers between devices, shifted(): return lax.ppermute(value, axis, pairs)  23.2 us
    ppermute x20, waiting for transfers between devices, shifted(): return lax.ppermute(value, axis, pairs)  19.8 us
    dot_general x1, matrix products, per_device(): jnp.einsum('tji,tjr->tir', own_tiles, jnp.take(blocks, route_pairs[:, 0],...  4.26 us
    dot_general x1, matrix products, per_device(): jnp.einsum('tij,tjr->tir', own_tiles, jnp.take(blocks, route_pairs[:, 1],...  3.03 us
    dot_general x1, local copies, waits for them, and re-layouts, per_device(): jnp.einsum('tji,tjr->tir', own_tiles, jnp.take(blocks, route_pairs[:, 0],...  2.89 us
  transfers between devices with their start and end apart: 20, of which 8 were waited for; matrix products, arithmetic and copies ran while one was open for 2% of the time, Pallas kernels for 0%

commit v1 on v0

v1 whole, which is shorter than its diff:
```python
import functools

import jax
import jax.numpy as jnp
from jax import lax
from jax.experimental import pallas as pl
from jax.experimental.pallas import tpu as pltpu
from jax.sharding import PartitionSpec as P

EXTRA = 8
VMEM_BYTES = 32 * 1024 * 1024


def shifted(value, steps):
    count = lax.axis_size("blk")
    pairs = [(source, (source + steps) % count) for source in range(count)]
    return lax.ppermute(value, "blk", pairs)


def within_plane(value, window, chips_ahead):
    count = lax.axis_size("blk")
    pairs = []
    for source in range(count):
        plane, place = divmod(source, window)
        pairs.append((source, plane * window + (place + 2 * chips_ahead) % window))
    return lax.ppermute(value, "blk", pairs)


def core_partner(value):
    count = lax.axis_size("blk")
    return lax.ppermute(value, "blk", [(source, source ^ 1) for source in range(count)])


def split_two(values):
    high = values.astype(jnp.bfloat16)
    low = (values - high.astype(jnp.float32)).astype(jnp.bfloat16)
    return high, low


def product_kernel(planes, chips, pairs_ref, core_ref, own_ref, *refs):
    window = 2 * chips
    far = refs[: planes - 1]
    even = refs[planes - 1 : planes + chips - 2]
    odd_ref, tiles_ref = refs[planes + chips - 2 : planes + chips]
    outs = refs[planes + chips :]
    message_ref, kept_ref = outs[:2]
    far_out = outs[2:planes]
    whole, parts, total = outs[planes:]
    rows, cols = own_ref.shape
    core = core_ref[0]

    def put(place, values):
        whole[place] = values
        high, low = split_two(values)
        parts[place, :, :cols] = high
        parts[place, :, cols:] = low

    put(0, own_ref[...])
    for k in range(1, planes):
        put(window - 1 + k, far[k - 1][...])
    for m in range(1, chips):
        put(2 * m, even[m - 1][...])
        put(2 * m + 1 - 2 * core, odd_ref[(m - 1) * rows : m * rows, :])
    put(jnp.where(core == 0, 1, window - 1), odd_ref[(chips - 1) * rows : chips * rows, :])

    total[...] = jnp.zeros_like(total)
    slots = tiles_ref.shape[0]

    def product(tile, place):
        high, low = split_two(tile)
        both = jnp.dot(high, parts[place], preferred_element_type=jnp.float32)
        rest = jnp.dot(low, parts[place, :, :cols], preferred_element_type=jnp.float32)
        return both[:, :cols] + (both[:, cols:] + rest)

    def visit(t, mirrored):
        row_place, col_place = pairs_ref[t, 0], pairs_ref[t, 1]
        tile = tiles_ref[t]
        total[row_place] += product(tile, col_place)
        if mirrored:
            total[col_place] += product(tile.T, row_place)

    visit(0, False)
    if slots <= 32:
        for t in range(1, slots - 1):
            visit(t, True)
    else:
        lax.fori_loop(1, slots - 1, lambda t, c: (visit(t, True), c)[1], 0)
    visit(slots - 1, False)

    dots = jnp.zeros((1, cols), jnp.float32)
    for place in range(whole.shape[0]):
        dots = dots + jnp.sum(whole[place] * total[place], axis=0, keepdims=True)
    own = own_ref[...]
    norm = jnp.sum(own * own, axis=0, keepdims=True)
    for m in range(1, chips):
        message_ref[(m - 1) * rows : m * rows, :] = total[2 * m + 1 - 2 * core]
    message_ref[(chips - 1) * rows : chips * rows, :] = total[jnp.where(core == 0, 1, window - 1)]
    message_ref[chips * rows :, :] = jnp.concatenate([norm, dots, jnp.zeros((EXTRA - 2, cols), jnp.float32)], axis=0)
    for m in range(chips):
        kept_ref[m] = total[2 * m]
    kept_ref[chips] = total[window]
    for k in range(2, planes):
        far_out[k - 2][...] = total[window - 1 + k]


def pair_kernel(chips, core_ref, sent_ref, kept_ref, got_ref, *outs):
    messages = outs[: chips - 1]
    near_ref, next_ref, sums_ref = outs[chips - 1 :]
    rows = kept_ref.shape[1]
    core = core_ref[0]
    sums = sent_ref[chips * rows :, :] + got_ref[chips * rows :, :]
    for m in range(1, chips):
        messages[m - 1][:rows, :] = kept_ref[m] + got_ref[(m - 1) * rows : m * rows, :]
        messages[m - 1][rows:, :] = sums
    spare = got_ref[(chips - 1) * rows : chips * rows, :]
    near_ref[...] = kept_ref[0] + jnp.where(core == 1, spare, 0.0)
    next_ref[...] = kept_ref[chips] + jnp.where(core == 0, spare, 0.0)
    sums_ref[...] = sums


def plane_kernel(planes, chips, chip_ref, near_ref, next_ref, sums_ref, *refs):
    got = refs[: chips - 1]
    far = refs[chips - 1 : chips + planes - 3]
    near_out = refs[chips + planes - 3]
    messages = refs[chips + planes - 2 : chips + 2 * planes - 3]
    sums_out = refs[chips + 2 * planes - 3]
    rows = near_ref.shape[0]
    chip = chip_ref[0]
    near, ahead, sums = near_ref[...], next_ref[...], sums_ref[...]
    for m in range(1, chips):
        block = got[m - 1][:rows, :]
        near = near + jnp.where(chip >= m, block, 0.0)
        ahead = ahead + jnp.where(chip >= m, 0.0, block)
        sums = sums + got[m - 1][rows:, :]
    near_out[...] = near
    sums_out[...] = sums
    messages[0][:rows, :] = ahead
    for k in range(2, planes):
        messages[k - 1][:rows, :] = far[k - 2][...]
    for k in range(1, planes):
        messages[k - 1][rows:, :] = sums


def final_kernel(planes, right_ref, near_ref, sums_ref, *refs):
    got = refs[: planes - 1]
    solution_ref, residual_ref = refs[planes - 1 :]
    rows = near_ref.shape[0]
    image, sums = near_ref[...], sums_ref[...]
    for k in range(1, planes):
        image = image + got[k - 1][:rows, :]
        sums = sums + got[k - 1][rows:, :]
    step_len = sums[0:1, :] / sums[1:2, :]
    right = right_ref[...]
    solution_ref[...] = step_len * right
    residual_ref[...] = right - step_len * image


def call(kernel, smem, operands, outs, scratch=()):
    vmem = pl.BlockSpec(memory_space=pltpu.VMEM)
    return pl.pallas_call(
        kernel,
        in_specs=[pl.BlockSpec(memory_space=pltpu.SMEM)] * len(smem) + [vmem] * len(operands),
        out_specs=[vmem] * len(outs),
        out_shape=[jax.ShapeDtypeStruct(shape, jnp.float32) for shape in outs],
        scratch_shapes=list(scratch),
        compiler_params=pltpu.CompilerParams(vmem_limit_bytes=VMEM_BYTES),
    )(*smem, *operands)


def per_device(right_side, kernel_tiles, route_pairs):
    count = lax.axis_size("blk")
    window = max(8, min(16, count // 8))
    planes, chips = count // window, window // 2
    rows, cols = right_side.shape
    cover_len = window + planes - 1
    place = lax.axis_index("blk")
    core = (place % 2).astype(jnp.int32)
    chip = (place % window // 2).astype(jnp.int32)

    far = [shifted(right_side, -k * window) for k in range(1, planes)]
    even = []
    for m in range(1, chips):
        sent = jnp.where(chip >= m, right_side, far[0])
        even.append(within_plane(sent, window, -m))
    odd = core_partner(jnp.concatenate(even + [jnp.where(core == 0, far[0], right_side)], axis=0))

    block, marked = (rows, cols), (rows + EXTRA, cols)
    sent, kept, *far_out = call(
        functools.partial(product_kernel, planes, chips),
        (route_pairs, core[None]),
        (right_side, *far, *even, odd, kernel_tiles[0]),
        [(chips * rows + EXTRA, cols), (chips + 1, rows, cols)] + [block] * (planes - 2),
        (
            pltpu.VMEM((cover_len, rows, cols), jnp.float32),
            pltpu.VMEM((cover_len, rows, 2 * cols), jnp.bfloat16),
            pltpu.VMEM((cover_len, rows, cols), jnp.float32),
        ),
    )
    got = core_partner(sent)
    *messages, near, ahead, sums = call(
        functools.partial(pair_kernel, chips),
        (core[None],),
        (sent, kept, got),
        [marked] * (chips - 1) + [block, block, (EXTRA, cols)],
    )
    got = [within_plane(messages[m - 1], window, m) for m in range(1, chips)]
    near, *messages, sums = call(
        functools.partial(plane_kernel, planes, chips),
        (chip[None],),
        (near, ahead, sums, *got, *far_out),
        [block] + [marked] * (planes - 1) + [(EXTRA, cols)],
    )
    got = [shifted(messages[k - 1], k * window) for k in range(1, planes)]
    solution, residual = call(
        functools.partial(final_kernel, planes),
        (),
        (right_side, near, sums, *got),
        [block, block],
    )
    return solution, residual


def solution(mesh):
    return jax.shard_map(
        per_device,
        mesh=mesh,
        in_specs=(P("blk", None), P("blk", None, None, None), P()),
        out_specs=(P("blk", None), P("blk", None)),
        check_vma=False,
    )
```

time: 104 us -> 48.4 us (0.47)
  blocking collectives: 39.7 us -> 0 us
  matrix products: 9.03 us -> 0 us
  local copies, waits for them, and re-layouts: 9.39 us -> 2.86 us
  Pallas kernels: 0 us -> 2.8 us
  starting transfers between devices: 23.2 us -> 21.8 us
  other arithmetic: 1.93 us -> 0.88 us
    psum x1 -> x0, blocking collectives: 39.7 us -> none  [column_total(): return lax.psum(jnp.sum(values, axis=0), 'blk')]
    dot_general x4 -> x0, matrix products: 9.03 us -> none  [the longest x1 4.26 us: per_device(): jnp.einsum('tji,tjr->tir', own_tiles, jnp.take(blocks, route_pairs[:, 0],...]
    dot_general x2 -> x0, local copies, waits for them, and re-layouts: 4.68 us -> none  [the longest x1 2.89 us: per_device(): jnp.einsum('tji,tjr->tir', own_tiles, jnp.take(blocks, route_pairs[:, 0],...]
    pallas_call x0 -> x4, Pallas kernels: none -> 2.8 us  [call(): pl.pallas_call(kernel, in_specs=[pl.BlockSpec(memory_space=pltpu.SMEM)] *...]
    gather x2 -> x0, local copies, waits for them, and re-layouts: 2.26 us -> none  [the longest x1 1.64 us: per_device(): jnp.take(blocks, route_pairs[:, 0], axis=0)]
    ppermute x20 -> x14, starting transfers between devices: 23.2 us -> 21.8 us  [the longest x6 13.6 us: shifted(): return lax.ppermute(value, 'blk', pairs)]
    unnamed x16 -> x7, local copies, waits for them, and re-layouts: 1.63 us -> 2.86 us
    ppermute x20 -> x14, waiting for transfers between devices: 19.8 us -> 19.1 us  [the longest x6 11 us: shifted(): return lax.ppermute(value, 'blk', pairs)]
  transfers between devices with their start and end apart: 20 -> 14, of which waited for: 8 -> 12; matrix products, arithmetic and copies ran while one was open for 2% -> 2% of each run, Pallas kernels for 0% -> 0%
where the time goes in v1:
time: 48.4 us; the launch traced here: 48.1 us
  starting transfers between devices  21.8 us (45%)
  waiting for transfers between devices  19.1 us (39%)
  local copies, waits for them, and re-layouts  2.86 us (6%)
  Pallas kernels  2.8 us (6%)
  other arithmetic  0.88 us (2%)
  between operations  0.69 us (1%)
    ppermute x6, starting transfers between devices, shifted(): return lax.ppermute(value, 'blk', pairs)  13.6 us
    ppermute x6, waiting for transfers between devices, shifted(): return lax.ppermute(value, 'blk', pairs)  11 us
    ppermute x6, starting transfers between devices, within_plane(): return lax.ppermute(value, 'blk', pairs)  7.98 us
    ppermute x6, waiting for transfers between devices, within_plane(): return lax.ppermute(value, 'blk', pairs)  6.6 us
    unnamed x7, local copies, waits for them, and re-layouts  2.86 us
    pallas_call x4, Pallas kernels, call(): pl.pallas_call(kernel, in_specs=[pl.BlockSpec(memory_space=pltpu.SMEM)] *...  2.8 us
    ppermute x2, waiting for transfers between devices, core_partner(): lax.ppermute(value, 'blk', [(source, source ^ 1) for source in range(coun...  1.48 us
  transfers between devices with their start and end apart: 14, of which 12 were waited for; matrix products, arithmetic and copies ran while one was open for 2% of the time, Pallas kernels for 0%

profile of v1, /device:TPU:0, one launch (start us, length us, event | category | flops | bytes accessed | tf_op | source)
XLA Modules:
  0.0 48.1 jit_solution(8062165523300348187)
XLA Ops:
  0.6 5.1 %collective-permute-start = (f32[128,128]{1,0:T(8,128)}, f32[128,128]{1,0:T(8,128)S(1)}, u32[]{:S(2)}, u32[]{:S(2)}) collective-permute-start(f32[128,128]{1,0:T(8,128)} %right_ref.1), channel_id=1, source_target_pairs={{0,24},{1,25},{2,26},{3,27},{4,28},{5,29},{6,30},{7,31},{8,0},{9,1... | collective-permute-start | bytes 196616 | tf_op jit(solution)/shard_map/ppermute | solution.py:17
  5.7 2.2 %collective-permute-done.refs_0_ = f32[128,128]{1,0:T(8,128)S(1)} collective-permute-done((f32[128,128]{1,0:T(8,128)}, f32[128,128]{1,0:T(8,128)S(1)}, u32[]{:S(2)}, u32[]{:S(2)}) %collective-permute-start) | collective-permute-done | bytes 65568 | tf_op jit(solution)/shard_map/ppermute | solution.py:17
  8.0 0.9 %broadcast_select_fusion = (f32[128,128]{1,0:T(8,128)S(1)}, f32[128,128]{1,0:T(8,128)S(1)}, f32[128,128]{1,0:T(8,128)S(1)}, f32[128,128]{1,0:T(8,128)S(1)}) fusion(f32[128,128]{1,0:T(8,128)S(1)} %collective-permute-done.refs_0_, f32[128,128]{1,0:T(8,128)} %right_ref.1, pred[]{:T(512)S(6)} %eq.6, pred[]{:T(512)S(6)} %ge.11, pred[]{:T(512)S(6)} %ge.10, pred[]{:T(512)S(6)} %ge.9), kind=kLoop, calls=%fused_computation.1 | loop fusion | flops 65536 | bytes 393220 | tf_op jit(solution)/shard_map/jit(_where)/select_n | solution.py:185
  8.8 1.5 %collective-permute-start.5 = (f32[128,128]{1,0:T(8,128)S(1)}, f32[128,128]{1,0:T(8,128)S(1)}, u32[]{:S(2)}, u32[]{:S(2)}) collective-permute-start(f32[128,128]{1,0:T(8,128)S(1)} %get-tuple-element.33), channel_id=1, source_target_pairs={{0,2},{1,3},{2,4},{3,5},{4,6},{5,7},{6,0},{7,1},{8,10},{9,11},{10,... | collective-permute-start | bytes 196616 | tf_op jit(solution)/shard_map/ppermute | solution.py:26
  10.4 1.5 %collective-permute-start.4 = (f32[128,128]{1,0:T(8,128)S(1)}, f32[128,128]{1,0:T(8,128)S(1)}, u32[]{:S(2)}, u32[]{:S(2)}) collective-permute-start(f32[128,128]{1,0:T(8,128)S(1)} %get-tuple-element.34), channel_id=1, source_target_pairs={{0,4},{1,5},{2,6},{3,7},{4,0},{5,1},{6,2},{7,3},{8,12},{9,13},{10,... | collective-permute-start | bytes 196616 | tf_op jit(solution)/shard_map/ppermute | solution.py:26
  11.9 1.4 %collective-permute-start.3 = (f32[128,128]{1,0:T(8,128)S(1)}, f32[128,128]{1,0:T(8,128)S(1)}, u32[]{:S(2)}, u32[]{:S(2)}) collective-permute-start(f32[128,128]{1,0:T(8,128)S(1)} %get-tuple-element.35), channel_id=1, source_target_pairs={{0,6},{1,7},{2,0},{3,1},{4,2},{5,3},{6,4},{7,5},{8,14},{9,15},{10,... | collective-permute-start | bytes 196616 | tf_op jit(solution)/shard_map/ppermute | solution.py:26
  13.3 1.0 %collective-permute-done.5.refs_5_ = f32[128,128]{1,0:T(8,128)S(1)} collective-permute-done((f32[128,128]{1,0:T(8,128)S(1)}, f32[128,128]{1,0:T(8,128)S(1)}, u32[]{:S(2)}, u32[]{:S(2)}) %collective-permute-start.5) | collective-permute-done | bytes 65568 | tf_op jit(solution)/shard_map/ppermute | solution.py:26
  14.3 0.7 %collective-permute-done.4.refs_4_ = f32[128,128]{1,0:T(8,128)S(1)} collective-permute-done((f32[128,128]{1,0:T(8,128)S(1)}, f32[128,128]{1,0:T(8,128)S(1)}, u32[]{:S(2)}, u32[]{:S(2)}) %collective-permute-start.4) | collective-permute-done | bytes 65568 | tf_op jit(solution)/shard_map/ppermute | solution.py:26
  14.9 1.2 %collective-permute-done.3.refs_3_ = f32[128,128]{1,0:T(8,128)S(1)} collective-permute-done((f32[128,128]{1,0:T(8,128)S(1)}, f32[128,128]{1,0:T(8,128)S(1)}, u32[]{:S(2)}, u32[]{:S(2)}) %collective-permute-start.3) | collective-permute-done | bytes 65568 | tf_op jit(solution)/shard_map/ppermute | solution.py:26
  16.2 0.1 collective-permute-start.6
  16.2 0.3 collective-permute-start.2
  16.5 4.4 %collective-permute-start.1 = (f32[128,128]{1,0:T(8,128)}, f32[128,128]{1,0:T(8,128)S(1)}, u32[]{:S(2)}, u32[]{:S(2)}) collective-permute-start(f32[128,128]{1,0:T(8,128)} %right_ref.1), channel_id=1, source_target_pairs={{0,16},{1,17},{2,18},{3,19},{4,20},{5,21},{6,22},{7,23},{8,24},{9,... | collective-permute-start | bytes 196616 | tf_op jit(solution)/shard_map/ppermute | solution.py:17
  20.9 0.8 %copy.5.pairs_ref = s32[17,2]{1,0:T(8,128)S(1)} copy(s32[17,2]{0,1:T(2,128)} %param.5) | data formatting | bytes 272 | tf_op args[2]
  21.7 1.9 %collective-permute-done.2.refs_2_ = f32[128,128]{1,0:T(8,128)S(1)} collective-permute-done((f32[128,128]{1,0:T(8,128)}, f32[128,128]{1,0:T(8,128)S(1)}, u32[]{:S(2)}, u32[]{:S(2)}) %collective-permute-start.2) | collective-permute-done | bytes 65568 | tf_op jit(solution)/shard_map/ppermute | solution.py:17
  23.6 2.5 %collective-permute-done.1.refs_1_ = f32[128,128]{1,0:T(8,128)S(1)} collective-permute-done((f32[128,128]{1,0:T(8,128)}, f32[128,128]{1,0:T(8,128)S(1)}, u32[]{:S(2)}, u32[]{:S(2)}) %collective-permute-start.1) | collective-permute-done | bytes 65568 | tf_op jit(solution)/shard_map/ppermute | solution.py:17
  26.1 0.0 collective-permute-done.6.refs_6_
  26.1 0.0 copy-start
  26.1 1.2 %copy-done = f32[1,17,128,128]{3,2,1,0:T(8,128)S(1)} copy-done((f32[1,17,128,128]{3,2,1,0:T(8,128)S(1)}, f32[1,17,128,128]{3,2,1,0:T(8,128)}, u32[]{:S(2)}) %copy-start) | copy-done | bytes 1114136
  27.3 0.0 copy-start.1
  27.3 0.8 %copy-done.1 = f32[128,128]{1,0:T(8,128)S(1)} copy-done((f32[128,128]{1,0:T(8,128)S(1)}, f32[128,128]{1,0:T(8,128)}, u32[]{:S(2)}) %copy-start.1) | copy-done | bytes 65560
  28.2 2.0 %shard_map.50 = (f32[520,128]{1,0:T(8,128)S(1)}, f32[5,128,128]{2,1,0:T(8,128)S(1)}, f32[128,128]{1,0:T(8,128)S(1)}, f32[128,128]{1,0:T(8,128)S(1)}) custom-call(s32[17,2]{1,0:T(8,128)S(1)} %copy.5.pairs_ref, s32[1]{0:T(128)} %bitcast.1.core_ref, f32[128,128]{1,0:T(8,128)S(1)} %copy-done.1, f32[128,128]{1,0:T(8,128)S(1)} %collective-permute-done.refs_0_, ...), custom_call_target="tpu_custom_call" | custom-call | tf_op jit(solution)/shard_map/pallas_call | solution.py:160
  30.2 0.0 copy-start.2
  30.2 0.1 collective-permute-start.7
  30.4 1.5 %collective-permute-done.7.got_ref = f32[520,128]{1,0:T(8,128)S(1)} collective-permute-done((f32[520,128]{1,0:T(8,128)S(1)}, f32[520,128]{1,0:T(8,128)S(1)}, u32[]{:S(2)}, u32[]{:S(2)}) %collective-permute-start.7) | collective-permute-done | bytes 266272 | tf_op jit(solution)/shard_map/ppermute | solution.py:31
  31.9 1.4 %collective-permute-start.8 = (f32[136,128]{1,0:T(8,128)S(1)}, f32[136,128]{1,0:T(8,128)S(1)}, u32[]{:S(2)}, u32[]{:S(2)}) collective-permute-start(f32[136,128]{1,0:T(8,128)S(1)} %get-tuple-element.22), channel_id=1, source_target_pairs={{0,2},{1,3},{2,4},{3,5},{4,6},{5,7},{6,0},{7,1},{8,10},{9,11},{10,... | collective-permute-start | bytes 208904 | tf_op jit(solution)/shard_map/ppermute | solution.py:26
  33.3 1.5 %collective-permute-start.9 = (f32[136,128]{1,0:T(8,128)S(1)}, f32[136,128]{1,0:T(8,128)S(1)}, u32[]{:S(2)}, u32[]{:S(2)}) collective-permute-start(f32[136,128]{1,0:T(8,128)S(1)} %get-tuple-element.23), channel_id=1, source_target_pairs={{0,4},{1,5},{2,6},{3,7},{4,0},{5,1},{6,2},{7,3},{8,12},{9,13},{10,... | collective-permute-start | bytes 208904 | tf_op jit(solution)/shard_map/ppermute | solution.py:26
  34.8 0.5 %collective-permute-start.10 = (f32[136,128]{1,0:T(8,128)S(1)}, f32[136,128]{1,0:T(8,128)S(1)}, u32[]{:S(2)}, u32[]{:S(2)}) collective-permute-start(f32[136,128]{1,0:T(8,128)S(1)} %get-tuple-element.24), channel_id=1, source_target_pairs={{0,6},{1,7},{2,0},{3,1},{4,2},{5,3},{6,4},{7,5},{8,14},{9,15},{10,... | collective-permute-start | bytes 208904 | tf_op jit(solution)/shard_map/ppermute | solution.py:26
  35.4 2.0 %collective-permute-done.8.refs_0_ = f32[136,128]{1,0:T(8,128)S(1)} collective-permute-done((f32[136,128]{1,0:T(8,128)S(1)}, f32[136,128]{1,0:T(8,128)S(1)}, u32[]{:S(2)}, u32[]{:S(2)}) %collective-permute-start.8) | collective-permute-done | bytes 69664 | tf_op jit(solution)/shard_map/ppermute | solution.py:26
  37.4 1.1 %collective-permute-done.9.refs_1_ = f32[136,128]{1,0:T(8,128)S(1)} collective-permute-done((f32[136,128]{1,0:T(8,128)S(1)}, f32[136,128]{1,0:T(8,128)S(1)}, u32[]{:S(2)}, u32[]{:S(2)}) %collective-permute-start.9) | collective-permute-done | bytes 69664 | tf_op jit(solution)/shard_map/ppermute | solution.py:26
  38.5 0.6 %collective-permute-done.10.refs_2_ = f32[136,128]{1,0:T(8,128)S(1)} collective-permute-done((f32[136,128]{1,0:T(8,128)S(1)}, f32[136,128]{1,0:T(8,128)S(1)}, u32[]{:S(2)}, u32[]{:S(2)}) %collective-permute-start.10) | collective-permute-done | bytes 69664 | tf_op jit(solution)/shard_map/ppermute | solution.py:26
  39.2 0.1 collective-permute-start.11
  39.2 1.8 %collective-permute-start.12 = (f32[136,128]{1,0:T(8,128)S(1)}, f32[136,128]{1,0:T(8,128)S(1)}, u32[]{:S(2)}, u32[]{:S(2)}) collective-permute-start(f32[136,128]{1,0:T(8,128)S(1)} %get-tuple-element.30), channel_id=1, source_target_pairs={{0,16},{1,17},{2,18},{3,19},{4,20},{5,21},{6,22},{7,23},{8,24},{9,... | collective-permute-start | bytes 208904 | tf_op jit(solution)/shard_map/ppermute | solution.py:17
  41.1 2.0 %collective-permute-start.13 = (f32[136,128]{1,0:T(8,128)S(1)}, f32[136,128]{1,0:T(8,128)S(1)}, u32[]{:S(2)}, u32[]{:S(2)}) collective-permute-start(f32[136,128]{1,0:T(8,128)S(1)} %get-tuple-element.31), channel_id=1, source_target_pairs={{0,24},{1,25},{2,26},{3,27},{4,28},{5,29},{6,30},{7,31},{8,0},{9,1... | collective-permute-start | bytes 208904 | tf_op jit(solution)/shard_map/ppermute | solution.py:17
  43.1 3.0 %collective-permute-done.11.refs_0_ = f32[136,128]{1,0:T(8,128)S(1)} collective-permute-done((f32[136,128]{1,0:T(8,128)S(1)}, f32[136,128]{1,0:T(8,128)S(1)}, u32[]{:S(2)}, u32[]{:S(2)}) %collective-permute-start.11) | collective-permute-done | bytes 69664 | tf_op jit(solution)/shard_map/ppermute | solution.py:17
  46.0 1.4 %collective-permute-done.12.refs_1_ = f32[136,128]{1,0:T(8,128)S(1)} collective-permute-done((f32[136,128]{1,0:T(8,128)S(1)}, f32[136,128]{1,0:T(8,128)S(1)}, u32[]{:S(2)}, u32[]{:S(2)}) %collective-permute-start.12) | collective-permute-done | bytes 69664 | tf_op jit(solution)/shard_map/ppermute | solution.py:17
  47.4 0.0 collective-permute-done.13.refs_2_
  47.4 0.0 copy-done.2
  47.4 0.7 %shard_map.53 = (f32[128,128]{1,0:T(8,128)}, f32[128,128]{1,0:T(8,128)}) custom-call(f32[128,128]{1,0:T(8,128)S(1)} %copy-done.2, f32[128,128]{1,0:T(8,128)S(1)} %get-tuple-element.27.near_ref, f32[8,128]{1,0:T(8,128)S(1)} %get-tuple-element.28.sums_ref, f32[136,128]{1,0:T(8,128)S(1)} %collective-permute-done.11.refs_0_, ...), custom_call_target="tpu_custom_call" | custom-call | tf_op jit(solution)/shard_map/pallas_call | solution.py:160
  (3 shorter events, 0.1 us)
Async XLA Ops:
  0.6 7.3 %collective-permute-start = (f32[128,128]{1,0:T(8,128)}, f32[128,128]{1,0:T(8,128)S(1)}, u32[]{:S(2)}, u32[]{:S(2)}) collective-permute-start(f32[128,128]{1,0:T(8,128)} %right_ref.1), channel_id=1, source_target_pairs={{0,24},{1,25},{2,26},{3,27},{4,28},{5,29},{6,30},{7,31},{8,0},{9,1... | collective-permute-start | bytes 196616 | tf_op jit(solution)/shard_map/ppermute | solution.py:17
  8.8 5.5 %collective-permute-start.5 = (f32[128,128]{1,0:T(8,128)S(1)}, f32[128,128]{1,0:T(8,128)S(1)}, u32[]{:S(2)}, u32[]{:S(2)}) collective-permute-start(f32[128,128]{1,0:T(8,128)S(1)} %get-tuple-element.33), channel_id=1, source_target_pairs={{0,2},{1,3},{2,4},{3,5},{4,6},{5,7},{6,0},{7,1},{8,10},{9,11},{10,... | collective-permute-start | bytes 196616 | tf_op jit(solution)/shard_map/ppermute | solution.py:26
  10.4 4.6 %collective-permute-start.4 = (f32[128,128]{1,0:T(8,128)S(1)}, f32[128,128]{1,0:T(8,128)S(1)}, u32[]{:S(2)}, u32[]{:S(2)}) collective-permute-start(f32[128,128]{1,0:T(8,128)S(1)} %get-tuple-element.34), channel_id=1, source_target_pairs={{0,4},{1,5},{2,6},{3,7},{4,0},{5,1},{6,2},{7,3},{8,12},{9,13},{10,... | collective-permute-start | bytes 196616 | tf_op jit(solution)/shard_map/ppermute | solution.py:26
  11.9 4.3 %collective-permute-start.3 = (f32[128,128]{1,0:T(8,128)S(1)}, f32[128,128]{1,0:T(8,128)S(1)}, u32[]{:S(2)}, u32[]{:S(2)}) collective-permute-start(f32[128,128]{1,0:T(8,128)S(1)} %get-tuple-element.35), channel_id=1, source_target_pairs={{0,6},{1,7},{2,0},{3,1},{4,2},{5,3},{6,4},{7,5},{8,14},{9,15},{10,... | collective-permute-start | bytes 196616 | tf_op jit(solution)/shard_map/ppermute | solution.py:26
  16.2 9.9 %collective-permute-start.6 = (f32[512,128]{1,0:T(8,128)S(1)}, f32[512,128]{1,0:T(8,128)S(1)}, u32[]{:S(2)}, u32[]{:S(2)}) collective-permute-start(f32[512,128]{1,0:T(8,128)S(1)} %pad_maximum_fusion), channel_id=1, source_target_pairs={{0,1},{1,0},{2,3},{3,2},{4,5},{5,4},{6,7},{7,6},{8,9},{9,8},{10,11... | collective-permute-start | bytes 786440 | tf_op jit(solution)/shard_map/ppermute | solution.py:31
  16.2 7.4 %collective-permute-start.2 = (f32[128,128]{1,0:T(8,128)}, f32[128,128]{1,0:T(8,128)S(1)}, u32[]{:S(2)}, u32[]{:S(2)}) collective-permute-start(f32[128,128]{1,0:T(8,128)} %right_ref.1), channel_id=1, source_target_pairs={{0,8},{1,9},{2,10},{3,11},{4,12},{5,13},{6,14},{7,15},{8,16},{9,17... | collective-permute-start | bytes 196616 | tf_op jit(solution)/shard_map/ppermute | solution.py:17
  16.5 9.5 %collective-permute-start.1 = (f32[128,128]{1,0:T(8,128)}, f32[128,128]{1,0:T(8,128)S(1)}, u32[]{:S(2)}, u32[]{:S(2)}) collective-permute-start(f32[128,128]{1,0:T(8,128)} %right_ref.1), channel_id=1, source_target_pairs={{0,16},{1,17},{2,18},{3,19},{4,20},{5,21},{6,22},{7,23},{8,24},{9,... | collective-permute-start | bytes 196616 | tf_op jit(solution)/shard_map/ppermute | solution.py:17
  26.1 1.2 %copy-start = (f32[1,17,128,128]{3,2,1,0:T(8,128)S(1)}, f32[1,17,128,128]{3,2,1,0:T(8,128)}, u32[]{:S(2)}) copy-start(f32[1,17,128,128]{3,2,1,0:T(8,128)} %param.4) | copy-start | bytes 3342340
  27.3 0.8 %copy-start.1 = (f32[128,128]{1,0:T(8,128)S(1)}, f32[128,128]{1,0:T(8,128)}, u32[]{:S(2)}) copy-start(f32[128,128]{1,0:T(8,128)} %right_ref.1) | copy-start | bytes 196612
  30.2 17.2 %copy-start.2 = (f32[128,128]{1,0:T(8,128)S(1)}, f32[128,128]{1,0:T(8,128)}, u32[]{:S(2)}) copy-start(f32[128,128]{1,0:T(8,128)} %right_ref.1) | copy-start | bytes 196612
  30.2 1.6 %collective-permute-start.7 = (f32[520,128]{1,0:T(8,128)S(1)}, f32[520,128]{1,0:T(8,128)S(1)}, u32[]{:S(2)}, u32[]{:S(2)}) collective-permute-start(f32[520,128]{1,0:T(8,128)S(1)} %get-tuple-element.17.sent_ref), channel_id=1, source_target_pairs={{0,1},{1,0},{2,3},{3,2},{4,5},{5,4},{6,7},{7,6},{8,9},{9,8},{10,11... | collective-permute-start | bytes 798728 | tf_op jit(solution)/shard_map/ppermute | solution.py:31
  31.9 5.5 %collective-permute-start.8 = (f32[136,128]{1,0:T(8,128)S(1)}, f32[136,128]{1,0:T(8,128)S(1)}, u32[]{:S(2)}, u32[]{:S(2)}) collective-permute-start(f32[136,128]{1,0:T(8,128)S(1)} %get-tuple-element.22), channel_id=1, source_target_pairs={{0,2},{1,3},{2,4},{3,5},{4,6},{5,7},{6,0},{7,1},{8,10},{9,11},{10,... | collective-permute-start | bytes 208904 | tf_op jit(solution)/shard_map/ppermute | solution.py:26
  33.3 5.2 %collective-permute-start.9 = (f32[136,128]{1,0:T(8,128)S(1)}, f32[136,128]{1,0:T(8,128)S(1)}, u32[]{:S(2)}, u32[]{:S(2)}) collective-permute-start(f32[136,128]{1,0:T(8,128)S(1)} %get-tuple-element.23), channel_id=1, source_target_pairs={{0,4},{1,5},{2,6},{3,7},{4,0},{5,1},{6,2},{7,3},{8,12},{9,13},{10,... | collective-permute-start | bytes 208904 | tf_op jit(solution)/shard_map/ppermute | solution.py:26
  34.8 4.3 %collective-permute-start.10 = (f32[136,128]{1,0:T(8,128)S(1)}, f32[136,128]{1,0:T(8,128)S(1)}, u32[]{:S(2)}, u32[]{:S(2)}) collective-permute-start(f32[136,128]{1,0:T(8,128)S(1)} %get-tuple-element.24), channel_id=1, source_target_pairs={{0,6},{1,7},{2,0},{3,1},{4,2},{5,3},{6,4},{7,5},{8,14},{9,15},{10,... | collective-permute-start | bytes 208904 | tf_op jit(solution)/shard_map/ppermute | solution.py:26
  39.2 6.8 %collective-permute-start.11 = (f32[136,128]{1,0:T(8,128)S(1)}, f32[136,128]{1,0:T(8,128)S(1)}, u32[]{:S(2)}, u32[]{:S(2)}) collective-permute-start(f32[136,128]{1,0:T(8,128)S(1)} %get-tuple-element.29), channel_id=1, source_target_pairs={{0,8},{1,9},{2,10},{3,11},{4,12},{5,13},{6,14},{7,15},{8,16},{9,17... | collective-permute-start | bytes 208904 | tf_op jit(solution)/shard_map/ppermute | solution.py:17
  39.2 8.2 %collective-permute-start.12 = (f32[136,128]{1,0:T(8,128)S(1)}, f32[136,128]{1,0:T(8,128)S(1)}, u32[]{:S(2)}, u32[]{:S(2)}) collective-permute-start(f32[136,128]{1,0:T(8,128)S(1)} %get-tuple-element.30), channel_id=1, source_target_pairs={{0,16},{1,17},{2,18},{3,19},{4,20},{5,21},{6,22},{7,23},{8,24},{9,... | collective-permute-start | bytes 208904 | tf_op jit(solution)/shard_map/ppermute | solution.py:17
  41.1 6.3 %collective-permute-start.13 = (f32[136,128]{1,0:T(8,128)S(1)}, f32[136,128]{1,0:T(8,128)S(1)}, u32[]{:S(2)}, u32[]{:S(2)}) collective-permute-start(f32[136,128]{1,0:T(8,128)S(1)} %get-tuple-element.31), channel_id=1, source_target_pairs={{0,24},{1,25},{2,26},{3,27},{4,28},{5,29},{6,30},{7,31},{8,0},{9,1... | collective-permute-start | bytes 208904 | tf_op jit(solution)/shard_map/ppermute | solution.py:17

commit v2 on v0

v2 whole, which is shorter than its diff:
```python
import functools

import jax
import jax.numpy as jnp
from jax import lax
from jax.experimental import pallas as pl
from jax.experimental.pallas import tpu as pltpu
from jax.sharding import PartitionSpec as P

EXTRA = 8
VMEM_BYTES = 48 * 1024 * 1024


def split_two(values):
    high = values.astype(jnp.bfloat16)
    low = (values - high.astype(jnp.float32)).astype(jnp.bfloat16)
    return high, low


def product_kernel(cover, pairs_ref, place_ref, blocks_ref, tiles_ref, out_ref, parts):
    count, marked, cols = out_ref.shape
    rows = marked - EXTRA
    place = place_ref[0]
    slots = tiles_ref.shape[0]

    def at(offset):
        return lax.rem(place + offset, count)

    def block_of(position):
        window = len(cover) - (count // (cover[-1] - cover[-2])) + 1
        offset = jnp.where(position < window, position, (position - window + 1) * window)
        return at(offset)

    out_ref[...] = jnp.zeros_like(out_ref)
    for position, offset in enumerate(cover):
        high, low = split_two(blocks_ref[at(offset)])
        parts[position, :, :cols] = high
        parts[position, :, cols:] = low

    def product(tile, position):
        high, low = split_two(tile)
        both = jnp.dot(high, parts[position], preferred_element_type=jnp.float32)
        rest = jnp.dot(low, parts[position, :, :cols], preferred_element_type=jnp.float32)
        return both[:, :cols] + (both[:, cols:] + rest)

    def visit(t, mirrored):
        row_place, col_place = pairs_ref[0, t], pairs_ref[1, t]
        tile = tiles_ref[t]
        out_ref[block_of(row_place), :rows, :] += product(tile, col_place)
        if mirrored:
            out_ref[block_of(col_place), :rows, :] += product(tile.T, row_place)

    visit(0, False)
    if slots <= 32:
        for t in range(1, slots - 1):
            visit(t, True)
    else:
        lax.fori_loop(1, slots - 1, lambda t, c: (visit(t, True), c)[1], 0)
    visit(slots - 1, False)

    dots = jnp.zeros((1, cols), jnp.float32)
    for offset in cover:
        block = at(offset)
        dots = dots + jnp.sum(blocks_ref[block] * out_ref[block, :rows, :], axis=0, keepdims=True)
    own = blocks_ref[place]
    norm = jnp.sum(own * own, axis=0, keepdims=True)
    sums = jnp.concatenate([norm, dots, jnp.zeros((EXTRA - 2, cols), jnp.float32)], axis=0)
    for block in range(count):
        out_ref[block, rows:, :] = sums


def final_kernel(right_ref, image_ref, solution_ref, residual_ref):
    rows = right_ref.shape[0]
    step_len = image_ref[rows : rows + 1, :] / image_ref[rows + 1 : rows + 2, :]
    right = right_ref[...]
    solution_ref[...] = step_len * right
    residual_ref[...] = right - step_len * image_ref[:rows, :]


def call(kernel, smem, operands, outs, scratch=()):
    vmem = pl.BlockSpec(memory_space=pltpu.VMEM)
    return pl.pallas_call(
        kernel,
        in_specs=[pl.BlockSpec(memory_space=pltpu.SMEM)] * len(smem) + [vmem] * len(operands),
        out_specs=[vmem] * len(outs),
        out_shape=[jax.ShapeDtypeStruct(shape, jnp.float32) for shape in outs],
        scratch_shapes=list(scratch),
        compiler_params=pltpu.CompilerParams(vmem_limit_bytes=VMEM_BYTES),
    )(*smem, *operands)


def per_device(right_side, kernel_tiles, route_pairs):
    count = lax.axis_size("blk")
    window = max(8, min(16, count // 8))
    cover = list(range(window)) + [k * window for k in range(1, count // window)]
    rows, cols = right_side.shape
    place = lax.axis_index("blk").astype(jnp.int32)
    blocks = lax.all_gather(right_side, "blk")
    (partial,) = call(
        functools.partial(product_kernel, cover),
        (route_pairs.T, place[None]),
        (blocks, kernel_tiles[0]),
        [(count, rows + EXTRA, cols)],
        (pltpu.VMEM((len(cover), rows, 2 * cols), jnp.bfloat16),),
    )
    image = lax.psum_scatter(partial, "blk", scatter_dimension=0)
    solution, residual = call(final_kernel, (), (right_side, image), [(rows, cols), (rows, cols)])
    return solution, residual


def solution(mesh):
    return jax.shard_map(
        per_device,
        mesh=mesh,
        in_specs=(P("blk", None), P("blk", None, None, None), P()),
        out_specs=(P("blk", None), P("blk", None)),
        check_vma=False,
    )
```

time: 104 us -> 222 us (2.13)
  waiting for transfers between devices: 19.8 us -> 199 us
  blocking collectives: 39.7 us -> 0 us
  starting transfers between devices: 23.2 us -> 0.08 us
  between operations: 0.82 us -> 14 us
  matrix products: 9.03 us -> 0 us
  local copies, waits for them, and re-layouts: 9.39 us -> 4.4 us
  Pallas kernels: 0 us -> 3.99 us
    unnamed x0 -> x3, waiting for transfers between devices: none -> 137 us
    all_gather x0 -> x1, waiting for transfers between devices: none -> 62 us  [per_device(): blocks = lax.all_gather(right_side, 'blk')]
    psum x1 -> x0, blocking collectives: 39.7 us -> none  [column_total(): return lax.psum(jnp.sum(values, axis=0), 'blk')]
    ppermute x20 -> x0, starting transfers between devices: 23.2 us -> none  [shifted(): return lax.ppermute(value, axis, pairs)]
    ppermute x20 -> x0, waiting for transfers between devices: 19.8 us -> none  [shifted(): return lax.ppermute(value, axis, pairs)]
    dot_general x4 -> x0, matrix products: 9.03 us -> none  [the longest x1 4.26 us: per_device(): jnp.einsum('tji,tjr->tir', own_tiles, jnp.take(blocks, route_pairs[:, 0],...]
    dot_general x2 -> x0, local copies, waits for them, and re-layouts: 4.68 us -> none  [the longest x1 2.89 us: per_device(): jnp.einsum('tji,tjr->tir', own_tiles, jnp.take(blocks, route_pairs[:, 0],...]
    pallas_call x0 -> x2, Pallas kernels: none -> 3.99 us  [call(): pl.pallas_call(kernel, in_specs=[pl.BlockSpec(memory_space=pltpu.SMEM)] *...]
  transfers between devices with their start and end apart: 20 -> 2, of which waited for: 8 -> 2; matrix products, arithmetic and copies ran while one was open for 2% -> 0% of each run, Pallas kernels for 0% -> 0%
where the time goes in v2:
time: 222 us
  waiting for transfers between devices  199 us (90%)
  between operations  14 us (6%)
  local copies, waits for them, and re-layouts  4.4 us (2%)
  Pallas kernels  3.99 us (2%)
    unnamed x3, waiting for transfers between devices  137 us
    all_gather x1, waiting for transfers between devices, per_device(): blocks = lax.all_gather(right_side, 'blk')  62 us
  transfers between devices with their start and end apart: 2, of which 2 were waited for; matrix products, arithmetic and copies ran while one was open for 0% of the time, Pallas kernels for 0%

profile of v2, /device:TPU:0, one launch (start us, length us, event | category | flops | bytes accessed | tf_op | source)
XLA Modules:
  0.0 221.6 jit_solution(14886009500717198752)
XLA Ops:
  7.2 0.0 all-gather.3.cloned.1.call-start
  7.2 0.7 all-gather.3.cloned.1.call-update
  7.9 0.0 reduce-scatter.5.cloned.1.call-start
  7.9 62.0 %all-gather.3.cloned.1.call-done = f32[4096,128]{1,0:T(8,128)} async-done(((f32[128,128]{1,0:T(8,128)}), f32[4096,128]{1,0:T(8,128)}) %all-gather.3.cloned.1.call-update) | async-done | bytes 2097168 | tf_op jit(solution)/shard_map/all_gather | solution.py:98
  70.0 0.0 copy-start
  70.0 1.6 copy-done
  71.6 0.0 copy-start.1
  71.6 1.2 copy-done.1
  72.8 0.0 copy-start.4
  72.8 0.7 copy-done.4
  73.5 3.3 %shard_map.50 = f32[32,136,128]{2,1,0:T(8,128)} custom-call(s32[2,17]{1,0:T(2,128)S(1)} %bitcast.8, s32[1]{0:T(128)} %bitcast.1.place_ref, f32[32,128,128]{2,1,0:T(8,128)S(1)} %bitcast.5, f32[17,128,128]{2,1,0:T(8,128)S(1)} %bitcast.6), custom_call_target="tpu_custom_call" | custom-call | tf_op jit(solution)/shard_map/pallas_call | solution.py:82
  76.8 0.0 copy-start.2
  76.8 0.0 reduce-scatter.5.cloned.1.call-update
  76.8 136.4 %reduce-scatter.5.cloned.1.call-done = f32[1,136,128]{2,1,0:T(8,128)} async-done(((f32[32,136,128]{2,1,0:T(8,128)}), f32[1,136,128]{2,1,0:T(8,128)}) %reduce-scatter.5.cloned.1.call-update) | async-done | bytes 69648
  213.2 0.0 copy-done.2
  213.2 0.0 copy-start.3
  213.2 0.9 copy-done.3
  214.1 0.7 shard_map.51
Async XLA Ops:
  7.2 62.8 %all-gather.3.cloned.1.call-start = ((), (), s32[]{:S(2)}) async-start(), calls=%async_computation.1 | async-start | bytes 2162688 | tf_op jit(solution)/shard_map/all_gather | solution.py:98
  7.9 205.3 %reduce-scatter.5.cloned.1.call-start = ((), (), s32[]{:S(2)}) async-start(), calls=%async_computation.2 | async-start | bytes 2297856
  70.0 1.6 copy-start
  71.6 1.2 copy-start.1
  72.8 0.7 copy-start.4
  76.8 136.4 %copy-start.2 = (f32[128,128]{1,0:T(8,128)S(1)}, f32[128,128]{1,0:T(8,128)}, u32[]{:S(2)}) copy-start(f32[128,128]{1,0:T(8,128)} %right_ref.1) | copy-start | bytes 196612
  213.2 0.9 copy-start.3
Sparse Core Ops, SparseCore 0:
  10.9 59.0 all-gather.2
  77.0 136.2 reduce-scatter.4

commit v3 on v2

v3 whole, which is shorter than its diff:
```python
import functools

import jax
import jax.numpy as jnp
from jax import lax
from jax.experimental import pallas as pl
from jax.experimental.pallas import tpu as pltpu
from jax.sharding import PartitionSpec as P

EXTRA = 8
VMEM_BYTES = 48 * 1024 * 1024


def core_partner(value):
    count = lax.axis_size("blk")
    return lax.ppermute(value, "blk", [(source, source ^ 1) for source in range(count)])


def exchange_in_plane(value, window):
    count = lax.axis_size("blk")
    groups = [
        [plane * window + 2 * chip + core for chip in range(window // 2)]
        for plane in range(count // window)
        for core in range(2)
    ]
    return lax.all_to_all(value, "blk", 0, 0, axis_index_groups=groups)


def exchange_planes(value, window):
    count = lax.axis_size("blk")
    groups = [[plane * window + place for plane in range(count // window)] for place in range(window)]
    return lax.all_to_all(value, "blk", 0, 0, axis_index_groups=groups)


def split_two(values):
    high = values.astype(jnp.bfloat16)
    low = (values - high.astype(jnp.float32)).astype(jnp.bfloat16)
    return high, low


def around(start, steps, count):
    return lax.rem(start + steps, count)


def split_kernel(tiles_ref, straight_ref, turned_ref):
    slots = tiles_ref.shape[0]

    def visit(t):
        tile = tiles_ref[t]
        straight_ref[t, 0], straight_ref[t, 1] = split_two(tile)
        turned_ref[t, 0], turned_ref[t, 1] = split_two(tile.T)

    if slots <= 32:
        for t in range(slots):
            visit(t)
    else:
        lax.fori_loop(0, slots, lambda t, c: (visit(t), c)[1], 0)


def product_kernel(
    planes, chips, pairs_ref, where_ref, own_ref, far_ref, even_ref, odd_ref, straight_ref, turned_ref,
    message_ref, kept_ref, far_out, whole, parts, total,
):
    window = 2 * chips
    rows, cols = own_ref.shape
    plane, chip, core = where_ref[0], where_ref[1], where_ref[2]
    spare = jnp.where(core == 0, 1, window - 1)

    def put(place, values):
        whole[place] = values
        high, low = split_two(values)
        parts[place, :, :cols] = high
        parts[place, :, cols:] = low

    put(0, own_ref[...])
    for k in range(1, planes):
        put(window - 1 + k, far_ref[around(plane, k, planes)])
    for m in range(1, chips):
        source = around(chip, m, chips)
        put(2 * m, even_ref[source])
        put(2 * m + 1 - 2 * core, odd_ref[source])
    put(spare, odd_ref[chip])

    total[...] = jnp.zeros_like(total)
    slots = straight_ref.shape[0]

    def product(split_ref, t, place):
        both = jnp.dot(split_ref[t, 0], parts[place], preferred_element_type=jnp.float32)
        rest = jnp.dot(split_ref[t, 1], parts[place, :, :cols], preferred_element_type=jnp.float32)
        return both[:, :cols] + (both[:, cols:] + rest)

    def visit(t, mirrored):
        row_place, col_place = pairs_ref[0, t], pairs_ref[1, t]
        total[row_place] += product(straight_ref, t, col_place)
        if mirrored:
            total[col_place] += product(turned_ref, t, row_place)

    visit(0, False)
    if slots <= 32:
        for t in range(1, slots - 1):
            visit(t, True)
    else:
        lax.fori_loop(1, slots - 1, lambda t, c: (visit(t, True), c)[1], 0)
    visit(slots - 1, False)

    dots = jnp.zeros((1, cols), jnp.float32)
    for place in range(whole.shape[0]):
        dots = dots + jnp.sum(whole[place] * total[place], axis=0, keepdims=True)
    own = own_ref[...]
    norm = jnp.sum(own * own, axis=0, keepdims=True)
    sums = jnp.concatenate([norm, dots, jnp.zeros((EXTRA - 2, cols), jnp.float32)], axis=0)
    for m in range(1, chips):
        message_ref[around(chip, m, chips), :rows, :] = total[2 * m + 1 - 2 * core]
    message_ref[chip, :rows, :] = total[spare]
    for m in range(chips):
        message_ref[m, rows:, :] = sums
        kept_ref[m] = total[2 * m]
    kept_ref[chips] = total[window]
    for k in range(2, planes):
        far_out[k - 2] = total[window - 1 + k]


def pair_kernel(chips, where_ref, sent_ref, kept_ref, got_ref, message_ref, ahead_ref):
    rows = kept_ref.shape[1]
    chip, core = where_ref[1], where_ref[2]
    sums = sent_ref[0, rows:, :] + got_ref[0, rows:, :]
    for m in range(1, chips):
        target = around(chip, m, chips)
        message_ref[target, :rows, :] = kept_ref[m] + got_ref[target, :rows, :]
    spare = got_ref[chip, :rows, :]
    message_ref[chip, :rows, :] = kept_ref[0] + jnp.where(core == 1, spare, 0.0)
    ahead_ref[...] = kept_ref[chips] + jnp.where(core == 0, spare, 0.0)
    for m in range(chips):
        message_ref[m, rows:, :] = sums


def plane_kernel(planes, chips, where_ref, ahead_ref, got_ref, far_ref, message_ref):
    rows, cols = ahead_ref.shape
    plane, chip = where_ref[0], where_ref[1]
    near, ahead, sums = got_ref[chip, :rows, :], ahead_ref[...], got_ref[chip, rows:, :]
    for m in range(1, chips):
        source = around(chip, m, chips)
        block = got_ref[source, :rows, :]
        near = near + jnp.where(source < chip, block, 0.0)
        ahead = ahead + jnp.where(source < chip, 0.0, block)
        sums = sums + got_ref[source, rows:, :]
    message_ref[plane, :rows, :] = near
    message_ref[around(plane, 1, planes), :rows, :] = ahead
    for k in range(2, planes):
        message_ref[around(plane, k, planes), :rows, :] = far_ref[k - 2]
    for k in range(planes):
        message_ref[k, rows:, :] = sums


def final_kernel(right_ref, got_ref, solution_ref, residual_ref):
    rows = right_ref.shape[0]
    both = got_ref[0]
    for k in range(1, got_ref.shape[0]):
        both = both + got_ref[k]
    step_len = both[rows : rows + 1, :] / both[rows + 1 : rows + 2, :]
    right = right_ref[...]
    solution_ref[...] = step_len * right
    residual_ref[...] = right - step_len * both[:rows, :]


def call(kernel, smem, operands, outs, scratch=()):
    vmem = pl.BlockSpec(memory_space=pltpu.VMEM)
    return pl.pallas_call(
        kernel,
        in_specs=[pl.BlockSpec(memory_space=pltpu.SMEM)] * len(smem) + [vmem] * len(operands),
        out_specs=[vmem] * len(outs),
        out_shape=[jax.ShapeDtypeStruct(shape, kind) for shape, kind in outs],
        scratch_shapes=list(scratch),
        compiler_params=pltpu.CompilerParams(vmem_limit_bytes=VMEM_BYTES),
    )(*smem, *operands)


def per_device(right_side, kernel_tiles, route_pairs):
    count = lax.axis_size("blk")
    window = max(8, min(16, count // 8))
    planes, chips = count // window, window // 2
    rows, cols = right_side.shape
    slots = kernel_tiles.shape[1]
    cover_len = window + planes - 1
    place = lax.axis_index("blk").astype(jnp.int32)
    plane, chip, core = place // window, place % window // 2, place % 2
    where = jnp.stack([plane, chip, core])
    single = jnp.float32

    straight, turned = call(
        split_kernel, (), (kernel_tiles[0],), [((slots, 2, rows, cols), jnp.bfloat16), ((slots, 2, cols, rows), jnp.bfloat16)]
    )
    far = exchange_planes(jnp.broadcast_to(right_side, (planes, rows, cols)), window)
    ahead = lax.dynamic_index_in_dim(far, (plane + 1) % planes, 0, keepdims=False)
    slot = jnp.arange(chips, dtype=jnp.int32)[:, None, None]
    spare = jnp.where(core == 0, ahead, right_side)
    even = exchange_in_plane(
        jnp.where(slot < chip, right_side, jnp.where(slot > chip, ahead, spare)), window
    )
    odd = core_partner(even)

    sent, kept, far_out = call(
        functools.partial(product_kernel, planes, chips),
        (route_pairs.T, where),
        (right_side, far, even, odd, straight, turned),
        [
            ((chips, rows + EXTRA, cols), single),
            ((chips + 1, rows, cols), single),
            ((planes - 2, rows, cols), single),
        ],
        (
            pltpu.VMEM((cover_len, rows, cols), single),
            pltpu.VMEM((cover_len, rows, 2 * cols), jnp.bfloat16),
            pltpu.VMEM((cover_len, rows, cols), single),
        ),
    )
    got = core_partner(sent)
    message, ahead = call(
        functools.partial(pair_kernel, chips),
        (where,),
        (sent, kept, got),
        [((chips, rows + EXTRA, cols), single), ((rows, cols), single)],
    )
    got = exchange_in_plane(message, window)
    (message,) = call(
        functools.partial(plane_kernel, planes, chips),
        (where,),
        (ahead, got, far_out),
        [((planes, rows + EXTRA, cols), single)],
    )
    got = exchange_planes(message, window)
    return call(final_kernel, (), (right_side, got), [((rows, cols), single), ((rows, cols), single)])


def solution(mesh):
    def run(*args):
        return tuple(per_device(*args))

    return jax.shard_map(
        run,
        mesh=mesh,
        in_specs=(P("blk", None), P("blk", None, None, None), P()),
        out_specs=(P("blk", None), P("blk", None)),
        check_vma=False,
    )
```

time: 222 us -> 54.3 us (0.24)
  waiting for transfers between devices: 199 us -> 11.4 us
  blocking collectives: 0 us -> 29.4 us
  between operations: 14 us -> 0.69 us
  starting transfers between devices: 0.08 us -> 6.52 us
  local copies, waits for them, and re-layouts: 4.4 us -> 1.67 us
    unnamed x3 -> x0, waiting for transfers between devices: 137 us -> none
    all_gather x1 -> x0, waiting for transfers between devices: 62 us -> none  [per_device(): blocks = lax.all_gather(right_side, 'blk')]
    all_to_all x0 -> x3, blocking collectives: none -> 29.4 us  [the longest x2 18.4 us: exchange_in_plane(): return lax.all_to_all(value, 'blk', 0, 0, axis_index_groups=groups)]
    all_to_all x0 -> x1, waiting for transfers between devices: none -> 8.91 us  [exchange_planes(): return lax.all_to_all(value, 'blk', 0, 0, axis_index_groups=groups)]
    all_to_all x0 -> x1, starting transfers between devices: none -> 6.32 us  [exchange_planes(): return lax.all_to_all(value, 'blk', 0, 0, axis_index_groups=groups)]
    unnamed x10 -> x6, local copies, waits for them, and re-layouts: 4.4 us -> 0.02 us
    ppermute x0 -> x2, waiting for transfers between devices: none -> 2.5 us  [core_partner(): lax.ppermute(value, 'blk', [(source, source ^ 1) for source in range(coun...]
  transfers between devices with their start and end apart: 2 -> 3, of which waited for: 2 -> 3; matrix products, arithmetic and copies ran while one was open for 0% -> 0% of each run, Pallas kernels for 0% -> 1%
where the time goes in v3:
time: 54.3 us; the launch traced here: 53.9 us
  blocking collectives  29.4 us (54%)
  waiting for transfers between devices  11.4 us (21%)
  starting transfers between devices  6.52 us (12%)
  Pallas kernels  4.05 us (7%)
  local copies, waits for them, and re-layouts  1.67 us (3%)
  between operations  0.69 us (1%)
    all_to_all x2, blocking collectives, exchange_in_plane(): return lax.all_to_all(value, 'blk', 0, 0, axis_index_groups=groups)  18.4 us
    all_to_all x1, blocking collectives, exchange_planes(): return lax.all_to_all(value, 'blk', 0, 0, axis_index_groups=groups)  11 us
    all_to_all x1, waiting for transfers between devices, exchange_planes(): return lax.all_to_all(value, 'blk', 0, 0, axis_index_groups=groups)  8.91 us
    all_to_all x1, starting transfers between devices, exchange_planes(): return lax.all_to_all(value, 'blk', 0, 0, axis_index_groups=groups)  6.32 us
    pallas_call x5, Pallas kernels, call(): pl.pallas_call(kernel, in_specs=[pl.BlockSpec(memory_space=pltpu.SMEM)] *...  4.05 us
    ppermute x2, waiting for transfers between devices, core_partner(): lax.ppermute(value, 'blk', [(source, source ^ 1) for source in range(coun...  2.5 us
    broadcast_in_dim x1, local copies, waits for them, and re-layouts, per_device(): jnp.broadcast_to(right_side, (planes, rows, cols))  1.66 us
  transfers between devices with their start and end apart: 3, of which 3 were waited for; matrix products, arithmetic and copies ran while one was open for 0% of the time, Pallas kernels for 1%

profile of v3, /device:TPU:0, one launch (start us, length us, event | category | flops | bytes accessed | tf_op | source)
XLA Modules:
  0.0 53.9 jit_solution(13785181060392461264)
XLA Ops:
  0.6 0.0 copy-start
  0.6 0.0 copy-start.1
  0.7 1.7 %broadcast_in_dim.30 = f32[4,128,128]{2,1,0:T(8,128)} broadcast(f32[128,128]{1,0:T(8,128)} %right_ref.1), dimensions={1,2} | broadcast | bytes 327680 | tf_op jit(solution)/shard_map/broadcast_in_dim | solution.py:193
  2.3 6.3 %all-to-all-start = ((f32[4,128,128]{2,1,0:T(8,128)}), f32[4,128,128]{2,1,0:T(8,128)S(1)}, u32[]{:S(2)}, u32[]{:S(2)}) async-start(f32[4,128,128]{2,1,0:T(8,128)} %broadcast_in_dim.30), calls=%async_computation | async-start | bytes 524288 | tf_op jit(solution)/shard_map/all_to_all | solution.py:32
  8.6 8.9 %all-to-all-done.far_ref = f32[4,128,128]{2,1,0:T(8,128)S(1)} async-done(((f32[4,128,128]{2,1,0:T(8,128)}), f32[4,128,128]{2,1,0:T(8,128)S(1)}, u32[]{:S(2)}, u32[]{:S(2)}) %all-to-all-start) | async-done | bytes 262176 | tf_op jit(solution)/shard_map/all_to_all | solution.py:32
  17.6 0.0 copy-start.2
  17.6 0.0 copy-done
  17.6 0.1 select_select_fusion
  17.7 9.2 %all_to_all.20.even_ref = f32[4,128,128]{2,1,0:T(8,128)S(1)} all-to-all(f32[4,128,128]{2,1,0:T(8,128)S(1)} %select_select_fusion), channel_id=1, replica_groups={{0,2,4,6},{1,3,5,7},{8,10,12,14},{9,11,13,15},{16,18,20,22},{17,19,21,2..., dimensions={0} | all-to-all | bytes 524288 | tf_op jit(solution)/shard_map/all_to_all | solution.py:26
  26.9 0.0 collective-permute-start
  26.9 0.0 copy-done.1
  26.9 0.4 shard_map.50
  27.3 0.1 pad_add_fusion.where_ref
  27.4 1.1 %collective-permute-done.odd_ref = f32[4,128,128]{2,1,0:T(8,128)S(1)} collective-permute-done((f32[4,128,128]{2,1,0:T(8,128)S(1)}, f32[4,128,128]{2,1,0:T(8,128)S(1)}, u32[]{:S(2)}, u32[]{:S(2)}) %collective-permute-start) | collective-permute-done | bytes 262176 | tf_op jit(solution)/shard_map/ppermute | solution.py:16
  28.5 0.0 copy-done.2
  28.5 1.8 %shard_map.51 = (f32[4,136,128]{2,1,0:T(8,128)S(1)}, f32[5,128,128]{2,1,0:T(8,128)S(1)}, f32[2,128,128]{2,1,0:T(8,128)S(1)}) custom-call(s32[2,17]{1,0:T(2,128)S(1)} %bitcast.9, s32[3]{0:T(128)S(1)} %pad_add_fusion.where_ref, f32[128,128]{1,0:T(8,128)S(1)} %copy-done, f32[4,128,128]{2,1,0:T(8,128)S(1)} %all-to-all-done.far_ref, ...), custom_call_target="tpu_custom_call" | custom-call | tf_op jit(solution)/shard_map/pallas_call | solution.py:168
  30.3 0.2 collective-permute-start.1
  30.5 1.4 %collective-permute-done.1.got_ref = f32[4,136,128]{2,1,0:T(8,128)S(1)} collective-permute-done((f32[4,136,128]{2,1,0:T(8,128)S(1)}, f32[4,136,128]{2,1,0:T(8,128)S(1)}, u32[]{:S(2)}, u32[]{:S(2)}) %collective-permute-start.1) | collective-permute-done | bytes 278560 | tf_op jit(solution)/shard_map/ppermute | solution.py:16
  31.9 0.6 %shard_map.52 = (f32[4,136,128]{2,1,0:T(8,128)S(1)}, f32[128,128]{1,0:T(8,128)S(1)}) custom-call(s32[3]{0:T(128)S(1)} %pad_add_fusion.where_ref, f32[4,136,128]{2,1,0:T(8,128)S(1)} %get-tuple-element.11.sent_ref, f32[5,128,128]{2,1,0:T(8,128)S(1)} %get-tuple-element.12.kept_ref, f32[4,136,128]{2,1,0:T(8,128)S(1)} %collective-permute-done.1.got_ref), custom_call_target="tpu_custom_call" | custom-call | tf_op jit(solution)/shard_map/pallas_call | solution.py:168
  32.5 9.1 %all_to_all.21.got_ref = f32[4,136,128]{2,1,0:T(8,128)S(1)} all-to-all(f32[4,136,128]{2,1,0:T(8,128)S(1)} %get-tuple-element.14), channel_id=1, replica_groups={{0,2,4,6},{1,3,5,7},{8,10,12,14},{9,11,13,15},{16,18,20,22},{17,19,21,2..., dimensions={0} | all-to-all | bytes 557056 | tf_op jit(solution)/shard_map/all_to_all | solution.py:26
  41.7 0.6 %shard_map.53 = f32[4,136,128]{2,1,0:T(8,128)S(1)} custom-call(s32[3]{0:T(128)S(1)} %pad_add_fusion.where_ref, f32[128,128]{1,0:T(8,128)S(1)} %get-tuple-element.13.ahead_ref, f32[4,136,128]{2,1,0:T(8,128)S(1)} %all_to_all.21.got_ref, f32[2,128,128]{2,1,0:T(8,128)S(1)} %get-tuple-element.15.far_ref), custom_call_target="tpu_custom_call" | custom-call | tf_op jit(solution)/shard_map/pallas_call | solution.py:168
  42.3 11.0 %all_to_all.22.got_ref = f32[4,136,128]{2,1,0:T(8,128)S(1)} all-to-all(f32[4,136,128]{2,1,0:T(8,128)S(1)} %shard_map.53), channel_id=1, replica_groups={{0,8,16,24},{1,9,17,25},{2,10,18,26},{3,11,19,27},{4,12,20,28},{5,13,21..., dimensions={0} | all-to-all | bytes 557056 | tf_op jit(solution)/shard_map/all_to_all | solution.py:32
  53.2 0.7 %shard_map.54 = (f32[128,128]{1,0:T(8,128)}, f32[128,128]{1,0:T(8,128)}) custom-call(f32[128,128]{1,0:T(8,128)S(1)} %copy-done, f32[4,136,128]{2,1,0:T(8,128)S(1)} %all_to_all.22.got_ref), custom_call_target="tpu_custom_call" | custom-call | tf_op jit(solution)/shard_map/pallas_call | solution.py:168
  (2 shorter events, 0.0 us)
Async XLA Ops:
  0.6 16.9 %copy-start = (f32[128,128]{1,0:T(8,128)S(1)}, f32[128,128]{1,0:T(8,128)}, u32[]{:S(2)}) copy-start(f32[128,128]{1,0:T(8,128)} %right_ref.1) | copy-start | bytes 196612
  0.6 26.3 %copy-start.1 = (f32[1,17,128,128]{3,2,1,0:T(8,128)S(1)}, f32[1,17,128,128]{3,2,1,0:T(8,128)}, u32[]{:S(2)}) copy-start(f32[1,17,128,128]{3,2,1,0:T(8,128)} %param.4) | copy-start | bytes 3342340
  2.3 15.2 %all-to-all-start = ((f32[4,128,128]{2,1,0:T(8,128)}), f32[4,128,128]{2,1,0:T(8,128)S(1)}, u32[]{:S(2)}, u32[]{:S(2)}) async-start(f32[4,128,128]{2,1,0:T(8,128)} %broadcast_in_dim.30), calls=%async_computation | async-start | bytes 524288 | tf_op jit(solution)/shard_map/all_to_all | solution.py:32
  17.6 10.9 %copy-start.2 = (s32[17,2]{0,1:T(2,128)S(1)}, s32[17,2]{0,1:T(2,128)}, u32[]{:S(2)}) copy-start(s32[17,2]{0,1:T(2,128)} %param.5) | copy-start | bytes 412
  26.9 1.5 %collective-permute-start = (f32[4,128,128]{2,1,0:T(8,128)S(1)}, f32[4,128,128]{2,1,0:T(8,128)S(1)}, u32[]{:S(2)}, u32[]{:S(2)}) collective-permute-start(f32[4,128,128]{2,1,0:T(8,128)S(1)} %all_to_all.20.even_ref), channel_id=1, source_target_pairs={{0,1},{1,0},{2,3},{3,2},{4,5},{5,4},{6,7},{7,6},{8,9},{9,8},{10,11... | collective-permute-start | bytes 786440 | tf_op jit(solution)/shard_map/ppermute | solution.py:16
  30.3 1.6 %collective-permute-start.1 = (f32[4,136,128]{2,1,0:T(8,128)S(1)}, f32[4,136,128]{2,1,0:T(8,128)S(1)}, u32[]{:S(2)}, u32[]{:S(2)}) collective-permute-start(f32[4,136,128]{2,1,0:T(8,128)S(1)} %get-tuple-element.11.sent_ref), channel_id=1, source_target_pairs={{0,1},{1,0},{2,3},{3,2},{4,5},{5,4},{6,7},{7,6},{8,9},{9,8},{10,11... | collective-permute-start | bytes 835592 | tf_op jit(solution)/shard_map/ppermute | solution.py:16

commit v4 on v1

v4 whole, which is shorter than its diff:
```python
import functools

import jax
import jax.numpy as jnp
from jax import lax
from jax.experimental import pallas as pl
from jax.experimental.pallas import tpu as pltpu
from jax.sharding import PartitionSpec as P

EXTRA = 8
VMEM_BYTES = 48 * 1024 * 1024


def shifted(value, steps):
    count = lax.axis_size("blk")
    pairs = [(source, (source + steps) % count) for source in range(count)]
    return lax.ppermute(value, "blk", pairs)


def chip_partner(value, mask):
    count = lax.axis_size("blk")
    return lax.ppermute(value, "blk", [(source, source ^ (2 * mask)) for source in range(count)])


def core_partner(value):
    count = lax.axis_size("blk")
    return lax.ppermute(value, "blk", [(source, source ^ 1) for source in range(count)])


def split_two(values):
    high = values.astype(jnp.bfloat16)
    low = (values - high.astype(jnp.float32)).astype(jnp.bfloat16)
    return high, low


def split_kernel(tiles_ref, own_ref, straight_ref, turned_ref, own_out):
    slots = tiles_ref.shape[0]
    own_out[...] = own_ref[...]

    def visit(t):
        tile = tiles_ref[t]
        straight_ref[t, 0], straight_ref[t, 1] = split_two(tile)
        turned_ref[t, 0], turned_ref[t, 1] = split_two(tile.T)

    if slots <= 32:
        for t in range(slots):
            visit(t)
    else:
        lax.fori_loop(0, slots, lambda t, c: (visit(t), c)[1], 0)


def steps_ahead(chip, mask, chips):
    return ((chip ^ mask) - chip) & (chips - 1)


def product_kernel(planes, chips, pairs_ref, where_ref, own_ref, *refs):
    window = 2 * chips
    far = refs[: planes - 1]
    even = refs[planes - 1 : planes + chips - 2]
    odd_ref, straight_ref, turned_ref, message_ref, kept_ref = refs[planes + chips - 2 : planes + chips + 3]
    far_out = refs[planes + chips + 3 : -3]
    whole, parts, total = refs[-3:]
    rows, cols = own_ref.shape
    chip, core = where_ref[0], where_ref[1]
    spare = jnp.where(core == 0, 1, window - 1)

    def put(place, values):
        whole[place] = values
        high, low = split_two(values)
        parts[place, :, :cols] = high
        parts[place, :, cols:] = low

    put(0, own_ref[...])
    for k in range(1, planes):
        put(window - 1 + k, far[k - 1][...])
    for m in range(1, chips):
        ahead = 2 * steps_ahead(chip, m, chips)
        put(ahead, even[m - 1][...])
        put(ahead + 1 - 2 * core, odd_ref[m])
    put(spare, odd_ref[0])

    total[...] = jnp.zeros_like(total)
    slots = straight_ref.shape[0]

    def product(split_ref, t, place):
        both = jnp.dot(split_ref[t, 0], parts[place], preferred_element_type=jnp.float32)
        rest = jnp.dot(split_ref[t, 1], parts[place, :, :cols], preferred_element_type=jnp.float32)
        return both[:, :cols] + (both[:, cols:] + rest)

    def visit(t, mirrored):
        row_place, col_place = pairs_ref[0, t], pairs_ref[1, t]
        total[row_place] += product(straight_ref, t, col_place)
        if mirrored:
            total[col_place] += product(turned_ref, t, row_place)

    visit(0, False)
    if slots <= 32:
        for t in range(1, slots - 1):
            visit(t, True)
    else:
        lax.fori_loop(1, slots - 1, lambda t, c: (visit(t, True), c)[1], 0)
    visit(slots - 1, False)

    dots = jnp.zeros((1, cols), jnp.float32)
    for place in range(whole.shape[0]):
        dots = dots + jnp.sum(whole[place] * total[place], axis=0, keepdims=True)
    own = own_ref[...]
    norm = jnp.sum(own * own, axis=0, keepdims=True)
    sums = jnp.concatenate([norm, dots, jnp.zeros((EXTRA - 2, cols), jnp.float32)], axis=0)
    message_ref[:rows, :] = total[spare]
    kept_ref[0] = total[0]
    for m in range(1, chips):
        ahead = 2 * steps_ahead(chip, m, chips)
        message_ref[m * rows : (m + 1) * rows, :] = total[ahead + 1 - 2 * core]
        kept_ref[m] = total[ahead]
    message_ref[chips * rows :, :] = sums
    kept_ref[chips] = total[window]
    for k in range(2, planes):
        far_out[k - 2][...] = total[window - 1 + k]


def pair_kernel(chips, where_ref, sent_ref, kept_ref, got_ref, *outs):
    messages = outs[: chips - 1]
    near_ref, next_ref, sums_ref = outs[chips - 1 :]
    rows = kept_ref.shape[1]
    core = where_ref[1]
    sums = sent_ref[chips * rows :, :] + got_ref[chips * rows :, :]
    for m in range(1, chips):
        messages[m - 1][:rows, :] = kept_ref[m] + got_ref[m * rows : (m + 1) * rows, :]
        messages[m - 1][rows:, :] = sums
    spare = got_ref[:rows, :]
    near_ref[...] = kept_ref[0] + jnp.where(core == 1, spare, 0.0)
    next_ref[...] = kept_ref[chips] + jnp.where(core == 0, spare, 0.0)
    sums_ref[...] = sums


def plane_kernel(chips, where_ref, near_ref, next_ref, sums_ref, *refs):
    got = refs[: chips - 1]
    far = refs[chips - 1 : -3]
    near_out, message, sums_out = refs[-3:]
    rows = near_ref.shape[0]
    chip = where_ref[0]
    near, ahead, sums = near_ref[...], next_ref[...], sums_ref[...]
    for m in range(1, chips):
        block = got[m - 1][:rows, :]
        same = (chip ^ m) < chip
        near = near + jnp.where(same, block, 0.0)
        ahead = ahead + jnp.where(same, 0.0, block)
        sums = sums + got[m - 1][rows:, :]
    for block in far:
        near = near + block[...]
    near_out[...] = near
    sums_out[...] = sums
    message[:rows, :] = ahead
    message[rows:, :] = sums


def final_kernel(right_ref, near_ref, sums_ref, got_ref, *refs):
    solution_ref, residual_ref = refs[-2:]
    rows = near_ref.shape[0]
    image = near_ref[...] + got_ref[:rows, :]
    sums = sums_ref[...] + got_ref[rows:, :]
    for more in refs[:-2]:
        sums = sums + more[...]
    step_len = sums[0:1, :] / sums[1:2, :]
    right = right_ref[...]
    solution_ref[...] = step_len * right
    residual_ref[...] = right - step_len * image


def call(kernel, smem, operands, outs, scratch=()):
    vmem = pl.BlockSpec(memory_space=pltpu.VMEM)
    return pl.pallas_call(
        kernel,
        in_specs=[pl.BlockSpec(memory_space=pltpu.SMEM)] * len(smem) + [vmem] * len(operands),
        out_specs=[vmem] * len(outs),
        out_shape=[jax.ShapeDtypeStruct(shape, kind) for shape, kind in outs],
        scratch_shapes=list(scratch),
        compiler_params=pltpu.CompilerParams(vmem_limit_bytes=VMEM_BYTES),
    )(*smem, *operands)


def per_device(right_side, kernel_tiles, route_pairs):
    count = lax.axis_size("blk")
    window = max(8, min(16, count // 8))
    planes, chips = count // window, window // 2
    rows, cols = right_side.shape
    slots = kernel_tiles.shape[1]
    cover_len = window + planes - 1
    place = lax.axis_index("blk").astype(jnp.int32)
    chip, core = place % window // 2, place % 2
    where = jnp.stack([chip, core])
    single, half = jnp.float32, jnp.bfloat16

    straight, turned, own = call(
        split_kernel,
        (),
        (kernel_tiles[0], right_side),
        [((slots, 2, rows, cols), half), ((slots, 2, cols, rows), half), ((rows, cols), single)],
    )
    far = [shifted(right_side, -k * window) for k in range(1, planes)]
    even = [chip_partner(jnp.where((chip ^ m) < chip, own, far[0]), m) for m in range(1, chips)]
    odd = jnp.stack([jnp.where(core == 0, far[0], own)] + even)
    odd, *rest = lax.optimization_barrier((odd, *far[1:]))
    far = far[:1] + rest
    odd = core_partner(odd)

    block, marked, extra = ((rows, cols), single), ((rows + EXTRA, cols), single), ((EXTRA, cols), single)
    sent, kept, *far_out = call(
        functools.partial(product_kernel, planes, chips),
        (route_pairs.T, where),
        (own, *far, *even, odd, straight, turned),
        [((chips * rows + EXTRA, cols), single), ((chips + 1, rows, cols), single)] + [block] * (planes - 2),
        (
            pltpu.VMEM((cover_len, rows, cols), single),
            pltpu.VMEM((cover_len, rows, 2 * cols), half),
            pltpu.VMEM((cover_len, rows, cols), single),
        ),
    )
    far_got = [shifted(value, k * window) for k, value in enumerate(far_out, 2)]
    got = core_partner(sent)
    *messages, near, ahead, sums = call(
        functools.partial(pair_kernel, chips), (where,), (sent, kept, got), [marked] * (chips - 1) + [block, block, extra]
    )
    got = [chip_partner(value, m) for m, value in enumerate(messages, 1)]
    near, message, sums = call(
        functools.partial(plane_kernel, chips), (where,), (near, ahead, sums, *got, *far_got), [block, marked, extra]
    )
    got = shifted(message, window)
    more = [shifted(sums, k * window) for k in range(2, planes)]
    return call(final_kernel, (), (own, near, sums, got, *more), [block, block])


def solution(mesh):
    def run(*args):
        return tuple(per_device(*args))

    return jax.shard_map(
        run,
        mesh=mesh,
        in_specs=(P("blk", None), P("blk", None, None, None), P()),
        out_specs=(P("blk", None), P("blk", None)),
        check_vma=False,
    )
```

time: 48.4 us -> 44.7 us (0.924)
  waiting for transfers between devices: 19.1 us -> 14.5 us
  Pallas kernels: 2.8 us -> 4.07 us
  starting transfers between devices: 21.8 us -> 23 us
  local copies, waits for them, and re-layouts: 2.86 us -> 2.09 us
  other arithmetic: 0.88 us -> 0.12 us
    ppermute x6, waiting for transfers between devices: 6.6 us -> 0.02 us  [chip_partner(): lax.ppermute(value, 'blk', [(source, source ^ 2 * mask) for source in ran...]
    ppermute x6 -> x8, starting transfers between devices: 13.6 us -> 15.6 us  [shifted(): return lax.ppermute(value, 'blk', pairs)]
    ppermute x2, waiting for transfers between devices: 1.48 us -> 2.85 us  [core_partner(): lax.ppermute(value, 'blk', [(source, source ^ 1) for source in range(coun...]
    pallas_call x4 -> x5, Pallas kernels: 2.8 us -> 4.07 us  [call(): pl.pallas_call(kernel, in_specs=[pl.BlockSpec(memory_space=pltpu.SMEM)] *...]
    ppermute x6, starting transfers between devices: 7.98 us -> 7.11 us  [chip_partner(): lax.ppermute(value, 'blk', [(source, source ^ 2 * mask) for source in ran...]
    select_n x1 -> x0, other arithmetic: 0.86 us -> none  [per_device(): jnp.where(core == 0, far[0], right_side)]
    unnamed x7 -> x6, local copies, waits for them, and re-layouts: 2.86 us -> 2.09 us
    ppermute x6 -> x8, waiting for transfers between devices: 11 us -> 11.7 us  [shifted(): return lax.ppermute(value, 'blk', pairs)]
  transfers between devices with their start and end apart: 14 -> 16, of which waited for: 12 -> 8; matrix products, arithmetic and copies ran while one was open for 2% -> 0% of each run, Pallas kernels for 0% -> 1%
where the time goes in v4:
time: 44.7 us; the launch traced here: 44.5 us
  starting transfers between devices  23 us (51%)
  waiting for transfers between devices  14.5 us (32%)
  Pallas kernels  4.07 us (9%)
  local copies, waits for them, and re-layouts  2.09 us (5%)
  between operations  0.7 us (2%)
    ppermute x8, starting transfers between devices, shifted(): return lax.ppermute(value, 'blk', pairs)  15.6 us
    ppermute x8, waiting for transfers between devices, shifted(): return lax.ppermute(value, 'blk', pairs)  11.7 us
    ppermute x6, starting transfers between devices, chip_partner(): lax.ppermute(value, 'blk', [(source, source ^ 2 * mask) for source in ran...  7.11 us
    pallas_call x5, Pallas kernels, call(): pl.pallas_call(kernel, in_specs=[pl.BlockSpec(memory_space=pltpu.SMEM)] *...  4.07 us
    ppermute x2, waiting for transfers between devices, core_partner(): lax.ppermute(value, 'blk', [(source, source ^ 1) for source in range(coun...  2.85 us
    unnamed x6, local copies, waits for them, and re-layouts  2.09 us
  transfers between devices with their start and end apart: 16, of which 8 were waited for; matrix products, arithmetic and copies ran while one was open for 0% of the time, Pallas kernels for 1%

profile of v4, /device:TPU:0, one launch (start us, length us, event | category | flops | bytes accessed | tf_op | source)
XLA Modules:
  0.0 44.5 jit_solution(9863987837132250142)
XLA Ops:
  0.6 0.0 copy-start.2
  0.6 5.1 %collective-permute-start = (f32[128,128]{1,0:T(8,128)}, f32[128,128]{1,0:T(8,128)S(1)}, u32[]{:S(2)}, u32[]{:S(2)}) collective-permute-start(f32[128,128]{1,0:T(8,128)} %own_ref.1), channel_id=1, source_target_pairs={{0,24},{1,25},{2,26},{3,27},{4,28},{5,29},{6,30},{7,31},{8,0},{9,1... | collective-permute-start | bytes 196616 | tf_op jit(solution)/shard_map/ppermute | solution.py:17
  5.7 0.0 copy-start
  5.7 1.2 %copy-done = f32[1,17,128,128]{3,2,1,0:T(8,128)S(1)} copy-done((f32[1,17,128,128]{3,2,1,0:T(8,128)S(1)}, f32[1,17,128,128]{3,2,1,0:T(8,128)}, u32[]{:S(2)}) %copy-start) | copy-done | bytes 1114136
  7.0 0.0 copy-start.1
  7.0 0.8 %copy-done.1 = f32[128,128]{1,0:T(8,128)S(1)} copy-done((f32[128,128]{1,0:T(8,128)S(1)}, f32[128,128]{1,0:T(8,128)}, u32[]{:S(2)}) %copy-start.1) | copy-done | bytes 65560
  7.8 0.4 shard_map.50
  8.2 0.0 collective-permute-done.refs_0_
  8.2 2.5 %collective-permute-start.3 = (f32[128,128]{1,0:T(8,128)S(1)}, f32[128,128]{1,0:T(8,128)S(1)}, u32[]{:S(2)}, u32[]{:S(2)}) collective-permute-start(f32[128,128]{1,0:T(8,128)S(1)} %get-tuple-element.41), channel_id=1, source_target_pairs={{0,6},{1,7},{2,4},{3,5},{4,2},{5,3},{6,0},{7,1},{8,14},{9,15},{10,... | collective-permute-start | bytes 196616 | tf_op jit(solution)/shard_map/ppermute | solution.py:22
  10.8 0.5 %collective-permute-start.2 = (f32[128,128]{1,0:T(8,128)S(1)}, f32[128,128]{1,0:T(8,128)S(1)}, u32[]{:S(2)}, u32[]{:S(2)}) collective-permute-start(f32[128,128]{1,0:T(8,128)S(1)} %get-tuple-element.42), channel_id=1, source_target_pairs={{0,4},{1,5},{2,6},{3,7},{4,0},{5,1},{6,2},{7,3},{8,12},{9,13},{10,... | collective-permute-start | bytes 196616 | tf_op jit(solution)/shard_map/ppermute | solution.py:22
  11.3 0.5 %collective-permute-start.1 = (f32[128,128]{1,0:T(8,128)S(1)}, f32[128,128]{1,0:T(8,128)S(1)}, u32[]{:S(2)}, u32[]{:S(2)}) collective-permute-start(f32[128,128]{1,0:T(8,128)S(1)} %get-tuple-element.43), channel_id=1, source_target_pairs={{0,2},{1,3},{2,0},{3,1},{4,6},{5,7},{6,4},{7,5},{8,10},{9,11},{10,... | collective-permute-start | bytes 196616 | tf_op jit(solution)/shard_map/ppermute | solution.py:22
  11.8 0.0 collective-permute-start.5
  11.8 4.4 %collective-permute-start.4 = (f32[128,128]{1,0:T(8,128)S(1)}, f32[128,128]{1,0:T(8,128)S(1)}, u32[]{:S(2)}, u32[]{:S(2)}) collective-permute-start(f32[128,128]{1,0:T(8,128)S(1)} %copy-done.1), channel_id=1, source_target_pairs={{0,16},{1,17},{2,18},{3,19},{4,20},{5,21},{6,22},{7,23},{8,24},{9,... | collective-permute-start | bytes 196616 | tf_op jit(solution)/shard_map/ppermute | solution.py:17
  16.2 0.0 collective-permute-done.3.refs_5_
  16.2 0.0 collective-permute-done.2.refs_4_
  16.2 0.0 collective-permute-done.1.refs_3_
  16.2 1.7 %collective-permute-done.5.refs_2_ = f32[128,128]{1,0:T(8,128)S(1)} collective-permute-done((f32[128,128]{1,0:T(8,128)S(1)}, f32[128,128]{1,0:T(8,128)S(1)}, u32[]{:S(2)}, u32[]{:S(2)}) %collective-permute-start.5) | collective-permute-done | bytes 65568 | tf_op jit(solution)/shard_map/ppermute | solution.py:17
  17.9 1.4 %collective-permute-done.4.refs_1_ = f32[128,128]{1,0:T(8,128)S(1)} collective-permute-done((f32[128,128]{1,0:T(8,128)S(1)}, f32[128,128]{1,0:T(8,128)S(1)}, u32[]{:S(2)}, u32[]{:S(2)}) %collective-permute-start.4) | collective-permute-done | bytes 65568 | tf_op jit(solution)/shard_map/ppermute | solution.py:17
  19.3 0.0 collective-permute-start.6
  19.3 0.1 pad_add_fusion.where_ref
  19.4 1.5 %collective-permute-done.6.refs_6_ = f32[4,128,128]{2,1,0:T(8,128)S(1)} collective-permute-done((f32[4,128,128]{2,1,0:T(8,128)S(1)}, f32[4,128,128]{2,1,0:T(8,128)S(1)}, u32[]{:S(2)}, u32[]{:S(2)}) %collective-permute-start.6) | collective-permute-done | bytes 262176 | tf_op jit(solution)/shard_map/ppermute | solution.py:27
  20.8 0.0 copy-done.2
  20.8 1.9 %shard_map.51 = (f32[520,128]{1,0:T(8,128)S(1)}, f32[5,128,128]{2,1,0:T(8,128)S(1)}, f32[128,128]{1,0:T(8,128)S(1)}, f32[128,128]{1,0:T(8,128)S(1)}) custom-call(s32[2,17]{1,0:T(2,128)S(1)} %bitcast.13, s32[2]{0:T(128)S(1)} %pad_add_fusion.where_ref, f32[128,128]{1,0:T(8,128)S(1)} %get-tuple-element.21.own_ref.right_ref, ...), custom_call_target="tpu_custom_call" | custom-call | tf_op jit(solution)/shard_map/pallas_call | solution.py:173
  22.7 0.2 collective-permute-start.7
  22.9 1.4 %collective-permute-done.7.got_ref = f32[520,128]{1,0:T(8,128)S(1)} collective-permute-done((f32[520,128]{1,0:T(8,128)S(1)}, f32[520,128]{1,0:T(8,128)S(1)}, u32[]{:S(2)}, u32[]{:S(2)}) %collective-permute-start.7) | collective-permute-done | bytes 266272 | tf_op jit(solution)/shard_map/ppermute | solution.py:27
  24.3 0.6 %shard_map.52 = (f32[136,128]{1,0:T(8,128)S(1)}, f32[136,128]{1,0:T(8,128)S(1)}, f32[136,128]{1,0:T(8,128)S(1)}, f32[128,128]{1,0:T(8,128)S(1)}, f32[128,128]{1,0:T(8,128)S(1)}, /*index=5*/f32[8,128]{1,0:T(8,128)S(1)}) custom-call(s32[2]{0:T(128)S(1)} %pad_add_fusion.where_ref, f32[520,128]{1,0:T(8,128)S(1)} %get-tuple-element.27.sent_ref, ...), custom_call_target="tpu_custom_call" | custom-call | tf_op jit(solution)/shard_map/pallas_call | solution.py:173
  24.9 1.6 %collective-permute-start.8 = (f32[136,128]{1,0:T(8,128)S(1)}, f32[136,128]{1,0:T(8,128)S(1)}, u32[]{:S(2)}, u32[]{:S(2)}) collective-permute-start(f32[136,128]{1,0:T(8,128)S(1)} %get-tuple-element.32), channel_id=1, source_target_pairs={{0,2},{1,3},{2,0},{3,1},{4,6},{5,7},{6,4},{7,5},{8,10},{9,11},{10,... | collective-permute-start | bytes 208904 | tf_op jit(solution)/shard_map/ppermute | solution.py:22
  26.4 1.5 %collective-permute-start.9 = (f32[136,128]{1,0:T(8,128)S(1)}, f32[136,128]{1,0:T(8,128)S(1)}, u32[]{:S(2)}, u32[]{:S(2)}) collective-permute-start(f32[136,128]{1,0:T(8,128)S(1)} %get-tuple-element.33), channel_id=1, source_target_pairs={{0,4},{1,5},{2,6},{3,7},{4,0},{5,1},{6,2},{7,3},{8,12},{9,13},{10,... | collective-permute-start | bytes 208904 | tf_op jit(solution)/shard_map/ppermute | solution.py:22
  27.9 0.5 %collective-permute-start.10 = (f32[136,128]{1,0:T(8,128)S(1)}, f32[136,128]{1,0:T(8,128)S(1)}, u32[]{:S(2)}, u32[]{:S(2)}) collective-permute-start(f32[136,128]{1,0:T(8,128)S(1)} %get-tuple-element.34), channel_id=1, source_target_pairs={{0,6},{1,7},{2,4},{3,5},{4,2},{5,3},{6,0},{7,1},{8,14},{9,15},{10,... | collective-permute-start | bytes 208904 | tf_op jit(solution)/shard_map/ppermute | solution.py:22
  28.4 2.1 %collective-permute-start.11 = (f32[128,128]{1,0:T(8,128)S(1)}, f32[128,128]{1,0:T(8,128)S(1)}, u32[]{:S(2)}, u32[]{:S(2)}) collective-permute-start(f32[128,128]{1,0:T(8,128)S(1)} %get-tuple-element.35), channel_id=1, source_target_pairs={{0,16},{1,17},{2,18},{3,19},{4,20},{5,21},{6,22},{7,23},{8,24},{9,... | collective-permute-start | bytes 196616 | tf_op jit(solution)/shard_map/ppermute | solution.py:17
  30.5 0.3 collective-permute-start.12
  30.7 3.4 %collective-permute-done.11.refs_3_ = f32[128,128]{1,0:T(8,128)S(1)} collective-permute-done((f32[128,128]{1,0:T(8,128)S(1)}, f32[128,128]{1,0:T(8,128)S(1)}, u32[]{:S(2)}, u32[]{:S(2)}) %collective-permute-start.11) | collective-permute-done | bytes 65568 | tf_op jit(solution)/shard_map/ppermute | solution.py:17
  34.1 0.7 %collective-permute-done.12.refs_4_ = f32[128,128]{1,0:T(8,128)S(1)} collective-permute-done((f32[128,128]{1,0:T(8,128)S(1)}, f32[128,128]{1,0:T(8,128)S(1)}, u32[]{:S(2)}, u32[]{:S(2)}) %collective-permute-start.12) | collective-permute-done | bytes 65568 | tf_op jit(solution)/shard_map/ppermute | solution.py:17
  34.8 0.0 collective-permute-done.8.refs_0_
  34.8 0.0 collective-permute-done.9.refs_1_
  34.8 0.0 collective-permute-done.10.refs_2_
  34.8 0.6 %shard_map.53 = (f32[128,128]{1,0:T(8,128)S(1)}, f32[136,128]{1,0:T(8,128)S(1)}, f32[8,128]{1,0:T(8,128)S(1)}) custom-call(s32[2]{0:T(128)S(1)} %pad_add_fusion.where_ref, f32[128,128]{1,0:T(8,128)S(1)} %get-tuple-element.29.near_ref, f32[128,128]{1,0:T(8,128)S(1)} %get-tuple-element.30.next_ref, f32[8,128]{1,0:T(8,128)S(1)} %get-tuple-element.31.sums_ref, ...), custom_call_target="tpu_custom_call" | custom-call | tf_op jit(solution)/shard_map/pallas_call | solution.py:173
  35.4 0.6 %collective-permute-start.13 = (f32[136,128]{1,0:T(8,128)S(1)}, f32[136,128]{1,0:T(8,128)S(1)}, u32[]{:S(2)}, u32[]{:S(2)}) collective-permute-start(f32[136,128]{1,0:T(8,128)S(1)} %get-tuple-element.39), channel_id=1, source_target_pairs={{0,8},{1,9},{2,10},{3,11},{4,12},{5,13},{6,14},{7,15},{8,16},{9,17... | collective-permute-start | bytes 208904 | tf_op jit(solution)/shard_map/ppermute | solution.py:17
  36.0 3.3 %collective-permute-start.15 = (f32[8,128]{1,0:T(8,128)S(1)}, f32[8,128]{1,0:T(8,128)S(1)}, u32[]{:S(2)}, u32[]{:S(2)}) collective-permute-start(f32[8,128]{1,0:T(8,128)S(1)} %get-tuple-element.38.sums_ref), channel_id=1, source_target_pairs={{0,24},{1,25},{2,26},{3,27},{4,28},{5,29},{6,30},{7,31},{8,0},{9,1... | collective-permute-start | bytes 12296 | tf_op jit(solution)/shard_map/ppermute | solution.py:17
  39.3 0.0 collective-permute-start.14
  39.3 1.3 %collective-permute-done.15.refs_1_ = f32[8,128]{1,0:T(8,128)S(1)} collective-permute-done((f32[8,128]{1,0:T(8,128)S(1)}, f32[8,128]{1,0:T(8,128)S(1)}, u32[]{:S(2)}, u32[]{:S(2)}) %collective-permute-start.15) | collective-permute-done | bytes 4128 | tf_op jit(solution)/shard_map/ppermute | solution.py:17
  40.6 3.2 %collective-permute-done.14.refs_0_ = f32[8,128]{1,0:T(8,128)S(1)} collective-permute-done((f32[8,128]{1,0:T(8,128)S(1)}, f32[8,128]{1,0:T(8,128)S(1)}, u32[]{:S(2)}, u32[]{:S(2)}) %collective-permute-start.14) | collective-permute-done | bytes 4128 | tf_op jit(solution)/shard_map/ppermute | solution.py:17
  43.8 0.0 collective-permute-done.13.got_ref
  43.8 0.7 %shard_map.54 = (f32[128,128]{1,0:T(8,128)}, f32[128,128]{1,0:T(8,128)}) custom-call(f32[128,128]{1,0:T(8,128)S(1)} %get-tuple-element.21.own_ref.right_ref, f32[128,128]{1,0:T(8,128)S(1)} %get-tuple-element.37.near_ref, f32[8,128]{1,0:T(8,128)S(1)} %get-tuple-element.38.sums_ref, f32[136,128]{1,0:T(8,128)S(1)} %collective-permute-done.13.got_ref, ...), custom_call_target="tpu_custom_call" | custom-call | tf_op jit(solution)/shard_map/pallas_call | solution.py:173
  (2 shorter events, 0.0 us)
Async XLA Ops:
  0.6 20.2 %copy-start.2 = (s32[17,2]{0,1:T(2,128)S(1)}, s32[17,2]{0,1:T(2,128)}, u32[]{:S(2)}) copy-start(s32[17,2]{0,1:T(2,128)} %param.5) | copy-start | bytes 412
  0.6 7.6 %collective-permute-start = (f32[128,128]{1,0:T(8,128)}, f32[128,128]{1,0:T(8,128)S(1)}, u32[]{:S(2)}, u32[]{:S(2)}) collective-permute-start(f32[128,128]{1,0:T(8,128)} %own_ref.1), channel_id=1, source_target_pairs={{0,24},{1,25},{2,26},{3,27},{4,28},{5,29},{6,30},{7,31},{8,0},{9,1... | collective-permute-start | bytes 196616 | tf_op jit(solution)/shard_map/ppermute | solution.py:17
  5.7 1.2 %copy-start = (f32[1,17,128,128]{3,2,1,0:T(8,128)S(1)}, f32[1,17,128,128]{3,2,1,0:T(8,128)}, u32[]{:S(2)}) copy-start(f32[1,17,128,128]{3,2,1,0:T(8,128)} %param.4) | copy-start | bytes 3342340
  7.0 0.8 %copy-start.1 = (f32[128,128]{1,0:T(8,128)S(1)}, f32[128,128]{1,0:T(8,128)}, u32[]{:S(2)}) copy-start(f32[128,128]{1,0:T(8,128)} %own_ref.1) | copy-start | bytes 196612
  8.2 7.9 %collective-permute-start.3 = (f32[128,128]{1,0:T(8,128)S(1)}, f32[128,128]{1,0:T(8,128)S(1)}, u32[]{:S(2)}, u32[]{:S(2)}) collective-permute-start(f32[128,128]{1,0:T(8,128)S(1)} %get-tuple-element.41), channel_id=1, source_target_pairs={{0,6},{1,7},{2,4},{3,5},{4,2},{5,3},{6,0},{7,1},{8,14},{9,15},{10,... | collective-permute-start | bytes 196616 | tf_op jit(solution)/shard_map/ppermute | solution.py:22
  10.8 5.4 %collective-permute-start.2 = (f32[128,128]{1,0:T(8,128)S(1)}, f32[128,128]{1,0:T(8,128)S(1)}, u32[]{:S(2)}, u32[]{:S(2)}) collective-permute-start(f32[128,128]{1,0:T(8,128)S(1)} %get-tuple-element.42), channel_id=1, source_target_pairs={{0,4},{1,5},{2,6},{3,7},{4,0},{5,1},{6,2},{7,3},{8,12},{9,13},{10,... | collective-permute-start | bytes 196616 | tf_op jit(solution)/shard_map/ppermute | solution.py:22
  11.3 4.9 %collective-permute-start.1 = (f32[128,128]{1,0:T(8,128)S(1)}, f32[128,128]{1,0:T(8,128)S(1)}, u32[]{:S(2)}, u32[]{:S(2)}) collective-permute-start(f32[128,128]{1,0:T(8,128)S(1)} %get-tuple-element.43), channel_id=1, source_target_pairs={{0,2},{1,3},{2,0},{3,1},{4,6},{5,7},{6,4},{7,5},{8,10},{9,11},{10,... | collective-permute-start | bytes 196616 | tf_op jit(solution)/shard_map/ppermute | solution.py:22
  11.8 6.1 %collective-permute-start.5 = (f32[128,128]{1,0:T(8,128)S(1)}, f32[128,128]{1,0:T(8,128)S(1)}, u32[]{:S(2)}, u32[]{:S(2)}) collective-permute-start(f32[128,128]{1,0:T(8,128)S(1)} %copy-done.1), channel_id=1, source_target_pairs={{0,8},{1,9},{2,10},{3,11},{4,12},{5,13},{6,14},{7,15},{8,16},{9,17... | collective-permute-start | bytes 196616 | tf_op jit(solution)/shard_map/ppermute | solution.py:17
  11.8 7.5 %collective-permute-start.4 = (f32[128,128]{1,0:T(8,128)S(1)}, f32[128,128]{1,0:T(8,128)S(1)}, u32[]{:S(2)}, u32[]{:S(2)}) collective-permute-start(f32[128,128]{1,0:T(8,128)S(1)} %copy-done.1), channel_id=1, source_target_pairs={{0,16},{1,17},{2,18},{3,19},{4,20},{5,21},{6,22},{7,23},{8,24},{9,... | collective-permute-start | bytes 196616 | tf_op jit(solution)/shard_map/ppermute | solution.py:17
  19.3 1.5 %collective-permute-start.6 = (f32[4,128,128]{2,1,0:T(8,128)S(1)}, f32[4,128,128]{2,1,0:T(8,128)S(1)}, u32[]{:S(2)}, u32[]{:S(2)}) collective-permute-start(f32[4,128,128]{2,1,0:T(8,128)S(1)} %pad_maximum_fusion), channel_id=1, source_target_pairs={{0,1},{1,0},{2,3},{3,2},{4,5},{5,4},{6,7},{7,6},{8,9},{9,8},{10,11... | collective-permute-start | bytes 786440 | tf_op jit(solution)/shard_map/ppermute | solution.py:27
  22.7 1.6 %collective-permute-start.7 = (f32[520,128]{1,0:T(8,128)S(1)}, f32[520,128]{1,0:T(8,128)S(1)}, u32[]{:S(2)}, u32[]{:S(2)}) collective-permute-start(f32[520,128]{1,0:T(8,128)S(1)} %get-tuple-element.27.sent_ref), channel_id=1, source_target_pairs={{0,1},{1,0},{2,3},{3,2},{4,5},{5,4},{6,7},{7,6},{8,9},{9,8},{10,11... | collective-permute-start | bytes 798728 | tf_op jit(solution)/shard_map/ppermute | solution.py:27
  24.9 10.0 %collective-permute-start.8 = (f32[136,128]{1,0:T(8,128)S(1)}, f32[136,128]{1,0:T(8,128)S(1)}, u32[]{:S(2)}, u32[]{:S(2)}) collective-permute-start(f32[136,128]{1,0:T(8,128)S(1)} %get-tuple-element.32), channel_id=1, source_target_pairs={{0,2},{1,3},{2,0},{3,1},{4,6},{5,7},{6,4},{7,5},{8,10},{9,11},{10,... | collective-permute-start | bytes 208904 | tf_op jit(solution)/shard_map/ppermute | solution.py:22
  26.4 8.4 %collective-permute-start.9 = (f32[136,128]{1,0:T(8,128)S(1)}, f32[136,128]{1,0:T(8,128)S(1)}, u32[]{:S(2)}, u32[]{:S(2)}) collective-permute-start(f32[136,128]{1,0:T(8,128)S(1)} %get-tuple-element.33), channel_id=1, source_target_pairs={{0,4},{1,5},{2,6},{3,7},{4,0},{5,1},{6,2},{7,3},{8,12},{9,13},{10,... | collective-permute-start | bytes 208904 | tf_op jit(solution)/shard_map/ppermute | solution.py:22
  27.9 6.9 %collective-permute-start.10 = (f32[136,128]{1,0:T(8,128)S(1)}, f32[136,128]{1,0:T(8,128)S(1)}, u32[]{:S(2)}, u32[]{:S(2)}) collective-permute-start(f32[136,128]{1,0:T(8,128)S(1)} %get-tuple-element.34), channel_id=1, source_target_pairs={{0,6},{1,7},{2,4},{3,5},{4,2},{5,3},{6,0},{7,1},{8,14},{9,15},{10,... | collective-permute-start | bytes 208904 | tf_op jit(solution)/shard_map/ppermute | solution.py:22
  28.4 5.7 %collective-permute-start.11 = (f32[128,128]{1,0:T(8,128)S(1)}, f32[128,128]{1,0:T(8,128)S(1)}, u32[]{:S(2)}, u32[]{:S(2)}) collective-permute-start(f32[128,128]{1,0:T(8,128)S(1)} %get-tuple-element.35), channel_id=1, source_target_pairs={{0,16},{1,17},{2,18},{3,19},{4,20},{5,21},{6,22},{7,23},{8,24},{9,... | collective-permute-start | bytes 196616 | tf_op jit(solution)/shard_map/ppermute | solution.py:17
  30.5 4.3 %collective-permute-start.12 = (f32[128,128]{1,0:T(8,128)S(1)}, f32[128,128]{1,0:T(8,128)S(1)}, u32[]{:S(2)}, u32[]{:S(2)}) collective-permute-start(f32[128,128]{1,0:T(8,128)S(1)} %get-tuple-element.36), channel_id=1, source_target_pairs={{0,24},{1,25},{2,26},{3,27},{4,28},{5,29},{6,30},{7,31},{8,0},{9,1... | collective-permute-start | bytes 196616 | tf_op jit(solution)/shard_map/ppermute | solution.py:17
  35.4 8.4 %collective-permute-start.13 = (f32[136,128]{1,0:T(8,128)S(1)}, f32[136,128]{1,0:T(8,128)S(1)}, u32[]{:S(2)}, u32[]{:S(2)}) collective-permute-start(f32[136,128]{1,0:T(8,128)S(1)} %get-tuple-element.39), channel_id=1, source_target_pairs={{0,8},{1,9},{2,10},{3,11},{4,12},{5,13},{6,14},{7,15},{8,16},{9,17... | collective-permute-start | bytes 208904 | tf_op jit(solution)/shard_map/ppermute | solution.py:17
  36.0 4.6 %collective-permute-start.15 = (f32[8,128]{1,0:T(8,128)S(1)}, f32[8,128]{1,0:T(8,128)S(1)}, u32[]{:S(2)}, u32[]{:S(2)}) collective-permute-start(f32[8,128]{1,0:T(8,128)S(1)} %get-tuple-element.38.sums_ref), channel_id=1, source_target_pairs={{0,24},{1,25},{2,26},{3,27},{4,28},{5,29},{6,30},{7,31},{8,0},{9,1... | collective-permute-start | bytes 12296 | tf_op jit(solution)/shard_map/ppermute | solution.py:17
  39.3 4.5 %collective-permute-start.14 = (f32[8,128]{1,0:T(8,128)S(1)}, f32[8,128]{1,0:T(8,128)S(1)}, u32[]{:S(2)}, u32[]{:S(2)}) collective-permute-start(f32[8,128]{1,0:T(8,128)S(1)} %get-tuple-element.38.sums_ref), channel_id=1, source_target_pairs={{0,16},{1,17},{2,18},{3,19},{4,20},{5,21},{6,22},{7,23},{8,24},{9,... | collective-permute-start | bytes 12296 | tf_op jit(solution)/shard_map/ppermute | solution.py:17

commit v5 on v2

v5 whole, which is shorter than its diff:
```python
import functools

import jax
import jax.numpy as jnp
from jax import lax
from jax.experimental import pallas as pl
from jax.experimental.pallas import tpu as pltpu
from jax.sharding import PartitionSpec as P

EXTRA = 8
VMEM_BYTES = 48 * 1024 * 1024
EVEN, ODD = 0, 1


def plane_steps(steps, count):
    return lambda source: (source + steps) % count


def chip_steps(mask):
    return lambda source: source ^ (2 * mask)


def send(value, even=None, odd=None):
    count = lax.axis_size("blk")
    ways = (even, odd)
    return lax.ppermute(value, "blk", [(source, ways[source % 2](source)) for source in range(count) if ways[source % 2]])


def core_partner(value):
    swap = lambda source: source ^ 1
    return send(value, swap, swap)


def place_of(place_ref, chips):
    place = place_ref[0]
    return (place // 2) % chips, place % 2


def split_two(values):
    high = values.astype(jnp.bfloat16)
    low = (values - high.astype(jnp.float32)).astype(jnp.bfloat16)
    return high, low


def split_kernel(tiles_ref, straight_ref, turned_ref):
    slots = tiles_ref.shape[0]

    def visit(t):
        tile = tiles_ref[t]
        straight_ref[t, 0], straight_ref[t, 1] = split_two(tile)
        turned_ref[t, 0], turned_ref[t, 1] = split_two(tile.T)

    if slots <= 32:
        for t in range(slots):
            visit(t)
    else:
        lax.fori_loop(0, slots, lambda t, c: (visit(t), c)[1], 0)


def fetch_kernel(own_ref, out_ref, done):
    copy = pltpu.make_async_copy(own_ref, out_ref, done)
    copy.start()
    copy.wait()


def steps_ahead(chip, mask, chips):
    return ((chip ^ mask) - chip) & (chips - 1)


def product_kernel(planes, chips, pairs_ref, place_ref, own_ref, pair_ref, swapped_ref, first_ref, *refs):
    window = 2 * chips
    later = refs[: planes - 3]
    plane = refs[planes - 3 : planes + chips - 4]
    straight_ref, turned_ref, message_ref, total, whole, parts = refs[planes + chips - 4 :]
    rows, cols = own_ref.shape
    chip, core = place_of(place_ref, chips)
    even = core == EVEN

    def put(place, values):
        whole[place] = values
        high, low = split_two(values)
        parts[place, :, :cols] = high
        parts[place, :, cols:] = low

    put(0, own_ref[...])
    put(jnp.where(even, 1, window - 1), jnp.where(even, pair_ref[1], first_ref[0]))
    put(window, jnp.where(even, swapped_ref[2 * chips - 2], first_ref[1]))
    for m in range(1, chips):
        ahead = 2 * steps_ahead(chip, m, chips) - core
        for column in range(2):
            slot = 2 * (m - 1) + column
            put(ahead + column, jnp.where(even, swapped_ref[slot], plane[m - 1][column]))
    for k in range(2, planes):
        held = first_ref if k == 2 else later[k - 3]
        put(window - 1 + k, jnp.where(even, held[0], swapped_ref[k - 2]))

    total[...] = jnp.zeros_like(total)
    slots = straight_ref.shape[0]

    def product(split_ref, t, place):
        both = jnp.dot(split_ref[t, 0], parts[place], preferred_element_type=jnp.float32)
        rest = jnp.dot(split_ref[t, 1], parts[place, :, :cols], preferred_element_type=jnp.float32)
        return both[:, :cols] + (both[:, cols:] + rest)

    def visit(t, mirrored):
        row_place, col_place = pairs_ref[0, t], pairs_ref[1, t]
        total[row_place] += product(straight_ref, t, col_place)
        if mirrored:
            total[col_place] += product(turned_ref, t, row_place)

    visit(0, False)
    if slots <= 32:
        for t in range(1, slots - 1):
            visit(t, True)
    else:
        lax.fori_loop(1, slots - 1, lambda t, c: (visit(t, True), c)[1], 0)
    visit(slots - 1, False)

    dots = jnp.zeros((1, cols), jnp.float32)
    for place in range(whole.shape[0]):
        dots = dots + jnp.sum(whole[place] * total[place], axis=0, keepdims=True)
    own = own_ref[...]
    norm = jnp.sum(own * own, axis=0, keepdims=True)
    count = message_ref.shape[0] // rows
    wanted = []
    for m in range(1, chips):
        ahead = 2 * steps_ahead(chip, m, chips)
        wanted += [ahead, ahead + 1]
    wanted += [window, 1]
    for slot in range(count):
        from_even = wanted[slot] if slot < len(wanted) else 0
        from_odd = window + 1 + slot if slot < planes - 2 else 0
        message_ref[slot * rows : (slot + 1) * rows, :] = total[jnp.where(even, from_even, from_odd)]
    sums = jnp.concatenate([norm, dots, jnp.zeros((EXTRA - 2, cols), jnp.float32)], axis=0)
    message_ref[count * rows :, :] = sums


def pair_kernel(planes, chips, place_ref, sent_ref, total_ref, got_ref, *outs):
    messages = outs[:-3]
    near_ref, next_ref, sums_ref = outs[-3:]
    window = 2 * chips
    rows = near_ref.shape[0]
    chip, core = place_of(place_ref, chips)
    even = core == EVEN
    tail = got_ref.shape[0] - EXTRA
    sums = sent_ref[tail:, :] + got_ref[tail:, :]

    def got(slot):
        return got_ref[slot * rows : (slot + 1) * rows, :]

    for i, message in enumerate(messages):
        for column in range(2):
            part = None
            if i < planes - 2:
                part = total_ref[window + 1 + i] if column == 0 else got(i)
            if i < chips - 1:
                ahead = 2 * steps_ahead(chip, i + 1, chips)
                plane = total_ref[jnp.where(even, 0, ahead - 1 + column)] + got(2 * i + column)
                part = plane if part is None else jnp.where(even, part, plane)
            message[column * rows : (column + 1) * rows, :] = part
        message[2 * rows :, :] = sums
    near_ref[...] = total_ref[0] + jnp.where(even, 0.0, got(2 * chips - 1))
    next_ref[:rows, :] = total_ref[window - 1] + got(2 * chips - 2)
    next_ref[rows:, :] = total_ref[window]
    sums_ref[...] = sums


def apart_kernel(planes, *refs):
    out_ref = refs[-1]
    rows = refs[0].shape[0] - EXTRA
    sums = refs[0][rows:, :]
    for more in refs[1:-1]:
        sums = sums + more[rows:, :]
    out_ref[...] = sums


def plane_kernel(planes, chips, place_ref, near_ref, next_ref, sums_ref, *refs):
    got = refs[:-2]
    pair_out, message = refs[-2:]
    rows = near_ref.shape[0]
    chip, core = place_of(place_ref, chips)
    even = core == EVEN
    sums = sums_ref[...]
    near = [jnp.where(even, near_ref[...], 0.0), jnp.where(even, 0.0, near_ref[...])]
    ahead = [next_ref[:rows, :], next_ref[rows:, :]]
    for i, value in enumerate(got):
        in_plane = i < chips - 1
        same = (chip ^ (i + 1)) < chip
        mine = even if i < planes - 2 else False
        if in_plane:
            mine = jnp.logical_or(mine, jnp.logical_and(core == ODD, same))
            sums = sums + value[2 * rows :, :]
        for column in range(2):
            block = value[column * rows : (column + 1) * rows, :]
            near[column] = near[column] + jnp.where(mine, block, 0.0)
            if in_plane:
                ahead[column] = ahead[column] + jnp.where(same, 0.0, block)
    for column in range(2):
        pair_out[column * rows : (column + 1) * rows, :] = near[column]
        message[column * rows : (column + 1) * rows, :] = ahead[column]
    message[2 * rows :, :] = sums


def last_kernel(place_ref, pair_ref, sent_ref, got_ref, apart_ref, mine_ref, message_ref):
    rows = mine_ref.shape[0]
    even = place_ref[0] % 2 == EVEN
    first = pair_ref[:rows, :] + got_ref[:rows, :]
    second = pair_ref[rows:, :] + got_ref[rows : 2 * rows, :]
    mine_ref[...] = jnp.where(even, first, second)
    message_ref[:rows, :] = jnp.where(even, second, first)
    message_ref[rows:, :] = jnp.where(even, apart_ref[...], sent_ref[2 * rows :, :] + got_ref[2 * rows :, :])


def final_kernel(right_ref, mine_ref, sent_ref, got_ref, solution_ref, residual_ref):
    rows = mine_ref.shape[0]
    image = mine_ref[...] + got_ref[:rows, :]
    sums = sent_ref[rows:, :] + got_ref[rows:, :]
    step_len = sums[0:1, :] / sums[1:2, :]
    right = right_ref[...]
    solution_ref[...] = step_len * right
    residual_ref[...] = right - step_len * image


def call(kernel, smem, operands, outs, scratch=(), space=pltpu.VMEM):
    vmem = pl.BlockSpec(memory_space=pltpu.VMEM)
    return pl.pallas_call(
        kernel,
        in_specs=[pl.BlockSpec(memory_space=pltpu.SMEM)] * len(smem) + [pl.BlockSpec(memory_space=space)] * len(operands),
        out_specs=[vmem] * len(outs),
        out_shape=[jax.ShapeDtypeStruct(shape, kind) for shape, kind in outs],
        scratch_shapes=list(scratch),
        compiler_params=pltpu.CompilerParams(vmem_limit_bytes=VMEM_BYTES),
    )(*smem, *operands)


def per_device(right_side, kernel_tiles, route_pairs):
    count = lax.axis_size("blk")
    window = max(8, min(16, count // 8))
    planes, chips = count // window, window // 2
    rows, cols = right_side.shape
    slots = kernel_tiles.shape[1]
    cover_len = window + planes - 1
    place = lax.axis_index("blk").astype(jnp.int32)
    chip, core = place // 2 % chips, place % 2
    where = place[None]
    even = core == EVEN
    single, half = jnp.float32, jnp.bfloat16

    (own,) = call(fetch_kernel, (), (right_side,), [((rows, cols), single)], [pltpu.SemaphoreType.DMA], pl.ANY)
    straight, turned = call(
        split_kernel, (), (kernel_tiles[0],), [((slots, 2, rows, cols), half), ((slots, 2, cols, rows), half)]
    )
    partner = core_partner(right_side)
    pair = jnp.where(even, jnp.stack([own, partner]), jnp.stack([partner, own]))
    first = send(pair, plane_steps(-2 * window, count), plane_steps(-window, count))
    later = [send(pair, even=plane_steps(-k * window, count)) for k in range(3, planes)]
    ahead, *later = lax.optimization_barrier((first, *later))
    plane = [
        send(jnp.where((chip ^ m) < chip, pair, ahead), odd=chip_steps(m)) for m in range(1, chips)
    ]
    to_even = [value[column] for value in plane for column in range(2)] + [ahead[0]]
    to_odd = [value[1] for value in [ahead, *later]]
    swapped = core_partner(
        jnp.stack([jnp.where(even, to_odd[i], value) if i < len(to_odd) else value for i, value in enumerate(to_even)])
    )

    block, extra = ((rows, cols), single), ((EXTRA, cols), single)
    two, marked = ((2 * rows, cols), single), ((2 * rows + EXTRA, cols), single)
    sent, total = call(
        functools.partial(product_kernel, planes, chips),
        (route_pairs.T, where),
        (own, pair, swapped, ahead, *later, *plane, straight, turned),
        [((max(2 * chips, planes - 2) * rows + EXTRA, cols), single), ((cover_len, rows, cols), single)],
        (pltpu.VMEM((cover_len, rows, cols), single), pltpu.VMEM((cover_len, rows, 2 * cols), half)),
    )
    got = core_partner(sent)
    *messages, near, ahead, sums = call(
        functools.partial(pair_kernel, planes, chips),
        (where,),
        (sent, total, got),
        [marked] * max(chips - 1, planes - 2) + [block, two, extra],
    )
    got = [
        send(
            value,
            even=plane_steps((i + 2) * window, count) if i < planes - 2 else None,
            odd=chip_steps(i + 1) if i < chips - 1 else None,
        )
        for i, value in enumerate(messages)
    ]
    (apart,) = call(functools.partial(apart_kernel, planes), (), got[: planes - 2], [extra])
    mask = 1
    while mask < chips:
        apart = apart + send(apart, even=chip_steps(mask))
        mask *= 2
    pair, message = call(
        functools.partial(plane_kernel, planes, chips), (where,), (near, ahead, sums, *got), [two, marked]
    )
    got = send(message, odd=plane_steps(window, count))
    mine, sent = call(last_kernel, (where,), (pair, message, got, apart), [block, ((rows + EXTRA, cols), single)])
    got = core_partner(sent)
    return call(final_kernel, (), (own, mine, sent, got), [block, block])


def solution(mesh):
    def run(*args):
        return tuple(per_device(*args))

    return jax.shard_map(
        run,
        mesh=mesh,
        in_specs=(P("blk", None), P("blk", None, None, None), P()),
        out_specs=(P("blk", None), P("blk", None)),
        check_vma=False,
    )
```

time: 222 us -> 50.6 us (0.23)
  waiting for transfers between devices: 199 us -> 17.1 us
  starting transfers between devices: 0.08 us -> 28.3 us
  between operations: 14 us -> 0.85 us
  local copies, waits for them, and re-layouts: 4.4 us -> 0.88 us
    unnamed x3 -> x0, waiting for transfers between devices: 137 us -> none
    all_gather x1 -> x0, waiting for transfers between devices: 62 us -> none  [per_device(): blocks = lax.all_gather(right_side, 'blk')]
    ppermute x0 -> x15, starting transfers between devices: none -> 28.3 us  [send(): lax.ppermute(value, 'blk', [(source, ways[source % 2](source)) for source...]
    ppermute x0 -> x15, waiting for transfers between devices: none -> 17.1 us  [send(): lax.ppermute(value, 'blk', [(source, ways[source % 2](source)) for source...]
    unnamed x10 -> x8, local copies, waits for them, and re-layouts: 4.4 us -> 0.87 us
  transfers between devices with their start and end apart: 2 -> 15, of which waited for: 2 -> 10; matrix products, arithmetic and copies ran while one was open for 0% -> 0% of each run, Pallas kernels for 0% -> 1%
where the time goes in v5:
time: 50.6 us; the launch traced here: 50.3 us
  starting transfers between devices  28.3 us (56%)
  waiting for transfers between devices  17.1 us (34%)
  Pallas kernels  3.12 us (6%)
  local copies, waits for them, and re-layouts  0.88 us (2%)
  between operations  0.85 us (2%)
    ppermute x15, starting transfers between devices, send(): lax.ppermute(value, 'blk', [(source, ways[source % 2](source)) for source...  28.3 us
    ppermute x15, waiting for transfers between devices, send(): lax.ppermute(value, 'blk', [(source, ways[source % 2](source)) for source...  17.1 us
    pallas_call x8, Pallas kernels, call(): pl.pallas_call(kernel, in_specs=[pl.BlockSpec(memory_space=pltpu.SMEM)] *...  3.12 us
  transfers between devices with their start and end apart: 15, of which 10 were waited for; matrix products, arithmetic and copies ran while one was open for 0% of the time, Pallas kernels for 1%

profile of v5, /device:TPU:0, one launch (start us, length us, event | category | flops | bytes accessed | tf_op | source)
XLA Modules:
  0.0 50.3 jit_solution(4539038986903492250)
XLA Ops:
  0.6 0.0 copy-start
  0.6 0.5 %collective-permute-start = (f32[128,128]{1,0:T(8,128)}, f32[128,128]{1,0:T(8,128)S(1)}, u32[]{:S(2)}, u32[]{:S(2)}) collective-permute-start(f32[128,128]{1,0:T(8,128)} %own_ref.1), channel_id=1, source_target_pairs={{0,1},{1,0},{2,3},{3,2},{4,5},{5,4},{6,7},{7,6},{8,9},{9,8},{10,11... | collective-permute-start | bytes 196616 | tf_op jit(solution)/shard_map/ppermute | solution.py:26
  1.2 0.0 copy-start.1
  1.2 0.8 %copy-done.1 = f32[128,128]{1,0:T(8,128)S(1)} copy-done((f32[128,128]{1,0:T(8,128)S(1)}, f32[128,128]{1,0:T(8,128)}, u32[]{:S(2)}) %copy-start.1) | copy-done | bytes 65560
  2.0 0.1 shard_map.50.own_ref.right_ref
  2.1 0.2 collective-permute-done
  2.3 4.8 %collective-permute-start.2 = (f32[2,128,128]{2,1,0:T(8,128)S(1)}, f32[2,128,128]{2,1,0:T(8,128)S(1)}, u32[]{:S(2)}, u32[]{:S(2)}) collective-permute-start(f32[2,128,128]{2,1,0:T(8,128)S(1)} %maximum_select_fusion.pair_ref), channel_id=1, source_target_pairs={{0,8},{2,10},{4,12},{6,14},{8,16},{10,18},{12,20},{14,22},{16,24},... | collective-permute-start | bytes 393224 | tf_op jit(solution)/shard_map/ppermute | solution.py:26
  7.1 2.6 %collective-permute-start.1 = (f32[2,128,128]{2,1,0:T(8,128)S(1)}, f32[2,128,128]{2,1,0:T(8,128)S(1)}, u32[]{:S(2)}, u32[]{:S(2)}) collective-permute-start(f32[2,128,128]{2,1,0:T(8,128)S(1)} %maximum_select_fusion.pair_ref), channel_id=1, source_target_pairs={{0,16},{1,25},{2,18},{3,27},{4,20},{5,29},{6,22},{7,31},{8,24},{9,... | collective-permute-start | bytes 393224 | tf_op jit(solution)/shard_map/ppermute | solution.py:26
  9.8 2.4 %collective-permute-done.2.refs_0_ = f32[2,128,128]{2,1,0:T(8,128)S(1)} collective-permute-done((f32[2,128,128]{2,1,0:T(8,128)S(1)}, f32[2,128,128]{2,1,0:T(8,128)S(1)}, u32[]{:S(2)}, u32[]{:S(2)}) %collective-permute-start.2) | collective-permute-done | bytes 131104 | tf_op jit(solution)/shard_map/ppermute | solution.py:26
  12.1 2.8 %collective-permute-done.1.first_ref = f32[2,128,128]{2,1,0:T(8,128)S(1)} collective-permute-done((f32[2,128,128]{2,1,0:T(8,128)S(1)}, f32[2,128,128]{2,1,0:T(8,128)S(1)}, u32[]{:S(2)}, u32[]{:S(2)}) %collective-permute-start.1) | collective-permute-done | bytes 131104 | tf_op jit(solution)/shard_map/ppermute | solution.py:26
  14.9 0.0 copy-start.2
  14.9 0.7 %collective-permute-start.3 = (f32[2,128,128]{2,1,0:T(8,128)S(1)}, f32[2,128,128]{2,1,0:T(8,128)S(1)}, u32[]{:S(2)}, u32[]{:S(2)}) collective-permute-start(f32[2,128,128]{2,1,0:T(8,128)S(1)} %get-tuple-element.36), channel_id=1, source_target_pairs={{1,3},{3,1},{5,7},{7,5},{9,11},{11,9},{13,15},{15,13},{17,19},{19,... | collective-permute-start | bytes 393224 | tf_op jit(solution)/shard_map/ppermute | solution.py:26
  15.6 0.7 %collective-permute-start.5 = (f32[2,128,128]{2,1,0:T(8,128)S(1)}, f32[2,128,128]{2,1,0:T(8,128)S(1)}, u32[]{:S(2)}, u32[]{:S(2)}) collective-permute-start(f32[2,128,128]{2,1,0:T(8,128)S(1)} %get-tuple-element.34), channel_id=1, source_target_pairs={{1,7},{3,5},{5,3},{7,1},{9,15},{11,13},{13,11},{15,9},{17,23},{19,... | collective-permute-start | bytes 393224 | tf_op jit(solution)/shard_map/ppermute | solution.py:26
  16.3 0.7 %collective-permute-start.4 = (f32[2,128,128]{2,1,0:T(8,128)S(1)}, f32[2,128,128]{2,1,0:T(8,128)S(1)}, u32[]{:S(2)}, u32[]{:S(2)}) collective-permute-start(f32[2,128,128]{2,1,0:T(8,128)S(1)} %get-tuple-element.35), channel_id=1, source_target_pairs={{1,5},{3,7},{5,1},{7,3},{9,13},{11,15},{13,9},{15,11},{17,21},{19,... | collective-permute-start | bytes 393224 | tf_op jit(solution)/shard_map/ppermute | solution.py:26
  17.0 0.0 collective-permute-done.3.refs_1_
  17.0 0.0 collective-permute-done.4.refs_2_
  17.0 0.0 collective-permute-done.5.refs_3_
  17.1 6.2 %collective-permute-start.6 = (f32[7,128,128]{2,1,0:T(8,128)S(1)}, f32[7,128,128]{2,1,0:T(8,128)S(1)}, u32[]{:S(2)}, u32[]{:S(2)}) collective-permute-start(f32[7,128,128]{2,1,0:T(8,128)S(1)} %slice_dynamic-update-slice_fusion), channel_id=1, source_target_pairs={{0,1},{1,0},{2,3},{3,2},{4,5},{5,4},{6,7},{7,6},{8,9},{9,8},{10,11... | collective-permute-start | bytes 1376264 | tf_op jit(solution)/shard_map/ppermute | solution.py:26
  23.3 0.0 copy-done
  23.3 0.4 shard_map.51
  23.7 1.1 %collective-permute-done.6.swapped_ref = f32[7,128,128]{2,1,0:T(8,128)S(1)} collective-permute-done((f32[7,128,128]{2,1,0:T(8,128)S(1)}, f32[7,128,128]{2,1,0:T(8,128)S(1)}, u32[]{:S(2)}, u32[]{:S(2)}) %collective-permute-start.6) | collective-permute-done | bytes 458784 | tf_op jit(solution)/shard_map/ppermute | solution.py:26
  24.7 0.0 copy-done.2
  24.7 1.9 %shard_map.52 = (f32[1032,128]{1,0:T(8,128)S(1)}, f32[11,128,128]{2,1,0:T(8,128)S(1)}) custom-call(s32[2,17]{1,0:T(2,128)S(1)} %bitcast.8, s32[1]{0:T(128)} %bitcast.place_ref, f32[128,128]{1,0:T(8,128)S(1)} %shard_map.50.own_ref.right_ref, f32[2,128,128]{2,1,0:T(8,128)S(1)} %maximum_select_fusion.pair_ref, ...), custom_call_target="tpu_custom_call" | custom-call | tf_op jit(solution)/shard_map/pallas_call | solution.py:226
  26.6 0.4 collective-permute-start.7
  27.0 1.5 %collective-permute-done.7.got_ref = f32[1032,128]{1,0:T(8,128)S(1)} collective-permute-done((f32[1032,128]{1,0:T(8,128)S(1)}, f32[1032,128]{1,0:T(8,128)S(1)}, u32[]{:S(2)}, u32[]{:S(2)}) %collective-permute-start.7) | collective-permute-done | bytes 528416 | tf_op jit(solution)/shard_map/ppermute | solution.py:26
  28.6 0.1 shard_map.53
  28.6 0.1 collective-permute-start.8
  28.7 4.2 %collective-permute-start.9 = (f32[264,128]{1,0:T(8,128)S(1)}, f32[264,128]{1,0:T(8,128)S(1)}, u32[]{:S(2)}, u32[]{:S(2)}) collective-permute-start(f32[264,128]{1,0:T(8,128)S(1)} %get-tuple-element.28), channel_id=1, source_target_pairs={{0,24},{1,5},{2,26},{3,7},{4,28},{5,1},{6,30},{7,3},{8,0},{9,13},{... | collective-permute-start | bytes 405512 | tf_op jit(solution)/shard_map/ppermute | solution.py:26
  32.9 0.7 %collective-permute-start.10 = (f32[264,128]{1,0:T(8,128)S(1)}, f32[264,128]{1,0:T(8,128)S(1)}, u32[]{:S(2)}, u32[]{:S(2)}) collective-permute-start(f32[264,128]{1,0:T(8,128)S(1)} %get-tuple-element.29), channel_id=1, source_target_pairs={{1,7},{3,5},{5,3},{7,1},{9,15},{11,13},{13,11},{15,9},{17,23},{19,... | collective-permute-start | bytes 405512 | tf_op jit(solution)/shard_map/ppermute | solution.py:26
  33.5 2.6 %collective-permute-done.8.refs_0_ = f32[264,128]{1,0:T(8,128)S(1)} collective-permute-done((f32[264,128]{1,0:T(8,128)S(1)}, f32[264,128]{1,0:T(8,128)S(1)}, u32[]{:S(2)}, u32[]{:S(2)}) %collective-permute-start.8) | collective-permute-done | bytes 135200 | tf_op jit(solution)/shard_map/ppermute | solution.py:26
  36.2 0.4 collective-permute-done.9.refs_1_
  36.5 0.0 collective-permute-done.10.refs_2_
  36.5 0.1 shard_map.54
  36.6 0.7 %collective-permute-start.11 = (f32[264,128]{1,0:T(8,128)S(1)}, f32[264,128]{1,0:T(8,128)S(1)}, u32[]{:S(2)}, u32[]{:S(2)}) collective-permute-start(f32[264,128]{1,0:T(8,128)S(1)} %get-tuple-element.31.sent_ref), channel_id=1, source_target_pairs={{1,9},{3,11},{5,13},{7,15},{9,17},{11,19},{13,21},{15,23},{17,25},... | collective-permute-start | bytes 405512 | tf_op jit(solution)/shard_map/ppermute | solution.py:26
  37.3 3.4 %collective-permute-start.12 = (f32[8,128]{1,0:T(8,128)S(1)}, f32[8,128]{1,0:T(8,128)S(1)}, u32[]{:S(2)}, u32[]{:S(2)}) collective-permute-start(f32[8,128]{1,0:T(8,128)S(1)} %shard_map.55), channel_id=1, source_target_pairs={{0,2},{2,0},{4,6},{6,4},{8,10},{10,8},{12,14},{14,12},{16,18},{18,... | collective-permute-start | bytes 12296 | tf_op jit(solution)/shard_map/ppermute | solution.py:26
  40.7 2.1 %collective-permute-done.12 = f32[8,128]{1,0:T(8,128)S(1)} collective-permute-done((f32[8,128]{1,0:T(8,128)S(1)}, f32[8,128]{1,0:T(8,128)S(1)}, u32[]{:S(2)}, u32[]{:S(2)}) %collective-permute-start.12) | collective-permute-done | bytes 4128 | tf_op jit(solution)/shard_map/ppermute | solution.py:26
  42.8 2.6 %collective-permute-start.13 = (f32[8,128]{1,0:T(8,128)S(1)}, f32[8,128]{1,0:T(8,128)S(1)}, u32[]{:S(2)}, u32[]{:S(2)}) collective-permute-start(f32[8,128]{1,0:T(8,128)S(1)} %add.16), channel_id=1, source_target_pairs={{0,4},{2,6},{4,0},{6,2},{8,12},{10,14},{12,8},{14,10},{16,20},{18,... | collective-permute-start | bytes 12296 | tf_op jit(solution)/shard_map/ppermute | solution.py:26
  45.4 2.9 %collective-permute-done.13 = f32[8,128]{1,0:T(8,128)S(1)} collective-permute-done((f32[8,128]{1,0:T(8,128)S(1)}, f32[8,128]{1,0:T(8,128)S(1)}, u32[]{:S(2)}, u32[]{:S(2)}) %collective-permute-start.13) | collective-permute-done | bytes 4128 | tf_op jit(solution)/shard_map/ppermute | solution.py:26
  48.3 0.0 collective-permute-done.11.got_ref
  48.3 0.1 collective-permute-start.14
  48.4 1.2 %collective-permute-done.14.got_ref = f32[136,128]{1,0:T(8,128)S(1)} collective-permute-done((f32[136,128]{1,0:T(8,128)S(1)}, f32[136,128]{1,0:T(8,128)S(1)}, u32[]{:S(2)}, u32[]{:S(2)}) %collective-permute-start.14) | collective-permute-done | bytes 69664 | tf_op jit(solution)/shard_map/ppermute | solution.py:26
  49.7 0.7 %shard_map.57 = (f32[128,128]{1,0:T(8,128)}, f32[128,128]{1,0:T(8,128)}) custom-call(f32[128,128]{1,0:T(8,128)S(1)} %shard_map.50.own_ref.right_ref, f32[128,128]{1,0:T(8,128)S(1)} %get-tuple-element.32.mine_ref, f32[136,128]{1,0:T(8,128)S(1)} %get-tuple-element.33.sent_ref, f32[136,128]{1,0:T(8,128)S(1)} %collective-permute-done.14.got_ref), custom_call_target="tpu_custom_call" | custom-call | tf_op jit(solution)/shard_map/pallas_call | solution.py:226
  (11 shorter events, 0.1 us)
Async XLA Ops:
  0.6 22.7 %copy-start = (f32[1,17,128,128]{3,2,1,0:T(8,128)S(1)}, f32[1,17,128,128]{3,2,1,0:T(8,128)}, u32[]{:S(2)}) copy-start(f32[1,17,128,128]{3,2,1,0:T(8,128)} %param.4) | copy-start | bytes 3342340
  0.6 1.6 %collective-permute-start = (f32[128,128]{1,0:T(8,128)}, f32[128,128]{1,0:T(8,128)S(1)}, u32[]{:S(2)}, u32[]{:S(2)}) collective-permute-start(f32[128,128]{1,0:T(8,128)} %own_ref.1), channel_id=1, source_target_pairs={{0,1},{1,0},{2,3},{3,2},{4,5},{5,4},{6,7},{7,6},{8,9},{9,8},{10,11... | collective-permute-start | bytes 196616 | tf_op jit(solution)/shard_map/ppermute | solution.py:26
  1.2 0.8 %copy-start.1 = (f32[128,128]{1,0:T(8,128)S(1)}, f32[128,128]{1,0:T(8,128)}, u32[]{:S(2)}) copy-start(f32[128,128]{1,0:T(8,128)} %own_ref.1) | copy-start | bytes 196612
  2.3 9.8 %collective-permute-start.2 = (f32[2,128,128]{2,1,0:T(8,128)S(1)}, f32[2,128,128]{2,1,0:T(8,128)S(1)}, u32[]{:S(2)}, u32[]{:S(2)}) collective-permute-start(f32[2,128,128]{2,1,0:T(8,128)S(1)} %maximum_select_fusion.pair_ref), channel_id=1, source_target_pairs={{0,8},{2,10},{4,12},{6,14},{8,16},{10,18},{12,20},{14,22},{16,24},... | collective-permute-start | bytes 393224 | tf_op jit(solution)/shard_map/ppermute | solution.py:26
  7.1 7.8 %collective-permute-start.1 = (f32[2,128,128]{2,1,0:T(8,128)S(1)}, f32[2,128,128]{2,1,0:T(8,128)S(1)}, u32[]{:S(2)}, u32[]{:S(2)}) collective-permute-start(f32[2,128,128]{2,1,0:T(8,128)S(1)} %maximum_select_fusion.pair_ref), channel_id=1, source_target_pairs={{0,16},{1,25},{2,18},{3,27},{4,20},{5,29},{6,22},{7,31},{8,24},{9,... | collective-permute-start | bytes 393224 | tf_op jit(solution)/shard_map/ppermute | solution.py:26
  14.9 9.8 %copy-start.2 = (s32[17,2]{0,1:T(2,128)S(1)}, s32[17,2]{0,1:T(2,128)}, u32[]{:S(2)}) copy-start(s32[17,2]{0,1:T(2,128)} %param.5) | copy-start | bytes 412
  14.9 2.0 %collective-permute-start.3 = (f32[2,128,128]{2,1,0:T(8,128)S(1)}, f32[2,128,128]{2,1,0:T(8,128)S(1)}, u32[]{:S(2)}, u32[]{:S(2)}) collective-permute-start(f32[2,128,128]{2,1,0:T(8,128)S(1)} %get-tuple-element.36), channel_id=1, source_target_pairs={{1,3},{3,1},{5,7},{7,5},{9,11},{11,9},{13,15},{15,13},{17,19},{19,... | collective-permute-start | bytes 393224 | tf_op jit(solution)/shard_map/ppermute | solution.py:26
  15.6 1.4 %collective-permute-start.5 = (f32[2,128,128]{2,1,0:T(8,128)S(1)}, f32[2,128,128]{2,1,0:T(8,128)S(1)}, u32[]{:S(2)}, u32[]{:S(2)}) collective-permute-start(f32[2,128,128]{2,1,0:T(8,128)S(1)} %get-tuple-element.34), channel_id=1, source_target_pairs={{1,7},{3,5},{5,3},{7,1},{9,15},{11,13},{13,11},{15,9},{17,23},{19,... | collective-permute-start | bytes 393224 | tf_op jit(solution)/shard_map/ppermute | solution.py:26
  16.3 0.7 %collective-permute-start.4 = (f32[2,128,128]{2,1,0:T(8,128)S(1)}, f32[2,128,128]{2,1,0:T(8,128)S(1)}, u32[]{:S(2)}, u32[]{:S(2)}) collective-permute-start(f32[2,128,128]{2,1,0:T(8,128)S(1)} %get-tuple-element.35), channel_id=1, source_target_pairs={{1,5},{3,7},{5,1},{7,3},{9,13},{11,15},{13,9},{15,11},{17,21},{19,... | collective-permute-start | bytes 393224 | tf_op jit(solution)/shard_map/ppermute | solution.py:26
  17.1 7.6 %collective-permute-start.6 = (f32[7,128,128]{2,1,0:T(8,128)S(1)}, f32[7,128,128]{2,1,0:T(8,128)S(1)}, u32[]{:S(2)}, u32[]{:S(2)}) collective-permute-start(f32[7,128,128]{2,1,0:T(8,128)S(1)} %slice_dynamic-update-slice_fusion), channel_id=1, source_target_pairs={{0,1},{1,0},{2,3},{3,2},{4,5},{5,4},{6,7},{7,6},{8,9},{9,8},{10,11... | collective-permute-start | bytes 1376264 | tf_op jit(solution)/shard_map/ppermute | solution.py:26
  26.6 2.0 %collective-permute-start.7 = (f32[1032,128]{1,0:T(8,128)S(1)}, f32[1032,128]{1,0:T(8,128)S(1)}, u32[]{:S(2)}, u32[]{:S(2)}) collective-permute-start(f32[1032,128]{1,0:T(8,128)S(1)} %get-tuple-element.22.sent_ref), channel_id=1, source_target_pairs={{0,1},{1,0},{2,3},{3,2},{4,5},{5,4},{6,7},{7,6},{8,9},{9,8},{10,11... | collective-permute-start | bytes 1585160 | tf_op jit(solution)/shard_map/ppermute | solution.py:26
  28.6 7.5 %collective-permute-start.8 = (f32[264,128]{1,0:T(8,128)S(1)}, f32[264,128]{1,0:T(8,128)S(1)}, u32[]{:S(2)}, u32[]{:S(2)}) collective-permute-start(f32[264,128]{1,0:T(8,128)S(1)} %get-tuple-element.27), channel_id=1, source_target_pairs={{0,16},{1,3},{2,18},{3,1},{4,20},{5,7},{6,22},{7,5},{8,24},{9,11},... | collective-permute-start | bytes 405512 | tf_op jit(solution)/shard_map/ppermute | solution.py:26
  28.7 7.8 %collective-permute-start.9 = (f32[264,128]{1,0:T(8,128)S(1)}, f32[264,128]{1,0:T(8,128)S(1)}, u32[]{:S(2)}, u32[]{:S(2)}) collective-permute-start(f32[264,128]{1,0:T(8,128)S(1)} %get-tuple-element.28), channel_id=1, source_target_pairs={{0,24},{1,5},{2,26},{3,7},{4,28},{5,1},{6,30},{7,3},{8,0},{9,13},{... | collective-permute-start | bytes 405512 | tf_op jit(solution)/shard_map/ppermute | solution.py:26
  32.9 3.7 %collective-permute-start.10 = (f32[264,128]{1,0:T(8,128)S(1)}, f32[264,128]{1,0:T(8,128)S(1)}, u32[]{:S(2)}, u32[]{:S(2)}) collective-permute-start(f32[264,128]{1,0:T(8,128)S(1)} %get-tuple-element.29), channel_id=1, source_target_pairs={{1,7},{3,5},{5,3},{7,1},{9,15},{11,13},{13,11},{15,9},{17,23},{19,... | collective-permute-start | bytes 405512 | tf_op jit(solution)/shard_map/ppermute | solution.py:26
  36.6 11.7 %collective-permute-start.11 = (f32[264,128]{1,0:T(8,128)S(1)}, f32[264,128]{1,0:T(8,128)S(1)}, u32[]{:S(2)}, u32[]{:S(2)}) collective-permute-start(f32[264,128]{1,0:T(8,128)S(1)} %get-tuple-element.31.sent_ref), channel_id=1, source_target_pairs={{1,9},{3,11},{5,13},{7,15},{9,17},{11,19},{13,21},{15,23},{17,25},... | collective-permute-start | bytes 405512 | tf_op jit(solution)/shard_map/ppermute | solution.py:26
  37.3 5.5 %collective-permute-start.12 = (f32[8,128]{1,0:T(8,128)S(1)}, f32[8,128]{1,0:T(8,128)S(1)}, u32[]{:S(2)}, u32[]{:S(2)}) collective-permute-start(f32[8,128]{1,0:T(8,128)S(1)} %shard_map.55), channel_id=1, source_target_pairs={{0,2},{2,0},{4,6},{6,4},{8,10},{10,8},{12,14},{14,12},{16,18},{18,... | collective-permute-start | bytes 12296 | tf_op jit(solution)/shard_map/ppermute | solution.py:26
  42.8 5.5 %collective-permute-start.13 = (f32[8,128]{1,0:T(8,128)S(1)}, f32[8,128]{1,0:T(8,128)S(1)}, u32[]{:S(2)}, u32[]{:S(2)}) collective-permute-start(f32[8,128]{1,0:T(8,128)S(1)} %add.16), channel_id=1, source_target_pairs={{0,4},{2,6},{4,0},{6,2},{8,12},{10,14},{12,8},{14,10},{16,20},{18,... | collective-permute-start | bytes 12296 | tf_op jit(solution)/shard_map/ppermute | solution.py:26
  48.3 1.3 %collective-permute-start.14 = (f32[136,128]{1,0:T(8,128)S(1)}, f32[136,128]{1,0:T(8,128)S(1)}, u32[]{:S(2)}, u32[]{:S(2)}) collective-permute-start(f32[136,128]{1,0:T(8,128)S(1)} %get-tuple-element.33.sent_ref), channel_id=1, source_target_pairs={{0,1},{1,0},{2,3},{3,2},{4,5},{5,4},{6,7},{7,6},{8,9},{9,8},{10,11... | collective-permute-start | bytes 208904 | tf_op jit(solution)/shard_map/ppermute | solution.py:26

commit v6 on v5

--- a/solution.py
+++ b/solution.py
@@ -22,8 +22,8 @@
 
 def send(value, even=None, odd=None):
     count = lax.axis_size("blk")
-    ways = (even, odd)
-    return lax.ppermute(value, "blk", [(source, ways[source % 2](source)) for source in range(count) if ways[source % 2]])
+    ways = [way or (lambda source: source) for way in (even, odd)]
+    return lax.ppermute(value, "blk", [(source, ways[source % 2](source)) for source in range(count)])
 
 
 def core_partner(value):
@@ -204,8 +204,8 @@
 def last_kernel(place_ref, pair_ref, sent_ref, got_ref, apart_ref, mine_ref, message_ref):
     rows = mine_ref.shape[0]
     even = place_ref[0] % 2 == EVEN
-    first = pair_ref[:rows, :] + got_ref[:rows, :]
-    second = pair_ref[rows:, :] + got_ref[rows : 2 * rows, :]
+    first = pair_ref[:rows, :] + jnp.where(even, 0.0, got_ref[:rows, :])
+    second = pair_ref[rows:, :] + jnp.where(even, 0.0, got_ref[rows : 2 * rows, :])
     mine_ref[...] = jnp.where(even, first, second)
     message_ref[:rows, :] = jnp.where(even, second, first)
     message_ref[rows:, :] = jnp.where(even, apart_ref[...], sent_ref[2 * rows :, :] + got_ref[2 * rows :, :])

time: 50.6 us -> 50.6 us (level)
  no operation moved by 1% of the time
where the time goes in v6:
time: 50.6 us; the launch traced here: 50.3 us
  starting transfers between devices  28.3 us (56%)
  waiting for transfers between devices  17.1 us (34%)
  Pallas kernels  3.13 us (6%)
  local copies, waits for them, and re-layouts  0.88 us (2%)
  between operations  0.85 us (2%)
    ppermute x15, starting transfers between devices, send(): lax.ppermute(value, 'blk', [(source, ways[source % 2](source)) for source...  28.3 us
    ppermute x15, waiting for transfers between devices, send(): lax.ppermute(value, 'blk', [(source, ways[source % 2](source)) for source...  17.1 us
    pallas_call x8, Pallas kernels, call(): pl.pallas_call(kernel, in_specs=[pl.BlockSpec(memory_space=pltpu.SMEM)] *...  3.13 us
  transfers between devices with their start and end apart: 15, of which 10 were waited for; matrix products, arithmetic and copies ran while one was open for 0% of the time, Pallas kernels for 1%

profile of v6, /device:TPU:0, one launch (start us, length us, event | category | flops | bytes accessed | tf_op | source)
XLA Modules:
  0.0 50.3 jit_solution(7170985350023307065)
XLA Ops:
  0.6 0.0 copy-start
  0.6 0.5 %collective-permute-start = (f32[128,128]{1,0:T(8,128)}, f32[128,128]{1,0:T(8,128)S(1)}, u32[]{:S(2)}, u32[]{:S(2)}) collective-permute-start(f32[128,128]{1,0:T(8,128)} %own_ref.1), channel_id=1, source_target_pairs={{0,1},{1,0},{2,3},{3,2},{4,5},{5,4},{6,7},{7,6},{8,9},{9,8},{10,11... | collective-permute-start | bytes 196616 | tf_op jit(solution)/shard_map/ppermute | solution.py:26
  1.2 0.0 copy-start.1
  1.2 0.8 %copy-done.1 = f32[128,128]{1,0:T(8,128)S(1)} copy-done((f32[128,128]{1,0:T(8,128)S(1)}, f32[128,128]{1,0:T(8,128)}, u32[]{:S(2)}) %copy-start.1) | copy-done | bytes 65560
  2.0 0.1 shard_map.50.own_ref.right_ref
  2.1 0.2 collective-permute-done
  2.3 4.8 %collective-permute-start.2 = (f32[2,128,128]{2,1,0:T(8,128)S(1)}, f32[2,128,128]{2,1,0:T(8,128)S(1)}, u32[]{:S(2)}, u32[]{:S(2)}) collective-permute-start(f32[2,128,128]{2,1,0:T(8,128)S(1)} %maximum_select_fusion.pair_ref), channel_id=1, source_target_pairs={{0,8},{1,1},{2,10},{3,3},{4,12},{5,5},{6,14},{7,7},{8,16},{9,9},{1... | collective-permute-start | bytes 393224 | tf_op jit(solution)/shard_map/ppermute | solution.py:26
  7.1 2.6 %collective-permute-start.1 = (f32[2,128,128]{2,1,0:T(8,128)S(1)}, f32[2,128,128]{2,1,0:T(8,128)S(1)}, u32[]{:S(2)}, u32[]{:S(2)}) collective-permute-start(f32[2,128,128]{2,1,0:T(8,128)S(1)} %maximum_select_fusion.pair_ref), channel_id=1, source_target_pairs={{0,16},{1,25},{2,18},{3,27},{4,20},{5,29},{6,22},{7,31},{8,24},{9,... | collective-permute-start | bytes 393224 | tf_op jit(solution)/shard_map/ppermute | solution.py:26
  9.8 2.4 %collective-permute-done.2.refs_0_ = f32[2,128,128]{2,1,0:T(8,128)S(1)} collective-permute-done((f32[2,128,128]{2,1,0:T(8,128)S(1)}, f32[2,128,128]{2,1,0:T(8,128)S(1)}, u32[]{:S(2)}, u32[]{:S(2)}) %collective-permute-start.2) | collective-permute-done | bytes 131104 | tf_op jit(solution)/shard_map/ppermute | solution.py:26
  12.1 2.8 %collective-permute-done.1.first_ref = f32[2,128,128]{2,1,0:T(8,128)S(1)} collective-permute-done((f32[2,128,128]{2,1,0:T(8,128)S(1)}, f32[2,128,128]{2,1,0:T(8,128)S(1)}, u32[]{:S(2)}, u32[]{:S(2)}) %collective-permute-start.1) | collective-permute-done | bytes 131104 | tf_op jit(solution)/shard_map/ppermute | solution.py:26
  14.9 0.0 copy-start.2
  14.9 0.7 %collective-permute-start.3 = (f32[2,128,128]{2,1,0:T(8,128)S(1)}, f32[2,128,128]{2,1,0:T(8,128)S(1)}, u32[]{:S(2)}, u32[]{:S(2)}) collective-permute-start(f32[2,128,128]{2,1,0:T(8,128)S(1)} %get-tuple-element.36), channel_id=1, source_target_pairs={{0,0},{1,3},{2,2},{3,1},{4,4},{5,7},{6,6},{7,5},{8,8},{9,11},{10,1... | collective-permute-start | bytes 393224 | tf_op jit(solution)/shard_map/ppermute | solution.py:26
  15.6 0.7 %collective-permute-start.5 = (f32[2,128,128]{2,1,0:T(8,128)S(1)}, f32[2,128,128]{2,1,0:T(8,128)S(1)}, u32[]{:S(2)}, u32[]{:S(2)}) collective-permute-start(f32[2,128,128]{2,1,0:T(8,128)S(1)} %get-tuple-element.34), channel_id=1, source_target_pairs={{0,0},{1,7},{2,2},{3,5},{4,4},{5,3},{6,6},{7,1},{8,8},{9,15},{10,1... | collective-permute-start | bytes 393224 | tf_op jit(solution)/shard_map/ppermute | solution.py:26
  16.3 0.7 %collective-permute-start.4 = (f32[2,128,128]{2,1,0:T(8,128)S(1)}, f32[2,128,128]{2,1,0:T(8,128)S(1)}, u32[]{:S(2)}, u32[]{:S(2)}) collective-permute-start(f32[2,128,128]{2,1,0:T(8,128)S(1)} %get-tuple-element.35), channel_id=1, source_target_pairs={{0,0},{1,5},{2,2},{3,7},{4,4},{5,1},{6,6},{7,3},{8,8},{9,13},{10,1... | collective-permute-start | bytes 393224 | tf_op jit(solution)/shard_map/ppermute | solution.py:26
  17.0 0.0 collective-permute-done.3.refs_1_
  17.0 0.0 collective-permute-done.4.refs_2_
  17.0 0.0 collective-permute-done.5.refs_3_
  17.1 6.2 %collective-permute-start.6 = (f32[7,128,128]{2,1,0:T(8,128)S(1)}, f32[7,128,128]{2,1,0:T(8,128)S(1)}, u32[]{:S(2)}, u32[]{:S(2)}) collective-permute-start(f32[7,128,128]{2,1,0:T(8,128)S(1)} %slice_dynamic-update-slice_fusion), channel_id=1, source_target_pairs={{0,1},{1,0},{2,3},{3,2},{4,5},{5,4},{6,7},{7,6},{8,9},{9,8},{10,11... | collective-permute-start | bytes 1376264 | tf_op jit(solution)/shard_map/ppermute | solution.py:26
  23.3 0.0 copy-done
  23.3 0.4 shard_map.51
  23.7 1.1 %collective-permute-done.6.swapped_ref = f32[7,128,128]{2,1,0:T(8,128)S(1)} collective-permute-done((f32[7,128,128]{2,1,0:T(8,128)S(1)}, f32[7,128,128]{2,1,0:T(8,128)S(1)}, u32[]{:S(2)}, u32[]{:S(2)}) %collective-permute-start.6) | collective-permute-done | bytes 458784 | tf_op jit(solution)/shard_map/ppermute | solution.py:26
  24.7 0.0 copy-done.2
  24.7 1.9 %shard_map.52 = (f32[1032,128]{1,0:T(8,128)S(1)}, f32[11,128,128]{2,1,0:T(8,128)S(1)}) custom-call(s32[2,17]{1,0:T(2,128)S(1)} %bitcast.8, s32[1]{0:T(128)} %bitcast.place_ref, f32[128,128]{1,0:T(8,128)S(1)} %shard_map.50.own_ref.right_ref, f32[2,128,128]{2,1,0:T(8,128)S(1)} %maximum_select_fusion.pair_ref, ...), custom_call_target="tpu_custom_call" | custom-call | tf_op jit(solution)/shard_map/pallas_call | solution.py:226
  26.6 0.4 collective-permute-start.7
  27.0 1.5 %collective-permute-done.7.got_ref = f32[1032,128]{1,0:T(8,128)S(1)} collective-permute-done((f32[1032,128]{1,0:T(8,128)S(1)}, f32[1032,128]{1,0:T(8,128)S(1)}, u32[]{:S(2)}, u32[]{:S(2)}) %collective-permute-start.7) | collective-permute-done | bytes 528416 | tf_op jit(solution)/shard_map/ppermute | solution.py:26
  28.6 0.1 shard_map.53
  28.6 0.1 collective-permute-start.8
  28.7 4.2 %collective-permute-start.9 = (f32[264,128]{1,0:T(8,128)S(1)}, f32[264,128]{1,0:T(8,128)S(1)}, u32[]{:S(2)}, u32[]{:S(2)}) collective-permute-start(f32[264,128]{1,0:T(8,128)S(1)} %get-tuple-element.28), channel_id=1, source_target_pairs={{0,24},{1,5},{2,26},{3,7},{4,28},{5,1},{6,30},{7,3},{8,0},{9,13},{... | collective-permute-start | bytes 405512 | tf_op jit(solution)/shard_map/ppermute | solution.py:26
  32.9 0.7 %collective-permute-start.10 = (f32[264,128]{1,0:T(8,128)S(1)}, f32[264,128]{1,0:T(8,128)S(1)}, u32[]{:S(2)}, u32[]{:S(2)}) collective-permute-start(f32[264,128]{1,0:T(8,128)S(1)} %get-tuple-element.29), channel_id=1, source_target_pairs={{0,0},{1,7},{2,2},{3,5},{4,4},{5,3},{6,6},{7,1},{8,8},{9,15},{10,1... | collective-permute-start | bytes 405512 | tf_op jit(solution)/shard_map/ppermute | solution.py:26
  33.5 2.6 %collective-permute-done.8.refs_0_ = f32[264,128]{1,0:T(8,128)S(1)} collective-permute-done((f32[264,128]{1,0:T(8,128)S(1)}, f32[264,128]{1,0:T(8,128)S(1)}, u32[]{:S(2)}, u32[]{:S(2)}) %collective-permute-start.8) | collective-permute-done | bytes 135200 | tf_op jit(solution)/shard_map/ppermute | solution.py:26
  36.2 0.4 collective-permute-done.9.refs_1_
  36.5 0.0 collective-permute-done.10.refs_2_
  36.5 0.1 shard_map.54
  36.6 0.7 %collective-permute-start.11 = (f32[264,128]{1,0:T(8,128)S(1)}, f32[264,128]{1,0:T(8,128)S(1)}, u32[]{:S(2)}, u32[]{:S(2)}) collective-permute-start(f32[264,128]{1,0:T(8,128)S(1)} %get-tuple-element.31.sent_ref), channel_id=1, source_target_pairs={{0,0},{1,9},{2,2},{3,11},{4,4},{5,13},{6,6},{7,15},{8,8},{9,17},{1... | collective-permute-start | bytes 405512 | tf_op jit(solution)/shard_map/ppermute | solution.py:26
  37.3 3.4 %collective-permute-start.12 = (f32[8,128]{1,0:T(8,128)S(1)}, f32[8,128]{1,0:T(8,128)S(1)}, u32[]{:S(2)}, u32[]{:S(2)}) collective-permute-start(f32[8,128]{1,0:T(8,128)S(1)} %shard_map.55), channel_id=1, source_target_pairs={{0,2},{1,1},{2,0},{3,3},{4,6},{5,5},{6,4},{7,7},{8,10},{9,9},{10,8... | collective-permute-start | bytes 12296 | tf_op jit(solution)/shard_map/ppermute | solution.py:26
  40.7 2.1 %collective-permute-done.12 = f32[8,128]{1,0:T(8,128)S(1)} collective-permute-done((f32[8,128]{1,0:T(8,128)S(1)}, f32[8,128]{1,0:T(8,128)S(1)}, u32[]{:S(2)}, u32[]{:S(2)}) %collective-permute-start.12) | collective-permute-done | bytes 4128 | tf_op jit(solution)/shard_map/ppermute | solution.py:26
  42.8 2.6 %collective-permute-start.13 = (f32[8,128]{1,0:T(8,128)S(1)}, f32[8,128]{1,0:T(8,128)S(1)}, u32[]{:S(2)}, u32[]{:S(2)}) collective-permute-start(f32[8,128]{1,0:T(8,128)S(1)} %add.16), channel_id=1, source_target_pairs={{0,4},{1,1},{2,6},{3,3},{4,0},{5,5},{6,2},{7,7},{8,12},{9,9},{10,1... | collective-permute-start | bytes 12296 | tf_op jit(solution)/shard_map/ppermute | solution.py:26
  45.4 2.9 %collective-permute-done.13 = f32[8,128]{1,0:T(8,128)S(1)} collective-permute-done((f32[8,128]{1,0:T(8,128)S(1)}, f32[8,128]{1,0:T(8,128)S(1)}, u32[]{:S(2)}, u32[]{:S(2)}) %collective-permute-start.13) | collective-permute-done | bytes 4128 | tf_op jit(solution)/shard_map/ppermute | solution.py:26
  48.3 0.0 collective-permute-done.11.got_ref
  48.3 0.1 collective-permute-start.14
  48.4 1.2 %collective-permute-done.14.got_ref = f32[136,128]{1,0:T(8,128)S(1)} collective-permute-done((f32[136,128]{1,0:T(8,128)S(1)}, f32[136,128]{1,0:T(8,128)S(1)}, u32[]{:S(2)}, u32[]{:S(2)}) %collective-permute-start.14) | collective-permute-done | bytes 69664 | tf_op jit(solution)/shard_map/ppermute | solution.py:26
  49.7 0.7 %shard_map.57 = (f32[128,128]{1,0:T(8,128)}, f32[128,128]{1,0:T(8,128)}) custom-call(f32[128,128]{1,0:T(8,128)S(1)} %shard_map.50.own_ref.right_ref, f32[128,128]{1,0:T(8,128)S(1)} %get-tuple-element.32.mine_ref, f32[136,128]{1,0:T(8,128)S(1)} %get-tuple-element.33.sent_ref, f32[136,128]{1,0:T(8,128)S(1)} %collective-permute-done.14.got_ref), custom_call_target="tpu_custom_call" | custom-call | tf_op jit(solution)/shard_map/pallas_call | solution.py:226
  (11 shorter events, 0.1 us)
Async XLA Ops:
  0.6 22.7 %copy-start = (f32[1,17,128,128]{3,2,1,0:T(8,128)S(1)}, f32[1,17,128,128]{3,2,1,0:T(8,128)}, u32[]{:S(2)}) copy-start(f32[1,17,128,128]{3,2,1,0:T(8,128)} %param.4) | copy-start | bytes 3342340
  0.6 1.6 %collective-permute-start = (f32[128,128]{1,0:T(8,128)}, f32[128,128]{1,0:T(8,128)S(1)}, u32[]{:S(2)}, u32[]{:S(2)}) collective-permute-start(f32[128,128]{1,0:T(8,128)} %own_ref.1), channel_id=1, source_target_pairs={{0,1},{1,0},{2,3},{3,2},{4,5},{5,4},{6,7},{7,6},{8,9},{9,8},{10,11... | collective-permute-start | bytes 196616 | tf_op jit(solution)/shard_map/ppermute | solution.py:26
  1.2 0.8 %copy-start.1 = (f32[128,128]{1,0:T(8,128)S(1)}, f32[128,128]{1,0:T(8,128)}, u32[]{:S(2)}) copy-start(f32[128,128]{1,0:T(8,128)} %own_ref.1) | copy-start | bytes 196612
  2.3 9.8 %collective-permute-start.2 = (f32[2,128,128]{2,1,0:T(8,128)S(1)}, f32[2,128,128]{2,1,0:T(8,128)S(1)}, u32[]{:S(2)}, u32[]{:S(2)}) collective-permute-start(f32[2,128,128]{2,1,0:T(8,128)S(1)} %maximum_select_fusion.pair_ref), channel_id=1, source_target_pairs={{0,8},{1,1},{2,10},{3,3},{4,12},{5,5},{6,14},{7,7},{8,16},{9,9},{1... | collective-permute-start | bytes 393224 | tf_op jit(solution)/shard_map/ppermute | solution.py:26
  7.1 7.8 %collective-permute-start.1 = (f32[2,128,128]{2,1,0:T(8,128)S(1)}, f32[2,128,128]{2,1,0:T(8,128)S(1)}, u32[]{:S(2)}, u32[]{:S(2)}) collective-permute-start(f32[2,128,128]{2,1,0:T(8,128)S(1)} %maximum_select_fusion.pair_ref), channel_id=1, source_target_pairs={{0,16},{1,25},{2,18},{3,27},{4,20},{5,29},{6,22},{7,31},{8,24},{9,... | collective-permute-start | bytes 393224 | tf_op jit(solution)/shard_map/ppermute | solution.py:26
  14.9 9.8 %copy-start.2 = (s32[17,2]{0,1:T(2,128)S(1)}, s32[17,2]{0,1:T(2,128)}, u32[]{:S(2)}) copy-start(s32[17,2]{0,1:T(2,128)} %param.5) | copy-start | bytes 412
  14.9 2.0 %collective-permute-start.3 = (f32[2,128,128]{2,1,0:T(8,128)S(1)}, f32[2,128,128]{2,1,0:T(8,128)S(1)}, u32[]{:S(2)}, u32[]{:S(2)}) collective-permute-start(f32[2,128,128]{2,1,0:T(8,128)S(1)} %get-tuple-element.36), channel_id=1, source_target_pairs={{0,0},{1,3},{2,2},{3,1},{4,4},{5,7},{6,6},{7,5},{8,8},{9,11},{10,1... | collective-permute-start | bytes 393224 | tf_op jit(solution)/shard_map/ppermute | solution.py:26
  15.6 1.4 %collective-permute-start.5 = (f32[2,128,128]{2,1,0:T(8,128)S(1)}, f32[2,128,128]{2,1,0:T(8,128)S(1)}, u32[]{:S(2)}, u32[]{:S(2)}) collective-permute-start(f32[2,128,128]{2,1,0:T(8,128)S(1)} %get-tuple-element.34), channel_id=1, source_target_pairs={{0,0},{1,7},{2,2},{3,5},{4,4},{5,3},{6,6},{7,1},{8,8},{9,15},{10,1... | collective-permute-start | bytes 393224 | tf_op jit(solution)/shard_map/ppermute | solution.py:26
  16.3 0.7 %collective-permute-start.4 = (f32[2,128,128]{2,1,0:T(8,128)S(1)}, f32[2,128,128]{2,1,0:T(8,128)S(1)}, u32[]{:S(2)}, u32[]{:S(2)}) collective-permute-start(f32[2,128,128]{2,1,0:T(8,128)S(1)} %get-tuple-element.35), channel_id=1, source_target_pairs={{0,0},{1,5},{2,2},{3,7},{4,4},{5,1},{6,6},{7,3},{8,8},{9,13},{10,1... | collective-permute-start | bytes 393224 | tf_op jit(solution)/shard_map/ppermute | solution.py:26
  17.1 7.6 %collective-permute-start.6 = (f32[7,128,128]{2,1,0:T(8,128)S(1)}, f32[7,128,128]{2,1,0:T(8,128)S(1)}, u32[]{:S(2)}, u32[]{:S(2)}) collective-permute-start(f32[7,128,128]{2,1,0:T(8,128)S(1)} %slice_dynamic-update-slice_fusion), channel_id=1, source_target_pairs={{0,1},{1,0},{2,3},{3,2},{4,5},{5,4},{6,7},{7,6},{8,9},{9,8},{10,11... | collective-permute-start | bytes 1376264 | tf_op jit(solution)/shard_map/ppermute | solution.py:26
  26.6 2.0 %collective-permute-start.7 = (f32[1032,128]{1,0:T(8,128)S(1)}, f32[1032,128]{1,0:T(8,128)S(1)}, u32[]{:S(2)}, u32[]{:S(2)}) collective-permute-start(f32[1032,128]{1,0:T(8,128)S(1)} %get-tuple-element.22.sent_ref), channel_id=1, source_target_pairs={{0,1},{1,0},{2,3},{3,2},{4,5},{5,4},{6,7},{7,6},{8,9},{9,8},{10,11... | collective-permute-start | bytes 1585160 | tf_op jit(solution)/shard_map/ppermute | solution.py:26
  28.6 7.5 %collective-permute-start.8 = (f32[264,128]{1,0:T(8,128)S(1)}, f32[264,128]{1,0:T(8,128)S(1)}, u32[]{:S(2)}, u32[]{:S(2)}) collective-permute-start(f32[264,128]{1,0:T(8,128)S(1)} %get-tuple-element.27), channel_id=1, source_target_pairs={{0,16},{1,3},{2,18},{3,1},{4,20},{5,7},{6,22},{7,5},{8,24},{9,11},... | collective-permute-start | bytes 405512 | tf_op jit(solution)/shard_map/ppermute | solution.py:26
  28.7 7.8 %collective-permute-start.9 = (f32[264,128]{1,0:T(8,128)S(1)}, f32[264,128]{1,0:T(8,128)S(1)}, u32[]{:S(2)}, u32[]{:S(2)}) collective-permute-start(f32[264,128]{1,0:T(8,128)S(1)} %get-tuple-element.28), channel_id=1, source_target_pairs={{0,24},{1,5},{2,26},{3,7},{4,28},{5,1},{6,30},{7,3},{8,0},{9,13},{... | collective-permute-start | bytes 405512 | tf_op jit(solution)/shard_map/ppermute | solution.py:26
  32.9 3.7 %collective-permute-start.10 = (f32[264,128]{1,0:T(8,128)S(1)}, f32[264,128]{1,0:T(8,128)S(1)}, u32[]{:S(2)}, u32[]{:S(2)}) collective-permute-start(f32[264,128]{1,0:T(8,128)S(1)} %get-tuple-element.29), channel_id=1, source_target_pairs={{0,0},{1,7},{2,2},{3,5},{4,4},{5,3},{6,6},{7,1},{8,8},{9,15},{10,1... | collective-permute-start | bytes 405512 | tf_op jit(solution)/shard_map/ppermute | solution.py:26
  36.6 11.7 %collective-permute-start.11 = (f32[264,128]{1,0:T(8,128)S(1)}, f32[264,128]{1,0:T(8,128)S(1)}, u32[]{:S(2)}, u32[]{:S(2)}) collective-permute-start(f32[264,128]{1,0:T(8,128)S(1)} %get-tuple-element.31.sent_ref), channel_id=1, source_target_pairs={{0,0},{1,9},{2,2},{3,11},{4,4},{5,13},{6,6},{7,15},{8,8},{9,17},{1... | collective-permute-start | bytes 405512 | tf_op jit(solution)/shard_map/ppermute | solution.py:26
  37.3 5.5 %collective-permute-start.12 = (f32[8,128]{1,0:T(8,128)S(1)}, f32[8,128]{1,0:T(8,128)S(1)}, u32[]{:S(2)}, u32[]{:S(2)}) collective-permute-start(f32[8,128]{1,0:T(8,128)S(1)} %shard_map.55), channel_id=1, source_target_pairs={{0,2},{1,1},{2,0},{3,3},{4,6},{5,5},{6,4},{7,7},{8,10},{9,9},{10,8... | collective-permute-start | bytes 12296 | tf_op jit(solution)/shard_map/ppermute | solution.py:26
  42.8 5.5 %collective-permute-start.13 = (f32[8,128]{1,0:T(8,128)S(1)}, f32[8,128]{1,0:T(8,128)S(1)}, u32[]{:S(2)}, u32[]{:S(2)}) collective-permute-start(f32[8,128]{1,0:T(8,128)S(1)} %add.16), channel_id=1, source_target_pairs={{0,4},{1,1},{2,6},{3,3},{4,0},{5,5},{6,2},{7,7},{8,12},{9,9},{10,1... | collective-permute-start | bytes 12296 | tf_op jit(solution)/shard_map/ppermute | solution.py:26
  48.3 1.3 %collective-permute-start.14 = (f32[136,128]{1,0:T(8,128)S(1)}, f32[136,128]{1,0:T(8,128)S(1)}, u32[]{:S(2)}, u32[]{:S(2)}) collective-permute-start(f32[136,128]{1,0:T(8,128)S(1)} %get-tuple-element.33.sent_ref), channel_id=1, source_target_pairs={{0,1},{1,0},{2,3},{3,2},{4,5},{5,4},{6,7},{7,6},{8,9},{9,8},{10,11... | collective-permute-start | bytes 208904 | tf_op jit(solution)/shard_map/ppermute | solution.py:26

commit v7 on v4

--- a/solution.py
+++ b/solution.py
@@ -33,9 +33,19 @@
     return high, low
 
 
-def split_kernel(tiles_ref, own_ref, straight_ref, turned_ref, own_out):
+def place_of(place_ref, chips):
+    place = place_ref[0]
+    return (place // 2) & (chips - 1), place & 1
+
+
+def fetch_kernel(own_ref, out_ref, done):
+    copy = pltpu.make_async_copy(own_ref, out_ref, done)
+    copy.start()
+    copy.wait()
+
+
+def split_kernel(tiles_ref, straight_ref, turned_ref):
     slots = tiles_ref.shape[0]
-    own_out[...] = own_ref[...]
 
     def visit(t):
         tile = tiles_ref[t]
@@ -53,7 +63,7 @@
     return ((chip ^ mask) - chip) & (chips - 1)
 
 
-def product_kernel(planes, chips, pairs_ref, where_ref, own_ref, *refs):
+def product_kernel(planes, chips, pairs_ref, place_ref, own_ref, *refs):
     window = 2 * chips
     far = refs[: planes - 1]
     even = refs[planes - 1 : planes + chips - 2]
@@ -61,7 +71,7 @@
     far_out = refs[planes + chips + 3 : -3]
     whole, parts, total = refs[-3:]
     rows, cols = own_ref.shape
-    chip, core = where_ref[0], where_ref[1]
+    chip, core = place_of(place_ref, chips)
     spare = jnp.where(core == 0, 1, window - 1)
 
     def put(place, values):
@@ -119,11 +129,11 @@
         far_out[k - 2][...] = total[window - 1 + k]
 
 
-def pair_kernel(chips, where_ref, sent_ref, kept_ref, got_ref, *outs):
+def pair_kernel(chips, place_ref, sent_ref, kept_ref, got_ref, *outs):
     messages = outs[: chips - 1]
     near_ref, next_ref, sums_ref = outs[chips - 1 :]
     rows = kept_ref.shape[1]
-    core = where_ref[1]
+    core = place_of(place_ref, chips)[1]
     sums = sent_ref[chips * rows :, :] + got_ref[chips * rows :, :]
     for m in range(1, chips):
         messages[m - 1][:rows, :] = kept_ref[m] + got_ref[m * rows : (m + 1) * rows, :]
@@ -134,12 +144,13 @@
     sums_ref[...] = sums
 
 
-def plane_kernel(chips, where_ref, near_ref, next_ref, sums_ref, *refs):
+def plane_kernel(planes, chips, place_ref, near_ref, next_ref, sums_ref, *refs):
     got = refs[: chips - 1]
-    far = refs[chips - 1 : -3]
-    near_out, message, sums_out = refs[-3:]
+    far = refs[chips - 1 : chips + planes - 3]
+    messages = refs[chips + planes - 3 : -2]
+    near_out, sums_out = refs[-2:]
     rows = near_ref.shape[0]
-    chip = where_ref[0]
+    chip = place_of(place_ref, chips)[0]
     near, ahead, sums = near_ref[...], next_ref[...], sums_ref[...]
     for m in range(1, chips):
         block = got[m - 1][:rows, :]
@@ -147,32 +158,33 @@
         near = near + jnp.where(same, block, 0.0)
         ahead = ahead + jnp.where(same, 0.0, block)
         sums = sums + got[m - 1][rows:, :]
-    for block in far:
-        near = near + block[...]
     near_out[...] = near
     sums_out[...] = sums
-    message[:rows, :] = ahead
-    message[rows:, :] = sums
-
-
-def final_kernel(right_ref, near_ref, sums_ref, got_ref, *refs):
+    messages[0][:rows, :] = ahead
+    for k in range(2, planes):
+        messages[k - 1][:rows, :] = far[k - 2][...]
+    for message in messages:
+        message[rows:, :] = sums
+
+
+def final_kernel(right_ref, near_ref, sums_ref, *refs):
     solution_ref, residual_ref = refs[-2:]
     rows = near_ref.shape[0]
-    image = near_ref[...] + got_ref[:rows, :]
-    sums = sums_ref[...] + got_ref[rows:, :]
-    for more in refs[:-2]:
-        sums = sums + more[...]
+    image, sums = near_ref[...], sums_ref[...]
+    for got in refs[:-2]:
+        image = image + got[:rows, :]
+        sums = sums + got[rows:, :]
     step_len = sums[0:1, :] / sums[1:2, :]
     right = right_ref[...]
     solution_ref[...] = step_len * right
     residual_ref[...] = right - step_len * image
 
 
-def call(kernel, smem, operands, outs, scratch=()):
+def call(kernel, smem, operands, outs, scratch=(), space=pltpu.VMEM):
     vmem = pl.BlockSpec(memory_space=pltpu.VMEM)
     return pl.pallas_call(
         kernel,
-        in_specs=[pl.BlockSpec(memory_space=pltpu.SMEM)] * len(smem) + [vmem] * len(operands),
+        in_specs=[pl.BlockSpec(memory_space=pltpu.SMEM)] * len(smem) + [pl.BlockSpec(memory_space=space)] * len(operands),
         out_specs=[vmem] * len(outs),
         out_shape=[jax.ShapeDtypeStruct(shape, kind) for shape, kind in outs],
         scratch_shapes=list(scratch),
@@ -189,21 +201,19 @@
     cover_len = window + planes - 1
     place = lax.axis_index("blk").astype(jnp.int32)
     chip, core = place % window // 2, place % 2
-    where = jnp.stack([chip, core])
+    where = place[None]
     single, half = jnp.float32, jnp.bfloat16
 
-    straight, turned, own = call(
-        split_kernel,
-        (),
-        (kernel_tiles[0], right_side),
-        [((slots, 2, rows, cols), half), ((slots, 2, cols, rows), half), ((rows, cols), single)],
+    (own,) = call(fetch_kernel, (), (right_side,), [((rows, cols), single)], [pltpu.SemaphoreType.DMA], pl.ANY)
+    straight, turned = call(
+        split_kernel, (), (kernel_tiles[0],), [((slots, 2, rows, cols), half), ((slots, 2, cols, rows), half)]
     )
     far = [shifted(right_side, -k * window) for k in range(1, planes)]
-    even = [chip_partner(jnp.where((chip ^ m) < chip, own, far[0]), m) for m in range(1, chips)]
-    odd = jnp.stack([jnp.where(core == 0, far[0], own)] + even)
-    odd, *rest = lax.optimization_barrier((odd, *far[1:]))
+    sent = [jnp.where((chip ^ m) < chip, own, far[0]) for m in range(1, chips)]
+    sent[-1], *rest = lax.optimization_barrier((sent[-1], *far[1:]))
     far = far[:1] + rest
-    odd = core_partner(odd)
+    even = [chip_partner(value, m) for m, value in enumerate(sent, 1)]
+    odd = core_partner(jnp.stack([jnp.where(core == 0, far[0], own)] + even))
 
     block, marked, extra = ((rows, cols), single), ((rows + EXTRA, cols), single), ((EXTRA, cols), single)
     sent, kept, *far_out = call(
@@ -217,18 +227,19 @@
             pltpu.VMEM((cover_len, rows, cols), single),
         ),
     )
-    far_got = [shifted(value, k * window) for k, value in enumerate(far_out, 2)]
     got = core_partner(sent)
     *messages, near, ahead, sums = call(
         functools.partial(pair_kernel, chips), (where,), (sent, kept, got), [marked] * (chips - 1) + [block, block, extra]
     )
     got = [chip_partner(value, m) for m, value in enumerate(messages, 1)]
-    near, message, sums = call(
-        functools.partial(plane_kernel, chips), (where,), (near, ahead, sums, *got, *far_got), [block, marked, extra]
-    )
-    got = shifted(message, window)
-    more = [shifted(sums, k * window) for k in range(2, planes)]
-    return call(final_kernel, (), (own, near, sums, got, *more), [block, block])
+    *messages, near, sums = call(
+        functools.partial(plane_kernel, planes, chips),
+        (where,),
+        (near, ahead, sums, *got, *far_out),
+        [marked] * (planes - 1) + [block, extra],
+    )
+    got = [shifted(value, k * window) for k, value in enumerate(messages, 1)]
+    return call(final_kernel, (), (own, near, sums, *got), [block, block])
 
 
 def solution(mesh):

time: 44.7 us -> 41.5 us (0.928)
  starting transfers between devices: 23 us -> 17.3 us
  waiting for transfers between devices: 14.5 us -> 19.3 us
  local copies, waits for them, and re-layouts: 2.09 us -> 0.88 us
  Pallas kernels: 4.07 us -> 3.04 us
    ppermute x6, waiting for transfers between devices: 0.02 us -> 7.5 us  [chip_partner(): lax.ppermute(value, 'blk', [(source, source ^ 2 * mask) for source in ran...]
    ppermute x8 -> x6, starting transfers between devices: 15.6 us -> 9.99 us  [shifted(): return lax.ppermute(value, 'blk', pairs)]
    ppermute x8 -> x6, waiting for transfers between devices: 11.7 us -> 9.27 us  [shifted(): return lax.ppermute(value, 'blk', pairs)]
    unnamed x6, local copies, waits for them, and re-layouts: 2.09 us -> 0.88 us
    pallas_call x5 -> x6, Pallas kernels: 4.07 us -> 3.04 us  [call(): pl.pallas_call(kernel, in_specs=[pl.BlockSpec(memory_space=pltpu.SMEM)] *...]
  transfers between devices with their start and end apart: 16 -> 14, of which waited for: 8 -> 13; matrix products, arithmetic and copies ran while one was open for 0% -> 0% of each run, Pallas kernels for 1% -> 1%
where the time goes in v7:
time: 41.5 us; the launch traced here: 41.3 us
  waiting for transfers between devices  19.3 us (47%)
  starting transfers between devices  17.3 us (42%)
  Pallas kernels  3.04 us (7%)
  local copies, waits for them, and re-layouts  0.88 us (2%)
  between operations  0.72 us (2%)
    ppermute x6, starting transfers between devices, shifted(): return lax.ppermute(value, 'blk', pairs)  9.99 us
    ppermute x6, waiting for transfers between devices, shifted(): return lax.ppermute(value, 'blk', pairs)  9.27 us
    ppermute x6, waiting for transfers between devices, chip_partner(): lax.ppermute(value, 'blk', [(source, source ^ 2 * mask) for source in ran...  7.5 us
    ppermute x6, starting transfers between devices, chip_partner(): lax.ppermute(value, 'blk', [(source, source ^ 2 * mask) for source in ran...  7.04 us
    pallas_call x6, Pallas kernels, call(): pl.pallas_call(kernel, in_specs=[pl.BlockSpec(memory_space=pltpu.SMEM)] *...  3.04 us
    ppermute x2, waiting for transfers between devices, core_partner(): lax.ppermute(value, 'blk', [(source, source ^ 1) for source in range(coun...  2.54 us
    unnamed x6, local copies, waits for them, and re-layouts  0.88 us
  transfers between devices with their start and end apart: 14, of which 13 were waited for; matrix products, arithmetic and copies ran while one was open for 0% of the time, Pallas kernels for 1%

profile of v7, /device:TPU:0, one launch (start us, length us, event | category | flops | bytes accessed | tf_op | source)
XLA Modules:
  0.0 41.3 jit_solution(12798373969303864092)
XLA Ops:
  0.6 0.0 copy-start
  0.6 5.1 %collective-permute-start = (f32[128,128]{1,0:T(8,128)}, f32[128,128]{1,0:T(8,128)S(1)}, u32[]{:S(2)}, u32[]{:S(2)}) collective-permute-start(f32[128,128]{1,0:T(8,128)} %own_ref.1), channel_id=1, source_target_pairs={{0,24},{1,25},{2,26},{3,27},{4,28},{5,29},{6,30},{7,31},{8,0},{9,1... | collective-permute-start | bytes 196616 | tf_op jit(solution)/shard_map/ppermute | solution.py:17
  5.7 0.0 collective-permute-start.2
  5.7 1.0 %collective-permute-start.1 = (f32[128,128]{1,0:T(8,128)}, f32[128,128]{1,0:T(8,128)S(1)}, u32[]{:S(2)}, u32[]{:S(2)}) collective-permute-start(f32[128,128]{1,0:T(8,128)} %own_ref.1), channel_id=1, source_target_pairs={{0,16},{1,17},{2,18},{3,19},{4,20},{5,21},{6,22},{7,23},{8,24},{9,... | collective-permute-start | bytes 196616 | tf_op jit(solution)/shard_map/ppermute | solution.py:17
  6.8 0.0 copy-start.1
  6.8 0.9 %copy-done.1 = f32[128,128]{1,0:T(8,128)S(1)} copy-done((f32[128,128]{1,0:T(8,128)S(1)}, f32[128,128]{1,0:T(8,128)}, u32[]{:S(2)}) %copy-start.1) | copy-done | bytes 65560
  7.6 0.0 copy-start.2
  7.6 0.1 shard_map.50.own_ref.right_ref
  7.7 0.8 %collective-permute-done.refs_0_ = f32[128,128]{1,0:T(8,128)S(1)} collective-permute-done((f32[128,128]{1,0:T(8,128)}, f32[128,128]{1,0:T(8,128)S(1)}, u32[]{:S(2)}, u32[]{:S(2)}) %collective-permute-start) | collective-permute-done | bytes 65568 | tf_op jit(solution)/shard_map/ppermute | solution.py:17
  8.6 3.5 %collective-permute-done.2.refs_2_ = f32[128,128]{1,0:T(8,128)S(1)} collective-permute-done((f32[128,128]{1,0:T(8,128)}, f32[128,128]{1,0:T(8,128)S(1)}, u32[]{:S(2)}, u32[]{:S(2)}) %collective-permute-start.2) | collective-permute-done | bytes 65568 | tf_op jit(solution)/shard_map/ppermute | solution.py:17
  12.1 1.3 %collective-permute-done.1.refs_1_ = f32[128,128]{1,0:T(8,128)S(1)} collective-permute-done((f32[128,128]{1,0:T(8,128)}, f32[128,128]{1,0:T(8,128)S(1)}, u32[]{:S(2)}, u32[]{:S(2)}) %collective-permute-start.1) | collective-permute-done | bytes 65568 | tf_op jit(solution)/shard_map/ppermute | solution.py:17
  13.4 2.4 %collective-permute-start.5 = (f32[128,128]{1,0:T(8,128)S(1)}, f32[128,128]{1,0:T(8,128)S(1)}, u32[]{:S(2)}, u32[]{:S(2)}) collective-permute-start(f32[128,128]{1,0:T(8,128)S(1)} %get-tuple-element.24), channel_id=1, source_target_pairs={{0,6},{1,7},{2,4},{3,5},{4,2},{5,3},{6,0},{7,1},{8,14},{9,15},{10,... | collective-permute-start | bytes 196616 | tf_op jit(solution)/shard_map/ppermute | solution.py:22
  15.9 0.5 %collective-permute-start.4 = (f32[128,128]{1,0:T(8,128)S(1)}, f32[128,128]{1,0:T(8,128)S(1)}, u32[]{:S(2)}, u32[]{:S(2)}) collective-permute-start(f32[128,128]{1,0:T(8,128)S(1)} %get-tuple-element.43), channel_id=1, source_target_pairs={{0,4},{1,5},{2,6},{3,7},{4,0},{5,1},{6,2},{7,3},{8,12},{9,13},{10,... | collective-permute-start | bytes 196616 | tf_op jit(solution)/shard_map/ppermute | solution.py:22
  16.4 0.5 %collective-permute-start.3 = (f32[128,128]{1,0:T(8,128)S(1)}, f32[128,128]{1,0:T(8,128)S(1)}, u32[]{:S(2)}, u32[]{:S(2)}) collective-permute-start(f32[128,128]{1,0:T(8,128)S(1)} %get-tuple-element.44), channel_id=1, source_target_pairs={{0,2},{1,3},{2,0},{3,1},{4,6},{5,7},{6,4},{7,5},{8,10},{9,11},{10,... | collective-permute-start | bytes 196616 | tf_op jit(solution)/shard_map/ppermute | solution.py:22
  16.9 1.7 %collective-permute-done.5.refs_5_ = f32[128,128]{1,0:T(8,128)S(1)} collective-permute-done((f32[128,128]{1,0:T(8,128)S(1)}, f32[128,128]{1,0:T(8,128)S(1)}, u32[]{:S(2)}, u32[]{:S(2)}) %collective-permute-start.5) | collective-permute-done | bytes 65568 | tf_op jit(solution)/shard_map/ppermute | solution.py:22
  18.6 1.5 %collective-permute-done.4.refs_4_ = f32[128,128]{1,0:T(8,128)S(1)} collective-permute-done((f32[128,128]{1,0:T(8,128)S(1)}, f32[128,128]{1,0:T(8,128)S(1)}, u32[]{:S(2)}, u32[]{:S(2)}) %collective-permute-start.4) | collective-permute-done | bytes 65568 | tf_op jit(solution)/shard_map/ppermute | solution.py:22
  20.1 0.5 %collective-permute-done.3.refs_3_ = f32[128,128]{1,0:T(8,128)S(1)} collective-permute-done((f32[128,128]{1,0:T(8,128)S(1)}, f32[128,128]{1,0:T(8,128)S(1)}, u32[]{:S(2)}, u32[]{:S(2)}) %collective-permute-start.3) | collective-permute-done | bytes 65568 | tf_op jit(solution)/shard_map/ppermute | solution.py:22
  20.7 0.1 collective-permute-start.6
  20.7 0.0 copy-done
  20.7 0.4 shard_map.51
  21.1 1.1 %collective-permute-done.6.refs_6_ = f32[4,128,128]{2,1,0:T(8,128)S(1)} collective-permute-done((f32[4,128,128]{2,1,0:T(8,128)S(1)}, f32[4,128,128]{2,1,0:T(8,128)S(1)}, u32[]{:S(2)}, u32[]{:S(2)}) %collective-permute-start.6) | collective-permute-done | bytes 262176 | tf_op jit(solution)/shard_map/ppermute | solution.py:27
  22.3 0.0 copy-done.2
  22.3 1.8 %shard_map.52 = (f32[520,128]{1,0:T(8,128)S(1)}, f32[5,128,128]{2,1,0:T(8,128)S(1)}, f32[128,128]{1,0:T(8,128)S(1)}, f32[128,128]{1,0:T(8,128)S(1)}) custom-call(s32[2,17]{1,0:T(2,128)S(1)} %bitcast.12, s32[1]{0:T(128)} %bitcast.place_ref, f32[128,128]{1,0:T(8,128)S(1)} %shard_map.50.own_ref.right_ref, f32[128,128]{1,0:T(8,128)S(1)} %collective-permute-done.refs_0_, ...), custom_call_target="tpu_custom_call" | custom-call | tf_op jit(solution)/shard_map/pallas_call | solution.py:185
  24.1 0.2 collective-permute-start.7
  24.3 1.4 %collective-permute-done.7.got_ref = f32[520,128]{1,0:T(8,128)S(1)} collective-permute-done((f32[520,128]{1,0:T(8,128)S(1)}, f32[520,128]{1,0:T(8,128)S(1)}, u32[]{:S(2)}, u32[]{:S(2)}) %collective-permute-start.7) | collective-permute-done | bytes 266272 | tf_op jit(solution)/shard_map/ppermute | solution.py:27
  25.7 0.6 %collective-permute-start.8 = (f32[136,128]{1,0:T(8,128)S(1)}, f32[136,128]{1,0:T(8,128)S(1)}, u32[]{:S(2)}, u32[]{:S(2)}) collective-permute-start(f32[136,128]{1,0:T(8,128)S(1)} %get-tuple-element.32), channel_id=1, source_target_pairs={{0,2},{1,3},{2,0},{3,1},{4,6},{5,7},{6,4},{7,5},{8,10},{9,11},{10,... | collective-permute-start | bytes 208904 | tf_op jit(solution)/shard_map/ppermute | solution.py:22
  26.3 1.5 %collective-permute-start.9 = (f32[136,128]{1,0:T(8,128)S(1)}, f32[136,128]{1,0:T(8,128)S(1)}, u32[]{:S(2)}, u32[]{:S(2)}) collective-permute-start(f32[136,128]{1,0:T(8,128)S(1)} %get-tuple-element.33), channel_id=1, source_target_pairs={{0,4},{1,5},{2,6},{3,7},{4,0},{5,1},{6,2},{7,3},{8,12},{9,13},{10,... | collective-permute-start | bytes 208904 | tf_op jit(solution)/shard_map/ppermute | solution.py:22
  27.9 1.4 %collective-permute-start.10 = (f32[136,128]{1,0:T(8,128)S(1)}, f32[136,128]{1,0:T(8,128)S(1)}, u32[]{:S(2)}, u32[]{:S(2)}) collective-permute-start(f32[136,128]{1,0:T(8,128)S(1)} %get-tuple-element.34), channel_id=1, source_target_pairs={{0,6},{1,7},{2,4},{3,5},{4,2},{5,3},{6,0},{7,1},{8,14},{9,15},{10,... | collective-permute-start | bytes 208904 | tf_op jit(solution)/shard_map/ppermute | solution.py:22
  29.3 1.0 %collective-permute-done.8.refs_0_ = f32[136,128]{1,0:T(8,128)S(1)} collective-permute-done((f32[136,128]{1,0:T(8,128)S(1)}, f32[136,128]{1,0:T(8,128)S(1)}, u32[]{:S(2)}, u32[]{:S(2)}) %collective-permute-start.8) | collective-permute-done | bytes 69664 | tf_op jit(solution)/shard_map/ppermute | solution.py:22
  30.3 0.3 collective-permute-done.9.refs_1_
  30.6 2.4 %collective-permute-done.10.refs_2_ = f32[136,128]{1,0:T(8,128)S(1)} collective-permute-done((f32[136,128]{1,0:T(8,128)S(1)}, f32[136,128]{1,0:T(8,128)S(1)}, u32[]{:S(2)}, u32[]{:S(2)}) %collective-permute-start.10) | collective-permute-done | bytes 69664 | tf_op jit(solution)/shard_map/ppermute | solution.py:22
  33.1 0.1 shard_map.54
  33.1 0.1 collective-permute-start.11
  33.2 2.2 %collective-permute-start.12 = (f32[136,128]{1,0:T(8,128)S(1)}, f32[136,128]{1,0:T(8,128)S(1)}, u32[]{:S(2)}, u32[]{:S(2)}) collective-permute-start(f32[136,128]{1,0:T(8,128)S(1)} %get-tuple-element.40), channel_id=1, source_target_pairs={{0,16},{1,17},{2,18},{3,19},{4,20},{5,21},{6,22},{7,23},{8,24},{9,... | collective-permute-start | bytes 208904 | tf_op jit(solution)/shard_map/ppermute | solution.py:17
  35.4 1.6 %collective-permute-start.13 = (f32[136,128]{1,0:T(8,128)S(1)}, f32[136,128]{1,0:T(8,128)S(1)}, u32[]{:S(2)}, u32[]{:S(2)}) collective-permute-start(f32[136,128]{1,0:T(8,128)S(1)} %get-tuple-element.41), channel_id=1, source_target_pairs={{0,24},{1,25},{2,26},{3,27},{4,28},{5,29},{6,30},{7,31},{8,0},{9,1... | collective-permute-start | bytes 208904 | tf_op jit(solution)/shard_map/ppermute | solution.py:17
  37.0 2.4 %collective-permute-done.11.refs_0_ = f32[136,128]{1,0:T(8,128)S(1)} collective-permute-done((f32[136,128]{1,0:T(8,128)S(1)}, f32[136,128]{1,0:T(8,128)S(1)}, u32[]{:S(2)}, u32[]{:S(2)}) %collective-permute-start.11) | collective-permute-done | bytes 69664 | tf_op jit(solution)/shard_map/ppermute | solution.py:17
  39.4 1.2 %collective-permute-done.12.refs_1_ = f32[136,128]{1,0:T(8,128)S(1)} collective-permute-done((f32[136,128]{1,0:T(8,128)S(1)}, f32[136,128]{1,0:T(8,128)S(1)}, u32[]{:S(2)}, u32[]{:S(2)}) %collective-permute-start.12) | collective-permute-done | bytes 69664 | tf_op jit(solution)/shard_map/ppermute | solution.py:17
  40.6 0.0 collective-permute-done.13.refs_2_
  40.6 0.7 %shard_map.55 = (f32[128,128]{1,0:T(8,128)}, f32[128,128]{1,0:T(8,128)}) custom-call(f32[128,128]{1,0:T(8,128)S(1)} %shard_map.50.own_ref.right_ref, f32[128,128]{1,0:T(8,128)S(1)} %get-tuple-element.37.near_ref, f32[8,128]{1,0:T(8,128)S(1)} %get-tuple-element.38.sums_ref, f32[136,128]{1,0:T(8,128)S(1)} %collective-permute-done.11.refs_0_, ...), custom_call_target="tpu_custom_call" | custom-call | tf_op jit(solution)/shard_map/pallas_call | solution.py:185
  (3 shorter events, 0.1 us)
Async XLA Ops:
  0.6 20.1 %copy-start = (f32[1,17,128,128]{3,2,1,0:T(8,128)S(1)}, f32[1,17,128,128]{3,2,1,0:T(8,128)}, u32[]{:S(2)}) copy-start(f32[1,17,128,128]{3,2,1,0:T(8,128)} %param.4) | copy-start | bytes 3342340
  0.6 7.9 %collective-permute-start = (f32[128,128]{1,0:T(8,128)}, f32[128,128]{1,0:T(8,128)S(1)}, u32[]{:S(2)}, u32[]{:S(2)}) collective-permute-start(f32[128,128]{1,0:T(8,128)} %own_ref.1), channel_id=1, source_target_pairs={{0,24},{1,25},{2,26},{3,27},{4,28},{5,29},{6,30},{7,31},{8,0},{9,1... | collective-permute-start | bytes 196616 | tf_op jit(solution)/shard_map/ppermute | solution.py:17
  5.7 6.4 %collective-permute-start.2 = (f32[128,128]{1,0:T(8,128)}, f32[128,128]{1,0:T(8,128)S(1)}, u32[]{:S(2)}, u32[]{:S(2)}) collective-permute-start(f32[128,128]{1,0:T(8,128)} %own_ref.1), channel_id=1, source_target_pairs={{0,8},{1,9},{2,10},{3,11},{4,12},{5,13},{6,14},{7,15},{8,16},{9,17... | collective-permute-start | bytes 196616 | tf_op jit(solution)/shard_map/ppermute | solution.py:17
  5.7 7.7 %collective-permute-start.1 = (f32[128,128]{1,0:T(8,128)}, f32[128,128]{1,0:T(8,128)S(1)}, u32[]{:S(2)}, u32[]{:S(2)}) collective-permute-start(f32[128,128]{1,0:T(8,128)} %own_ref.1), channel_id=1, source_target_pairs={{0,16},{1,17},{2,18},{3,19},{4,20},{5,21},{6,22},{7,23},{8,24},{9,... | collective-permute-start | bytes 196616 | tf_op jit(solution)/shard_map/ppermute | solution.py:17
  6.8 0.9 %copy-start.1 = (f32[128,128]{1,0:T(8,128)S(1)}, f32[128,128]{1,0:T(8,128)}, u32[]{:S(2)}) copy-start(f32[128,128]{1,0:T(8,128)} %own_ref.1) | copy-start | bytes 196612
  7.6 14.6 %copy-start.2 = (s32[17,2]{0,1:T(2,128)S(1)}, s32[17,2]{0,1:T(2,128)}, u32[]{:S(2)}) copy-start(s32[17,2]{0,1:T(2,128)} %param.5) | copy-start | bytes 412
  13.4 5.2 %collective-permute-start.5 = (f32[128,128]{1,0:T(8,128)S(1)}, f32[128,128]{1,0:T(8,128)S(1)}, u32[]{:S(2)}, u32[]{:S(2)}) collective-permute-start(f32[128,128]{1,0:T(8,128)S(1)} %get-tuple-element.24), channel_id=1, source_target_pairs={{0,6},{1,7},{2,4},{3,5},{4,2},{5,3},{6,0},{7,1},{8,14},{9,15},{10,... | collective-permute-start | bytes 196616 | tf_op jit(solution)/shard_map/ppermute | solution.py:22
  15.9 4.3 %collective-permute-start.4 = (f32[128,128]{1,0:T(8,128)S(1)}, f32[128,128]{1,0:T(8,128)S(1)}, u32[]{:S(2)}, u32[]{:S(2)}) collective-permute-start(f32[128,128]{1,0:T(8,128)S(1)} %get-tuple-element.43), channel_id=1, source_target_pairs={{0,4},{1,5},{2,6},{3,7},{4,0},{5,1},{6,2},{7,3},{8,12},{9,13},{10,... | collective-permute-start | bytes 196616 | tf_op jit(solution)/shard_map/ppermute | solution.py:22
  16.4 4.3 %collective-permute-start.3 = (f32[128,128]{1,0:T(8,128)S(1)}, f32[128,128]{1,0:T(8,128)S(1)}, u32[]{:S(2)}, u32[]{:S(2)}) collective-permute-start(f32[128,128]{1,0:T(8,128)S(1)} %get-tuple-element.44), channel_id=1, source_target_pairs={{0,2},{1,3},{2,0},{3,1},{4,6},{5,7},{6,4},{7,5},{8,10},{9,11},{10,... | collective-permute-start | bytes 196616 | tf_op jit(solution)/shard_map/ppermute | solution.py:22
  20.7 1.6 %collective-permute-start.6 = (f32[4,128,128]{2,1,0:T(8,128)S(1)}, f32[4,128,128]{2,1,0:T(8,128)S(1)}, u32[]{:S(2)}, u32[]{:S(2)}) collective-permute-start(f32[4,128,128]{2,1,0:T(8,128)S(1)} %pad_maximum_fusion), channel_id=1, source_target_pairs={{0,1},{1,0},{2,3},{3,2},{4,5},{5,4},{6,7},{7,6},{8,9},{9,8},{10,11... | collective-permute-start | bytes 786440 | tf_op jit(solution)/shard_map/ppermute | solution.py:27
  24.1 1.6 %collective-permute-start.7 = (f32[520,128]{1,0:T(8,128)S(1)}, f32[520,128]{1,0:T(8,128)S(1)}, u32[]{:S(2)}, u32[]{:S(2)}) collective-permute-start(f32[520,128]{1,0:T(8,128)S(1)} %get-tuple-element.27.sent_ref), channel_id=1, source_target_pairs={{0,1},{1,0},{2,3},{3,2},{4,5},{5,4},{6,7},{7,6},{8,9},{9,8},{10,11... | collective-permute-start | bytes 798728 | tf_op jit(solution)/shard_map/ppermute | solution.py:27
  25.7 4.6 %collective-permute-start.8 = (f32[136,128]{1,0:T(8,128)S(1)}, f32[136,128]{1,0:T(8,128)S(1)}, u32[]{:S(2)}, u32[]{:S(2)}) collective-permute-start(f32[136,128]{1,0:T(8,128)S(1)} %get-tuple-element.32), channel_id=1, source_target_pairs={{0,2},{1,3},{2,0},{3,1},{4,6},{5,7},{6,4},{7,5},{8,10},{9,11},{10,... | collective-permute-start | bytes 208904 | tf_op jit(solution)/shard_map/ppermute | solution.py:22
  26.3 4.3 %collective-permute-start.9 = (f32[136,128]{1,0:T(8,128)S(1)}, f32[136,128]{1,0:T(8,128)S(1)}, u32[]{:S(2)}, u32[]{:S(2)}) collective-permute-start(f32[136,128]{1,0:T(8,128)S(1)} %get-tuple-element.33), channel_id=1, source_target_pairs={{0,4},{1,5},{2,6},{3,7},{4,0},{5,1},{6,2},{7,3},{8,12},{9,13},{10,... | collective-permute-start | bytes 208904 | tf_op jit(solution)/shard_map/ppermute | solution.py:22
  27.9 5.2 %collective-permute-start.10 = (f32[136,128]{1,0:T(8,128)S(1)}, f32[136,128]{1,0:T(8,128)S(1)}, u32[]{:S(2)}, u32[]{:S(2)}) collective-permute-start(f32[136,128]{1,0:T(8,128)S(1)} %get-tuple-element.34), channel_id=1, source_target_pairs={{0,6},{1,7},{2,4},{3,5},{4,2},{5,3},{6,0},{7,1},{8,14},{9,15},{10,... | collective-permute-start | bytes 208904 | tf_op jit(solution)/shard_map/ppermute | solution.py:22
  33.1 6.3 %collective-permute-start.11 = (f32[136,128]{1,0:T(8,128)S(1)}, f32[136,128]{1,0:T(8,128)S(1)}, u32[]{:S(2)}, u32[]{:S(2)}) collective-permute-start(f32[136,128]{1,0:T(8,128)S(1)} %get-tuple-element.39), channel_id=1, source_target_pairs={{0,8},{1,9},{2,10},{3,11},{4,12},{5,13},{6,14},{7,15},{8,16},{9,17... | collective-permute-start | bytes 208904 | tf_op jit(solution)/shard_map/ppermute | solution.py:17
  33.2 7.4 %collective-permute-start.12 = (f32[136,128]{1,0:T(8,128)S(1)}, f32[136,128]{1,0:T(8,128)S(1)}, u32[]{:S(2)}, u32[]{:S(2)}) collective-permute-start(f32[136,128]{1,0:T(8,128)S(1)} %get-tuple-element.40), channel_id=1, source_target_pairs={{0,16},{1,17},{2,18},{3,19},{4,20},{5,21},{6,22},{7,23},{8,24},{9,... | collective-permute-start | bytes 208904 | tf_op jit(solution)/shard_map/ppermute | solution.py:17
  35.4 5.2 %collective-permute-start.13 = (f32[136,128]{1,0:T(8,128)S(1)}, f32[136,128]{1,0:T(8,128)S(1)}, u32[]{:S(2)}, u32[]{:S(2)}) collective-permute-start(f32[136,128]{1,0:T(8,128)S(1)} %get-tuple-element.41), channel_id=1, source_target_pairs={{0,24},{1,25},{2,26},{3,27},{4,28},{5,29},{6,30},{7,31},{8,0},{9,1... | collective-permute-start | bytes 208904 | tf_op jit(solution)/shard_map/ppermute | solution.py:17

commit v8 on v7

--- a/solution.py
+++ b/solution.py
@@ -11,15 +11,28 @@
 VMEM_BYTES = 48 * 1024 * 1024
 
 
-def shifted(value, steps):
-    count = lax.axis_size("blk")
-    pairs = [(source, (source + steps) % count) for source in range(count)]
+def shifted(value, window, planes_on):
+    count = lax.axis_size("blk")
+    pairs = [(source, (source + planes_on[source % 2] * window) % count) for source in range(count)]
     return lax.ppermute(value, "blk", pairs)
 
 
-def chip_partner(value, mask):
-    count = lax.axis_size("blk")
-    return lax.ppermute(value, "blk", [(source, source ^ (2 * mask)) for source in range(count)])
+def chip_partner(value, masks):
+    count = lax.axis_size("blk")
+    return lax.ppermute(value, "blk", [(source, source ^ (2 * masks[source % 2])) for source in range(count)])
+
+
+def mask_order(chips):
+    bits = chips.bit_length() - 1
+    return [(m, sum(1 << (bits - 1 - b) for b in range(bits) if m >> b & 1)) for m in range(1, chips)]
+
+
+def plane_order(planes):
+    return [(1, 1)] + [(k, planes + 1 - k) for k in range(2, planes)]
+
+
+def of_core(core, pair):
+    return pair[0] if pair[0] == pair[1] else jnp.where(core == 0, *pair)
 
 
 def core_partner(value):
@@ -81,12 +94,11 @@
         parts[place, :, cols:] = low
 
     put(0, own_ref[...])
-    for k in range(1, planes):
-        put(window - 1 + k, far[k - 1][...])
-    for m in range(1, chips):
-        ahead = 2 * steps_ahead(chip, m, chips)
-        put(ahead, even[m - 1][...])
-        put(ahead + 1 - 2 * core, odd_ref[m])
+    for i, pair in enumerate(plane_order(planes)):
+        put(window - 1 + of_core(core, pair), far[i][...])
+    for i, pair in enumerate(mask_order(chips)):
+        put(2 * steps_ahead(chip, of_core(core, pair), chips), even[i][...])
+        put(2 * steps_ahead(chip, of_core(1 - core, pair), chips) + 1 - 2 * core, odd_ref[i + 1])
     put(spare, odd_ref[0])
 
     total[...] = jnp.zeros_like(total)
@@ -125,8 +137,8 @@
         kept_ref[m] = total[ahead]
     message_ref[chips * rows :, :] = sums
     kept_ref[chips] = total[window]
-    for k in range(2, planes):
-        far_out[k - 2][...] = total[window - 1 + k]
+    for i, pair in enumerate(plane_order(planes)[1:]):
+        far_out[i][...] = total[window - 1 + of_core(core, pair)]
 
 
 def pair_kernel(chips, place_ref, sent_ref, kept_ref, got_ref, *outs):
@@ -135,9 +147,10 @@
     rows = kept_ref.shape[1]
     core = place_of(place_ref, chips)[1]
     sums = sent_ref[chips * rows :, :] + got_ref[chips * rows :, :]
-    for m in range(1, chips):
-        messages[m - 1][:rows, :] = kept_ref[m] + got_ref[m * rows : (m + 1) * rows, :]
-        messages[m - 1][rows:, :] = sums
+    for message, pair in zip(messages, mask_order(chips)):
+        mask = of_core(core, pair)
+        message[:rows, :] = kept_ref[mask] + got_ref[pl.ds(pl.multiple_of(mask * rows, rows), rows), :]
+        message[rows:, :] = sums
     spare = got_ref[:rows, :]
     near_ref[...] = kept_ref[0] + jnp.where(core == 1, spare, 0.0)
     next_ref[...] = kept_ref[chips] + jnp.where(core == 0, spare, 0.0)
@@ -150,14 +163,14 @@
     messages = refs[chips + planes - 3 : -2]
     near_out, sums_out = refs[-2:]
     rows = near_ref.shape[0]
-    chip = place_of(place_ref, chips)[0]
+    chip, core = place_of(place_ref, chips)
     near, ahead, sums = near_ref[...], next_ref[...], sums_ref[...]
-    for m in range(1, chips):
-        block = got[m - 1][:rows, :]
-        same = (chip ^ m) < chip
+    for i, pair in enumerate(mask_order(chips)):
+        block = got[i][:rows, :]
+        same = (chip ^ of_core(core, pair)) < chip
         near = near + jnp.where(same, block, 0.0)
         ahead = ahead + jnp.where(same, 0.0, block)
-        sums = sums + got[m - 1][rows:, :]
+        sums = sums + got[i][rows:, :]
     near_out[...] = near
     sums_out[...] = sums
     messages[0][:rows, :] = ahead
@@ -208,18 +221,20 @@
     straight, turned = call(
         split_kernel, (), (kernel_tiles[0],), [((slots, 2, rows, cols), half), ((slots, 2, cols, rows), half)]
     )
-    far = [shifted(right_side, -k * window) for k in range(1, planes)]
-    sent = [jnp.where((chip ^ m) < chip, own, far[0]) for m in range(1, chips)]
-    sent[-1], *rest = lax.optimization_barrier((sent[-1], *far[1:]))
+    far = [shifted(right_side, window, (-even, -odd)) for even, odd in plane_order(planes)]
+    near = []
+    for pair in mask_order(chips):
+        near.append(chip_partner(jnp.where((chip ^ of_core(core, pair)) < chip, own, far[0]), pair))
+    sent = jnp.stack([jnp.where(core == 0, far[0], own)] + near)
+    sent, *rest = lax.optimization_barrier((sent, *far[1:]))
     far = far[:1] + rest
-    even = [chip_partner(value, m) for m, value in enumerate(sent, 1)]
-    odd = core_partner(jnp.stack([jnp.where(core == 0, far[0], own)] + even))
+    odd = core_partner(sent)
 
     block, marked, extra = ((rows, cols), single), ((rows + EXTRA, cols), single), ((EXTRA, cols), single)
     sent, kept, *far_out = call(
         functools.partial(product_kernel, planes, chips),
         (route_pairs.T, where),
-        (own, *far, *even, odd, straight, turned),
+        (own, *far, *near, odd, straight, turned),
         [((chips * rows + EXTRA, cols), single), ((chips + 1, rows, cols), single)] + [block] * (planes - 2),
         (
             pltpu.VMEM((cover_len, rows, cols), single),
@@ -231,14 +246,14 @@
     *messages, near, ahead, sums = call(
         functools.partial(pair_kernel, chips), (where,), (sent, kept, got), [marked] * (chips - 1) + [block, block, extra]
     )
-    got = [chip_partner(value, m) for m, value in enumerate(messages, 1)]
+    got = [chip_partner(value, pair) for value, pair in zip(messages, mask_order(chips))]
     *messages, near, sums = call(
         functools.partial(plane_kernel, planes, chips),
         (where,),
         (near, ahead, sums, *got, *far_out),
         [marked] * (planes - 1) + [block, extra],
     )
-    got = [shifted(value, k * window) for k, value in enumerate(messages, 1)]
+    got = [shifted(value, window, pair) for value, pair in zip(messages, plane_order(planes))]
     return call(final_kernel, (), (own, near, sums, *got), [block, block])
 
 

time: 41.5 us -> 41.6 us (level)
  starting transfers between devices: 17.3 us -> 22.1 us
  waiting for transfers between devices: 19.3 us -> 14.7 us
    ppermute x6, starting transfers between devices: 9.99 us -> 14.8 us  [shifted(): return lax.ppermute(value, 'blk', pairs)]
    ppermute x6, waiting for transfers between devices: 7.5 us -> 4.75 us  [chip_partner(): lax.ppermute(value, 'blk', [(source, source ^ 2 * masks[source % 2]) for...]
    ppermute x6, waiting for transfers between devices: 9.27 us -> 7.37 us  [shifted(): return lax.ppermute(value, 'blk', pairs)]
  transfers between devices with their start and end apart: 14 -> 14, of which waited for: 13 -> 10; matrix products, arithmetic and copies ran while one was open for 0% -> 0% of each run, Pallas kernels for 1% -> 1%
where the time goes in v8:
time: 41.6 us; the launch traced here: 41.5 us
  starting transfers between devices  22.1 us (53%)
  waiting for transfers between devices  14.7 us (35%)
  Pallas kernels  3.03 us (7%)
  local copies, waits for them, and re-layouts  0.88 us (2%)
  between operations  0.74 us (2%)
    ppermute x6, starting transfers between devices, shifted(): return lax.ppermute(value, 'blk', pairs)  14.8 us
    ppermute x6, waiting for transfers between devices, shifted(): return lax.ppermute(value, 'blk', pairs)  7.37 us
    ppermute x6, starting transfers between devices, chip_partner(): lax.ppermute(value, 'blk', [(source, source ^ 2 * masks[source % 2]) for...  7.11 us
    ppermute x6, waiting for transfers between devices, chip_partner(): lax.ppermute(value, 'blk', [(source, source ^ 2 * masks[source % 2]) for...  4.75 us
    pallas_call x6, Pallas kernels, call(): pl.pallas_call(kernel, in_specs=[pl.BlockSpec(memory_space=pltpu.SMEM)] *...  3.03 us
    ppermute x2, waiting for transfers between devices, core_partner(): lax.ppermute(value, 'blk', [(source, source ^ 1) for source in range(coun...  2.55 us
    unnamed x6, local copies, waits for them, and re-layouts  0.88 us
  transfers between devices with their start and end apart: 14, of which 10 were waited for; matrix products, arithmetic and copies ran while one was open for 0% of the time, Pallas kernels for 1%

profile of v8, /device:TPU:0, one launch (start us, length us, event | category | flops | bytes accessed | tf_op | source)
XLA Modules:
  0.0 41.5 jit_solution(14458472413273179462)
XLA Ops:
  0.6 0.0 copy-start
  0.6 5.1 %collective-permute-start = (f32[128,128]{1,0:T(8,128)}, f32[128,128]{1,0:T(8,128)S(1)}, u32[]{:S(2)}, u32[]{:S(2)}) collective-permute-start(f32[128,128]{1,0:T(8,128)} %own_ref.1), channel_id=1, source_target_pairs={{0,24},{1,25},{2,26},{3,27},{4,28},{5,29},{6,30},{7,31},{8,0},{9,1... | collective-permute-start | bytes 196616 | tf_op jit(solution)/shard_map/ppermute | solution.py:17
  5.7 0.0 copy-start.1
  5.7 0.9 %copy-done.1 = f32[128,128]{1,0:T(8,128)S(1)} copy-done((f32[128,128]{1,0:T(8,128)S(1)}, f32[128,128]{1,0:T(8,128)}, u32[]{:S(2)}) %copy-start.1) | copy-done | bytes 65560
  6.6 0.0 copy-start.2
  6.6 0.1 shard_map.50.own_ref.right_ref
  6.7 1.2 %collective-permute-done.refs_0_ = f32[128,128]{1,0:T(8,128)S(1)} collective-permute-done((f32[128,128]{1,0:T(8,128)}, f32[128,128]{1,0:T(8,128)S(1)}, u32[]{:S(2)}, u32[]{:S(2)}) %collective-permute-start) | collective-permute-done | bytes 65568 | tf_op jit(solution)/shard_map/ppermute | solution.py:17
  8.0 2.5 %collective-permute-start.3 = (f32[128,128]{1,0:T(8,128)S(1)}, f32[128,128]{1,0:T(8,128)S(1)}, u32[]{:S(2)}, u32[]{:S(2)}) collective-permute-start(f32[128,128]{1,0:T(8,128)S(1)} %get-tuple-element.43), channel_id=1, source_target_pairs={{0,6},{1,7},{2,4},{3,5},{4,2},{5,3},{6,0},{7,1},{8,14},{9,15},{10,... | collective-permute-start | bytes 196616 | tf_op jit(solution)/shard_map/ppermute | solution.py:22
  10.5 0.5 %collective-permute-start.2 = (f32[128,128]{1,0:T(8,128)S(1)}, f32[128,128]{1,0:T(8,128)S(1)}, u32[]{:S(2)}, u32[]{:S(2)}) collective-permute-start(f32[128,128]{1,0:T(8,128)S(1)} %get-tuple-element.44), channel_id=1, source_target_pairs={{0,4},{1,3},{2,6},{3,1},{4,0},{5,7},{6,2},{7,5},{8,12},{9,11},{10,... | collective-permute-start | bytes 196616 | tf_op jit(solution)/shard_map/ppermute | solution.py:22
  11.0 0.5 %collective-permute-start.1 = (f32[128,128]{1,0:T(8,128)S(1)}, f32[128,128]{1,0:T(8,128)S(1)}, u32[]{:S(2)}, u32[]{:S(2)}) collective-permute-start(f32[128,128]{1,0:T(8,128)S(1)} %get-tuple-element.45), channel_id=1, source_target_pairs={{0,2},{1,5},{2,0},{3,7},{4,6},{5,1},{6,4},{7,3},{8,10},{9,13},{10,... | collective-permute-start | bytes 196616 | tf_op jit(solution)/shard_map/ppermute | solution.py:22
  11.5 0.2 collective-permute-start.5
  11.8 4.4 %collective-permute-start.4 = (f32[128,128]{1,0:T(8,128)}, f32[128,128]{1,0:T(8,128)S(1)}, u32[]{:S(2)}, u32[]{:S(2)}) collective-permute-start(f32[128,128]{1,0:T(8,128)} %own_ref.1), channel_id=1, source_target_pairs={{0,16},{1,9},{2,18},{3,11},{4,20},{5,13},{6,22},{7,15},{8,24},{9,1... | collective-permute-start | bytes 196616 | tf_op jit(solution)/shard_map/ppermute | solution.py:17
  16.2 0.0 collective-permute-done.3.refs_5_
  16.2 0.0 collective-permute-done.2.refs_4_
  16.2 0.0 collective-permute-done.1.refs_3_
  16.2 1.9 %collective-permute-done.5.refs_2_ = f32[128,128]{1,0:T(8,128)S(1)} collective-permute-done((f32[128,128]{1,0:T(8,128)}, f32[128,128]{1,0:T(8,128)S(1)}, u32[]{:S(2)}, u32[]{:S(2)}) %collective-permute-start.5) | collective-permute-done | bytes 65568 | tf_op jit(solution)/shard_map/ppermute | solution.py:17
  18.1 1.4 %collective-permute-done.4.refs_1_ = f32[128,128]{1,0:T(8,128)S(1)} collective-permute-done((f32[128,128]{1,0:T(8,128)}, f32[128,128]{1,0:T(8,128)S(1)}, u32[]{:S(2)}, u32[]{:S(2)}) %collective-permute-start.4) | collective-permute-done | bytes 65568 | tf_op jit(solution)/shard_map/ppermute | solution.py:17
  19.5 0.0 collective-permute-start.6
  19.5 0.0 copy-done
  19.5 0.4 shard_map.51
  19.8 1.2 %collective-permute-done.6.refs_6_ = f32[4,128,128]{2,1,0:T(8,128)S(1)} collective-permute-done((f32[4,128,128]{2,1,0:T(8,128)S(1)}, f32[4,128,128]{2,1,0:T(8,128)S(1)}, u32[]{:S(2)}, u32[]{:S(2)}) %collective-permute-start.6) | collective-permute-done | bytes 262176 | tf_op jit(solution)/shard_map/ppermute | solution.py:40
  21.0 0.0 copy-done.2
  21.0 1.8 %shard_map.52 = (f32[520,128]{1,0:T(8,128)S(1)}, f32[5,128,128]{2,1,0:T(8,128)S(1)}, f32[128,128]{1,0:T(8,128)S(1)}, f32[128,128]{1,0:T(8,128)S(1)}) custom-call(s32[2,17]{1,0:T(2,128)S(1)} %bitcast.12, s32[1]{0:T(128)} %bitcast.place_ref, f32[128,128]{1,0:T(8,128)S(1)} %shard_map.50.own_ref.right_ref, f32[128,128]{1,0:T(8,128)S(1)} %collective-permute-done.refs_0_, ...), custom_call_target="tpu_custom_call" | custom-call | tf_op jit(solution)/shard_map/pallas_call | solution.py:198
  22.8 0.2 collective-permute-start.7
  23.0 1.4 %collective-permute-done.7.got_ref = f32[520,128]{1,0:T(8,128)S(1)} collective-permute-done((f32[520,128]{1,0:T(8,128)S(1)}, f32[520,128]{1,0:T(8,128)S(1)}, u32[]{:S(2)}, u32[]{:S(2)}) %collective-permute-start.7) | collective-permute-done | bytes 266272 | tf_op jit(solution)/shard_map/ppermute | solution.py:40
  24.5 1.6 %collective-permute-start.8 = (f32[136,128]{1,0:T(8,128)S(1)}, f32[136,128]{1,0:T(8,128)S(1)}, u32[]{:S(2)}, u32[]{:S(2)}) collective-permute-start(f32[136,128]{1,0:T(8,128)S(1)} %get-tuple-element.32), channel_id=1, source_target_pairs={{0,2},{1,5},{2,0},{3,7},{4,6},{5,1},{6,4},{7,3},{8,10},{9,13},{10,... | collective-permute-start | bytes 208904 | tf_op jit(solution)/shard_map/ppermute | solution.py:22
  26.0 1.5 %collective-permute-start.9 = (f32[136,128]{1,0:T(8,128)S(1)}, f32[136,128]{1,0:T(8,128)S(1)}, u32[]{:S(2)}, u32[]{:S(2)}) collective-permute-start(f32[136,128]{1,0:T(8,128)S(1)} %get-tuple-element.33), channel_id=1, source_target_pairs={{0,4},{1,3},{2,6},{3,1},{4,0},{5,7},{6,2},{7,5},{8,12},{9,11},{10,... | collective-permute-start | bytes 208904 | tf_op jit(solution)/shard_map/ppermute | solution.py:22
  27.6 0.5 %collective-permute-start.10 = (f32[136,128]{1,0:T(8,128)S(1)}, f32[136,128]{1,0:T(8,128)S(1)}, u32[]{:S(2)}, u32[]{:S(2)}) collective-permute-start(f32[136,128]{1,0:T(8,128)S(1)} %get-tuple-element.34), channel_id=1, source_target_pairs={{0,6},{1,7},{2,4},{3,5},{4,2},{5,3},{6,0},{7,1},{8,14},{9,15},{10,... | collective-permute-start | bytes 208904 | tf_op jit(solution)/shard_map/ppermute | solution.py:22
  28.0 1.2 %collective-permute-done.8.refs_0_ = f32[136,128]{1,0:T(8,128)S(1)} collective-permute-done((f32[136,128]{1,0:T(8,128)S(1)}, f32[136,128]{1,0:T(8,128)S(1)}, u32[]{:S(2)}, u32[]{:S(2)}) %collective-permute-start.8) | collective-permute-done | bytes 69664 | tf_op jit(solution)/shard_map/ppermute | solution.py:22
  29.3 1.1 %collective-permute-done.9.refs_1_ = f32[136,128]{1,0:T(8,128)S(1)} collective-permute-done((f32[136,128]{1,0:T(8,128)S(1)}, f32[136,128]{1,0:T(8,128)S(1)}, u32[]{:S(2)}, u32[]{:S(2)}) %collective-permute-start.9) | collective-permute-done | bytes 69664 | tf_op jit(solution)/shard_map/ppermute | solution.py:22
  30.3 2.4 %collective-permute-done.10.refs_2_ = f32[136,128]{1,0:T(8,128)S(1)} collective-permute-done((f32[136,128]{1,0:T(8,128)S(1)}, f32[136,128]{1,0:T(8,128)S(1)}, u32[]{:S(2)}, u32[]{:S(2)}) %collective-permute-start.10) | collective-permute-done | bytes 69664 | tf_op jit(solution)/shard_map/ppermute | solution.py:22
  32.8 0.1 shard_map.54
  32.8 0.1 collective-permute-start.11
  32.9 2.1 %collective-permute-start.12 = (f32[136,128]{1,0:T(8,128)S(1)}, f32[136,128]{1,0:T(8,128)S(1)}, u32[]{:S(2)}, u32[]{:S(2)}) collective-permute-start(f32[136,128]{1,0:T(8,128)S(1)} %get-tuple-element.40), channel_id=1, source_target_pairs={{0,16},{1,25},{2,18},{3,27},{4,20},{5,29},{6,22},{7,31},{8,24},{9,... | collective-permute-start | bytes 208904 | tf_op jit(solution)/shard_map/ppermute | solution.py:17
  35.0 2.9 %collective-permute-start.13 = (f32[136,128]{1,0:T(8,128)S(1)}, f32[136,128]{1,0:T(8,128)S(1)}, u32[]{:S(2)}, u32[]{:S(2)}) collective-permute-start(f32[136,128]{1,0:T(8,128)S(1)} %get-tuple-element.41), channel_id=1, source_target_pairs={{0,24},{1,17},{2,26},{3,19},{4,28},{5,21},{6,30},{7,23},{8,0},{9,2... | collective-permute-start | bytes 208904 | tf_op jit(solution)/shard_map/ppermute | solution.py:17
  37.9 1.1 %collective-permute-done.11.refs_0_ = f32[136,128]{1,0:T(8,128)S(1)} collective-permute-done((f32[136,128]{1,0:T(8,128)S(1)}, f32[136,128]{1,0:T(8,128)S(1)}, u32[]{:S(2)}, u32[]{:S(2)}) %collective-permute-start.11) | collective-permute-done | bytes 69664 | tf_op jit(solution)/shard_map/ppermute | solution.py:17
  39.0 1.8 %collective-permute-done.12.refs_1_ = f32[136,128]{1,0:T(8,128)S(1)} collective-permute-done((f32[136,128]{1,0:T(8,128)S(1)}, f32[136,128]{1,0:T(8,128)S(1)}, u32[]{:S(2)}, u32[]{:S(2)}) %collective-permute-start.12) | collective-permute-done | bytes 69664 | tf_op jit(solution)/shard_map/ppermute | solution.py:17
  40.8 0.0 collective-permute-done.13.refs_2_
  40.8 0.7 %shard_map.55 = (f32[128,128]{1,0:T(8,128)}, f32[128,128]{1,0:T(8,128)}) custom-call(f32[128,128]{1,0:T(8,128)S(1)} %shard_map.50.own_ref.right_ref, f32[128,128]{1,0:T(8,128)S(1)} %get-tuple-element.37.near_ref, f32[8,128]{1,0:T(8,128)S(1)} %get-tuple-element.38.sums_ref, f32[136,128]{1,0:T(8,128)S(1)} %collective-permute-done.11.refs_0_, ...), custom_call_target="tpu_custom_call" | custom-call | tf_op jit(solution)/shard_map/pallas_call | solution.py:198
  (3 shorter events, 0.1 us)
Async XLA Ops:
  0.6 18.8 %copy-start = (f32[1,17,128,128]{3,2,1,0:T(8,128)S(1)}, f32[1,17,128,128]{3,2,1,0:T(8,128)}, u32[]{:S(2)}) copy-start(f32[1,17,128,128]{3,2,1,0:T(8,128)} %param.4) | copy-start | bytes 3342340
  0.6 7.3 %collective-permute-start = (f32[128,128]{1,0:T(8,128)}, f32[128,128]{1,0:T(8,128)S(1)}, u32[]{:S(2)}, u32[]{:S(2)}) collective-permute-start(f32[128,128]{1,0:T(8,128)} %own_ref.1), channel_id=1, source_target_pairs={{0,24},{1,25},{2,26},{3,27},{4,28},{5,29},{6,30},{7,31},{8,0},{9,1... | collective-permute-start | bytes 196616 | tf_op jit(solution)/shard_map/ppermute | solution.py:17
  5.7 0.9 %copy-start.1 = (f32[128,128]{1,0:T(8,128)S(1)}, f32[128,128]{1,0:T(8,128)}, u32[]{:S(2)}) copy-start(f32[128,128]{1,0:T(8,128)} %own_ref.1) | copy-start | bytes 196612
  6.6 14.4 %copy-start.2 = (s32[17,2]{0,1:T(2,128)S(1)}, s32[17,2]{0,1:T(2,128)}, u32[]{:S(2)}) copy-start(s32[17,2]{0,1:T(2,128)} %param.5) | copy-start | bytes 412
  8.0 8.2 %collective-permute-start.3 = (f32[128,128]{1,0:T(8,128)S(1)}, f32[128,128]{1,0:T(8,128)S(1)}, u32[]{:S(2)}, u32[]{:S(2)}) collective-permute-start(f32[128,128]{1,0:T(8,128)S(1)} %get-tuple-element.43), channel_id=1, source_target_pairs={{0,6},{1,7},{2,4},{3,5},{4,2},{5,3},{6,0},{7,1},{8,14},{9,15},{10,... | collective-permute-start | bytes 196616 | tf_op jit(solution)/shard_map/ppermute | solution.py:22
  10.5 5.7 %collective-permute-start.2 = (f32[128,128]{1,0:T(8,128)S(1)}, f32[128,128]{1,0:T(8,128)S(1)}, u32[]{:S(2)}, u32[]{:S(2)}) collective-permute-start(f32[128,128]{1,0:T(8,128)S(1)} %get-tuple-element.44), channel_id=1, source_target_pairs={{0,4},{1,3},{2,6},{3,1},{4,0},{5,7},{6,2},{7,5},{8,12},{9,11},{10,... | collective-permute-start | bytes 196616 | tf_op jit(solution)/shard_map/ppermute | solution.py:22
  11.0 5.2 %collective-permute-start.1 = (f32[128,128]{1,0:T(8,128)S(1)}, f32[128,128]{1,0:T(8,128)S(1)}, u32[]{:S(2)}, u32[]{:S(2)}) collective-permute-start(f32[128,128]{1,0:T(8,128)S(1)} %get-tuple-element.45), channel_id=1, source_target_pairs={{0,2},{1,5},{2,0},{3,7},{4,6},{5,1},{6,4},{7,3},{8,10},{9,13},{10,... | collective-permute-start | bytes 196616 | tf_op jit(solution)/shard_map/ppermute | solution.py:22
  11.5 6.5 %collective-permute-start.5 = (f32[128,128]{1,0:T(8,128)}, f32[128,128]{1,0:T(8,128)S(1)}, u32[]{:S(2)}, u32[]{:S(2)}) collective-permute-start(f32[128,128]{1,0:T(8,128)} %own_ref.1), channel_id=1, source_target_pairs={{0,8},{1,17},{2,10},{3,19},{4,12},{5,21},{6,14},{7,23},{8,16},{9,2... | collective-permute-start | bytes 196616 | tf_op jit(solution)/shard_map/ppermute | solution.py:17
  11.8 7.7 %collective-permute-start.4 = (f32[128,128]{1,0:T(8,128)}, f32[128,128]{1,0:T(8,128)S(1)}, u32[]{:S(2)}, u32[]{:S(2)}) collective-permute-start(f32[128,128]{1,0:T(8,128)} %own_ref.1), channel_id=1, source_target_pairs={{0,16},{1,9},{2,18},{3,11},{4,20},{5,13},{6,22},{7,15},{8,24},{9,1... | collective-permute-start | bytes 196616 | tf_op jit(solution)/shard_map/ppermute | solution.py:17
  19.5 1.5 %collective-permute-start.6 = (f32[4,128,128]{2,1,0:T(8,128)S(1)}, f32[4,128,128]{2,1,0:T(8,128)S(1)}, u32[]{:S(2)}, u32[]{:S(2)}) collective-permute-start(f32[4,128,128]{2,1,0:T(8,128)S(1)} %pad_maximum_fusion), channel_id=1, source_target_pairs={{0,1},{1,0},{2,3},{3,2},{4,5},{5,4},{6,7},{7,6},{8,9},{9,8},{10,11... | collective-permute-start | bytes 786440 | tf_op jit(solution)/shard_map/ppermute | solution.py:40
  22.8 1.6 %collective-permute-start.7 = (f32[520,128]{1,0:T(8,128)S(1)}, f32[520,128]{1,0:T(8,128)S(1)}, u32[]{:S(2)}, u32[]{:S(2)}) collective-permute-start(f32[520,128]{1,0:T(8,128)S(1)} %get-tuple-element.27.sent_ref), channel_id=1, source_target_pairs={{0,1},{1,0},{2,3},{3,2},{4,5},{5,4},{6,7},{7,6},{8,9},{9,8},{10,11... | collective-permute-start | bytes 798728 | tf_op jit(solution)/shard_map/ppermute | solution.py:40
  24.5 4.8 %collective-permute-start.8 = (f32[136,128]{1,0:T(8,128)S(1)}, f32[136,128]{1,0:T(8,128)S(1)}, u32[]{:S(2)}, u32[]{:S(2)}) collective-permute-start(f32[136,128]{1,0:T(8,128)S(1)} %get-tuple-element.32), channel_id=1, source_target_pairs={{0,2},{1,5},{2,0},{3,7},{4,6},{5,1},{6,4},{7,3},{8,10},{9,13},{10,... | collective-permute-start | bytes 208904 | tf_op jit(solution)/shard_map/ppermute | solution.py:22
  26.0 4.3 %collective-permute-start.9 = (f32[136,128]{1,0:T(8,128)S(1)}, f32[136,128]{1,0:T(8,128)S(1)}, u32[]{:S(2)}, u32[]{:S(2)}) collective-permute-start(f32[136,128]{1,0:T(8,128)S(1)} %get-tuple-element.33), channel_id=1, source_target_pairs={{0,4},{1,3},{2,6},{3,1},{4,0},{5,7},{6,2},{7,5},{8,12},{9,11},{10,... | collective-permute-start | bytes 208904 | tf_op jit(solution)/shard_map/ppermute | solution.py:22
  27.6 5.2 %collective-permute-start.10 = (f32[136,128]{1,0:T(8,128)S(1)}, f32[136,128]{1,0:T(8,128)S(1)}, u32[]{:S(2)}, u32[]{:S(2)}) collective-permute-start(f32[136,128]{1,0:T(8,128)S(1)} %get-tuple-element.34), channel_id=1, source_target_pairs={{0,6},{1,7},{2,4},{3,5},{4,2},{5,3},{6,0},{7,1},{8,14},{9,15},{10,... | collective-permute-start | bytes 208904 | tf_op jit(solution)/shard_map/ppermute | solution.py:22
  32.8 6.2 %collective-permute-start.11 = (f32[136,128]{1,0:T(8,128)S(1)}, f32[136,128]{1,0:T(8,128)S(1)}, u32[]{:S(2)}, u32[]{:S(2)}) collective-permute-start(f32[136,128]{1,0:T(8,128)S(1)} %get-tuple-element.39), channel_id=1, source_target_pairs={{0,8},{1,9},{2,10},{3,11},{4,12},{5,13},{6,14},{7,15},{8,16},{9,17... | collective-permute-start | bytes 208904 | tf_op jit(solution)/shard_map/ppermute | solution.py:17
  32.9 7.9 %collective-permute-start.12 = (f32[136,128]{1,0:T(8,128)S(1)}, f32[136,128]{1,0:T(8,128)S(1)}, u32[]{:S(2)}, u32[]{:S(2)}) collective-permute-start(f32[136,128]{1,0:T(8,128)S(1)} %get-tuple-element.40), channel_id=1, source_target_pairs={{0,16},{1,25},{2,18},{3,27},{4,20},{5,29},{6,22},{7,31},{8,24},{9,... | collective-permute-start | bytes 208904 | tf_op jit(solution)/shard_map/ppermute | solution.py:17
  35.0 5.8 %collective-permute-start.13 = (f32[136,128]{1,0:T(8,128)S(1)}, f32[136,128]{1,0:T(8,128)S(1)}, u32[]{:S(2)}, u32[]{:S(2)}) collective-permute-start(f32[136,128]{1,0:T(8,128)S(1)} %get-tuple-element.41), channel_id=1, source_target_pairs={{0,24},{1,17},{2,26},{3,19},{4,28},{5,21},{6,30},{7,23},{8,0},{9,2... | collective-permute-start | bytes 208904 | tf_op jit(solution)/shard_map/ppermute | solution.py:17

commit v9 on v7

--- a/solution.py
+++ b/solution.py
@@ -208,11 +208,10 @@
     straight, turned = call(
         split_kernel, (), (kernel_tiles[0],), [((slots, 2, rows, cols), half), ((slots, 2, cols, rows), half)]
     )
-    far = [shifted(right_side, -k * window) for k in range(1, planes)]
-    sent = [jnp.where((chip ^ m) < chip, own, far[0]) for m in range(1, chips)]
-    sent[-1], *rest = lax.optimization_barrier((sent[-1], *far[1:]))
-    far = far[:1] + rest
-    even = [chip_partner(value, m) for m, value in enumerate(sent, 1)]
+    order = [planes - 1, *range(1, planes - 1)]
+    own, *far = lax.optimization_barrier((own, *[shifted(right_side, -k * window) for k in order]))
+    far = [value for _, value in sorted(zip(order, far), key=lambda item: item[0])]
+    even = [chip_partner(jnp.where((chip ^ m) < chip, own, far[0]), m) for m in range(1, chips)]
     odd = core_partner(jnp.stack([jnp.where(core == 0, far[0], own)] + even))
 
     block, marked, extra = ((rows, cols), single), ((rows + EXTRA, cols), single), ((EXTRA, cols), single)

time: 41.5 us -> 40.5 us (0.976)
  waiting for transfers between devices: 19.3 us -> 17.3 us
  starting transfers between devices: 17.3 us -> 18.4 us
    ppermute x6, waiting for transfers between devices: 9.27 us -> 7.18 us  [shifted(): return lax.ppermute(value, 'blk', pairs)]
    ppermute x6, starting transfers between devices: 9.99 us -> 11 us  [shifted(): return lax.ppermute(value, 'blk', pairs)]
where the time goes in v9:
time: 40.5 us; the launch traced here: 40.4 us
  starting transfers between devices  18.4 us (45%)
  waiting for transfers between devices  17.3 us (43%)
  Pallas kernels  3.04 us (8%)
  local copies, waits for them, and re-layouts  0.88 us (2%)
  between operations  0.72 us (2%)
    ppermute x6, starting transfers between devices, shifted(): return lax.ppermute(value, 'blk', pairs)  11 us
    ppermute x6, waiting for transfers between devices, chip_partner(): lax.ppermute(value, 'blk', [(source, source ^ 2 * mask) for source in ran...  7.55 us
    ppermute x6, waiting for transfers between devices, shifted(): return lax.ppermute(value, 'blk', pairs)  7.18 us
    ppermute x6, starting transfers between devices, chip_partner(): lax.ppermute(value, 'blk', [(source, source ^ 2 * mask) for source in ran...  7.11 us
    pallas_call x6, Pallas kernels, call(): pl.pallas_call(kernel, in_specs=[pl.BlockSpec(memory_space=pltpu.SMEM)] *...  3.04 us
    ppermute x2, waiting for transfers between devices, core_partner(): lax.ppermute(value, 'blk', [(source, source ^ 1) for source in range(coun...  2.54 us
    unnamed x6, local copies, waits for them, and re-layouts  0.88 us
  transfers between devices with their start and end apart: 14, of which 13 were waited for; matrix products, arithmetic and copies ran while one was open for 0% of the time, Pallas kernels for 1%

profile of v9, /device:TPU:0, one launch (start us, length us, event | category | flops | bytes accessed | tf_op | source)
XLA Modules:
  0.0 40.4 jit_solution(7633874707325945480)
XLA Ops:
  0.6 0.0 copy-start
  0.6 3.1 %collective-permute-start = (f32[128,128]{1,0:T(8,128)}, f32[128,128]{1,0:T(8,128)S(1)}, u32[]{:S(2)}, u32[]{:S(2)}) collective-permute-start(f32[128,128]{1,0:T(8,128)} %own_ref.1), channel_id=1, source_target_pairs={{0,8},{1,9},{2,10},{3,11},{4,12},{5,13},{6,14},{7,15},{8,16},{9,17... | collective-permute-start | bytes 196616 | tf_op jit(solution)/shard_map/ppermute | solution.py:17
  3.7 2.6 %collective-permute-start.2 = (f32[128,128]{1,0:T(8,128)}, f32[128,128]{1,0:T(8,128)S(1)}, u32[]{:S(2)}, u32[]{:S(2)}) collective-permute-start(f32[128,128]{1,0:T(8,128)} %own_ref.1), channel_id=1, source_target_pairs={{0,16},{1,17},{2,18},{3,19},{4,20},{5,21},{6,22},{7,23},{8,24},{9,... | collective-permute-start | bytes 196616 | tf_op jit(solution)/shard_map/ppermute | solution.py:17
  6.3 1.3 %collective-permute-start.1 = (f32[128,128]{1,0:T(8,128)}, f32[128,128]{1,0:T(8,128)S(1)}, u32[]{:S(2)}, u32[]{:S(2)}) collective-permute-start(f32[128,128]{1,0:T(8,128)} %own_ref.1), channel_id=1, source_target_pairs={{0,24},{1,25},{2,26},{3,27},{4,28},{5,29},{6,30},{7,31},{8,0},{9,1... | collective-permute-start | bytes 196616 | tf_op jit(solution)/shard_map/ppermute | solution.py:17
  7.7 0.0 copy-start.1
  7.7 0.9 %copy-done.1 = f32[128,128]{1,0:T(8,128)S(1)} copy-done((f32[128,128]{1,0:T(8,128)S(1)}, f32[128,128]{1,0:T(8,128)}, u32[]{:S(2)}) %copy-start.1) | copy-done | bytes 65560
  8.5 0.0 copy-start.2
  8.5 0.1 shard_map.50.own_ref.right_ref
  8.6 0.0 collective-permute-done.refs_2_
  8.6 2.4 %collective-permute-done.2.refs_1_ = f32[128,128]{1,0:T(8,128)S(1)} collective-permute-done((f32[128,128]{1,0:T(8,128)}, f32[128,128]{1,0:T(8,128)S(1)}, u32[]{:S(2)}, u32[]{:S(2)}) %collective-permute-start.2) | collective-permute-done | bytes 65568 | tf_op jit(solution)/shard_map/ppermute | solution.py:17
  11.0 0.2 collective-permute-done.1.refs_0_
  11.3 2.6 %collective-permute-start.5 = (f32[128,128]{1,0:T(8,128)S(1)}, f32[128,128]{1,0:T(8,128)S(1)}, u32[]{:S(2)}, u32[]{:S(2)}) collective-permute-start(f32[128,128]{1,0:T(8,128)S(1)} %get-tuple-element.45), channel_id=1, source_target_pairs={{0,6},{1,7},{2,4},{3,5},{4,2},{5,3},{6,0},{7,1},{8,14},{9,15},{10,... | collective-permute-start | bytes 196616 | tf_op jit(solution)/shard_map/ppermute | solution.py:22
  13.8 0.5 %collective-permute-start.4 = (f32[128,128]{1,0:T(8,128)S(1)}, f32[128,128]{1,0:T(8,128)S(1)}, u32[]{:S(2)}, u32[]{:S(2)}) collective-permute-start(f32[128,128]{1,0:T(8,128)S(1)} %get-tuple-element.46), channel_id=1, source_target_pairs={{0,4},{1,5},{2,6},{3,7},{4,0},{5,1},{6,2},{7,3},{8,12},{9,13},{10,... | collective-permute-start | bytes 196616 | tf_op jit(solution)/shard_map/ppermute | solution.py:22
  14.3 0.5 %collective-permute-start.3 = (f32[128,128]{1,0:T(8,128)S(1)}, f32[128,128]{1,0:T(8,128)S(1)}, u32[]{:S(2)}, u32[]{:S(2)}) collective-permute-start(f32[128,128]{1,0:T(8,128)S(1)} %get-tuple-element.47), channel_id=1, source_target_pairs={{0,2},{1,3},{2,0},{3,1},{4,6},{5,7},{6,4},{7,5},{8,10},{9,11},{10,... | collective-permute-start | bytes 196616 | tf_op jit(solution)/shard_map/ppermute | solution.py:22
  14.8 2.1 %collective-permute-done.5.refs_5_ = f32[128,128]{1,0:T(8,128)S(1)} collective-permute-done((f32[128,128]{1,0:T(8,128)S(1)}, f32[128,128]{1,0:T(8,128)S(1)}, u32[]{:S(2)}, u32[]{:S(2)}) %collective-permute-start.5) | collective-permute-done | bytes 65568 | tf_op jit(solution)/shard_map/ppermute | solution.py:22
  16.9 1.2 %collective-permute-done.4.refs_4_ = f32[128,128]{1,0:T(8,128)S(1)} collective-permute-done((f32[128,128]{1,0:T(8,128)S(1)}, f32[128,128]{1,0:T(8,128)S(1)}, u32[]{:S(2)}, u32[]{:S(2)}) %collective-permute-start.4) | collective-permute-done | bytes 65568 | tf_op jit(solution)/shard_map/ppermute | solution.py:22
  18.1 0.5 %collective-permute-done.3.refs_3_ = f32[128,128]{1,0:T(8,128)S(1)} collective-permute-done((f32[128,128]{1,0:T(8,128)S(1)}, f32[128,128]{1,0:T(8,128)S(1)}, u32[]{:S(2)}, u32[]{:S(2)}) %collective-permute-start.3) | collective-permute-done | bytes 65568 | tf_op jit(solution)/shard_map/ppermute | solution.py:22
  18.6 0.1 collective-permute-start.6
  18.7 0.0 copy-done
  18.7 0.4 shard_map.51
  19.1 1.1 %collective-permute-done.6.refs_6_ = f32[4,128,128]{2,1,0:T(8,128)S(1)} collective-permute-done((f32[4,128,128]{2,1,0:T(8,128)S(1)}, f32[4,128,128]{2,1,0:T(8,128)S(1)}, u32[]{:S(2)}, u32[]{:S(2)}) %collective-permute-start.6) | collective-permute-done | bytes 262176 | tf_op jit(solution)/shard_map/ppermute | solution.py:27
  20.2 0.0 copy-done.2
  20.2 1.8 %shard_map.52 = (f32[520,128]{1,0:T(8,128)S(1)}, f32[5,128,128]{2,1,0:T(8,128)S(1)}, f32[128,128]{1,0:T(8,128)S(1)}, f32[128,128]{1,0:T(8,128)S(1)}) custom-call(s32[2,17]{1,0:T(2,128)S(1)} %bitcast.12, s32[1]{0:T(128)} %bitcast.place_ref, f32[128,128]{1,0:T(8,128)S(1)} %shard_map.50.own_ref.right_ref, f32[128,128]{1,0:T(8,128)S(1)} %collective-permute-done.1.refs_0_, ...), custom_call_target="tpu_custom_call" | custom-call | tf_op jit(solution)/shard_map/pallas_call | solution.py:185
  22.0 0.2 collective-permute-start.7
  22.3 1.4 %collective-permute-done.7.got_ref = f32[520,128]{1,0:T(8,128)S(1)} collective-permute-done((f32[520,128]{1,0:T(8,128)S(1)}, f32[520,128]{1,0:T(8,128)S(1)}, u32[]{:S(2)}, u32[]{:S(2)}) %collective-permute-start.7) | collective-permute-done | bytes 266272 | tf_op jit(solution)/shard_map/ppermute | solution.py:27
  23.7 0.6 %collective-permute-start.8 = (f32[136,128]{1,0:T(8,128)S(1)}, f32[136,128]{1,0:T(8,128)S(1)}, u32[]{:S(2)}, u32[]{:S(2)}) collective-permute-start(f32[136,128]{1,0:T(8,128)S(1)} %get-tuple-element.34), channel_id=1, source_target_pairs={{0,2},{1,3},{2,0},{3,1},{4,6},{5,7},{6,4},{7,5},{8,10},{9,11},{10,... | collective-permute-start | bytes 208904 | tf_op jit(solution)/shard_map/ppermute | solution.py:22
  24.3 1.6 %collective-permute-start.9 = (f32[136,128]{1,0:T(8,128)S(1)}, f32[136,128]{1,0:T(8,128)S(1)}, u32[]{:S(2)}, u32[]{:S(2)}) collective-permute-start(f32[136,128]{1,0:T(8,128)S(1)} %get-tuple-element.35), channel_id=1, source_target_pairs={{0,4},{1,5},{2,6},{3,7},{4,0},{5,1},{6,2},{7,3},{8,12},{9,13},{10,... | collective-permute-start | bytes 208904 | tf_op jit(solution)/shard_map/ppermute | solution.py:22
  25.8 1.4 %collective-permute-start.10 = (f32[136,128]{1,0:T(8,128)S(1)}, f32[136,128]{1,0:T(8,128)S(1)}, u32[]{:S(2)}, u32[]{:S(2)}) collective-permute-start(f32[136,128]{1,0:T(8,128)S(1)} %get-tuple-element.36), channel_id=1, source_target_pairs={{0,6},{1,7},{2,4},{3,5},{4,2},{5,3},{6,0},{7,1},{8,14},{9,15},{10,... | collective-permute-start | bytes 208904 | tf_op jit(solution)/shard_map/ppermute | solution.py:22
  27.3 1.1 %collective-permute-done.8.refs_0_ = f32[136,128]{1,0:T(8,128)S(1)} collective-permute-done((f32[136,128]{1,0:T(8,128)S(1)}, f32[136,128]{1,0:T(8,128)S(1)}, u32[]{:S(2)}, u32[]{:S(2)}) %collective-permute-start.8) | collective-permute-done | bytes 69664 | tf_op jit(solution)/shard_map/ppermute | solution.py:22
  28.3 0.2 collective-permute-done.9.refs_1_
  28.6 2.5 %collective-permute-done.10.refs_2_ = f32[136,128]{1,0:T(8,128)S(1)} collective-permute-done((f32[136,128]{1,0:T(8,128)S(1)}, f32[136,128]{1,0:T(8,128)S(1)}, u32[]{:S(2)}, u32[]{:S(2)}) %collective-permute-start.10) | collective-permute-done | bytes 69664 | tf_op jit(solution)/shard_map/ppermute | solution.py:22
  31.0 0.1 shard_map.54
  31.1 1.6 %collective-permute-start.11 = (f32[136,128]{1,0:T(8,128)S(1)}, f32[136,128]{1,0:T(8,128)S(1)}, u32[]{:S(2)}, u32[]{:S(2)}) collective-permute-start(f32[136,128]{1,0:T(8,128)S(1)} %get-tuple-element.41), channel_id=1, source_target_pairs={{0,8},{1,9},{2,10},{3,11},{4,12},{5,13},{6,14},{7,15},{8,16},{9,17... | collective-permute-start | bytes 208904 | tf_op jit(solution)/shard_map/ppermute | solution.py:17
  32.7 2.0 %collective-permute-start.12 = (f32[136,128]{1,0:T(8,128)S(1)}, f32[136,128]{1,0:T(8,128)S(1)}, u32[]{:S(2)}, u32[]{:S(2)}) collective-permute-start(f32[136,128]{1,0:T(8,128)S(1)} %get-tuple-element.42), channel_id=1, source_target_pairs={{0,16},{1,17},{2,18},{3,19},{4,20},{5,21},{6,22},{7,23},{8,24},{9,... | collective-permute-start | bytes 208904 | tf_op jit(solution)/shard_map/ppermute | solution.py:17
  34.7 0.4 %collective-permute-start.13 = (f32[136,128]{1,0:T(8,128)S(1)}, f32[136,128]{1,0:T(8,128)S(1)}, u32[]{:S(2)}, u32[]{:S(2)}) collective-permute-start(f32[136,128]{1,0:T(8,128)S(1)} %get-tuple-element.43), channel_id=1, source_target_pairs={{0,24},{1,25},{2,26},{3,27},{4,28},{5,29},{6,30},{7,31},{8,0},{9,1... | collective-permute-start | bytes 208904 | tf_op jit(solution)/shard_map/ppermute | solution.py:17
  35.1 2.3 %collective-permute-done.11.refs_0_ = f32[136,128]{1,0:T(8,128)S(1)} collective-permute-done((f32[136,128]{1,0:T(8,128)S(1)}, f32[136,128]{1,0:T(8,128)S(1)}, u32[]{:S(2)}, u32[]{:S(2)}) %collective-permute-start.11) | collective-permute-done | bytes 69664 | tf_op jit(solution)/shard_map/ppermute | solution.py:17
  37.4 2.0 %collective-permute-done.12.refs_1_ = f32[136,128]{1,0:T(8,128)S(1)} collective-permute-done((f32[136,128]{1,0:T(8,128)S(1)}, f32[136,128]{1,0:T(8,128)S(1)}, u32[]{:S(2)}, u32[]{:S(2)}) %collective-permute-start.12) | collective-permute-done | bytes 69664 | tf_op jit(solution)/shard_map/ppermute | solution.py:17
  39.4 0.3 collective-permute-done.13.refs_2_
  39.7 0.7 %shard_map.55 = (f32[128,128]{1,0:T(8,128)}, f32[128,128]{1,0:T(8,128)}) custom-call(f32[128,128]{1,0:T(8,128)S(1)} %shard_map.50.own_ref.right_ref, f32[128,128]{1,0:T(8,128)S(1)} %get-tuple-element.39.near_ref, f32[8,128]{1,0:T(8,128)S(1)} %get-tuple-element.40.sums_ref, f32[136,128]{1,0:T(8,128)S(1)} %collective-permute-done.11.refs_0_, ...), custom_call_target="tpu_custom_call" | custom-call | tf_op jit(solution)/shard_map/pallas_call | solution.py:185
  (3 shorter events, 0.1 us)
Async XLA Ops:
  0.6 18.1 %copy-start = (f32[1,17,128,128]{3,2,1,0:T(8,128)S(1)}, f32[1,17,128,128]{3,2,1,0:T(8,128)}, u32[]{:S(2)}) copy-start(f32[1,17,128,128]{3,2,1,0:T(8,128)} %param.4) | copy-start | bytes 3342340
  0.6 8.0 %collective-permute-start = (f32[128,128]{1,0:T(8,128)}, f32[128,128]{1,0:T(8,128)S(1)}, u32[]{:S(2)}, u32[]{:S(2)}) collective-permute-start(f32[128,128]{1,0:T(8,128)} %own_ref.1), channel_id=1, source_target_pairs={{0,8},{1,9},{2,10},{3,11},{4,12},{5,13},{6,14},{7,15},{8,16},{9,17... | collective-permute-start | bytes 196616 | tf_op jit(solution)/shard_map/ppermute | solution.py:17
  3.7 7.3 %collective-permute-start.2 = (f32[128,128]{1,0:T(8,128)}, f32[128,128]{1,0:T(8,128)S(1)}, u32[]{:S(2)}, u32[]{:S(2)}) collective-permute-start(f32[128,128]{1,0:T(8,128)} %own_ref.1), channel_id=1, source_target_pairs={{0,16},{1,17},{2,18},{3,19},{4,20},{5,21},{6,22},{7,23},{8,24},{9,... | collective-permute-start | bytes 196616 | tf_op jit(solution)/shard_map/ppermute | solution.py:17
  6.3 4.9 %collective-permute-start.1 = (f32[128,128]{1,0:T(8,128)}, f32[128,128]{1,0:T(8,128)S(1)}, u32[]{:S(2)}, u32[]{:S(2)}) collective-permute-start(f32[128,128]{1,0:T(8,128)} %own_ref.1), channel_id=1, source_target_pairs={{0,24},{1,25},{2,26},{3,27},{4,28},{5,29},{6,30},{7,31},{8,0},{9,1... | collective-permute-start | bytes 196616 | tf_op jit(solution)/shard_map/ppermute | solution.py:17
  7.7 0.9 %copy-start.1 = (f32[128,128]{1,0:T(8,128)S(1)}, f32[128,128]{1,0:T(8,128)}, u32[]{:S(2)}) copy-start(f32[128,128]{1,0:T(8,128)} %own_ref.1) | copy-start | bytes 196612
  8.5 11.7 %copy-start.2 = (s32[17,2]{0,1:T(2,128)S(1)}, s32[17,2]{0,1:T(2,128)}, u32[]{:S(2)}) copy-start(s32[17,2]{0,1:T(2,128)} %param.5) | copy-start | bytes 412
  11.3 5.7 %collective-permute-start.5 = (f32[128,128]{1,0:T(8,128)S(1)}, f32[128,128]{1,0:T(8,128)S(1)}, u32[]{:S(2)}, u32[]{:S(2)}) collective-permute-start(f32[128,128]{1,0:T(8,128)S(1)} %get-tuple-element.45), channel_id=1, source_target_pairs={{0,6},{1,7},{2,4},{3,5},{4,2},{5,3},{6,0},{7,1},{8,14},{9,15},{10,... | collective-permute-start | bytes 196616 | tf_op jit(solution)/shard_map/ppermute | solution.py:22
  13.8 4.3 %collective-permute-start.4 = (f32[128,128]{1,0:T(8,128)S(1)}, f32[128,128]{1,0:T(8,128)S(1)}, u32[]{:S(2)}, u32[]{:S(2)}) collective-permute-start(f32[128,128]{1,0:T(8,128)S(1)} %get-tuple-element.46), channel_id=1, source_target_pairs={{0,4},{1,5},{2,6},{3,7},{4,0},{5,1},{6,2},{7,3},{8,12},{9,13},{10,... | collective-permute-start | bytes 196616 | tf_op jit(solution)/shard_map/ppermute | solution.py:22
  14.3 4.3 %collective-permute-start.3 = (f32[128,128]{1,0:T(8,128)S(1)}, f32[128,128]{1,0:T(8,128)S(1)}, u32[]{:S(2)}, u32[]{:S(2)}) collective-permute-start(f32[128,128]{1,0:T(8,128)S(1)} %get-tuple-element.47), channel_id=1, source_target_pairs={{0,2},{1,3},{2,0},{3,1},{4,6},{5,7},{6,4},{7,5},{8,10},{9,11},{10,... | collective-permute-start | bytes 196616 | tf_op jit(solution)/shard_map/ppermute | solution.py:22
  18.6 1.6 %collective-permute-start.6 = (f32[4,128,128]{2,1,0:T(8,128)S(1)}, f32[4,128,128]{2,1,0:T(8,128)S(1)}, u32[]{:S(2)}, u32[]{:S(2)}) collective-permute-start(f32[4,128,128]{2,1,0:T(8,128)S(1)} %pad_maximum_fusion), channel_id=1, source_target_pairs={{0,1},{1,0},{2,3},{3,2},{4,5},{5,4},{6,7},{7,6},{8,9},{9,8},{10,11... | collective-permute-start | bytes 786440 | tf_op jit(solution)/shard_map/ppermute | solution.py:27
  22.0 1.6 %collective-permute-start.7 = (f32[520,128]{1,0:T(8,128)S(1)}, f32[520,128]{1,0:T(8,128)S(1)}, u32[]{:S(2)}, u32[]{:S(2)}) collective-permute-start(f32[520,128]{1,0:T(8,128)S(1)} %get-tuple-element.29.sent_ref), channel_id=1, source_target_pairs={{0,1},{1,0},{2,3},{3,2},{4,5},{5,4},{6,7},{7,6},{8,9},{9,8},{10,11... | collective-permute-start | bytes 798728 | tf_op jit(solution)/shard_map/ppermute | solution.py:27
  23.7 4.6 %collective-permute-start.8 = (f32[136,128]{1,0:T(8,128)S(1)}, f32[136,128]{1,0:T(8,128)S(1)}, u32[]{:S(2)}, u32[]{:S(2)}) collective-permute-start(f32[136,128]{1,0:T(8,128)S(1)} %get-tuple-element.34), channel_id=1, source_target_pairs={{0,2},{1,3},{2,0},{3,1},{4,6},{5,7},{6,4},{7,5},{8,10},{9,11},{10,... | collective-permute-start | bytes 208904 | tf_op jit(solution)/shard_map/ppermute | solution.py:22
  24.3 4.3 %collective-permute-start.9 = (f32[136,128]{1,0:T(8,128)S(1)}, f32[136,128]{1,0:T(8,128)S(1)}, u32[]{:S(2)}, u32[]{:S(2)}) collective-permute-start(f32[136,128]{1,0:T(8,128)S(1)} %get-tuple-element.35), channel_id=1, source_target_pairs={{0,4},{1,5},{2,6},{3,7},{4,0},{5,1},{6,2},{7,3},{8,12},{9,13},{10,... | collective-permute-start | bytes 208904 | tf_op jit(solution)/shard_map/ppermute | solution.py:22
  25.8 5.2 %collective-permute-start.10 = (f32[136,128]{1,0:T(8,128)S(1)}, f32[136,128]{1,0:T(8,128)S(1)}, u32[]{:S(2)}, u32[]{:S(2)}) collective-permute-start(f32[136,128]{1,0:T(8,128)S(1)} %get-tuple-element.36), channel_id=1, source_target_pairs={{0,6},{1,7},{2,4},{3,5},{4,2},{5,3},{6,0},{7,1},{8,14},{9,15},{10,... | collective-permute-start | bytes 208904 | tf_op jit(solution)/shard_map/ppermute | solution.py:22
  31.1 6.3 %collective-permute-start.11 = (f32[136,128]{1,0:T(8,128)S(1)}, f32[136,128]{1,0:T(8,128)S(1)}, u32[]{:S(2)}, u32[]{:S(2)}) collective-permute-start(f32[136,128]{1,0:T(8,128)S(1)} %get-tuple-element.41), channel_id=1, source_target_pairs={{0,8},{1,9},{2,10},{3,11},{4,12},{5,13},{6,14},{7,15},{8,16},{9,17... | collective-permute-start | bytes 208904 | tf_op jit(solution)/shard_map/ppermute | solution.py:17
  32.7 6.8 %collective-permute-start.12 = (f32[136,128]{1,0:T(8,128)S(1)}, f32[136,128]{1,0:T(8,128)S(1)}, u32[]{:S(2)}, u32[]{:S(2)}) collective-permute-start(f32[136,128]{1,0:T(8,128)S(1)} %get-tuple-element.42), channel_id=1, source_target_pairs={{0,16},{1,17},{2,18},{3,19},{4,20},{5,21},{6,22},{7,23},{8,24},{9,... | collective-permute-start | bytes 208904 | tf_op jit(solution)/shard_map/ppermute | solution.py:17
  34.7 5.0 %collective-permute-start.13 = (f32[136,128]{1,0:T(8,128)S(1)}, f32[136,128]{1,0:T(8,128)S(1)}, u32[]{:S(2)}, u32[]{:S(2)}) collective-permute-start(f32[136,128]{1,0:T(8,128)S(1)} %get-tuple-element.43), channel_id=1, source_target_pairs={{0,24},{1,25},{2,26},{3,27},{4,28},{5,29},{6,30},{7,31},{8,0},{9,1... | collective-permute-start | bytes 208904 | tf_op jit(solution)/shard_map/ppermute | solution.py:17

commit v10 on v9

--- a/solution.py
+++ b/solution.py
@@ -9,6 +9,7 @@
 
 EXTRA = 8
 VMEM_BYTES = 48 * 1024 * 1024
+BESIDE = pl.CostEstimate(flops=10**10, bytes_accessed=0, transcendentals=0)
 
 
 def shifted(value, steps):
@@ -59,6 +60,20 @@
         lax.fori_loop(0, slots, lambda t, c: (visit(t), c)[1], 0)
 
 
+def split_blocks_kernel(*refs):
+    out_ref = refs[-1]
+    cols = out_ref.shape[2] // 2
+    for i, block in enumerate(refs[:-1]):
+        out_ref[i, :, :cols], out_ref[i, :, cols:] = split_two(block[...])
+
+
+def add_kernel(*refs):
+    total = refs[0][...]
+    for block in refs[1:-1]:
+        total = total + block[...]
+    refs[-1][...] = total
+
+
 def steps_ahead(chip, mask, chips):
     return ((chip ^ mask) - chip) & (chips - 1)
 
@@ -67,8 +82,8 @@
     window = 2 * chips
     far = refs[: planes - 1]
     even = refs[planes - 1 : planes + chips - 2]
-    odd_ref, straight_ref, turned_ref, message_ref, kept_ref = refs[planes + chips - 2 : planes + chips + 3]
-    far_out = refs[planes + chips + 3 : -3]
+    odd_ref, middle_ref, straight_ref, turned_ref, message_ref, kept_ref = refs[planes + chips - 2 : planes + chips + 4]
+    far_out = refs[planes + chips + 4 : -3]
     whole, parts, total = refs[-3:]
     rows, cols = own_ref.shape
     chip, core = place_of(place_ref, chips)
@@ -81,8 +96,11 @@
         parts[place, :, cols:] = low
 
     put(0, own_ref[...])
-    for k in range(1, planes):
+    for k in (1, planes - 1):
         put(window - 1 + k, far[k - 1][...])
+    for k in range(2, planes - 1):
+        whole[window - 1 + k] = far[k - 1][...]
+        parts[window - 1 + k] = middle_ref[k - 2]
     for m in range(1, chips):
         ahead = 2 * steps_ahead(chip, m, chips)
         put(ahead, even[m - 1][...])
@@ -144,11 +162,9 @@
     sums_ref[...] = sums
 
 
-def plane_kernel(planes, chips, place_ref, near_ref, next_ref, sums_ref, *refs):
+def plane_kernel(chips, place_ref, near_ref, next_ref, sums_ref, last_ref, *refs):
     got = refs[: chips - 1]
-    far = refs[chips - 1 : chips + planes - 3]
-    messages = refs[chips + planes - 3 : -2]
-    near_out, sums_out = refs[-2:]
+    next_out, last_out, near_out, sums_out = refs[chips - 1 :]
     rows = near_ref.shape[0]
     chip = place_of(place_ref, chips)[0]
     near, ahead, sums = near_ref[...], next_ref[...], sums_ref[...]
@@ -160,27 +176,28 @@
         sums = sums + got[m - 1][rows:, :]
     near_out[...] = near
     sums_out[...] = sums
-    messages[0][:rows, :] = ahead
-    for k in range(2, planes):
-        messages[k - 1][:rows, :] = far[k - 2][...]
-    for message in messages:
+    next_out[:rows, :] = ahead
+    last_out[:rows, :] = last_ref[...]
+    for message in (next_out, last_out):
         message[rows:, :] = sums
 
 
-def final_kernel(right_ref, near_ref, sums_ref, *refs):
+def final_kernel(right_ref, near_ref, middle_ref, sums_ref, *refs):
     solution_ref, residual_ref = refs[-2:]
     rows = near_ref.shape[0]
-    image, sums = near_ref[...], sums_ref[...]
-    for got in refs[:-2]:
+    image, sums = near_ref[...] + middle_ref[...], sums_ref[...]
+    for got in refs[:2]:
         image = image + got[:rows, :]
         sums = sums + got[rows:, :]
+    for got in refs[2:-2]:
+        sums = sums + got[...]
     step_len = sums[0:1, :] / sums[1:2, :]
     right = right_ref[...]
     solution_ref[...] = step_len * right
     residual_ref[...] = right - step_len * image
 
 
-def call(kernel, smem, operands, outs, scratch=(), space=pltpu.VMEM):
+def call(kernel, smem, operands, outs, scratch=(), space=pltpu.VMEM, cost=None):
     vmem = pl.BlockSpec(memory_space=pltpu.VMEM)
     return pl.pallas_call(
         kernel,
@@ -188,6 +205,7 @@
         out_specs=[vmem] * len(outs),
         out_shape=[jax.ShapeDtypeStruct(shape, kind) for shape, kind in outs],
         scratch_shapes=list(scratch),
+        cost_estimate=cost,
         compiler_params=pltpu.CompilerParams(vmem_limit_bytes=VMEM_BYTES),
     )(*smem, *operands)
 
@@ -208,17 +226,20 @@
     straight, turned = call(
         split_kernel, (), (kernel_tiles[0],), [((slots, 2, rows, cols), half), ((slots, 2, cols, rows), half)]
     )
-    order = [planes - 1, *range(1, planes - 1)]
-    own, *far = lax.optimization_barrier((own, *[shifted(right_side, -k * window) for k in order]))
-    far = [value for _, value in sorted(zip(order, far), key=lambda item: item[0])]
-    even = [chip_partner(jnp.where((chip ^ m) < chip, own, far[0]), m) for m in range(1, chips)]
-    odd = core_partner(jnp.stack([jnp.where(core == 0, far[0], own)] + even))
+    far = {k: shifted(right_side, -k * window) for k in (planes - 1, *range(1, planes - 1))}
+    own, far[planes - 1], far[1] = lax.optimization_barrier((own, far[planes - 1], far[1]))
+    middle = range(2, planes - 1)
+    (middle_parts,) = call(
+        split_blocks_kernel, (), [far[k] for k in middle], [((len(middle), rows, 2 * cols), half)], cost=BESIDE
+    )
+    even = [chip_partner(jnp.where((chip ^ m) < chip, own, far[1]), m) for m in range(1, chips)]
+    odd = core_partner(jnp.stack([jnp.where(core == 0, far[1], own)] + even))
 
     block, marked, extra = ((rows, cols), single), ((rows + EXTRA, cols), single), ((EXTRA, cols), single)
     sent, kept, *far_out = call(
         functools.partial(product_kernel, planes, chips),
         (route_pairs.T, where),
-        (own, *far, *even, odd, straight, turned),
+        (own, *[far[k] for k in range(1, planes)], *even, odd, middle_parts, straight, turned),
         [((chips * rows + EXTRA, cols), single), ((chips + 1, rows, cols), single)] + [block] * (planes - 2),
         (
             pltpu.VMEM((cover_len, rows, cols), single),
@@ -230,15 +251,16 @@
     *messages, near, ahead, sums = call(
         functools.partial(pair_kernel, chips), (where,), (sent, kept, got), [marked] * (chips - 1) + [block, block, extra]
     )
+    middle_got = [shifted(far_out[k - 2], k * window) for k in middle]
+    (middle_sum,) = call(add_kernel, (), middle_got, [block], cost=BESIDE)
     got = [chip_partner(value, m) for m, value in enumerate(messages, 1)]
-    *messages, near, sums = call(
-        functools.partial(plane_kernel, planes, chips),
-        (where,),
-        (near, ahead, sums, *got, *far_out),
-        [marked] * (planes - 1) + [block, extra],
-    )
-    got = [shifted(value, k * window) for k, value in enumerate(messages, 1)]
-    return call(final_kernel, (), (own, near, sums, *got), [block, block])
+    ahead, last, near, sums = call(
+        functools.partial(plane_kernel, chips), (where,), (near, ahead, sums, far_out[-1], *got), [marked, marked, block, extra]
+    )
+    got = [shifted(ahead, window), *[shifted(sums, k * window) for k in middle], shifted(last, (planes - 1) * window)]
+    return call(
+        final_kernel, (), (own, near, middle_sum, sums, got[0], got[-1], *got[1:-1]), [block, block]
+    )
 
 
 def solution(mesh):

time: 40.5 us -> 39.5 us (0.975)
  waiting for transfers between devices: 17.3 us -> 12.7 us
  starting transfers between devices: 18.4 us -> 20.6 us
  local copies, waits for them, and re-layouts: 0.88 us -> 2.13 us
    ppermute x6, waiting for transfers between devices: 7.55 us -> 3.72 us  [chip_partner(): lax.ppermute(value, 'blk', [(source, source ^ 2 * mask) for source in ran...]
    ppermute x6 -> x7, starting transfers between devices: 11 us -> 13.4 us  [shifted(): return lax.ppermute(value, 'blk', pairs)]
    unnamed x6, local copies, waits for them, and re-layouts: 0.88 us -> 2.13 us
    ppermute x2, waiting for transfers between devices: 2.54 us -> 1.53 us  [core_partner(): lax.ppermute(value, 'blk', [(source, source ^ 1) for source in range(coun...]
    ppermute x6 -> x7, waiting for transfers between devices: 7.18 us -> 7.47 us  [shifted(): return lax.ppermute(value, 'blk', pairs)]
    pallas_call x6 -> x8, Pallas kernels: 3.04 us -> 3.02 us  [call(): pl.pallas_call(kernel, in_specs=[pl.BlockSpec(memory_space=pltpu.SMEM)] *...]
  transfers between devices with their start and end apart: 14 -> 15, of which waited for: 13 -> 9; matrix products, arithmetic and copies ran while one was open for 0% -> 0% of each run, Pallas kernels for 1% -> 1%
where the time goes in v10:
time: 39.5 us; the launch traced here: 39.3 us
  starting transfers between devices  20.6 us (52%)
  waiting for transfers between devices  12.7 us (32%)
  Pallas kernels  3.02 us (8%)
  local copies, waits for them, and re-layouts  2.13 us (5%)
  between operations  0.76 us (2%)
    ppermute x7, starting transfers between devices, shifted(): return lax.ppermute(value, 'blk', pairs)  13.4 us
    ppermute x7, waiting for transfers between devices, shifted(): return lax.ppermute(value, 'blk', pairs)  7.47 us
    ppermute x6, starting transfers between devices, chip_partner(): lax.ppermute(value, 'blk', [(source, source ^ 2 * mask) for source in ran...  7.11 us
    ppermute x6, waiting for transfers between devices, chip_partner(): lax.ppermute(value, 'blk', [(source, source ^ 2 * mask) for source in ran...  3.72 us
    pallas_call x8, Pallas kernels, call(): pl.pallas_call(kernel, in_specs=[pl.BlockSpec(memory_space=pltpu.SMEM)] *...  3.02 us
    unnamed x6, local copies, waits for them, and re-layouts  2.13 us
    ppermute x2, waiting for transfers between devices, core_partner(): lax.ppermute(value, 'blk', [(source, source ^ 1) for source in range(coun...  1.53 us
  transfers between devices with their start and end apart: 15, of which 9 were waited for; matrix products, arithmetic and copies ran while one was open for 0% of the time, Pallas kernels for 1%

profile of v10, /device:TPU:0, one launch (start us, length us, event | category | flops | bytes accessed | tf_op | source)
XLA Modules:
  0.0 39.3 jit_solution(7231956301619737104)
XLA Ops:
  0.6 3.1 %collective-permute-start = (f32[128,128]{1,0:T(8,128)}, f32[128,128]{1,0:T(8,128)S(1)}, u32[]{:S(2)}, u32[]{:S(2)}) collective-permute-start(f32[128,128]{1,0:T(8,128)} %own_ref.1), channel_id=1, source_target_pairs={{0,8},{1,9},{2,10},{3,11},{4,12},{5,13},{6,14},{7,15},{8,16},{9,17... | collective-permute-start | bytes 196616 | tf_op jit(solution)/shard_map/ppermute | solution.py:18
  3.7 2.1 %collective-permute-start.1 = (f32[128,128]{1,0:T(8,128)}, f32[128,128]{1,0:T(8,128)S(1)}, u32[]{:S(2)}, u32[]{:S(2)}) collective-permute-start(f32[128,128]{1,0:T(8,128)} %own_ref.1), channel_id=1, source_target_pairs={{0,24},{1,25},{2,26},{3,27},{4,28},{5,29},{6,30},{7,31},{8,0},{9,1... | collective-permute-start | bytes 196616 | tf_op jit(solution)/shard_map/ppermute | solution.py:18
  5.8 0.0 copy-start.1
  5.8 0.9 %copy-done.1 = f32[128,128]{1,0:T(8,128)S(1)} copy-done((f32[128,128]{1,0:T(8,128)S(1)}, f32[128,128]{1,0:T(8,128)}, u32[]{:S(2)}) %copy-start.1) | copy-done | bytes 65560
  6.7 0.1 shard_map.50.own_ref.right_ref
  6.8 1.6 %collective-permute-done.refs_2_ = f32[128,128]{1,0:T(8,128)S(1)} collective-permute-done((f32[128,128]{1,0:T(8,128)}, f32[128,128]{1,0:T(8,128)S(1)}, u32[]{:S(2)}, u32[]{:S(2)}) %collective-permute-start) | collective-permute-done | bytes 65568 | tf_op jit(solution)/shard_map/ppermute | solution.py:18
  8.4 0.5 %collective-permute-done.1.refs_0_ = f32[128,128]{1,0:T(8,128)S(1)} collective-permute-done((f32[128,128]{1,0:T(8,128)}, f32[128,128]{1,0:T(8,128)S(1)}, u32[]{:S(2)}, u32[]{:S(2)}) %collective-permute-start.1) | collective-permute-done | bytes 65568 | tf_op jit(solution)/shard_map/ppermute | solution.py:18
  8.9 2.5 %collective-permute-start.5 = (f32[128,128]{1,0:T(8,128)S(1)}, f32[128,128]{1,0:T(8,128)S(1)}, u32[]{:S(2)}, u32[]{:S(2)}) collective-permute-start(f32[128,128]{1,0:T(8,128)S(1)} %get-tuple-element.41), channel_id=1, source_target_pairs={{0,6},{1,7},{2,4},{3,5},{4,2},{5,3},{6,0},{7,1},{8,14},{9,15},{10,... | collective-permute-start | bytes 196616 | tf_op jit(solution)/shard_map/ppermute | solution.py:23
  11.4 0.5 %collective-permute-start.4 = (f32[128,128]{1,0:T(8,128)S(1)}, f32[128,128]{1,0:T(8,128)S(1)}, u32[]{:S(2)}, u32[]{:S(2)}) collective-permute-start(f32[128,128]{1,0:T(8,128)S(1)} %get-tuple-element.42), channel_id=1, source_target_pairs={{0,4},{1,5},{2,6},{3,7},{4,0},{5,1},{6,2},{7,3},{8,12},{9,13},{10,... | collective-permute-start | bytes 196616 | tf_op jit(solution)/shard_map/ppermute | solution.py:23
  11.9 0.5 %collective-permute-start.3 = (f32[128,128]{1,0:T(8,128)S(1)}, f32[128,128]{1,0:T(8,128)S(1)}, u32[]{:S(2)}, u32[]{:S(2)}) collective-permute-start(f32[128,128]{1,0:T(8,128)S(1)} %get-tuple-element.43), channel_id=1, source_target_pairs={{0,2},{1,3},{2,0},{3,1},{4,6},{5,7},{6,4},{7,5},{8,10},{9,11},{10,... | collective-permute-start | bytes 196616 | tf_op jit(solution)/shard_map/ppermute | solution.py:23
  12.5 1.9 %collective-permute-start.2 = (f32[128,128]{1,0:T(8,128)}, f32[128,128]{1,0:T(8,128)S(1)}, u32[]{:S(2)}, u32[]{:S(2)}) collective-permute-start(f32[128,128]{1,0:T(8,128)} %own_ref.1), channel_id=1, source_target_pairs={{0,16},{1,17},{2,18},{3,19},{4,20},{5,21},{6,22},{7,23},{8,24},{9,... | collective-permute-start | bytes 196616 | tf_op jit(solution)/shard_map/ppermute | solution.py:18
  14.4 0.0 copy-start
  14.4 1.2 %copy-done = f32[1,17,128,128]{3,2,1,0:T(8,128)S(1)} copy-done((f32[1,17,128,128]{3,2,1,0:T(8,128)S(1)}, f32[1,17,128,128]{3,2,1,0:T(8,128)}, u32[]{:S(2)}) %copy-start) | copy-done | bytes 1114136
  15.6 0.4 shard_map.52
  16.0 0.0 collective-permute-done.5.refs_5_
  16.0 0.0 collective-permute-done.4.refs_4_
  16.0 0.2 collective-permute-done.3.refs_3_
  16.2 0.0 copy-start.2
  16.2 0.1 collective-permute-start.6
  16.3 2.2 %collective-permute-done.2.refs_0_.refs_1_ = f32[128,128]{1,0:T(8,128)S(1)} collective-permute-done((f32[128,128]{1,0:T(8,128)}, f32[128,128]{1,0:T(8,128)S(1)}, u32[]{:S(2)}, u32[]{:S(2)}) %collective-permute-start.2) | collective-permute-done | bytes 65568 | tf_op jit(solution)/shard_map/ppermute | solution.py:18
  18.6 0.0 collective-permute-done.6.refs_6_
  18.6 0.0 copy-done.2
  18.6 1.8 %shard_map.53 = (f32[520,128]{1,0:T(8,128)S(1)}, f32[5,128,128]{2,1,0:T(8,128)S(1)}, f32[128,128]{1,0:T(8,128)S(1)}, f32[128,128]{1,0:T(8,128)S(1)}) custom-call(s32[2,17]{1,0:T(2,128)S(1)} %bitcast.12, s32[1]{0:T(128)} %bitcast.place_ref, f32[128,128]{1,0:T(8,128)S(1)} %shard_map.50.own_ref.right_ref, f32[128,128]{1,0:T(8,128)S(1)} %collective-permute-done.1.refs_0_, ...), custom_call_target="tpu_custom_call" | custom-call | tf_op jit(solution)/shard_map/pallas_call | solution.py:202
  20.4 0.1 collective-permute-start.7
  20.5 1.5 %collective-permute-done.7.got_ref = f32[520,128]{1,0:T(8,128)S(1)} collective-permute-done((f32[520,128]{1,0:T(8,128)S(1)}, f32[520,128]{1,0:T(8,128)S(1)}, u32[]{:S(2)}, u32[]{:S(2)}) %collective-permute-start.7) | collective-permute-done | bytes 266272 | tf_op jit(solution)/shard_map/ppermute | solution.py:28
  22.0 1.6 %collective-permute-start.8 = (f32[136,128]{1,0:T(8,128)S(1)}, f32[136,128]{1,0:T(8,128)S(1)}, u32[]{:S(2)}, u32[]{:S(2)}) collective-permute-start(f32[136,128]{1,0:T(8,128)S(1)} %get-tuple-element.32), channel_id=1, source_target_pairs={{0,2},{1,3},{2,0},{3,1},{4,6},{5,7},{6,4},{7,5},{8,10},{9,11},{10,... | collective-permute-start | bytes 208904 | tf_op jit(solution)/shard_map/ppermute | solution.py:23
  23.6 1.5 %collective-permute-start.9 = (f32[136,128]{1,0:T(8,128)S(1)}, f32[136,128]{1,0:T(8,128)S(1)}, u32[]{:S(2)}, u32[]{:S(2)}) collective-permute-start(f32[136,128]{1,0:T(8,128)S(1)} %get-tuple-element.33), channel_id=1, source_target_pairs={{0,4},{1,5},{2,6},{3,7},{4,0},{5,1},{6,2},{7,3},{8,12},{9,13},{10,... | collective-permute-start | bytes 208904 | tf_op jit(solution)/shard_map/ppermute | solution.py:23
  25.1 0.5 %collective-permute-start.10 = (f32[136,128]{1,0:T(8,128)S(1)}, f32[136,128]{1,0:T(8,128)S(1)}, u32[]{:S(2)}, u32[]{:S(2)}) collective-permute-start(f32[136,128]{1,0:T(8,128)S(1)} %get-tuple-element.34), channel_id=1, source_target_pairs={{0,6},{1,7},{2,4},{3,5},{4,2},{5,3},{6,0},{7,1},{8,14},{9,15},{10,... | collective-permute-start | bytes 208904 | tf_op jit(solution)/shard_map/ppermute | solution.py:23
  25.6 1.2 %collective-permute-start.11 = (f32[128,128]{1,0:T(8,128)S(1)}, f32[128,128]{1,0:T(8,128)S(1)}, u32[]{:S(2)}, u32[]{:S(2)}) collective-permute-start(f32[128,128]{1,0:T(8,128)S(1)} %get-tuple-element.36), channel_id=1, source_target_pairs={{0,16},{1,17},{2,18},{3,19},{4,20},{5,21},{6,22},{7,23},{8,24},{9,... | collective-permute-start | bytes 196616 | tf_op jit(solution)/shard_map/ppermute | solution.py:18
  26.8 0.0 collective-permute-done.8.refs_0_
  26.8 1.1 %collective-permute-done.9.refs_1_ = f32[136,128]{1,0:T(8,128)S(1)} collective-permute-done((f32[136,128]{1,0:T(8,128)S(1)}, f32[136,128]{1,0:T(8,128)S(1)}, u32[]{:S(2)}, u32[]{:S(2)}) %collective-permute-start.9) | collective-permute-done | bytes 69664 | tf_op jit(solution)/shard_map/ppermute | solution.py:23
  27.9 2.4 %collective-permute-done.10.refs_2_ = f32[136,128]{1,0:T(8,128)S(1)} collective-permute-done((f32[136,128]{1,0:T(8,128)S(1)}, f32[136,128]{1,0:T(8,128)S(1)}, u32[]{:S(2)}, u32[]{:S(2)}) %collective-permute-start.10) | collective-permute-done | bytes 69664 | tf_op jit(solution)/shard_map/ppermute | solution.py:23
  30.4 1.3 %collective-permute-start.14 = (f32[8,128]{1,0:T(8,128)S(1)}, f32[8,128]{1,0:T(8,128)S(1)}, u32[]{:S(2)}, u32[]{:S(2)}) collective-permute-start(f32[8,128]{1,0:T(8,128)S(1)} %get-tuple-element.37.sums_ref), channel_id=1, source_target_pairs={{0,16},{1,17},{2,18},{3,19},{4,20},{5,21},{6,22},{7,23},{8,24},{9,... | collective-permute-start | bytes 12296 | tf_op jit(solution)/shard_map/ppermute | solution.py:18
  31.6 2.1 %collective-permute-start.12 = (f32[136,128]{1,0:T(8,128)S(1)}, f32[136,128]{1,0:T(8,128)S(1)}, u32[]{:S(2)}, u32[]{:S(2)}) collective-permute-start(f32[136,128]{1,0:T(8,128)S(1)} %get-tuple-element.38), channel_id=1, source_target_pairs={{0,8},{1,9},{2,10},{3,11},{4,12},{5,13},{6,14},{7,15},{8,16},{9,17... | collective-permute-start | bytes 208904 | tf_op jit(solution)/shard_map/ppermute | solution.py:18
  33.8 1.7 %collective-permute-start.13 = (f32[136,128]{1,0:T(8,128)S(1)}, f32[136,128]{1,0:T(8,128)S(1)}, u32[]{:S(2)}, u32[]{:S(2)}) collective-permute-start(f32[136,128]{1,0:T(8,128)S(1)} %get-tuple-element.39), channel_id=1, source_target_pairs={{0,24},{1,25},{2,26},{3,27},{4,28},{5,29},{6,30},{7,31},{8,0},{9,1... | collective-permute-start | bytes 208904 | tf_op jit(solution)/shard_map/ppermute | solution.py:18
  35.5 0.0 collective-permute-done.11.refs_0_
  35.5 0.0 collective-permute-done.14.refs_2_
  35.5 2.4 %collective-permute-done.12.refs_0_ = f32[136,128]{1,0:T(8,128)S(1)} collective-permute-done((f32[136,128]{1,0:T(8,128)S(1)}, f32[136,128]{1,0:T(8,128)S(1)}, u32[]{:S(2)}, u32[]{:S(2)}) %collective-permute-start.12) | collective-permute-done | bytes 69664 | tf_op jit(solution)/shard_map/ppermute | solution.py:18
  37.9 0.7 %collective-permute-done.13.refs_1_ = f32[136,128]{1,0:T(8,128)S(1)} collective-permute-done((f32[136,128]{1,0:T(8,128)S(1)}, f32[136,128]{1,0:T(8,128)S(1)}, u32[]{:S(2)}, u32[]{:S(2)}) %collective-permute-start.13) | collective-permute-done | bytes 69664 | tf_op jit(solution)/shard_map/ppermute | solution.py:18
  38.6 0.7 %shard_map.57 = (f32[128,128]{1,0:T(8,128)}, f32[128,128]{1,0:T(8,128)}) custom-call(f32[128,128]{1,0:T(8,128)S(1)} %shard_map.50.own_ref.right_ref, f32[128,128]{1,0:T(8,128)S(1)} %get-tuple-element.35.near_ref, f32[128,128]{1,0:T(8,128)S(1)} %shard_map.56.middle_ref, f32[8,128]{1,0:T(8,128)S(1)} %get-tuple-element.37.sums_ref, ...), custom_call_target="tpu_custom_call" | custom-call | tf_op jit(solution)/shard_map/pallas_call | solution.py:202
  (6 shorter events, 0.1 us)
Async XLA Ops:
  0.6 7.7 %collective-permute-start = (f32[128,128]{1,0:T(8,128)}, f32[128,128]{1,0:T(8,128)S(1)}, u32[]{:S(2)}, u32[]{:S(2)}) collective-permute-start(f32[128,128]{1,0:T(8,128)} %own_ref.1), channel_id=1, source_target_pairs={{0,8},{1,9},{2,10},{3,11},{4,12},{5,13},{6,14},{7,15},{8,16},{9,17... | collective-permute-start | bytes 196616 | tf_op jit(solution)/shard_map/ppermute | solution.py:18
  3.7 5.2 %collective-permute-start.1 = (f32[128,128]{1,0:T(8,128)}, f32[128,128]{1,0:T(8,128)S(1)}, u32[]{:S(2)}, u32[]{:S(2)}) collective-permute-start(f32[128,128]{1,0:T(8,128)} %own_ref.1), channel_id=1, source_target_pairs={{0,24},{1,25},{2,26},{3,27},{4,28},{5,29},{6,30},{7,31},{8,0},{9,1... | collective-permute-start | bytes 196616 | tf_op jit(solution)/shard_map/ppermute | solution.py:18
  5.8 0.9 %copy-start.1 = (f32[128,128]{1,0:T(8,128)S(1)}, f32[128,128]{1,0:T(8,128)}, u32[]{:S(2)}) copy-start(f32[128,128]{1,0:T(8,128)} %own_ref.1) | copy-start | bytes 196612
  8.9 7.1 %collective-permute-start.5 = (f32[128,128]{1,0:T(8,128)S(1)}, f32[128,128]{1,0:T(8,128)S(1)}, u32[]{:S(2)}, u32[]{:S(2)}) collective-permute-start(f32[128,128]{1,0:T(8,128)S(1)} %get-tuple-element.41), channel_id=1, source_target_pairs={{0,6},{1,7},{2,4},{3,5},{4,2},{5,3},{6,0},{7,1},{8,14},{9,15},{10,... | collective-permute-start | bytes 196616 | tf_op jit(solution)/shard_map/ppermute | solution.py:23
  11.4 4.6 %collective-permute-start.4 = (f32[128,128]{1,0:T(8,128)S(1)}, f32[128,128]{1,0:T(8,128)S(1)}, u32[]{:S(2)}, u32[]{:S(2)}) collective-permute-start(f32[128,128]{1,0:T(8,128)S(1)} %get-tuple-element.42), channel_id=1, source_target_pairs={{0,4},{1,5},{2,6},{3,7},{4,0},{5,1},{6,2},{7,3},{8,12},{9,13},{10,... | collective-permute-start | bytes 196616 | tf_op jit(solution)/shard_map/ppermute | solution.py:23
  11.9 4.3 %collective-permute-start.3 = (f32[128,128]{1,0:T(8,128)S(1)}, f32[128,128]{1,0:T(8,128)S(1)}, u32[]{:S(2)}, u32[]{:S(2)}) collective-permute-start(f32[128,128]{1,0:T(8,128)S(1)} %get-tuple-element.43), channel_id=1, source_target_pairs={{0,2},{1,3},{2,0},{3,1},{4,6},{5,7},{6,4},{7,5},{8,10},{9,11},{10,... | collective-permute-start | bytes 196616 | tf_op jit(solution)/shard_map/ppermute | solution.py:23
  12.5 6.1 %collective-permute-start.2 = (f32[128,128]{1,0:T(8,128)}, f32[128,128]{1,0:T(8,128)S(1)}, u32[]{:S(2)}, u32[]{:S(2)}) collective-permute-start(f32[128,128]{1,0:T(8,128)} %own_ref.1), channel_id=1, source_target_pairs={{0,16},{1,17},{2,18},{3,19},{4,20},{5,21},{6,22},{7,23},{8,24},{9,... | collective-permute-start | bytes 196616 | tf_op jit(solution)/shard_map/ppermute | solution.py:18
  14.4 1.2 %copy-start = (f32[1,17,128,128]{3,2,1,0:T(8,128)S(1)}, f32[1,17,128,128]{3,2,1,0:T(8,128)}, u32[]{:S(2)}) copy-start(f32[1,17,128,128]{3,2,1,0:T(8,128)} %param.4) | copy-start | bytes 3342340
  16.2 2.4 %copy-start.2 = (s32[17,2]{0,1:T(2,128)S(1)}, s32[17,2]{0,1:T(2,128)}, u32[]{:S(2)}) copy-start(s32[17,2]{0,1:T(2,128)} %param.5) | copy-start | bytes 412
  16.2 2.3 %collective-permute-start.6 = (f32[4,128,128]{2,1,0:T(8,128)S(1)}, f32[4,128,128]{2,1,0:T(8,128)S(1)}, u32[]{:S(2)}, u32[]{:S(2)}) collective-permute-start(f32[4,128,128]{2,1,0:T(8,128)S(1)} %pad_maximum_fusion), channel_id=1, source_target_pairs={{0,1},{1,0},{2,3},{3,2},{4,5},{5,4},{6,7},{7,6},{8,9},{9,8},{10,11... | collective-permute-start | bytes 786440 | tf_op jit(solution)/shard_map/ppermute | solution.py:28
  20.4 1.6 %collective-permute-start.7 = (f32[520,128]{1,0:T(8,128)S(1)}, f32[520,128]{1,0:T(8,128)S(1)}, u32[]{:S(2)}, u32[]{:S(2)}) collective-permute-start(f32[520,128]{1,0:T(8,128)S(1)} %get-tuple-element.26.sent_ref), channel_id=1, source_target_pairs={{0,1},{1,0},{2,3},{3,2},{4,5},{5,4},{6,7},{7,6},{8,9},{9,8},{10,11... | collective-permute-start | bytes 798728 | tf_op jit(solution)/shard_map/ppermute | solution.py:28
  22.0 4.8 %collective-permute-start.8 = (f32[136,128]{1,0:T(8,128)S(1)}, f32[136,128]{1,0:T(8,128)S(1)}, u32[]{:S(2)}, u32[]{:S(2)}) collective-permute-start(f32[136,128]{1,0:T(8,128)S(1)} %get-tuple-element.32), channel_id=1, source_target_pairs={{0,2},{1,3},{2,0},{3,1},{4,6},{5,7},{6,4},{7,5},{8,10},{9,11},{10,... | collective-permute-start | bytes 208904 | tf_op jit(solution)/shard_map/ppermute | solution.py:23
  23.6 4.3 %collective-permute-start.9 = (f32[136,128]{1,0:T(8,128)S(1)}, f32[136,128]{1,0:T(8,128)S(1)}, u32[]{:S(2)}, u32[]{:S(2)}) collective-permute-start(f32[136,128]{1,0:T(8,128)S(1)} %get-tuple-element.33), channel_id=1, source_target_pairs={{0,4},{1,5},{2,6},{3,7},{4,0},{5,1},{6,2},{7,3},{8,12},{9,13},{10,... | collective-permute-start | bytes 208904 | tf_op jit(solution)/shard_map/ppermute | solution.py:23
  25.1 5.2 %collective-permute-start.10 = (f32[136,128]{1,0:T(8,128)S(1)}, f32[136,128]{1,0:T(8,128)S(1)}, u32[]{:S(2)}, u32[]{:S(2)}) collective-permute-start(f32[136,128]{1,0:T(8,128)S(1)} %get-tuple-element.34), channel_id=1, source_target_pairs={{0,6},{1,7},{2,4},{3,5},{4,2},{5,3},{6,0},{7,1},{8,14},{9,15},{10,... | collective-permute-start | bytes 208904 | tf_op jit(solution)/shard_map/ppermute | solution.py:23
  25.6 9.9 %collective-permute-start.11 = (f32[128,128]{1,0:T(8,128)S(1)}, f32[128,128]{1,0:T(8,128)S(1)}, u32[]{:S(2)}, u32[]{:S(2)}) collective-permute-start(f32[128,128]{1,0:T(8,128)S(1)} %get-tuple-element.36), channel_id=1, source_target_pairs={{0,16},{1,17},{2,18},{3,19},{4,20},{5,21},{6,22},{7,23},{8,24},{9,... | collective-permute-start | bytes 196616 | tf_op jit(solution)/shard_map/ppermute | solution.py:18
  30.4 5.1 %collective-permute-start.14 = (f32[8,128]{1,0:T(8,128)S(1)}, f32[8,128]{1,0:T(8,128)S(1)}, u32[]{:S(2)}, u32[]{:S(2)}) collective-permute-start(f32[8,128]{1,0:T(8,128)S(1)} %get-tuple-element.37.sums_ref), channel_id=1, source_target_pairs={{0,16},{1,17},{2,18},{3,19},{4,20},{5,21},{6,22},{7,23},{8,24},{9,... | collective-permute-start | bytes 12296 | tf_op jit(solution)/shard_map/ppermute | solution.py:18
  31.6 6.3 %collective-permute-start.12 = (f32[136,128]{1,0:T(8,128)S(1)}, f32[136,128]{1,0:T(8,128)S(1)}, u32[]{:S(2)}, u32[]{:S(2)}) collective-permute-start(f32[136,128]{1,0:T(8,128)S(1)} %get-tuple-element.38), channel_id=1, source_target_pairs={{0,8},{1,9},{2,10},{3,11},{4,12},{5,13},{6,14},{7,15},{8,16},{9,17... | collective-permute-start | bytes 208904 | tf_op jit(solution)/shard_map/ppermute | solution.py:18
  33.8 4.8 %collective-permute-start.13 = (f32[136,128]{1,0:T(8,128)S(1)}, f32[136,128]{1,0:T(8,128)S(1)}, u32[]{:S(2)}, u32[]{:S(2)}) collective-permute-start(f32[136,128]{1,0:T(8,128)S(1)} %get-tuple-element.39), channel_id=1, source_target_pairs={{0,24},{1,25},{2,26},{3,27},{4,28},{5,29},{6,30},{7,31},{8,0},{9,1... | collective-permute-start | bytes 208904 | tf_op jit(solution)/shard_map/ppermute | solution.py:18

commit v11 on v10

--- a/solution.py
+++ b/solution.py
@@ -39,19 +39,14 @@
     return (place // 2) & (chips - 1), place & 1
 
 
-def fetch_kernel(own_ref, out_ref, done):
-    copy = pltpu.make_async_copy(own_ref, out_ref, done)
-    copy.start()
-    copy.wait()
-
-
-def split_kernel(tiles_ref, straight_ref, turned_ref):
-    slots = tiles_ref.shape[0]
+def prepare_kernel(own_ref, tiles_ref, own_out, straight_ref, turned_ref):
+    own_out[...] = own_ref[...]
+    slots, rows, cols = tiles_ref.shape
 
     def visit(t):
         tile = tiles_ref[t]
-        straight_ref[t, 0], straight_ref[t, 1] = split_two(tile)
-        turned_ref[t, 0], turned_ref[t, 1] = split_two(tile.T)
+        straight_ref[t, :rows, :], straight_ref[t, rows:, :] = split_two(tile)
+        turned_ref[t, :cols, :], turned_ref[t, cols:, :] = split_two(tile.T)
 
     if slots <= 32:
         for t in range(slots):
@@ -67,11 +62,13 @@
         out_ref[i, :, :cols], out_ref[i, :, cols:] = split_two(block[...])
 
 
-def add_kernel(*refs):
+def middle_kernel(sums_ref, *refs):
+    total_ref, sums_out = refs[-2:]
     total = refs[0][...]
-    for block in refs[1:-1]:
+    for block in refs[1:-2]:
         total = total + block[...]
-    refs[-1][...] = total
+    total_ref[...] = total
+    sums_out[...] = sums_ref[...]
 
 
 def steps_ahead(chip, mask, chips):
@@ -111,9 +108,9 @@
     slots = straight_ref.shape[0]
 
     def product(split_ref, t, place):
-        both = jnp.dot(split_ref[t, 0], parts[place], preferred_element_type=jnp.float32)
-        rest = jnp.dot(split_ref[t, 1], parts[place, :, :cols], preferred_element_type=jnp.float32)
-        return both[:, :cols] + (both[:, cols:] + rest)
+        both = jnp.dot(split_ref[t], parts[place], preferred_element_type=jnp.float32)
+        high, low = both[:rows], both[rows:]
+        return high[:, :cols] + ((high[:, cols:] + low[:, :cols]) + low[:, cols:])
 
     def visit(t, mirrored):
         row_place, col_place = pairs_ref[0, t], pairs_ref[1, t]
@@ -197,11 +194,11 @@
     residual_ref[...] = right - step_len * image
 
 
-def call(kernel, smem, operands, outs, scratch=(), space=pltpu.VMEM, cost=None):
+def call(kernel, smem, operands, outs, scratch=(), cost=None):
     vmem = pl.BlockSpec(memory_space=pltpu.VMEM)
     return pl.pallas_call(
         kernel,
-        in_specs=[pl.BlockSpec(memory_space=pltpu.SMEM)] * len(smem) + [pl.BlockSpec(memory_space=space)] * len(operands),
+        in_specs=[pl.BlockSpec(memory_space=pltpu.SMEM)] * len(smem) + [vmem] * len(operands),
         out_specs=[vmem] * len(outs),
         out_shape=[jax.ShapeDtypeStruct(shape, kind) for shape, kind in outs],
         scratch_shapes=list(scratch),
@@ -222,9 +219,11 @@
     where = place[None]
     single, half = jnp.float32, jnp.bfloat16
 
-    (own,) = call(fetch_kernel, (), (right_side,), [((rows, cols), single)], [pltpu.SemaphoreType.DMA], pl.ANY)
-    straight, turned = call(
-        split_kernel, (), (kernel_tiles[0],), [((slots, 2, rows, cols), half), ((slots, 2, cols, rows), half)]
+    own, straight, turned = call(
+        prepare_kernel,
+        (),
+        (right_side, kernel_tiles[0]),
+        [((rows, cols), single), ((slots, 2 * rows, cols), half), ((slots, 2 * cols, rows), half)],
     )
     far = {k: shifted(right_side, -k * window) for k in (planes - 1, *range(1, planes - 1))}
     own, far[planes - 1], far[1] = lax.optimization_barrier((own, far[planes - 1], far[1]))
@@ -252,12 +251,12 @@
         functools.partial(pair_kernel, chips), (where,), (sent, kept, got), [marked] * (chips - 1) + [block, block, extra]
     )
     middle_got = [shifted(far_out[k - 2], k * window) for k in middle]
-    (middle_sum,) = call(add_kernel, (), middle_got, [block], cost=BESIDE)
     got = [chip_partner(value, m) for m, value in enumerate(messages, 1)]
     ahead, last, near, sums = call(
         functools.partial(plane_kernel, chips), (where,), (near, ahead, sums, far_out[-1], *got), [marked, marked, block, extra]
     )
-    got = [shifted(ahead, window), *[shifted(sums, k * window) for k in middle], shifted(last, (planes - 1) * window)]
+    middle_sum, passed = call(middle_kernel, (), (sums, *middle_got), [block, extra], cost=BESIDE)
+    got = [shifted(ahead, window), *[shifted(passed, k * window) for k in middle], shifted(last, (planes - 1) * window)]
     return call(
         final_kernel, (), (own, near, middle_sum, sums, got[0], got[-1], *got[1:-1]), [block, block]
     )

time: 39.5 us -> 39.8 us (level)
  waiting for transfers between devices: 12.7 us -> 13.9 us
  starting transfers between devices: 20.6 us -> 19.6 us
    ppermute x6, waiting for transfers between devices: 3.72 us -> 5.23 us  [chip_partner(): lax.ppermute(value, 'blk', [(source, source ^ 2 * mask) for source in ran...]
    ppermute x7, starting transfers between devices: 13.4 us -> 12.3 us  [shifted(): return lax.ppermute(value, 'blk', pairs)]
    pallas_call x8 -> x7, Pallas kernels: 3.02 us -> 3.27 us  [call(): pl.pallas_call(kernel, in_specs=[pl.BlockSpec(memory_space=pltpu.SMEM)] *...]
  transfers between devices with their start and end apart: 15 -> 15, of which waited for: 9 -> 10; matrix products, arithmetic and copies ran while one was open for 0% -> 0% of each run, Pallas kernels for 1% -> 1%
where the time goes in v11:
time: 39.8 us; the launch traced here: 39.6 us
  starting transfers between devices  19.6 us (49%)
  waiting for transfers between devices  13.9 us (35%)
  Pallas kernels  3.27 us (8%)
  local copies, waits for them, and re-layouts  2.09 us (5%)
  between operations  0.72 us (2%)
    ppermute x7, starting transfers between devices, shifted(): return lax.ppermute(value, 'blk', pairs)  12.3 us
    ppermute x7, waiting for transfers between devices, shifted(): return lax.ppermute(value, 'blk', pairs)  7.15 us
    ppermute x6, starting transfers between devices, chip_partner(): lax.ppermute(value, 'blk', [(source, source ^ 2 * mask) for source in ran...  7.11 us
    ppermute x6, waiting for transfers between devices, chip_partner(): lax.ppermute(value, 'blk', [(source, source ^ 2 * mask) for source in ran...  5.23 us
    pallas_call x7, Pallas kernels, call(): pl.pallas_call(kernel, in_specs=[pl.BlockSpec(memory_space=pltpu.SMEM)] *...  3.27 us
    unnamed x6, local copies, waits for them, and re-layouts  2.09 us
    ppermute x2, waiting for transfers between devices, core_partner(): lax.ppermute(value, 'blk', [(source, source ^ 1) for source in range(coun...  1.53 us
  transfers between devices with their start and end apart: 15, of which 10 were waited for; matrix products, arithmetic and copies ran while one was open for 0% of the time, Pallas kernels for 1%

profile of v11, /device:TPU:0, one launch (start us, length us, event | category | flops | bytes accessed | tf_op | source)
XLA Modules:
  0.0 39.6 jit_solution(8991811431642650051)
XLA Ops:
  0.6 3.1 %collective-permute-start = (f32[128,128]{1,0:T(8,128)}, f32[128,128]{1,0:T(8,128)S(1)}, u32[]{:S(2)}, u32[]{:S(2)}) collective-permute-start(f32[128,128]{1,0:T(8,128)} %own_ref.1), channel_id=1, source_target_pairs={{0,8},{1,9},{2,10},{3,11},{4,12},{5,13},{6,14},{7,15},{8,16},{9,17... | collective-permute-start | bytes 196616 | tf_op jit(solution)/shard_map/ppermute | solution.py:18
  3.7 2.1 %collective-permute-start.1 = (f32[128,128]{1,0:T(8,128)}, f32[128,128]{1,0:T(8,128)S(1)}, u32[]{:S(2)}, u32[]{:S(2)}) collective-permute-start(f32[128,128]{1,0:T(8,128)} %own_ref.1), channel_id=1, source_target_pairs={{0,24},{1,25},{2,26},{3,27},{4,28},{5,29},{6,30},{7,31},{8,0},{9,1... | collective-permute-start | bytes 196616 | tf_op jit(solution)/shard_map/ppermute | solution.py:18
  5.8 0.0 copy-start
  5.8 1.2 %copy-done = f32[1,17,128,128]{3,2,1,0:T(8,128)S(1)} copy-done((f32[1,17,128,128]{3,2,1,0:T(8,128)S(1)}, f32[1,17,128,128]{3,2,1,0:T(8,128)}, u32[]{:S(2)}) %copy-start) | copy-done | bytes 1114136
  7.0 0.0 copy-start.1
  7.0 0.8 %copy-done.1 = f32[128,128]{1,0:T(8,128)S(1)} copy-done((f32[128,128]{1,0:T(8,128)S(1)}, f32[128,128]{1,0:T(8,128)}, u32[]{:S(2)}) %copy-start.1) | copy-done | bytes 65560
  7.9 0.4 shard_map.50
  8.3 0.1 collective-permute-done.refs_2_
  8.3 0.5 %collective-permute-done.1.refs_0_ = f32[128,128]{1,0:T(8,128)S(1)} collective-permute-done((f32[128,128]{1,0:T(8,128)}, f32[128,128]{1,0:T(8,128)S(1)}, u32[]{:S(2)}, u32[]{:S(2)}) %collective-permute-start.1) | collective-permute-done | bytes 65568 | tf_op jit(solution)/shard_map/ppermute | solution.py:18
  8.9 2.5 %collective-permute-start.5 = (f32[128,128]{1,0:T(8,128)S(1)}, f32[128,128]{1,0:T(8,128)S(1)}, u32[]{:S(2)}, u32[]{:S(2)}) collective-permute-start(f32[128,128]{1,0:T(8,128)S(1)} %get-tuple-element.47), channel_id=1, source_target_pairs={{0,6},{1,7},{2,4},{3,5},{4,2},{5,3},{6,0},{7,1},{8,14},{9,15},{10,... | collective-permute-start | bytes 196616 | tf_op jit(solution)/shard_map/ppermute | solution.py:23
  11.4 0.5 %collective-permute-start.4 = (f32[128,128]{1,0:T(8,128)S(1)}, f32[128,128]{1,0:T(8,128)S(1)}, u32[]{:S(2)}, u32[]{:S(2)}) collective-permute-start(f32[128,128]{1,0:T(8,128)S(1)} %get-tuple-element.48), channel_id=1, source_target_pairs={{0,4},{1,5},{2,6},{3,7},{4,0},{5,1},{6,2},{7,3},{8,12},{9,13},{10,... | collective-permute-start | bytes 196616 | tf_op jit(solution)/shard_map/ppermute | solution.py:23
  11.9 0.5 %collective-permute-start.3 = (f32[128,128]{1,0:T(8,128)S(1)}, f32[128,128]{1,0:T(8,128)S(1)}, u32[]{:S(2)}, u32[]{:S(2)}) collective-permute-start(f32[128,128]{1,0:T(8,128)S(1)} %get-tuple-element.49), channel_id=1, source_target_pairs={{0,2},{1,3},{2,0},{3,1},{4,6},{5,7},{6,4},{7,5},{8,10},{9,11},{10,... | collective-permute-start | bytes 196616 | tf_op jit(solution)/shard_map/ppermute | solution.py:23
  12.5 1.9 %collective-permute-start.2 = (f32[128,128]{1,0:T(8,128)S(1)}, f32[128,128]{1,0:T(8,128)S(1)}, u32[]{:S(2)}, u32[]{:S(2)}) collective-permute-start(f32[128,128]{1,0:T(8,128)S(1)} %copy-done.1), channel_id=1, source_target_pairs={{0,16},{1,17},{2,18},{3,19},{4,20},{5,21},{6,22},{7,23},{8,24},{9,... | collective-permute-start | bytes 196616 | tf_op jit(solution)/shard_map/ppermute | solution.py:18
  14.4 0.1 collective-permute-done.5.refs_5_
  14.5 1.2 %collective-permute-done.4.refs_4_ = f32[128,128]{1,0:T(8,128)S(1)} collective-permute-done((f32[128,128]{1,0:T(8,128)S(1)}, f32[128,128]{1,0:T(8,128)S(1)}, u32[]{:S(2)}, u32[]{:S(2)}) %collective-permute-start.4) | collective-permute-done | bytes 65568 | tf_op jit(solution)/shard_map/ppermute | solution.py:23
  15.7 0.5 %collective-permute-done.3.refs_3_ = f32[128,128]{1,0:T(8,128)S(1)} collective-permute-done((f32[128,128]{1,0:T(8,128)S(1)}, f32[128,128]{1,0:T(8,128)S(1)}, u32[]{:S(2)}, u32[]{:S(2)}) %collective-permute-start.3) | collective-permute-done | bytes 65568 | tf_op jit(solution)/shard_map/ppermute | solution.py:23
  16.2 0.0 copy-start.2
  16.2 0.1 collective-permute-start.6
  16.3 2.0 %collective-permute-done.2.refs_0_.refs_1_ = f32[128,128]{1,0:T(8,128)S(1)} collective-permute-done((f32[128,128]{1,0:T(8,128)S(1)}, f32[128,128]{1,0:T(8,128)S(1)}, u32[]{:S(2)}, u32[]{:S(2)}) %collective-permute-start.2) | collective-permute-done | bytes 65568 | tf_op jit(solution)/shard_map/ppermute | solution.py:18
  18.3 0.0 collective-permute-done.6.refs_6_
  18.4 0.0 copy-done.2
  18.4 2.1 %shard_map.52 = (f32[520,128]{1,0:T(8,128)S(1)}, f32[5,128,128]{2,1,0:T(8,128)S(1)}, f32[128,128]{1,0:T(8,128)S(1)}, f32[128,128]{1,0:T(8,128)S(1)}) custom-call(s32[2,17]{1,0:T(2,128)S(1)} %bitcast.12, s32[1]{0:T(128)} %bitcast.1.place_ref, f32[128,128]{1,0:T(8,128)S(1)} %get-tuple-element.25.own_ref.right_ref, ...), custom_call_target="tpu_custom_call" | custom-call | tf_op jit(solution)/shard_map/pallas_call | solution.py:199
  20.5 0.1 collective-permute-start.7
  20.6 1.5 %collective-permute-done.7.got_ref = f32[520,128]{1,0:T(8,128)S(1)} collective-permute-done((f32[520,128]{1,0:T(8,128)S(1)}, f32[520,128]{1,0:T(8,128)S(1)}, u32[]{:S(2)}, u32[]{:S(2)}) %collective-permute-start.7) | collective-permute-done | bytes 266272 | tf_op jit(solution)/shard_map/ppermute | solution.py:28
  22.1 1.6 %collective-permute-start.8 = (f32[136,128]{1,0:T(8,128)S(1)}, f32[136,128]{1,0:T(8,128)S(1)}, u32[]{:S(2)}, u32[]{:S(2)}) collective-permute-start(f32[136,128]{1,0:T(8,128)S(1)} %get-tuple-element.36), channel_id=1, source_target_pairs={{0,2},{1,3},{2,0},{3,1},{4,6},{5,7},{6,4},{7,5},{8,10},{9,11},{10,... | collective-permute-start | bytes 208904 | tf_op jit(solution)/shard_map/ppermute | solution.py:23
  23.7 1.5 %collective-permute-start.9 = (f32[136,128]{1,0:T(8,128)S(1)}, f32[136,128]{1,0:T(8,128)S(1)}, u32[]{:S(2)}, u32[]{:S(2)}) collective-permute-start(f32[136,128]{1,0:T(8,128)S(1)} %get-tuple-element.37), channel_id=1, source_target_pairs={{0,4},{1,5},{2,6},{3,7},{4,0},{5,1},{6,2},{7,3},{8,12},{9,13},{10,... | collective-permute-start | bytes 208904 | tf_op jit(solution)/shard_map/ppermute | solution.py:23
  25.2 0.5 %collective-permute-start.10 = (f32[136,128]{1,0:T(8,128)S(1)}, f32[136,128]{1,0:T(8,128)S(1)}, u32[]{:S(2)}, u32[]{:S(2)}) collective-permute-start(f32[136,128]{1,0:T(8,128)S(1)} %get-tuple-element.38), channel_id=1, source_target_pairs={{0,6},{1,7},{2,4},{3,5},{4,2},{5,3},{6,0},{7,1},{8,14},{9,15},{10,... | collective-permute-start | bytes 208904 | tf_op jit(solution)/shard_map/ppermute | solution.py:23
  25.7 1.3 %collective-permute-start.11 = (f32[128,128]{1,0:T(8,128)S(1)}, f32[128,128]{1,0:T(8,128)S(1)}, u32[]{:S(2)}, u32[]{:S(2)}) collective-permute-start(f32[128,128]{1,0:T(8,128)S(1)} %get-tuple-element.41), channel_id=1, source_target_pairs={{0,16},{1,17},{2,18},{3,19},{4,20},{5,21},{6,22},{7,23},{8,24},{9,... | collective-permute-start | bytes 196616 | tf_op jit(solution)/shard_map/ppermute | solution.py:18
  27.0 0.0 collective-permute-done.8.refs_0_
  27.0 1.0 %collective-permute-done.9.refs_1_ = f32[136,128]{1,0:T(8,128)S(1)} collective-permute-done((f32[136,128]{1,0:T(8,128)S(1)}, f32[136,128]{1,0:T(8,128)S(1)}, u32[]{:S(2)}, u32[]{:S(2)}) %collective-permute-start.9) | collective-permute-done | bytes 69664 | tf_op jit(solution)/shard_map/ppermute | solution.py:23
  28.0 2.4 %collective-permute-done.10.refs_2_ = f32[136,128]{1,0:T(8,128)S(1)} collective-permute-done((f32[136,128]{1,0:T(8,128)S(1)}, f32[136,128]{1,0:T(8,128)S(1)}, u32[]{:S(2)}, u32[]{:S(2)}) %collective-permute-start.10) | collective-permute-done | bytes 69664 | tf_op jit(solution)/shard_map/ppermute | solution.py:23
  30.5 0.6 %collective-permute-start.12 = (f32[136,128]{1,0:T(8,128)S(1)}, f32[136,128]{1,0:T(8,128)S(1)}, u32[]{:S(2)}, u32[]{:S(2)}) collective-permute-start(f32[136,128]{1,0:T(8,128)S(1)} %get-tuple-element.43), channel_id=1, source_target_pairs={{0,8},{1,9},{2,10},{3,11},{4,12},{5,13},{6,14},{7,15},{8,16},{9,17... | collective-permute-start | bytes 208904 | tf_op jit(solution)/shard_map/ppermute | solution.py:18
  31.0 3.3 %collective-permute-start.13 = (f32[136,128]{1,0:T(8,128)S(1)}, f32[136,128]{1,0:T(8,128)S(1)}, u32[]{:S(2)}, u32[]{:S(2)}) collective-permute-start(f32[136,128]{1,0:T(8,128)S(1)} %get-tuple-element.44), channel_id=1, source_target_pairs={{0,24},{1,25},{2,26},{3,27},{4,28},{5,29},{6,30},{7,31},{8,0},{9,1... | collective-permute-start | bytes 208904 | tf_op jit(solution)/shard_map/ppermute | solution.py:18
  34.4 0.0 collective-permute-done.11.refs_0_
  34.4 0.1 collective-permute-start.14
  34.4 4.5 %collective-permute-done.14.refs_2_ = f32[8,128]{1,0:T(8,128)S(1)} collective-permute-done((f32[8,128]{1,0:T(8,128)S(1)}, f32[8,128]{1,0:T(8,128)S(1)}, u32[]{:S(2)}, u32[]{:S(2)}) %collective-permute-start.14) | collective-permute-done | bytes 4128 | tf_op jit(solution)/shard_map/ppermute | solution.py:18
  38.9 0.0 collective-permute-done.12.refs_0_
  38.9 0.0 collective-permute-done.13.refs_1_
  38.9 0.7 %shard_map.56 = (f32[128,128]{1,0:T(8,128)}, f32[128,128]{1,0:T(8,128)}) custom-call(f32[128,128]{1,0:T(8,128)S(1)} %get-tuple-element.25.own_ref.right_ref, f32[128,128]{1,0:T(8,128)S(1)} %get-tuple-element.39.near_ref, f32[128,128]{1,0:T(8,128)S(1)} %get-tuple-element.42.middle_ref, f32[8,128]{1,0:T(8,128)S(1)} %get-tuple-element.40.sums_ref, ...), custom_call_target="tpu_custom_call" | custom-call | tf_op jit(solution)/shard_map/pallas_call | solution.py:199
  (6 shorter events, 0.1 us)
Async XLA Ops:
  0.6 7.7 %collective-permute-start = (f32[128,128]{1,0:T(8,128)}, f32[128,128]{1,0:T(8,128)S(1)}, u32[]{:S(2)}, u32[]{:S(2)}) collective-permute-start(f32[128,128]{1,0:T(8,128)} %own_ref.1), channel_id=1, source_target_pairs={{0,8},{1,9},{2,10},{3,11},{4,12},{5,13},{6,14},{7,15},{8,16},{9,17... | collective-permute-start | bytes 196616 | tf_op jit(solution)/shard_map/ppermute | solution.py:18
  3.7 5.2 %collective-permute-start.1 = (f32[128,128]{1,0:T(8,128)}, f32[128,128]{1,0:T(8,128)S(1)}, u32[]{:S(2)}, u32[]{:S(2)}) collective-permute-start(f32[128,128]{1,0:T(8,128)} %own_ref.1), channel_id=1, source_target_pairs={{0,24},{1,25},{2,26},{3,27},{4,28},{5,29},{6,30},{7,31},{8,0},{9,1... | collective-permute-start | bytes 196616 | tf_op jit(solution)/shard_map/ppermute | solution.py:18
  5.8 1.2 %copy-start = (f32[1,17,128,128]{3,2,1,0:T(8,128)S(1)}, f32[1,17,128,128]{3,2,1,0:T(8,128)}, u32[]{:S(2)}) copy-start(f32[1,17,128,128]{3,2,1,0:T(8,128)} %param.4) | copy-start | bytes 3342340
  7.0 0.8 %copy-start.1 = (f32[128,128]{1,0:T(8,128)S(1)}, f32[128,128]{1,0:T(8,128)}, u32[]{:S(2)}) copy-start(f32[128,128]{1,0:T(8,128)} %own_ref.1) | copy-start | bytes 196612
  8.9 5.6 %collective-permute-start.5 = (f32[128,128]{1,0:T(8,128)S(1)}, f32[128,128]{1,0:T(8,128)S(1)}, u32[]{:S(2)}, u32[]{:S(2)}) collective-permute-start(f32[128,128]{1,0:T(8,128)S(1)} %get-tuple-element.47), channel_id=1, source_target_pairs={{0,6},{1,7},{2,4},{3,5},{4,2},{5,3},{6,0},{7,1},{8,14},{9,15},{10,... | collective-permute-start | bytes 196616 | tf_op jit(solution)/shard_map/ppermute | solution.py:23
  11.4 4.3 %collective-permute-start.4 = (f32[128,128]{1,0:T(8,128)S(1)}, f32[128,128]{1,0:T(8,128)S(1)}, u32[]{:S(2)}, u32[]{:S(2)}) collective-permute-start(f32[128,128]{1,0:T(8,128)S(1)} %get-tuple-element.48), channel_id=1, source_target_pairs={{0,4},{1,5},{2,6},{3,7},{4,0},{5,1},{6,2},{7,3},{8,12},{9,13},{10,... | collective-permute-start | bytes 196616 | tf_op jit(solution)/shard_map/ppermute | solution.py:23
  11.9 4.3 %collective-permute-start.3 = (f32[128,128]{1,0:T(8,128)S(1)}, f32[128,128]{1,0:T(8,128)S(1)}, u32[]{:S(2)}, u32[]{:S(2)}) collective-permute-start(f32[128,128]{1,0:T(8,128)S(1)} %get-tuple-element.49), channel_id=1, source_target_pairs={{0,2},{1,3},{2,0},{3,1},{4,6},{5,7},{6,4},{7,5},{8,10},{9,11},{10,... | collective-permute-start | bytes 196616 | tf_op jit(solution)/shard_map/ppermute | solution.py:23
  12.5 5.9 %collective-permute-start.2 = (f32[128,128]{1,0:T(8,128)S(1)}, f32[128,128]{1,0:T(8,128)S(1)}, u32[]{:S(2)}, u32[]{:S(2)}) collective-permute-start(f32[128,128]{1,0:T(8,128)S(1)} %copy-done.1), channel_id=1, source_target_pairs={{0,16},{1,17},{2,18},{3,19},{4,20},{5,21},{6,22},{7,23},{8,24},{9,... | collective-permute-start | bytes 196616 | tf_op jit(solution)/shard_map/ppermute | solution.py:18
  16.2 2.1 %copy-start.2 = (s32[17,2]{0,1:T(2,128)S(1)}, s32[17,2]{0,1:T(2,128)}, u32[]{:S(2)}) copy-start(s32[17,2]{0,1:T(2,128)} %param.5) | copy-start | bytes 412
  16.2 2.1 %collective-permute-start.6 = (f32[4,128,128]{2,1,0:T(8,128)S(1)}, f32[4,128,128]{2,1,0:T(8,128)S(1)}, u32[]{:S(2)}, u32[]{:S(2)}) collective-permute-start(f32[4,128,128]{2,1,0:T(8,128)S(1)} %pad_maximum_fusion), channel_id=1, source_target_pairs={{0,1},{1,0},{2,3},{3,2},{4,5},{5,4},{6,7},{7,6},{8,9},{9,8},{10,11... | collective-permute-start | bytes 786440 | tf_op jit(solution)/shard_map/ppermute | solution.py:28
  20.5 1.6 %collective-permute-start.7 = (f32[520,128]{1,0:T(8,128)S(1)}, f32[520,128]{1,0:T(8,128)S(1)}, u32[]{:S(2)}, u32[]{:S(2)}) collective-permute-start(f32[520,128]{1,0:T(8,128)S(1)} %get-tuple-element.30.sent_ref), channel_id=1, source_target_pairs={{0,1},{1,0},{2,3},{3,2},{4,5},{5,4},{6,7},{7,6},{8,9},{9,8},{10,11... | collective-permute-start | bytes 798728 | tf_op jit(solution)/shard_map/ppermute | solution.py:28
  22.1 4.9 %collective-permute-start.8 = (f32[136,128]{1,0:T(8,128)S(1)}, f32[136,128]{1,0:T(8,128)S(1)}, u32[]{:S(2)}, u32[]{:S(2)}) collective-permute-start(f32[136,128]{1,0:T(8,128)S(1)} %get-tuple-element.36), channel_id=1, source_target_pairs={{0,2},{1,3},{2,0},{3,1},{4,6},{5,7},{6,4},{7,5},{8,10},{9,11},{10,... | collective-permute-start | bytes 208904 | tf_op jit(solution)/shard_map/ppermute | solution.py:23
  23.7 4.3 %collective-permute-start.9 = (f32[136,128]{1,0:T(8,128)S(1)}, f32[136,128]{1,0:T(8,128)S(1)}, u32[]{:S(2)}, u32[]{:S(2)}) collective-permute-start(f32[136,128]{1,0:T(8,128)S(1)} %get-tuple-element.37), channel_id=1, source_target_pairs={{0,4},{1,5},{2,6},{3,7},{4,0},{5,1},{6,2},{7,3},{8,12},{9,13},{10,... | collective-permute-start | bytes 208904 | tf_op jit(solution)/shard_map/ppermute | solution.py:23
  25.2 5.2 %collective-permute-start.10 = (f32[136,128]{1,0:T(8,128)S(1)}, f32[136,128]{1,0:T(8,128)S(1)}, u32[]{:S(2)}, u32[]{:S(2)}) collective-permute-start(f32[136,128]{1,0:T(8,128)S(1)} %get-tuple-element.38), channel_id=1, source_target_pairs={{0,6},{1,7},{2,4},{3,5},{4,2},{5,3},{6,0},{7,1},{8,14},{9,15},{10,... | collective-permute-start | bytes 208904 | tf_op jit(solution)/shard_map/ppermute | solution.py:23
  25.7 8.7 %collective-permute-start.11 = (f32[128,128]{1,0:T(8,128)S(1)}, f32[128,128]{1,0:T(8,128)S(1)}, u32[]{:S(2)}, u32[]{:S(2)}) collective-permute-start(f32[128,128]{1,0:T(8,128)S(1)} %get-tuple-element.41), channel_id=1, source_target_pairs={{0,16},{1,17},{2,18},{3,19},{4,20},{5,21},{6,22},{7,23},{8,24},{9,... | collective-permute-start | bytes 196616 | tf_op jit(solution)/shard_map/ppermute | solution.py:18
  30.5 8.5 %collective-permute-start.12 = (f32[136,128]{1,0:T(8,128)S(1)}, f32[136,128]{1,0:T(8,128)S(1)}, u32[]{:S(2)}, u32[]{:S(2)}) collective-permute-start(f32[136,128]{1,0:T(8,128)S(1)} %get-tuple-element.43), channel_id=1, source_target_pairs={{0,8},{1,9},{2,10},{3,11},{4,12},{5,13},{6,14},{7,15},{8,16},{9,17... | collective-permute-start | bytes 208904 | tf_op jit(solution)/shard_map/ppermute | solution.py:18
  31.0 7.9 %collective-permute-start.13 = (f32[136,128]{1,0:T(8,128)S(1)}, f32[136,128]{1,0:T(8,128)S(1)}, u32[]{:S(2)}, u32[]{:S(2)}) collective-permute-start(f32[136,128]{1,0:T(8,128)S(1)} %get-tuple-element.44), channel_id=1, source_target_pairs={{0,24},{1,25},{2,26},{3,27},{4,28},{5,29},{6,30},{7,31},{8,0},{9,1... | collective-permute-start | bytes 208904 | tf_op jit(solution)/shard_map/ppermute | solution.py:18
  34.4 4.6 %collective-permute-start.14 = (f32[8,128]{1,0:T(8,128)S(1)}, f32[8,128]{1,0:T(8,128)S(1)}, u32[]{:S(2)}, u32[]{:S(2)}) collective-permute-start(f32[8,128]{1,0:T(8,128)S(1)} %get-tuple-element.45), channel_id=1, source_target_pairs={{0,16},{1,17},{2,18},{3,19},{4,20},{5,21},{6,22},{7,23},{8,24},{9,... | collective-permute-start | bytes 12296 | tf_op jit(solution)/shard_map/ppermute | solution.py:18

commit v12 on v11

--- a/solution.py
+++ b/solution.py
@@ -62,13 +62,17 @@
         out_ref[i, :, :cols], out_ref[i, :, cols:] = split_two(block[...])
 
 
-def middle_kernel(sums_ref, *refs):
-    total_ref, sums_out = refs[-2:]
+def add_kernel(*refs):
     total = refs[0][...]
-    for block in refs[1:-2]:
+    for block in refs[1:-1]:
         total = total + block[...]
-    total_ref[...] = total
-    sums_out[...] = sums_ref[...]
+    refs[-1][...] = total
+
+
+def near_kernel(near_ref, middle_ref, sums_ref, next_ref, near_out, sums_out):
+    rows = near_ref.shape[0]
+    near_out[...] = near_ref[...] + middle_ref[...] + next_ref[:rows, :]
+    sums_out[...] = sums_ref[...] + next_ref[rows:, :]
 
 
 def steps_ahead(chip, mask, chips):
@@ -108,9 +112,9 @@
     slots = straight_ref.shape[0]
 
     def product(split_ref, t, place):
-        both = jnp.dot(split_ref[t], parts[place], preferred_element_type=jnp.float32)
-        high, low = both[:rows], both[rows:]
-        return high[:, :cols] + ((high[:, cols:] + low[:, :cols]) + low[:, cols:])
+        high = jnp.dot(split_ref[t, :rows], parts[place], preferred_element_type=jnp.float32)
+        low = jnp.dot(split_ref[t, rows:], parts[place, :, :cols], preferred_element_type=jnp.float32)
+        return high[:, :cols] + (high[:, cols:] + low)
 
     def visit(t, mirrored):
         row_place, col_place = pairs_ref[0, t], pairs_ref[1, t]
@@ -179,15 +183,13 @@
         message[rows:, :] = sums
 
 
-def final_kernel(right_ref, near_ref, middle_ref, sums_ref, *refs):
+def final_kernel(right_ref, near_ref, sums_ref, last_ref, *refs):
     solution_ref, residual_ref = refs[-2:]
     rows = near_ref.shape[0]
-    image, sums = near_ref[...] + middle_ref[...], sums_ref[...]
-    for got in refs[:2]:
-        image = image + got[:rows, :]
-        sums = sums + got[rows:, :]
-    for got in refs[2:-2]:
-        sums = sums + got[...]
+    image = near_ref[...] + last_ref[:rows, :]
+    sums = sums_ref[...] + last_ref[rows:, :]
+    for more in refs[:-2]:
+        sums = sums + more[...]
     step_len = sums[0:1, :] / sums[1:2, :]
     right = right_ref[...]
     solution_ref[...] = step_len * right
@@ -232,7 +234,9 @@
         split_blocks_kernel, (), [far[k] for k in middle], [((len(middle), rows, 2 * cols), half)], cost=BESIDE
     )
     even = [chip_partner(jnp.where((chip ^ m) < chip, own, far[1]), m) for m in range(1, chips)]
-    odd = core_partner(jnp.stack([jnp.where(core == 0, far[1], own)] + even))
+    sent = jnp.stack([jnp.where(core == 0, far[1], own)] + even)
+    sent, middle_parts = lax.optimization_barrier((sent, middle_parts))
+    odd = core_partner(sent)
 
     block, marked, extra = ((rows, cols), single), ((rows + EXTRA, cols), single), ((EXTRA, cols), single)
     sent, kept, *far_out = call(
@@ -253,13 +257,17 @@
     middle_got = [shifted(far_out[k - 2], k * window) for k in middle]
     got = [chip_partner(value, m) for m, value in enumerate(messages, 1)]
     ahead, last, near, sums = call(
-        functools.partial(plane_kernel, chips), (where,), (near, ahead, sums, far_out[-1], *got), [marked, marked, block, extra]
-    )
-    middle_sum, passed = call(middle_kernel, (), (sums, *middle_got), [block, extra], cost=BESIDE)
-    got = [shifted(ahead, window), *[shifted(passed, k * window) for k in middle], shifted(last, (planes - 1) * window)]
-    return call(
-        final_kernel, (), (own, near, middle_sum, sums, got[0], got[-1], *got[1:-1]), [block, block]
-    )
+        functools.partial(plane_kernel, chips),
+        (where,),
+        (near, ahead, sums, far_out[-1], *got),
+        [marked, marked, block, extra],
+    )
+    got = shifted(ahead, window)
+    more = [shifted(sums, k * window) for k in middle]
+    last = shifted(last, (planes - 1) * window)
+    (middle_sum,) = call(add_kernel, (), middle_got, [block], cost=BESIDE)
+    near, sums = call(near_kernel, (), (near, middle_sum, sums, got), [block, extra], cost=BESIDE)
+    return call(final_kernel, (), (own, near, sums, last, *more), [block, block])
 
 
 def solution(mesh):

time: 39.8 us -> 38.5 us (0.967)
  waiting for transfers between devices: 13.9 us -> 11.1 us
  starting transfers between devices: 19.6 us -> 21.4 us
    ppermute x7, waiting for transfers between devices: 7.15 us -> 2.78 us  [shifted(): return lax.ppermute(value, 'blk', pairs)]
    ppermute x7, starting transfers between devices: 12.3 us -> 14 us  [shifted(): return lax.ppermute(value, 'blk', pairs)]
    ppermute x2, waiting for transfers between devices: 1.53 us -> 2.93 us  [core_partner(): lax.ppermute(value, 'blk', [(source, source ^ 1) for source in range(coun...]
    pallas_call x7 -> x8, Pallas kernels: 3.27 us -> 2.99 us  [call(): pl.pallas_call(kernel, in_specs=[pl.BlockSpec(memory_space=pltpu.SMEM)] *...]
  transfers between devices with their start and end apart: 15 -> 15, of which waited for: 10 -> 8; matrix products, arithmetic and copies ran while one was open for 0% -> 0% of each run, Pallas kernels for 1% -> 1%
where the time goes in v12:
time: 38.5 us; the launch traced here: 38.3 us
  starting transfers between devices  21.4 us (56%)
  waiting for transfers between devices  11.1 us (29%)
  Pallas kernels  2.99 us (8%)
  local copies, waits for them, and re-layouts  2.09 us (5%)
  between operations  0.7 us (2%)
    ppermute x7, starting transfers between devices, shifted(): return lax.ppermute(value, 'blk', pairs)  14 us
    ppermute x6, starting transfers between devices, chip_partner(): lax.ppermute(value, 'blk', [(source, source ^ 2 * mask) for source in ran...  7.11 us
    ppermute x6, waiting for transfers between devices, chip_partner(): lax.ppermute(value, 'blk', [(source, source ^ 2 * mask) for source in ran...  5.35 us
    pallas_call x8, Pallas kernels, call(): pl.pallas_call(kernel, in_specs=[pl.BlockSpec(memory_space=pltpu.SMEM)] *...  2.99 us
    ppermute x2, waiting for transfers between devices, core_partner(): lax.ppermute(value, 'blk', [(source, source ^ 1) for source in range(coun...  2.93 us
    ppermute x7, waiting for transfers between devices, shifted(): return lax.ppermute(value, 'blk', pairs)  2.78 us
    unnamed x6, local copies, waits for them, and re-layouts  2.09 us
  transfers between devices with their start and end apart: 15, of which 8 were waited for; matrix products, arithmetic and copies ran while one was open for 0% of the time, Pallas kernels for 1%

profile of v12, /device:TPU:0, one launch (start us, length us, event | category | flops | bytes accessed | tf_op | source)
XLA Modules:
  0.0 38.3 jit_solution(13297308058581825808)
XLA Ops:
  0.6 3.1 %collective-permute-start = (f32[128,128]{1,0:T(8,128)}, f32[128,128]{1,0:T(8,128)S(1)}, u32[]{:S(2)}, u32[]{:S(2)}) collective-permute-start(f32[128,128]{1,0:T(8,128)} %own_ref.1), channel_id=1, source_target_pairs={{0,8},{1,9},{2,10},{3,11},{4,12},{5,13},{6,14},{7,15},{8,16},{9,17... | collective-permute-start | bytes 196616 | tf_op jit(solution)/shard_map/ppermute | solution.py:18
  3.7 2.1 %collective-permute-start.1 = (f32[128,128]{1,0:T(8,128)}, f32[128,128]{1,0:T(8,128)S(1)}, u32[]{:S(2)}, u32[]{:S(2)}) collective-permute-start(f32[128,128]{1,0:T(8,128)} %own_ref.1), channel_id=1, source_target_pairs={{0,24},{1,25},{2,26},{3,27},{4,28},{5,29},{6,30},{7,31},{8,0},{9,1... | collective-permute-start | bytes 196616 | tf_op jit(solution)/shard_map/ppermute | solution.py:18
  5.8 0.9 %collective-permute-start.2 = (f32[128,128]{1,0:T(8,128)}, f32[128,128]{1,0:T(8,128)S(1)}, u32[]{:S(2)}, u32[]{:S(2)}) collective-permute-start(f32[128,128]{1,0:T(8,128)} %own_ref.1), channel_id=1, source_target_pairs={{0,16},{1,17},{2,18},{3,19},{4,20},{5,21},{6,22},{7,23},{8,24},{9,... | collective-permute-start | bytes 196616 | tf_op jit(solution)/shard_map/ppermute | solution.py:18
  6.7 0.0 copy-start
  6.7 1.2 %copy-done = f32[1,17,128,128]{3,2,1,0:T(8,128)S(1)} copy-done((f32[1,17,128,128]{3,2,1,0:T(8,128)S(1)}, f32[1,17,128,128]{3,2,1,0:T(8,128)}, u32[]{:S(2)}) %copy-start) | copy-done | bytes 1114136
  8.0 0.0 copy-start.1
  8.0 0.8 %copy-done.1 = f32[128,128]{1,0:T(8,128)S(1)} copy-done((f32[128,128]{1,0:T(8,128)S(1)}, f32[128,128]{1,0:T(8,128)}, u32[]{:S(2)}) %copy-start.1) | copy-done | bytes 65560
  8.8 0.4 shard_map.50
  9.2 0.0 collective-permute-done.refs_2_
  9.2 0.0 collective-permute-done.1.refs_0_
  9.3 2.5 %collective-permute-start.5 = (f32[128,128]{1,0:T(8,128)S(1)}, f32[128,128]{1,0:T(8,128)S(1)}, u32[]{:S(2)}, u32[]{:S(2)}) collective-permute-start(f32[128,128]{1,0:T(8,128)S(1)} %get-tuple-element.51), channel_id=1, source_target_pairs={{0,6},{1,7},{2,4},{3,5},{4,2},{5,3},{6,0},{7,1},{8,14},{9,15},{10,... | collective-permute-start | bytes 196616 | tf_op jit(solution)/shard_map/ppermute | solution.py:23
  11.8 0.5 %collective-permute-start.4 = (f32[128,128]{1,0:T(8,128)S(1)}, f32[128,128]{1,0:T(8,128)S(1)}, u32[]{:S(2)}, u32[]{:S(2)}) collective-permute-start(f32[128,128]{1,0:T(8,128)S(1)} %get-tuple-element.52), channel_id=1, source_target_pairs={{0,4},{1,5},{2,6},{3,7},{4,0},{5,1},{6,2},{7,3},{8,12},{9,13},{10,... | collective-permute-start | bytes 196616 | tf_op jit(solution)/shard_map/ppermute | solution.py:23
  12.3 0.0 copy-start.2
  12.3 0.5 %collective-permute-start.3 = (f32[128,128]{1,0:T(8,128)S(1)}, f32[128,128]{1,0:T(8,128)S(1)}, u32[]{:S(2)}, u32[]{:S(2)}) collective-permute-start(f32[128,128]{1,0:T(8,128)S(1)} %get-tuple-element.53), channel_id=1, source_target_pairs={{0,2},{1,3},{2,0},{3,1},{4,6},{5,7},{6,4},{7,5},{8,10},{9,11},{10,... | collective-permute-start | bytes 196616 | tf_op jit(solution)/shard_map/ppermute | solution.py:23
  12.8 0.0 collective-permute-done.2.refs_0_.refs_1_
  12.8 1.9 %collective-permute-done.5.refs_5_ = f32[128,128]{1,0:T(8,128)S(1)} collective-permute-done((f32[128,128]{1,0:T(8,128)S(1)}, f32[128,128]{1,0:T(8,128)S(1)}, u32[]{:S(2)}, u32[]{:S(2)}) %collective-permute-start.5) | collective-permute-done | bytes 65568 | tf_op jit(solution)/shard_map/ppermute | solution.py:23
  14.8 1.3 %collective-permute-done.4.refs_4_ = f32[128,128]{1,0:T(8,128)S(1)} collective-permute-done((f32[128,128]{1,0:T(8,128)S(1)}, f32[128,128]{1,0:T(8,128)S(1)}, u32[]{:S(2)}, u32[]{:S(2)}) %collective-permute-start.4) | collective-permute-done | bytes 65568 | tf_op jit(solution)/shard_map/ppermute | solution.py:23
  16.0 0.5 %collective-permute-done.3.refs_3_ = f32[128,128]{1,0:T(8,128)S(1)} collective-permute-done((f32[128,128]{1,0:T(8,128)S(1)}, f32[128,128]{1,0:T(8,128)S(1)}, u32[]{:S(2)}, u32[]{:S(2)}) %collective-permute-start.3) | collective-permute-done | bytes 65568 | tf_op jit(solution)/shard_map/ppermute | solution.py:23
  16.6 0.1 collective-permute-start.6
  16.7 1.5 %collective-permute-done.6.refs_6_ = f32[4,128,128]{2,1,0:T(8,128)S(1)} collective-permute-done((f32[4,128,128]{2,1,0:T(8,128)S(1)}, f32[4,128,128]{2,1,0:T(8,128)S(1)}, u32[]{:S(2)}, u32[]{:S(2)}) %collective-permute-start.6) | collective-permute-done | bytes 262176 | tf_op jit(solution)/shard_map/ppermute | solution.py:28
  18.2 0.0 copy-done.2
  18.2 1.8 %shard_map.52 = (f32[520,128]{1,0:T(8,128)S(1)}, f32[5,128,128]{2,1,0:T(8,128)S(1)}, f32[128,128]{1,0:T(8,128)S(1)}, f32[128,128]{1,0:T(8,128)S(1)}) custom-call(s32[2,17]{1,0:T(2,128)S(1)} %bitcast.12, s32[1]{0:T(128)} %bitcast.1.place_ref, f32[128,128]{1,0:T(8,128)S(1)} %get-tuple-element.27.own_ref.right_ref, ...), custom_call_target="tpu_custom_call" | custom-call | tf_op jit(solution)/shard_map/pallas_call | solution.py:201
  20.0 0.2 collective-permute-start.7
  20.2 1.4 %collective-permute-done.7.got_ref = f32[520,128]{1,0:T(8,128)S(1)} collective-permute-done((f32[520,128]{1,0:T(8,128)S(1)}, f32[520,128]{1,0:T(8,128)S(1)}, u32[]{:S(2)}, u32[]{:S(2)}) %collective-permute-start.7) | collective-permute-done | bytes 266272 | tf_op jit(solution)/shard_map/ppermute | solution.py:28
  21.7 0.6 %collective-permute-start.8 = (f32[136,128]{1,0:T(8,128)S(1)}, f32[136,128]{1,0:T(8,128)S(1)}, u32[]{:S(2)}, u32[]{:S(2)}) collective-permute-start(f32[136,128]{1,0:T(8,128)S(1)} %get-tuple-element.40), channel_id=1, source_target_pairs={{0,2},{1,3},{2,0},{3,1},{4,6},{5,7},{6,4},{7,5},{8,10},{9,11},{10,... | collective-permute-start | bytes 208904 | tf_op jit(solution)/shard_map/ppermute | solution.py:23
  22.3 1.5 %collective-permute-start.9 = (f32[136,128]{1,0:T(8,128)S(1)}, f32[136,128]{1,0:T(8,128)S(1)}, u32[]{:S(2)}, u32[]{:S(2)}) collective-permute-start(f32[136,128]{1,0:T(8,128)S(1)} %get-tuple-element.41), channel_id=1, source_target_pairs={{0,4},{1,5},{2,6},{3,7},{4,0},{5,1},{6,2},{7,3},{8,12},{9,13},{10,... | collective-permute-start | bytes 208904 | tf_op jit(solution)/shard_map/ppermute | solution.py:23
  23.8 1.4 %collective-permute-start.10 = (f32[136,128]{1,0:T(8,128)S(1)}, f32[136,128]{1,0:T(8,128)S(1)}, u32[]{:S(2)}, u32[]{:S(2)}) collective-permute-start(f32[136,128]{1,0:T(8,128)S(1)} %get-tuple-element.42), channel_id=1, source_target_pairs={{0,6},{1,7},{2,4},{3,5},{4,2},{5,3},{6,0},{7,1},{8,14},{9,15},{10,... | collective-permute-start | bytes 208904 | tf_op jit(solution)/shard_map/ppermute | solution.py:23
  25.2 2.1 %collective-permute-start.11 = (f32[128,128]{1,0:T(8,128)S(1)}, f32[128,128]{1,0:T(8,128)S(1)}, u32[]{:S(2)}, u32[]{:S(2)}) collective-permute-start(f32[128,128]{1,0:T(8,128)S(1)} %get-tuple-element.44), channel_id=1, source_target_pairs={{0,16},{1,17},{2,18},{3,19},{4,20},{5,21},{6,22},{7,23},{8,24},{9,... | collective-permute-start | bytes 196616 | tf_op jit(solution)/shard_map/ppermute | solution.py:18
  27.3 0.0 collective-permute-done.8.refs_0_
  27.4 0.0 collective-permute-done.9.refs_1_
  27.4 1.6 %collective-permute-done.10.refs_2_ = f32[136,128]{1,0:T(8,128)S(1)} collective-permute-done((f32[136,128]{1,0:T(8,128)S(1)}, f32[136,128]{1,0:T(8,128)S(1)}, u32[]{:S(2)}, u32[]{:S(2)}) %collective-permute-start.10) | collective-permute-done | bytes 69664 | tf_op jit(solution)/shard_map/ppermute | solution.py:23
  29.0 1.9 %collective-permute-start.12 = (f32[136,128]{1,0:T(8,128)S(1)}, f32[136,128]{1,0:T(8,128)S(1)}, u32[]{:S(2)}, u32[]{:S(2)}) collective-permute-start(f32[136,128]{1,0:T(8,128)S(1)} %get-tuple-element.46), channel_id=1, source_target_pairs={{0,8},{1,9},{2,10},{3,11},{4,12},{5,13},{6,14},{7,15},{8,16},{9,17... | collective-permute-start | bytes 208904 | tf_op jit(solution)/shard_map/ppermute | solution.py:18
  30.9 0.0 collective-permute-done.11.refs_0_
  31.0 2.0 %collective-permute-start.14 = (f32[8,128]{1,0:T(8,128)S(1)}, f32[8,128]{1,0:T(8,128)S(1)}, u32[]{:S(2)}, u32[]{:S(2)}) collective-permute-start(f32[8,128]{1,0:T(8,128)S(1)} %get-tuple-element.45.sums_ref), channel_id=1, source_target_pairs={{0,16},{1,17},{2,18},{3,19},{4,20},{5,21},{6,22},{7,23},{8,24},{9,... | collective-permute-start | bytes 12296 | tf_op jit(solution)/shard_map/ppermute | solution.py:18
  32.9 1.9 %collective-permute-start.13 = (f32[136,128]{1,0:T(8,128)S(1)}, f32[136,128]{1,0:T(8,128)S(1)}, u32[]{:S(2)}, u32[]{:S(2)}) collective-permute-start(f32[136,128]{1,0:T(8,128)S(1)} %get-tuple-element.49), channel_id=1, source_target_pairs={{0,24},{1,25},{2,26},{3,27},{4,28},{5,29},{6,30},{7,31},{8,0},{9,1... | collective-permute-start | bytes 208904 | tf_op jit(solution)/shard_map/ppermute | solution.py:18
  34.9 0.8 %collective-permute-done.12.next_ref = f32[136,128]{1,0:T(8,128)S(1)} collective-permute-done((f32[136,128]{1,0:T(8,128)S(1)}, f32[136,128]{1,0:T(8,128)S(1)}, u32[]{:S(2)}, u32[]{:S(2)}) %collective-permute-start.12) | collective-permute-done | bytes 69664 | tf_op jit(solution)/shard_map/ppermute | solution.py:18
  35.6 0.0 collective-permute-done.14.refs_0_
  35.7 1.9 %collective-permute-done.13.last_ref = f32[136,128]{1,0:T(8,128)S(1)} collective-permute-done((f32[136,128]{1,0:T(8,128)S(1)}, f32[136,128]{1,0:T(8,128)S(1)}, u32[]{:S(2)}, u32[]{:S(2)}) %collective-permute-start.13) | collective-permute-done | bytes 69664 | tf_op jit(solution)/shard_map/ppermute | solution.py:18
  37.6 0.7 %shard_map.57 = (f32[128,128]{1,0:T(8,128)}, f32[128,128]{1,0:T(8,128)}) custom-call(f32[128,128]{1,0:T(8,128)S(1)} %get-tuple-element.27.own_ref.right_ref, f32[128,128]{1,0:T(8,128)S(1)} %get-tuple-element.47.near_ref, f32[8,128]{1,0:T(8,128)S(1)} %get-tuple-element.48.sums_ref, f32[136,128]{1,0:T(8,128)S(1)} %collective-permute-done.13.last_ref, ...), custom_call_target="tpu_custom_call" | custom-call | tf_op jit(solution)/shard_map/pallas_call | solution.py:201
  (7 shorter events, 0.2 us)
Async XLA Ops:
  0.6 8.6 %collective-permute-start = (f32[128,128]{1,0:T(8,128)}, f32[128,128]{1,0:T(8,128)S(1)}, u32[]{:S(2)}, u32[]{:S(2)}) collective-permute-start(f32[128,128]{1,0:T(8,128)} %own_ref.1), channel_id=1, source_target_pairs={{0,8},{1,9},{2,10},{3,11},{4,12},{5,13},{6,14},{7,15},{8,16},{9,17... | collective-permute-start | bytes 196616 | tf_op jit(solution)/shard_map/ppermute | solution.py:18
  3.7 5.5 %collective-permute-start.1 = (f32[128,128]{1,0:T(8,128)}, f32[128,128]{1,0:T(8,128)S(1)}, u32[]{:S(2)}, u32[]{:S(2)}) collective-permute-start(f32[128,128]{1,0:T(8,128)} %own_ref.1), channel_id=1, source_target_pairs={{0,24},{1,25},{2,26},{3,27},{4,28},{5,29},{6,30},{7,31},{8,0},{9,1... | collective-permute-start | bytes 196616 | tf_op jit(solution)/shard_map/ppermute | solution.py:18
  5.8 7.0 %collective-permute-start.2 = (f32[128,128]{1,0:T(8,128)}, f32[128,128]{1,0:T(8,128)S(1)}, u32[]{:S(2)}, u32[]{:S(2)}) collective-permute-start(f32[128,128]{1,0:T(8,128)} %own_ref.1), channel_id=1, source_target_pairs={{0,16},{1,17},{2,18},{3,19},{4,20},{5,21},{6,22},{7,23},{8,24},{9,... | collective-permute-start | bytes 196616 | tf_op jit(solution)/shard_map/ppermute | solution.py:18
  6.7 1.2 %copy-start = (f32[1,17,128,128]{3,2,1,0:T(8,128)S(1)}, f32[1,17,128,128]{3,2,1,0:T(8,128)}, u32[]{:S(2)}) copy-start(f32[1,17,128,128]{3,2,1,0:T(8,128)} %param.4) | copy-start | bytes 3342340
  8.0 0.8 %copy-start.1 = (f32[128,128]{1,0:T(8,128)S(1)}, f32[128,128]{1,0:T(8,128)}, u32[]{:S(2)}) copy-start(f32[128,128]{1,0:T(8,128)} %own_ref.1) | copy-start | bytes 196612
  9.3 5.5 %collective-permute-start.5 = (f32[128,128]{1,0:T(8,128)S(1)}, f32[128,128]{1,0:T(8,128)S(1)}, u32[]{:S(2)}, u32[]{:S(2)}) collective-permute-start(f32[128,128]{1,0:T(8,128)S(1)} %get-tuple-element.51), channel_id=1, source_target_pairs={{0,6},{1,7},{2,4},{3,5},{4,2},{5,3},{6,0},{7,1},{8,14},{9,15},{10,... | collective-permute-start | bytes 196616 | tf_op jit(solution)/shard_map/ppermute | solution.py:23
  11.8 4.3 %collective-permute-start.4 = (f32[128,128]{1,0:T(8,128)S(1)}, f32[128,128]{1,0:T(8,128)S(1)}, u32[]{:S(2)}, u32[]{:S(2)}) collective-permute-start(f32[128,128]{1,0:T(8,128)S(1)} %get-tuple-element.52), channel_id=1, source_target_pairs={{0,4},{1,5},{2,6},{3,7},{4,0},{5,1},{6,2},{7,3},{8,12},{9,13},{10,... | collective-permute-start | bytes 196616 | tf_op jit(solution)/shard_map/ppermute | solution.py:23
  12.3 5.9 %copy-start.2 = (s32[17,2]{0,1:T(2,128)S(1)}, s32[17,2]{0,1:T(2,128)}, u32[]{:S(2)}) copy-start(s32[17,2]{0,1:T(2,128)} %param.5) | copy-start | bytes 412
  12.3 4.3 %collective-permute-start.3 = (f32[128,128]{1,0:T(8,128)S(1)}, f32[128,128]{1,0:T(8,128)S(1)}, u32[]{:S(2)}, u32[]{:S(2)}) collective-permute-start(f32[128,128]{1,0:T(8,128)S(1)} %get-tuple-element.53), channel_id=1, source_target_pairs={{0,2},{1,3},{2,0},{3,1},{4,6},{5,7},{6,4},{7,5},{8,10},{9,11},{10,... | collective-permute-start | bytes 196616 | tf_op jit(solution)/shard_map/ppermute | solution.py:23
  16.6 1.6 %collective-permute-start.6 = (f32[4,128,128]{2,1,0:T(8,128)S(1)}, f32[4,128,128]{2,1,0:T(8,128)S(1)}, u32[]{:S(2)}, u32[]{:S(2)}) collective-permute-start(f32[4,128,128]{2,1,0:T(8,128)S(1)} %pad_maximum_fusion), channel_id=1, source_target_pairs={{0,1},{1,0},{2,3},{3,2},{4,5},{5,4},{6,7},{7,6},{8,9},{9,8},{10,11... | collective-permute-start | bytes 786440 | tf_op jit(solution)/shard_map/ppermute | solution.py:28
  20.0 1.6 %collective-permute-start.7 = (f32[520,128]{1,0:T(8,128)S(1)}, f32[520,128]{1,0:T(8,128)S(1)}, u32[]{:S(2)}, u32[]{:S(2)}) collective-permute-start(f32[520,128]{1,0:T(8,128)S(1)} %get-tuple-element.34.sent_ref), channel_id=1, source_target_pairs={{0,1},{1,0},{2,3},{3,2},{4,5},{5,4},{6,7},{7,6},{8,9},{9,8},{10,11... | collective-permute-start | bytes 798728 | tf_op jit(solution)/shard_map/ppermute | solution.py:28
  21.7 5.7 %collective-permute-start.8 = (f32[136,128]{1,0:T(8,128)S(1)}, f32[136,128]{1,0:T(8,128)S(1)}, u32[]{:S(2)}, u32[]{:S(2)}) collective-permute-start(f32[136,128]{1,0:T(8,128)S(1)} %get-tuple-element.40), channel_id=1, source_target_pairs={{0,2},{1,3},{2,0},{3,1},{4,6},{5,7},{6,4},{7,5},{8,10},{9,11},{10,... | collective-permute-start | bytes 208904 | tf_op jit(solution)/shard_map/ppermute | solution.py:23
  22.3 5.1 %collective-permute-start.9 = (f32[136,128]{1,0:T(8,128)S(1)}, f32[136,128]{1,0:T(8,128)S(1)}, u32[]{:S(2)}, u32[]{:S(2)}) collective-permute-start(f32[136,128]{1,0:T(8,128)S(1)} %get-tuple-element.41), channel_id=1, source_target_pairs={{0,4},{1,5},{2,6},{3,7},{4,0},{5,1},{6,2},{7,3},{8,12},{9,13},{10,... | collective-permute-start | bytes 208904 | tf_op jit(solution)/shard_map/ppermute | solution.py:23
  23.8 5.2 %collective-permute-start.10 = (f32[136,128]{1,0:T(8,128)S(1)}, f32[136,128]{1,0:T(8,128)S(1)}, u32[]{:S(2)}, u32[]{:S(2)}) collective-permute-start(f32[136,128]{1,0:T(8,128)S(1)} %get-tuple-element.42), channel_id=1, source_target_pairs={{0,6},{1,7},{2,4},{3,5},{4,2},{5,3},{6,0},{7,1},{8,14},{9,15},{10,... | collective-permute-start | bytes 208904 | tf_op jit(solution)/shard_map/ppermute | solution.py:23
  25.2 5.7 %collective-permute-start.11 = (f32[128,128]{1,0:T(8,128)S(1)}, f32[128,128]{1,0:T(8,128)S(1)}, u32[]{:S(2)}, u32[]{:S(2)}) collective-permute-start(f32[128,128]{1,0:T(8,128)S(1)} %get-tuple-element.44), channel_id=1, source_target_pairs={{0,16},{1,17},{2,18},{3,19},{4,20},{5,21},{6,22},{7,23},{8,24},{9,... | collective-permute-start | bytes 196616 | tf_op jit(solution)/shard_map/ppermute | solution.py:18
  29.0 6.6 %collective-permute-start.12 = (f32[136,128]{1,0:T(8,128)S(1)}, f32[136,128]{1,0:T(8,128)S(1)}, u32[]{:S(2)}, u32[]{:S(2)}) collective-permute-start(f32[136,128]{1,0:T(8,128)S(1)} %get-tuple-element.46), channel_id=1, source_target_pairs={{0,8},{1,9},{2,10},{3,11},{4,12},{5,13},{6,14},{7,15},{8,16},{9,17... | collective-permute-start | bytes 208904 | tf_op jit(solution)/shard_map/ppermute | solution.py:18
  31.0 4.7 %collective-permute-start.14 = (f32[8,128]{1,0:T(8,128)S(1)}, f32[8,128]{1,0:T(8,128)S(1)}, u32[]{:S(2)}, u32[]{:S(2)}) collective-permute-start(f32[8,128]{1,0:T(8,128)S(1)} %get-tuple-element.45.sums_ref), channel_id=1, source_target_pairs={{0,16},{1,17},{2,18},{3,19},{4,20},{5,21},{6,22},{7,23},{8,24},{9,... | collective-permute-start | bytes 12296 | tf_op jit(solution)/shard_map/ppermute | solution.py:18
  32.9 4.7 %collective-permute-start.13 = (f32[136,128]{1,0:T(8,128)S(1)}, f32[136,128]{1,0:T(8,128)S(1)}, u32[]{:S(2)}, u32[]{:S(2)}) collective-permute-start(f32[136,128]{1,0:T(8,128)S(1)} %get-tuple-element.49), channel_id=1, source_target_pairs={{0,24},{1,25},{2,26},{3,27},{4,28},{5,29},{6,30},{7,31},{8,0},{9,1... | collective-permute-start | bytes 208904 | tf_op jit(solution)/shard_map/ppermute | solution.py:18

commit v13 on v12

--- a/solution.py
+++ b/solution.py
@@ -69,9 +69,9 @@
     refs[-1][...] = total
 
 
-def near_kernel(near_ref, middle_ref, sums_ref, next_ref, near_out, sums_out):
+def near_kernel(near_ref, sums_ref, next_ref, near_out, sums_out):
     rows = near_ref.shape[0]
-    near_out[...] = near_ref[...] + middle_ref[...] + next_ref[:rows, :]
+    near_out[...] = near_ref[...] + next_ref[:rows, :]
     sums_out[...] = sums_ref[...] + next_ref[rows:, :]
 
 
@@ -183,10 +183,10 @@
         message[rows:, :] = sums
 
 
-def final_kernel(right_ref, near_ref, sums_ref, last_ref, *refs):
+def final_kernel(right_ref, near_ref, middle_ref, sums_ref, last_ref, *refs):
     solution_ref, residual_ref = refs[-2:]
     rows = near_ref.shape[0]
-    image = near_ref[...] + last_ref[:rows, :]
+    image = near_ref[...] + middle_ref[...] + last_ref[:rows, :]
     sums = sums_ref[...] + last_ref[rows:, :]
     for more in refs[:-2]:
         sums = sums + more[...]
@@ -266,8 +266,8 @@
     more = [shifted(sums, k * window) for k in middle]
     last = shifted(last, (planes - 1) * window)
     (middle_sum,) = call(add_kernel, (), middle_got, [block], cost=BESIDE)
-    near, sums = call(near_kernel, (), (near, middle_sum, sums, got), [block, extra], cost=BESIDE)
-    return call(final_kernel, (), (own, near, sums, last, *more), [block, block])
+    near, sums = call(near_kernel, (), (near, sums, got), [block, extra])
+    return call(final_kernel, (), (own, near, middle_sum, sums, last, *more), [block, block])
 
 
 def solution(mesh):

time: 38.5 us -> 38.8 us (level)
  no operation moved by 1% of the time
where the time goes in v13:
time: 38.8 us; the launch traced here: 38.6 us
  starting transfers between devices  21.6 us (56%)
  waiting for transfers between devices  11.1 us (29%)
  Pallas kernels  2.99 us (8%)
  local copies, waits for them, and re-layouts  2.09 us (5%)
  between operations  0.71 us (2%)
    ppermute x7, starting transfers between devices, shifted(): return lax.ppermute(value, 'blk', pairs)  14.3 us
    ppermute x6, starting transfers between devices, chip_partner(): lax.ppermute(value, 'blk', [(source, source ^ 2 * mask) for source in ran...  7.11 us
    ppermute x6, waiting for transfers between devices, chip_partner(): lax.ppermute(value, 'blk', [(source, source ^ 2 * mask) for source in ran...  5.35 us
    pallas_call x8, Pallas kernels, call(): pl.pallas_call(kernel, in_specs=[pl.BlockSpec(memory_space=pltpu.SMEM)] *...  2.99 us
    ppermute x2, waiting for transfers between devices, core_partner(): lax.ppermute(value, 'blk', [(source, source ^ 1) for source in range(coun...  2.93 us
    ppermute x7, waiting for transfers between devices, shifted(): return lax.ppermute(value, 'blk', pairs)  2.84 us
    unnamed x6, local copies, waits for them, and re-layouts  2.09 us
  transfers between devices with their start and end apart: 15, of which 8 were waited for; matrix products, arithmetic and copies ran while one was open for 0% of the time, Pallas kernels for 1%

profile of v13, /device:TPU:0, one launch (start us, length us, event | category | flops | bytes accessed | tf_op | source)
XLA Modules:
  0.0 38.6 jit_solution(16904653807870895393)
XLA Ops:
  0.6 3.1 %collective-permute-start = (f32[128,128]{1,0:T(8,128)}, f32[128,128]{1,0:T(8,128)S(1)}, u32[]{:S(2)}, u32[]{:S(2)}) collective-permute-start(f32[128,128]{1,0:T(8,128)} %own_ref.1), channel_id=1, source_target_pairs={{0,8},{1,9},{2,10},{3,11},{4,12},{5,13},{6,14},{7,15},{8,16},{9,17... | collective-permute-start | bytes 196616 | tf_op jit(solution)/shard_map/ppermute | solution.py:18
  3.7 2.1 %collective-permute-start.1 = (f32[128,128]{1,0:T(8,128)}, f32[128,128]{1,0:T(8,128)S(1)}, u32[]{:S(2)}, u32[]{:S(2)}) collective-permute-start(f32[128,128]{1,0:T(8,128)} %own_ref.1), channel_id=1, source_target_pairs={{0,24},{1,25},{2,26},{3,27},{4,28},{5,29},{6,30},{7,31},{8,0},{9,1... | collective-permute-start | bytes 196616 | tf_op jit(solution)/shard_map/ppermute | solution.py:18
  5.8 0.9 %collective-permute-start.2 = (f32[128,128]{1,0:T(8,128)}, f32[128,128]{1,0:T(8,128)S(1)}, u32[]{:S(2)}, u32[]{:S(2)}) collective-permute-start(f32[128,128]{1,0:T(8,128)} %own_ref.1), channel_id=1, source_target_pairs={{0,16},{1,17},{2,18},{3,19},{4,20},{5,21},{6,22},{7,23},{8,24},{9,... | collective-permute-start | bytes 196616 | tf_op jit(solution)/shard_map/ppermute | solution.py:18
  6.7 0.0 copy-start
  6.7 1.2 %copy-done = f32[1,17,128,128]{3,2,1,0:T(8,128)S(1)} copy-done((f32[1,17,128,128]{3,2,1,0:T(8,128)S(1)}, f32[1,17,128,128]{3,2,1,0:T(8,128)}, u32[]{:S(2)}) %copy-start) | copy-done | bytes 1114136
  8.0 0.0 copy-start.1
  8.0 0.8 %copy-done.1 = f32[128,128]{1,0:T(8,128)S(1)} copy-done((f32[128,128]{1,0:T(8,128)S(1)}, f32[128,128]{1,0:T(8,128)}, u32[]{:S(2)}) %copy-start.1) | copy-done | bytes 65560
  8.8 0.4 shard_map.50
  9.2 0.0 collective-permute-done.refs_2_
  9.2 0.0 collective-permute-done.1.refs_0_
  9.3 2.5 %collective-permute-start.5 = (f32[128,128]{1,0:T(8,128)S(1)}, f32[128,128]{1,0:T(8,128)S(1)}, u32[]{:S(2)}, u32[]{:S(2)}) collective-permute-start(f32[128,128]{1,0:T(8,128)S(1)} %get-tuple-element.51), channel_id=1, source_target_pairs={{0,6},{1,7},{2,4},{3,5},{4,2},{5,3},{6,0},{7,1},{8,14},{9,15},{10,... | collective-permute-start | bytes 196616 | tf_op jit(solution)/shard_map/ppermute | solution.py:23
  11.8 0.5 %collective-permute-start.4 = (f32[128,128]{1,0:T(8,128)S(1)}, f32[128,128]{1,0:T(8,128)S(1)}, u32[]{:S(2)}, u32[]{:S(2)}) collective-permute-start(f32[128,128]{1,0:T(8,128)S(1)} %get-tuple-element.52), channel_id=1, source_target_pairs={{0,4},{1,5},{2,6},{3,7},{4,0},{5,1},{6,2},{7,3},{8,12},{9,13},{10,... | collective-permute-start | bytes 196616 | tf_op jit(solution)/shard_map/ppermute | solution.py:23
  12.3 0.0 copy-start.2
  12.3 0.5 %collective-permute-start.3 = (f32[128,128]{1,0:T(8,128)S(1)}, f32[128,128]{1,0:T(8,128)S(1)}, u32[]{:S(2)}, u32[]{:S(2)}) collective-permute-start(f32[128,128]{1,0:T(8,128)S(1)} %get-tuple-element.53), channel_id=1, source_target_pairs={{0,2},{1,3},{2,0},{3,1},{4,6},{5,7},{6,4},{7,5},{8,10},{9,11},{10,... | collective-permute-start | bytes 196616 | tf_op jit(solution)/shard_map/ppermute | solution.py:23
  12.8 0.0 collective-permute-done.2.refs_0_.refs_1_
  12.8 1.9 %collective-permute-done.5.refs_5_ = f32[128,128]{1,0:T(8,128)S(1)} collective-permute-done((f32[128,128]{1,0:T(8,128)S(1)}, f32[128,128]{1,0:T(8,128)S(1)}, u32[]{:S(2)}, u32[]{:S(2)}) %collective-permute-start.5) | collective-permute-done | bytes 65568 | tf_op jit(solution)/shard_map/ppermute | solution.py:23
  14.8 1.3 %collective-permute-done.4.refs_4_ = f32[128,128]{1,0:T(8,128)S(1)} collective-permute-done((f32[128,128]{1,0:T(8,128)S(1)}, f32[128,128]{1,0:T(8,128)S(1)}, u32[]{:S(2)}, u32[]{:S(2)}) %collective-permute-start.4) | collective-permute-done | bytes 65568 | tf_op jit(solution)/shard_map/ppermute | solution.py:23
  16.0 0.5 %collective-permute-done.3.refs_3_ = f32[128,128]{1,0:T(8,128)S(1)} collective-permute-done((f32[128,128]{1,0:T(8,128)S(1)}, f32[128,128]{1,0:T(8,128)S(1)}, u32[]{:S(2)}, u32[]{:S(2)}) %collective-permute-start.3) | collective-permute-done | bytes 65568 | tf_op jit(solution)/shard_map/ppermute | solution.py:23
  16.6 0.1 collective-permute-start.6
  16.7 1.5 %collective-permute-done.6.refs_6_ = f32[4,128,128]{2,1,0:T(8,128)S(1)} collective-permute-done((f32[4,128,128]{2,1,0:T(8,128)S(1)}, f32[4,128,128]{2,1,0:T(8,128)S(1)}, u32[]{:S(2)}, u32[]{:S(2)}) %collective-permute-start.6) | collective-permute-done | bytes 262176 | tf_op jit(solution)/shard_map/ppermute | solution.py:28
  18.2 0.0 copy-done.2
  18.2 1.8 %shard_map.52 = (f32[520,128]{1,0:T(8,128)S(1)}, f32[5,128,128]{2,1,0:T(8,128)S(1)}, f32[128,128]{1,0:T(8,128)S(1)}, f32[128,128]{1,0:T(8,128)S(1)}) custom-call(s32[2,17]{1,0:T(2,128)S(1)} %bitcast.12, s32[1]{0:T(128)} %bitcast.1.place_ref, f32[128,128]{1,0:T(8,128)S(1)} %get-tuple-element.27.own_ref.right_ref, ...), custom_call_target="tpu_custom_call" | custom-call | tf_op jit(solution)/shard_map/pallas_call | solution.py:201
  20.0 0.2 collective-permute-start.7
  20.2 1.4 %collective-permute-done.7.got_ref = f32[520,128]{1,0:T(8,128)S(1)} collective-permute-done((f32[520,128]{1,0:T(8,128)S(1)}, f32[520,128]{1,0:T(8,128)S(1)}, u32[]{:S(2)}, u32[]{:S(2)}) %collective-permute-start.7) | collective-permute-done | bytes 266272 | tf_op jit(solution)/shard_map/ppermute | solution.py:28
  21.7 0.6 %collective-permute-start.8 = (f32[136,128]{1,0:T(8,128)S(1)}, f32[136,128]{1,0:T(8,128)S(1)}, u32[]{:S(2)}, u32[]{:S(2)}) collective-permute-start(f32[136,128]{1,0:T(8,128)S(1)} %get-tuple-element.40), channel_id=1, source_target_pairs={{0,2},{1,3},{2,0},{3,1},{4,6},{5,7},{6,4},{7,5},{8,10},{9,11},{10,... | collective-permute-start | bytes 208904 | tf_op jit(solution)/shard_map/ppermute | solution.py:23
  22.3 1.5 %collective-permute-start.9 = (f32[136,128]{1,0:T(8,128)S(1)}, f32[136,128]{1,0:T(8,128)S(1)}, u32[]{:S(2)}, u32[]{:S(2)}) collective-permute-start(f32[136,128]{1,0:T(8,128)S(1)} %get-tuple-element.41), channel_id=1, source_target_pairs={{0,4},{1,5},{2,6},{3,7},{4,0},{5,1},{6,2},{7,3},{8,12},{9,13},{10,... | collective-permute-start | bytes 208904 | tf_op jit(solution)/shard_map/ppermute | solution.py:23
  23.8 1.4 %collective-permute-start.10 = (f32[136,128]{1,0:T(8,128)S(1)}, f32[136,128]{1,0:T(8,128)S(1)}, u32[]{:S(2)}, u32[]{:S(2)}) collective-permute-start(f32[136,128]{1,0:T(8,128)S(1)} %get-tuple-element.42), channel_id=1, source_target_pairs={{0,6},{1,7},{2,4},{3,5},{4,2},{5,3},{6,0},{7,1},{8,14},{9,15},{10,... | collective-permute-start | bytes 208904 | tf_op jit(solution)/shard_map/ppermute | solution.py:23
  25.2 2.1 %collective-permute-start.12 = (f32[128,128]{1,0:T(8,128)S(1)}, f32[128,128]{1,0:T(8,128)S(1)}, u32[]{:S(2)}, u32[]{:S(2)}) collective-permute-start(f32[128,128]{1,0:T(8,128)S(1)} %get-tuple-element.47), channel_id=1, source_target_pairs={{0,16},{1,17},{2,18},{3,19},{4,20},{5,21},{6,22},{7,23},{8,24},{9,... | collective-permute-start | bytes 196616 | tf_op jit(solution)/shard_map/ppermute | solution.py:18
  27.3 0.0 collective-permute-done.8.refs_0_
  27.4 0.0 collective-permute-done.9.refs_1_
  27.4 1.6 %collective-permute-done.10.refs_2_ = f32[136,128]{1,0:T(8,128)S(1)} collective-permute-done((f32[136,128]{1,0:T(8,128)S(1)}, f32[136,128]{1,0:T(8,128)S(1)}, u32[]{:S(2)}, u32[]{:S(2)}) %collective-permute-start.10) | collective-permute-done | bytes 69664 | tf_op jit(solution)/shard_map/ppermute | solution.py:23
  29.0 2.2 %collective-permute-start.14 = (f32[8,128]{1,0:T(8,128)S(1)}, f32[8,128]{1,0:T(8,128)S(1)}, u32[]{:S(2)}, u32[]{:S(2)}) collective-permute-start(f32[8,128]{1,0:T(8,128)S(1)} %get-tuple-element.44.sums_ref), channel_id=1, source_target_pairs={{0,16},{1,17},{2,18},{3,19},{4,20},{5,21},{6,22},{7,23},{8,24},{9,... | collective-permute-start | bytes 12296 | tf_op jit(solution)/shard_map/ppermute | solution.py:18
  31.2 1.6 %collective-permute-start.11 = (f32[136,128]{1,0:T(8,128)S(1)}, f32[136,128]{1,0:T(8,128)S(1)}, u32[]{:S(2)}, u32[]{:S(2)}) collective-permute-start(f32[136,128]{1,0:T(8,128)S(1)} %get-tuple-element.45), channel_id=1, source_target_pairs={{0,8},{1,9},{2,10},{3,11},{4,12},{5,13},{6,14},{7,15},{8,16},{9,17... | collective-permute-start | bytes 208904 | tf_op jit(solution)/shard_map/ppermute | solution.py:18
  32.9 2.2 %collective-permute-start.13 = (f32[136,128]{1,0:T(8,128)S(1)}, f32[136,128]{1,0:T(8,128)S(1)}, u32[]{:S(2)}, u32[]{:S(2)}) collective-permute-start(f32[136,128]{1,0:T(8,128)S(1)} %get-tuple-element.49), channel_id=1, source_target_pairs={{0,24},{1,25},{2,26},{3,27},{4,28},{5,29},{6,30},{7,31},{8,0},{9,1... | collective-permute-start | bytes 208904 | tf_op jit(solution)/shard_map/ppermute | solution.py:18
  35.1 0.0 collective-permute-done.12.refs_0_
  35.1 2.4 %collective-permute-done.11.next_ref = f32[136,128]{1,0:T(8,128)S(1)} collective-permute-done((f32[136,128]{1,0:T(8,128)S(1)}, f32[136,128]{1,0:T(8,128)S(1)}, u32[]{:S(2)}, u32[]{:S(2)}) %collective-permute-start.11) | collective-permute-done | bytes 69664 | tf_op jit(solution)/shard_map/ppermute | solution.py:18
  37.5 0.0 collective-permute-done.14.refs_0_
  37.5 0.5 %collective-permute-done.13.last_ref = f32[136,128]{1,0:T(8,128)S(1)} collective-permute-done((f32[136,128]{1,0:T(8,128)S(1)}, f32[136,128]{1,0:T(8,128)S(1)}, u32[]{:S(2)}, u32[]{:S(2)}) %collective-permute-start.13) | collective-permute-done | bytes 69664 | tf_op jit(solution)/shard_map/ppermute | solution.py:18
  37.9 0.7 %shard_map.57 = (f32[128,128]{1,0:T(8,128)}, f32[128,128]{1,0:T(8,128)}) custom-call(f32[128,128]{1,0:T(8,128)S(1)} %get-tuple-element.27.own_ref.right_ref, f32[128,128]{1,0:T(8,128)S(1)} %get-tuple-element.46.near_ref, f32[128,128]{1,0:T(8,128)S(1)} %shard_map.56.middle_ref, f32[8,128]{1,0:T(8,128)S(1)} %get-tuple-element.48.sums_ref, ...), custom_call_target="tpu_custom_call" | custom-call | tf_op jit(solution)/shard_map/pallas_call | solution.py:201
  (7 shorter events, 0.2 us)
Async XLA Ops:
  0.6 8.6 %collective-permute-start = (f32[128,128]{1,0:T(8,128)}, f32[128,128]{1,0:T(8,128)S(1)}, u32[]{:S(2)}, u32[]{:S(2)}) collective-permute-start(f32[128,128]{1,0:T(8,128)} %own_ref.1), channel_id=1, source_target_pairs={{0,8},{1,9},{2,10},{3,11},{4,12},{5,13},{6,14},{7,15},{8,16},{9,17... | collective-permute-start | bytes 196616 | tf_op jit(solution)/shard_map/ppermute | solution.py:18
  3.7 5.5 %collective-permute-start.1 = (f32[128,128]{1,0:T(8,128)}, f32[128,128]{1,0:T(8,128)S(1)}, u32[]{:S(2)}, u32[]{:S(2)}) collective-permute-start(f32[128,128]{1,0:T(8,128)} %own_ref.1), channel_id=1, source_target_pairs={{0,24},{1,25},{2,26},{3,27},{4,28},{5,29},{6,30},{7,31},{8,0},{9,1... | collective-permute-start | bytes 196616 | tf_op jit(solution)/shard_map/ppermute | solution.py:18
  5.8 7.0 %collective-permute-start.2 = (f32[128,128]{1,0:T(8,128)}, f32[128,128]{1,0:T(8,128)S(1)}, u32[]{:S(2)}, u32[]{:S(2)}) collective-permute-start(f32[128,128]{1,0:T(8,128)} %own_ref.1), channel_id=1, source_target_pairs={{0,16},{1,17},{2,18},{3,19},{4,20},{5,21},{6,22},{7,23},{8,24},{9,... | collective-permute-start | bytes 196616 | tf_op jit(solution)/shard_map/ppermute | solution.py:18
  6.7 1.2 %copy-start = (f32[1,17,128,128]{3,2,1,0:T(8,128)S(1)}, f32[1,17,128,128]{3,2,1,0:T(8,128)}, u32[]{:S(2)}) copy-start(f32[1,17,128,128]{3,2,1,0:T(8,128)} %param.4) | copy-start | bytes 3342340
  8.0 0.8 %copy-start.1 = (f32[128,128]{1,0:T(8,128)S(1)}, f32[128,128]{1,0:T(8,128)}, u32[]{:S(2)}) copy-start(f32[128,128]{1,0:T(8,128)} %own_ref.1) | copy-start | bytes 196612
  9.3 5.5 %collective-permute-start.5 = (f32[128,128]{1,0:T(8,128)S(1)}, f32[128,128]{1,0:T(8,128)S(1)}, u32[]{:S(2)}, u32[]{:S(2)}) collective-permute-start(f32[128,128]{1,0:T(8,128)S(1)} %get-tuple-element.51), channel_id=1, source_target_pairs={{0,6},{1,7},{2,4},{3,5},{4,2},{5,3},{6,0},{7,1},{8,14},{9,15},{10,... | collective-permute-start | bytes 196616 | tf_op jit(solution)/shard_map/ppermute | solution.py:23
  11.8 4.3 %collective-permute-start.4 = (f32[128,128]{1,0:T(8,128)S(1)}, f32[128,128]{1,0:T(8,128)S(1)}, u32[]{:S(2)}, u32[]{:S(2)}) collective-permute-start(f32[128,128]{1,0:T(8,128)S(1)} %get-tuple-element.52), channel_id=1, source_target_pairs={{0,4},{1,5},{2,6},{3,7},{4,0},{5,1},{6,2},{7,3},{8,12},{9,13},{10,... | collective-permute-start | bytes 196616 | tf_op jit(solution)/shard_map/ppermute | solution.py:23
  12.3 5.9 %copy-start.2 = (s32[17,2]{0,1:T(2,128)S(1)}, s32[17,2]{0,1:T(2,128)}, u32[]{:S(2)}) copy-start(s32[17,2]{0,1:T(2,128)} %param.5) | copy-start | bytes 412
  12.3 4.3 %collective-permute-start.3 = (f32[128,128]{1,0:T(8,128)S(1)}, f32[128,128]{1,0:T(8,128)S(1)}, u32[]{:S(2)}, u32[]{:S(2)}) collective-permute-start(f32[128,128]{1,0:T(8,128)S(1)} %get-tuple-element.53), channel_id=1, source_target_pairs={{0,2},{1,3},{2,0},{3,1},{4,6},{5,7},{6,4},{7,5},{8,10},{9,11},{10,... | collective-permute-start | bytes 196616 | tf_op jit(solution)/shard_map/ppermute | solution.py:23
  16.6 1.6 %collective-permute-start.6 = (f32[4,128,128]{2,1,0:T(8,128)S(1)}, f32[4,128,128]{2,1,0:T(8,128)S(1)}, u32[]{:S(2)}, u32[]{:S(2)}) collective-permute-start(f32[4,128,128]{2,1,0:T(8,128)S(1)} %pad_maximum_fusion), channel_id=1, source_target_pairs={{0,1},{1,0},{2,3},{3,2},{4,5},{5,4},{6,7},{7,6},{8,9},{9,8},{10,11... | collective-permute-start | bytes 786440 | tf_op jit(solution)/shard_map/ppermute | solution.py:28
  20.0 1.6 %collective-permute-start.7 = (f32[520,128]{1,0:T(8,128)S(1)}, f32[520,128]{1,0:T(8,128)S(1)}, u32[]{:S(2)}, u32[]{:S(2)}) collective-permute-start(f32[520,128]{1,0:T(8,128)S(1)} %get-tuple-element.34.sent_ref), channel_id=1, source_target_pairs={{0,1},{1,0},{2,3},{3,2},{4,5},{5,4},{6,7},{7,6},{8,9},{9,8},{10,11... | collective-permute-start | bytes 798728 | tf_op jit(solution)/shard_map/ppermute | solution.py:28
  21.7 5.7 %collective-permute-start.8 = (f32[136,128]{1,0:T(8,128)S(1)}, f32[136,128]{1,0:T(8,128)S(1)}, u32[]{:S(2)}, u32[]{:S(2)}) collective-permute-start(f32[136,128]{1,0:T(8,128)S(1)} %get-tuple-element.40), channel_id=1, source_target_pairs={{0,2},{1,3},{2,0},{3,1},{4,6},{5,7},{6,4},{7,5},{8,10},{9,11},{10,... | collective-permute-start | bytes 208904 | tf_op jit(solution)/shard_map/ppermute | solution.py:23
  22.3 5.1 %collective-permute-start.9 = (f32[136,128]{1,0:T(8,128)S(1)}, f32[136,128]{1,0:T(8,128)S(1)}, u32[]{:S(2)}, u32[]{:S(2)}) collective-permute-start(f32[136,128]{1,0:T(8,128)S(1)} %get-tuple-element.41), channel_id=1, source_target_pairs={{0,4},{1,5},{2,6},{3,7},{4,0},{5,1},{6,2},{7,3},{8,12},{9,13},{10,... | collective-permute-start | bytes 208904 | tf_op jit(solution)/shard_map/ppermute | solution.py:23
  23.8 5.2 %collective-permute-start.10 = (f32[136,128]{1,0:T(8,128)S(1)}, f32[136,128]{1,0:T(8,128)S(1)}, u32[]{:S(2)}, u32[]{:S(2)}) collective-permute-start(f32[136,128]{1,0:T(8,128)S(1)} %get-tuple-element.42), channel_id=1, source_target_pairs={{0,6},{1,7},{2,4},{3,5},{4,2},{5,3},{6,0},{7,1},{8,14},{9,15},{10,... | collective-permute-start | bytes 208904 | tf_op jit(solution)/shard_map/ppermute | solution.py:23
  25.2 9.8 %collective-permute-start.12 = (f32[128,128]{1,0:T(8,128)S(1)}, f32[128,128]{1,0:T(8,128)S(1)}, u32[]{:S(2)}, u32[]{:S(2)}) collective-permute-start(f32[128,128]{1,0:T(8,128)S(1)} %get-tuple-element.47), channel_id=1, source_target_pairs={{0,16},{1,17},{2,18},{3,19},{4,20},{5,21},{6,22},{7,23},{8,24},{9,... | collective-permute-start | bytes 196616 | tf_op jit(solution)/shard_map/ppermute | solution.py:18
  29.0 8.4 %collective-permute-start.14 = (f32[8,128]{1,0:T(8,128)S(1)}, f32[8,128]{1,0:T(8,128)S(1)}, u32[]{:S(2)}, u32[]{:S(2)}) collective-permute-start(f32[8,128]{1,0:T(8,128)S(1)} %get-tuple-element.44.sums_ref), channel_id=1, source_target_pairs={{0,16},{1,17},{2,18},{3,19},{4,20},{5,21},{6,22},{7,23},{8,24},{9,... | collective-permute-start | bytes 12296 | tf_op jit(solution)/shard_map/ppermute | solution.py:18
  31.2 6.2 %collective-permute-start.11 = (f32[136,128]{1,0:T(8,128)S(1)}, f32[136,128]{1,0:T(8,128)S(1)}, u32[]{:S(2)}, u32[]{:S(2)}) collective-permute-start(f32[136,128]{1,0:T(8,128)S(1)} %get-tuple-element.45), channel_id=1, source_target_pairs={{0,8},{1,9},{2,10},{3,11},{4,12},{5,13},{6,14},{7,15},{8,16},{9,17... | collective-permute-start | bytes 208904 | tf_op jit(solution)/shard_map/ppermute | solution.py:18
  32.9 5.1 %collective-permute-start.13 = (f32[136,128]{1,0:T(8,128)S(1)}, f32[136,128]{1,0:T(8,128)S(1)}, u32[]{:S(2)}, u32[]{:S(2)}) collective-permute-start(f32[136,128]{1,0:T(8,128)S(1)} %get-tuple-element.49), channel_id=1, source_target_pairs={{0,24},{1,25},{2,26},{3,27},{4,28},{5,29},{6,30},{7,31},{8,0},{9,1... | collective-permute-start | bytes 208904 | tf_op jit(solution)/shard_map/ppermute | solution.py:18

commit v14 on v12

--- a/solution.py
+++ b/solution.py
@@ -69,9 +69,9 @@
     refs[-1][...] = total
 
 
-def near_kernel(near_ref, middle_ref, sums_ref, next_ref, near_out, sums_out):
+def near_kernel(near_ref, sums_ref, next_ref, near_out, sums_out):
     rows = near_ref.shape[0]
-    near_out[...] = near_ref[...] + middle_ref[...] + next_ref[:rows, :]
+    near_out[...] = near_ref[...] + next_ref[:rows, :]
     sums_out[...] = sums_ref[...] + next_ref[rows:, :]
 
 
@@ -163,12 +163,12 @@
     sums_ref[...] = sums
 
 
-def plane_kernel(chips, place_ref, near_ref, next_ref, sums_ref, last_ref, *refs):
+def plane_kernel(chips, place_ref, near_ref, middle_ref, next_ref, sums_ref, last_ref, *refs):
     got = refs[: chips - 1]
     next_out, last_out, near_out, sums_out = refs[chips - 1 :]
     rows = near_ref.shape[0]
     chip = place_of(place_ref, chips)[0]
-    near, ahead, sums = near_ref[...], next_ref[...], sums_ref[...]
+    near, ahead, sums = near_ref[...] + middle_ref[...], next_ref[...], sums_ref[...]
     for m in range(1, chips):
         block = got[m - 1][:rows, :]
         same = (chip ^ m) < chip
@@ -256,17 +256,17 @@
     )
     middle_got = [shifted(far_out[k - 2], k * window) for k in middle]
     got = [chip_partner(value, m) for m, value in enumerate(messages, 1)]
+    (middle_sum,) = call(add_kernel, (), middle_got, [block], cost=BESIDE)
     ahead, last, near, sums = call(
         functools.partial(plane_kernel, chips),
         (where,),
-        (near, ahead, sums, far_out[-1], *got),
+        (near, middle_sum, ahead, sums, far_out[-1], *got),
         [marked, marked, block, extra],
     )
     got = shifted(ahead, window)
     more = [shifted(sums, k * window) for k in middle]
     last = shifted(last, (planes - 1) * window)
-    (middle_sum,) = call(add_kernel, (), middle_got, [block], cost=BESIDE)
-    near, sums = call(near_kernel, (), (near, middle_sum, sums, got), [block, extra], cost=BESIDE)
+    near, sums = call(near_kernel, (), (near, sums, got), [block, extra], cost=BESIDE)
     return call(final_kernel, (), (own, near, sums, last, *more), [block, block])
 
 

time: 38.5 us -> 38 us (0.987)
  starting transfers between devices: 21.4 us -> 20 us
  waiting for transfers between devices: 11.1 us -> 12 us
    ppermute x7, starting transfers between devices: 14 us -> 12.6 us  [shifted(): return lax.ppermute(value, 'blk', pairs)]
    ppermute x2, waiting for transfers between devices: 2.93 us -> 1.52 us  [core_partner(): lax.ppermute(value, 'blk', [(source, source ^ 1) for source in range(coun...]
    ppermute x6, waiting for transfers between devices: 5.35 us -> 6.55 us  [chip_partner(): lax.ppermute(value, 'blk', [(source, source ^ 2 * mask) for source in ran...]
    ppermute x7, waiting for transfers between devices: 2.78 us -> 3.94 us  [shifted(): return lax.ppermute(value, 'blk', pairs)]
  transfers between devices with their start and end apart: 15 -> 15, of which waited for: 8 -> 10; matrix products, arithmetic and copies ran while one was open for 0% -> 0% of each run, Pallas kernels for 1% -> 1%
where the time goes in v14:
time: 38 us; the launch traced here: 37.8 us
  starting transfers between devices  20 us (53%)
  waiting for transfers between devices  12 us (32%)
  Pallas kernels  2.99 us (8%)
  local copies, waits for them, and re-layouts  2.09 us (6%)
  between operations  0.7 us (2%)
    ppermute x7, starting transfers between devices, shifted(): return lax.ppermute(value, 'blk', pairs)  12.6 us
    ppermute x6, starting transfers between devices, chip_partner(): lax.ppermute(value, 'blk', [(source, source ^ 2 * mask) for source in ran...  7.11 us
    ppermute x6, waiting for transfers between devices, chip_partner(): lax.ppermute(value, 'blk', [(source, source ^ 2 * mask) for source in ran...  6.55 us
    ppermute x7, waiting for transfers between devices, shifted(): return lax.ppermute(value, 'blk', pairs)  3.94 us
    pallas_call x8, Pallas kernels, call(): pl.pallas_call(kernel, in_specs=[pl.BlockSpec(memory_space=pltpu.SMEM)] *...  2.99 us
    unnamed x6, local copies, waits for them, and re-layouts  2.09 us
    ppermute x2, waiting for transfers between devices, core_partner(): lax.ppermute(value, 'blk', [(source, source ^ 1) for source in range(coun...  1.52 us
  transfers between devices with their start and end apart: 15, of which 10 were waited for; matrix products, arithmetic and copies ran while one was open for 0% of the time, Pallas kernels for 1%

profile of v14, /device:TPU:0, one launch (start us, length us, event | category | flops | bytes accessed | tf_op | source)
XLA Modules:
  0.0 37.8 jit_solution(10750411670423108469)
XLA Ops:
  0.6 3.1 %collective-permute-start = (f32[128,128]{1,0:T(8,128)}, f32[128,128]{1,0:T(8,128)S(1)}, u32[]{:S(2)}, u32[]{:S(2)}) collective-permute-start(f32[128,128]{1,0:T(8,128)} %own_ref.1), channel_id=1, source_target_pairs={{0,8},{1,9},{2,10},{3,11},{4,12},{5,13},{6,14},{7,15},{8,16},{9,17... | collective-permute-start | bytes 196616 | tf_op jit(solution)/shard_map/ppermute | solution.py:18
  3.7 2.1 %collective-permute-start.1 = (f32[128,128]{1,0:T(8,128)}, f32[128,128]{1,0:T(8,128)S(1)}, u32[]{:S(2)}, u32[]{:S(2)}) collective-permute-start(f32[128,128]{1,0:T(8,128)} %own_ref.1), channel_id=1, source_target_pairs={{0,24},{1,25},{2,26},{3,27},{4,28},{5,29},{6,30},{7,31},{8,0},{9,1... | collective-permute-start | bytes 196616 | tf_op jit(solution)/shard_map/ppermute | solution.py:18
  5.8 0.9 %collective-permute-start.2 = (f32[128,128]{1,0:T(8,128)}, f32[128,128]{1,0:T(8,128)S(1)}, u32[]{:S(2)}, u32[]{:S(2)}) collective-permute-start(f32[128,128]{1,0:T(8,128)} %own_ref.1), channel_id=1, source_target_pairs={{0,16},{1,17},{2,18},{3,19},{4,20},{5,21},{6,22},{7,23},{8,24},{9,... | collective-permute-start | bytes 196616 | tf_op jit(solution)/shard_map/ppermute | solution.py:18
  6.7 0.0 copy-start
  6.7 1.2 %copy-done = f32[1,17,128,128]{3,2,1,0:T(8,128)S(1)} copy-done((f32[1,17,128,128]{3,2,1,0:T(8,128)S(1)}, f32[1,17,128,128]{3,2,1,0:T(8,128)}, u32[]{:S(2)}) %copy-start) | copy-done | bytes 1114136
  8.0 0.0 copy-start.1
  8.0 0.8 %copy-done.1 = f32[128,128]{1,0:T(8,128)S(1)} copy-done((f32[128,128]{1,0:T(8,128)S(1)}, f32[128,128]{1,0:T(8,128)}, u32[]{:S(2)}) %copy-start.1) | copy-done | bytes 65560
  8.8 0.4 shard_map.50
  9.2 0.0 collective-permute-done.refs_2_
  9.2 0.0 collective-permute-done.1.refs_0_
  9.3 2.5 %collective-permute-start.5 = (f32[128,128]{1,0:T(8,128)S(1)}, f32[128,128]{1,0:T(8,128)S(1)}, u32[]{:S(2)}, u32[]{:S(2)}) collective-permute-start(f32[128,128]{1,0:T(8,128)S(1)} %get-tuple-element.51), channel_id=1, source_target_pairs={{0,6},{1,7},{2,4},{3,5},{4,2},{5,3},{6,0},{7,1},{8,14},{9,15},{10,... | collective-permute-start | bytes 196616 | tf_op jit(solution)/shard_map/ppermute | solution.py:23
  11.8 0.5 %collective-permute-start.4 = (f32[128,128]{1,0:T(8,128)S(1)}, f32[128,128]{1,0:T(8,128)S(1)}, u32[]{:S(2)}, u32[]{:S(2)}) collective-permute-start(f32[128,128]{1,0:T(8,128)S(1)} %get-tuple-element.52), channel_id=1, source_target_pairs={{0,4},{1,5},{2,6},{3,7},{4,0},{5,1},{6,2},{7,3},{8,12},{9,13},{10,... | collective-permute-start | bytes 196616 | tf_op jit(solution)/shard_map/ppermute | solution.py:23
  12.3 0.0 copy-start.2
  12.3 0.5 %collective-permute-start.3 = (f32[128,128]{1,0:T(8,128)S(1)}, f32[128,128]{1,0:T(8,128)S(1)}, u32[]{:S(2)}, u32[]{:S(2)}) collective-permute-start(f32[128,128]{1,0:T(8,128)S(1)} %get-tuple-element.53), channel_id=1, source_target_pairs={{0,2},{1,3},{2,0},{3,1},{4,6},{5,7},{6,4},{7,5},{8,10},{9,11},{10,... | collective-permute-start | bytes 196616 | tf_op jit(solution)/shard_map/ppermute | solution.py:23
  12.8 0.0 collective-permute-done.2.refs_0_.refs_1_
  12.8 1.9 %collective-permute-done.5.refs_5_ = f32[128,128]{1,0:T(8,128)S(1)} collective-permute-done((f32[128,128]{1,0:T(8,128)S(1)}, f32[128,128]{1,0:T(8,128)S(1)}, u32[]{:S(2)}, u32[]{:S(2)}) %collective-permute-start.5) | collective-permute-done | bytes 65568 | tf_op jit(solution)/shard_map/ppermute | solution.py:23
  14.8 1.3 %collective-permute-done.4.refs_4_ = f32[128,128]{1,0:T(8,128)S(1)} collective-permute-done((f32[128,128]{1,0:T(8,128)S(1)}, f32[128,128]{1,0:T(8,128)S(1)}, u32[]{:S(2)}, u32[]{:S(2)}) %collective-permute-start.4) | collective-permute-done | bytes 65568 | tf_op jit(solution)/shard_map/ppermute | solution.py:23
  16.0 0.5 %collective-permute-done.3.refs_3_ = f32[128,128]{1,0:T(8,128)S(1)} collective-permute-done((f32[128,128]{1,0:T(8,128)S(1)}, f32[128,128]{1,0:T(8,128)S(1)}, u32[]{:S(2)}, u32[]{:S(2)}) %collective-permute-start.3) | collective-permute-done | bytes 65568 | tf_op jit(solution)/shard_map/ppermute | solution.py:23
  16.6 0.1 collective-permute-start.6
  16.7 1.5 %collective-permute-done.6.refs_6_ = f32[4,128,128]{2,1,0:T(8,128)S(1)} collective-permute-done((f32[4,128,128]{2,1,0:T(8,128)S(1)}, f32[4,128,128]{2,1,0:T(8,128)S(1)}, u32[]{:S(2)}, u32[]{:S(2)}) %collective-permute-start.6) | collective-permute-done | bytes 262176 | tf_op jit(solution)/shard_map/ppermute | solution.py:28
  18.2 0.0 copy-done.2
  18.2 1.8 %shard_map.52 = (f32[520,128]{1,0:T(8,128)S(1)}, f32[5,128,128]{2,1,0:T(8,128)S(1)}, f32[128,128]{1,0:T(8,128)S(1)}, f32[128,128]{1,0:T(8,128)S(1)}) custom-call(s32[2,17]{1,0:T(2,128)S(1)} %bitcast.12, s32[1]{0:T(128)} %bitcast.1.place_ref, f32[128,128]{1,0:T(8,128)S(1)} %get-tuple-element.27.own_ref.right_ref, ...), custom_call_target="tpu_custom_call" | custom-call | tf_op jit(solution)/shard_map/pallas_call | solution.py:201
  20.0 0.2 collective-permute-start.7
  20.2 2.1 %collective-permute-start.8 = (f32[128,128]{1,0:T(8,128)S(1)}, f32[128,128]{1,0:T(8,128)S(1)}, u32[]{:S(2)}, u32[]{:S(2)}) collective-permute-start(f32[128,128]{1,0:T(8,128)S(1)} %get-tuple-element.37), channel_id=1, source_target_pairs={{0,16},{1,17},{2,18},{3,19},{4,20},{5,21},{6,22},{7,23},{8,24},{9,... | collective-permute-start | bytes 196616 | tf_op jit(solution)/shard_map/ppermute | solution.py:18
  22.4 0.0 collective-permute-done.7.got_ref
  22.4 0.5 %collective-permute-start.9 = (f32[136,128]{1,0:T(8,128)S(1)}, f32[136,128]{1,0:T(8,128)S(1)}, u32[]{:S(2)}, u32[]{:S(2)}) collective-permute-start(f32[136,128]{1,0:T(8,128)S(1)} %get-tuple-element.41), channel_id=1, source_target_pairs={{0,2},{1,3},{2,0},{3,1},{4,6},{5,7},{6,4},{7,5},{8,10},{9,11},{10,... | collective-permute-start | bytes 208904 | tf_op jit(solution)/shard_map/ppermute | solution.py:23
  22.9 1.7 %collective-permute-start.10 = (f32[136,128]{1,0:T(8,128)S(1)}, f32[136,128]{1,0:T(8,128)S(1)}, u32[]{:S(2)}, u32[]{:S(2)}) collective-permute-start(f32[136,128]{1,0:T(8,128)S(1)} %get-tuple-element.42), channel_id=1, source_target_pairs={{0,4},{1,5},{2,6},{3,7},{4,0},{5,1},{6,2},{7,3},{8,12},{9,13},{10,... | collective-permute-start | bytes 208904 | tf_op jit(solution)/shard_map/ppermute | solution.py:23
  24.5 1.4 %collective-permute-start.11 = (f32[136,128]{1,0:T(8,128)S(1)}, f32[136,128]{1,0:T(8,128)S(1)}, u32[]{:S(2)}, u32[]{:S(2)}) collective-permute-start(f32[136,128]{1,0:T(8,128)S(1)} %get-tuple-element.43), channel_id=1, source_target_pairs={{0,6},{1,7},{2,4},{3,5},{4,2},{5,3},{6,0},{7,1},{8,14},{9,15},{10,... | collective-permute-start | bytes 208904 | tf_op jit(solution)/shard_map/ppermute | solution.py:23
  26.0 0.9 %collective-permute-done.8.refs_0_ = f32[128,128]{1,0:T(8,128)S(1)} collective-permute-done((f32[128,128]{1,0:T(8,128)S(1)}, f32[128,128]{1,0:T(8,128)S(1)}, u32[]{:S(2)}, u32[]{:S(2)}) %collective-permute-start.8) | collective-permute-done | bytes 65568 | tf_op jit(solution)/shard_map/ppermute | solution.py:18
  26.9 0.3 collective-permute-done.9.refs_0_
  27.2 0.0 collective-permute-done.10.refs_1_
  27.2 2.5 %collective-permute-done.11.refs_2_ = f32[136,128]{1,0:T(8,128)S(1)} collective-permute-done((f32[136,128]{1,0:T(8,128)S(1)}, f32[136,128]{1,0:T(8,128)S(1)}, u32[]{:S(2)}, u32[]{:S(2)}) %collective-permute-start.11) | collective-permute-done | bytes 69664 | tf_op jit(solution)/shard_map/ppermute | solution.py:23
  29.8 1.7 %collective-permute-start.12 = (f32[136,128]{1,0:T(8,128)S(1)}, f32[136,128]{1,0:T(8,128)S(1)}, u32[]{:S(2)}, u32[]{:S(2)}) collective-permute-start(f32[136,128]{1,0:T(8,128)S(1)} %get-tuple-element.46), channel_id=1, source_target_pairs={{0,8},{1,9},{2,10},{3,11},{4,12},{5,13},{6,14},{7,15},{8,16},{9,17... | collective-permute-start | bytes 208904 | tf_op jit(solution)/shard_map/ppermute | solution.py:18
  31.5 1.4 %collective-permute-start.14 = (f32[8,128]{1,0:T(8,128)S(1)}, f32[8,128]{1,0:T(8,128)S(1)}, u32[]{:S(2)}, u32[]{:S(2)}) collective-permute-start(f32[8,128]{1,0:T(8,128)S(1)} %get-tuple-element.45.sums_ref), channel_id=1, source_target_pairs={{0,16},{1,17},{2,18},{3,19},{4,20},{5,21},{6,22},{7,23},{8,24},{9,... | collective-permute-start | bytes 12296 | tf_op jit(solution)/shard_map/ppermute | solution.py:18
  32.9 1.3 %collective-permute-start.13 = (f32[136,128]{1,0:T(8,128)S(1)}, f32[136,128]{1,0:T(8,128)S(1)}, u32[]{:S(2)}, u32[]{:S(2)}) collective-permute-start(f32[136,128]{1,0:T(8,128)S(1)} %get-tuple-element.49), channel_id=1, source_target_pairs={{0,24},{1,25},{2,26},{3,27},{4,28},{5,29},{6,30},{7,31},{8,0},{9,1... | collective-permute-start | bytes 208904 | tf_op jit(solution)/shard_map/ppermute | solution.py:18
  34.1 1.8 %collective-permute-done.12.next_ref = f32[136,128]{1,0:T(8,128)S(1)} collective-permute-done((f32[136,128]{1,0:T(8,128)S(1)}, f32[136,128]{1,0:T(8,128)S(1)}, u32[]{:S(2)}, u32[]{:S(2)}) %collective-permute-start.12) | collective-permute-done | bytes 69664 | tf_op jit(solution)/shard_map/ppermute | solution.py:18
  36.0 0.1 collective-permute-done.14.refs_0_
  36.0 1.1 %collective-permute-done.13.last_ref = f32[136,128]{1,0:T(8,128)S(1)} collective-permute-done((f32[136,128]{1,0:T(8,128)S(1)}, f32[136,128]{1,0:T(8,128)S(1)}, u32[]{:S(2)}, u32[]{:S(2)}) %collective-permute-start.13) | collective-permute-done | bytes 69664 | tf_op jit(solution)/shard_map/ppermute | solution.py:18
  37.2 0.7 %shard_map.57 = (f32[128,128]{1,0:T(8,128)}, f32[128,128]{1,0:T(8,128)}) custom-call(f32[128,128]{1,0:T(8,128)S(1)} %get-tuple-element.27.own_ref.right_ref, f32[128,128]{1,0:T(8,128)S(1)} %get-tuple-element.47.near_ref, f32[8,128]{1,0:T(8,128)S(1)} %get-tuple-element.48.sums_ref, f32[136,128]{1,0:T(8,128)S(1)} %collective-permute-done.13.last_ref, ...), custom_call_target="tpu_custom_call" | custom-call | tf_op jit(solution)/shard_map/pallas_call | solution.py:201
  (7 shorter events, 0.2 us)
Async XLA Ops:
  0.6 8.6 %collective-permute-start = (f32[128,128]{1,0:T(8,128)}, f32[128,128]{1,0:T(8,128)S(1)}, u32[]{:S(2)}, u32[]{:S(2)}) collective-permute-start(f32[128,128]{1,0:T(8,128)} %own_ref.1), channel_id=1, source_target_pairs={{0,8},{1,9},{2,10},{3,11},{4,12},{5,13},{6,14},{7,15},{8,16},{9,17... | collective-permute-start | bytes 196616 | tf_op jit(solution)/shard_map/ppermute | solution.py:18
  3.7 5.5 %collective-permute-start.1 = (f32[128,128]{1,0:T(8,128)}, f32[128,128]{1,0:T(8,128)S(1)}, u32[]{:S(2)}, u32[]{:S(2)}) collective-permute-start(f32[128,128]{1,0:T(8,128)} %own_ref.1), channel_id=1, source_target_pairs={{0,24},{1,25},{2,26},{3,27},{4,28},{5,29},{6,30},{7,31},{8,0},{9,1... | collective-permute-start | bytes 196616 | tf_op jit(solution)/shard_map/ppermute | solution.py:18
  5.8 7.0 %collective-permute-start.2 = (f32[128,128]{1,0:T(8,128)}, f32[128,128]{1,0:T(8,128)S(1)}, u32[]{:S(2)}, u32[]{:S(2)}) collective-permute-start(f32[128,128]{1,0:T(8,128)} %own_ref.1), channel_id=1, source_target_pairs={{0,16},{1,17},{2,18},{3,19},{4,20},{5,21},{6,22},{7,23},{8,24},{9,... | collective-permute-start | bytes 196616 | tf_op jit(solution)/shard_map/ppermute | solution.py:18
  6.7 1.2 %copy-start = (f32[1,17,128,128]{3,2,1,0:T(8,128)S(1)}, f32[1,17,128,128]{3,2,1,0:T(8,128)}, u32[]{:S(2)}) copy-start(f32[1,17,128,128]{3,2,1,0:T(8,128)} %param.4) | copy-start | bytes 3342340
  8.0 0.8 %copy-start.1 = (f32[128,128]{1,0:T(8,128)S(1)}, f32[128,128]{1,0:T(8,128)}, u32[]{:S(2)}) copy-start(f32[128,128]{1,0:T(8,128)} %own_ref.1) | copy-start | bytes 196612
  9.3 5.5 %collective-permute-start.5 = (f32[128,128]{1,0:T(8,128)S(1)}, f32[128,128]{1,0:T(8,128)S(1)}, u32[]{:S(2)}, u32[]{:S(2)}) collective-permute-start(f32[128,128]{1,0:T(8,128)S(1)} %get-tuple-element.51), channel_id=1, source_target_pairs={{0,6},{1,7},{2,4},{3,5},{4,2},{5,3},{6,0},{7,1},{8,14},{9,15},{10,... | collective-permute-start | bytes 196616 | tf_op jit(solution)/shard_map/ppermute | solution.py:23
  11.8 4.3 %collective-permute-start.4 = (f32[128,128]{1,0:T(8,128)S(1)}, f32[128,128]{1,0:T(8,128)S(1)}, u32[]{:S(2)}, u32[]{:S(2)}) collective-permute-start(f32[128,128]{1,0:T(8,128)S(1)} %get-tuple-element.52), channel_id=1, source_target_pairs={{0,4},{1,5},{2,6},{3,7},{4,0},{5,1},{6,2},{7,3},{8,12},{9,13},{10,... | collective-permute-start | bytes 196616 | tf_op jit(solution)/shard_map/ppermute | solution.py:23
  12.3 5.9 %copy-start.2 = (s32[17,2]{0,1:T(2,128)S(1)}, s32[17,2]{0,1:T(2,128)}, u32[]{:S(2)}) copy-start(s32[17,2]{0,1:T(2,128)} %param.5) | copy-start | bytes 412
  12.3 4.3 %collective-permute-start.3 = (f32[128,128]{1,0:T(8,128)S(1)}, f32[128,128]{1,0:T(8,128)S(1)}, u32[]{:S(2)}, u32[]{:S(2)}) collective-permute-start(f32[128,128]{1,0:T(8,128)S(1)} %get-tuple-element.53), channel_id=1, source_target_pairs={{0,2},{1,3},{2,0},{3,1},{4,6},{5,7},{6,4},{7,5},{8,10},{9,11},{10,... | collective-permute-start | bytes 196616 | tf_op jit(solution)/shard_map/ppermute | solution.py:23
  16.6 1.6 %collective-permute-start.6 = (f32[4,128,128]{2,1,0:T(8,128)S(1)}, f32[4,128,128]{2,1,0:T(8,128)S(1)}, u32[]{:S(2)}, u32[]{:S(2)}) collective-permute-start(f32[4,128,128]{2,1,0:T(8,128)S(1)} %pad_maximum_fusion), channel_id=1, source_target_pairs={{0,1},{1,0},{2,3},{3,2},{4,5},{5,4},{6,7},{7,6},{8,9},{9,8},{10,11... | collective-permute-start | bytes 786440 | tf_op jit(solution)/shard_map/ppermute | solution.py:28
  20.0 2.4 %collective-permute-start.7 = (f32[520,128]{1,0:T(8,128)S(1)}, f32[520,128]{1,0:T(8,128)S(1)}, u32[]{:S(2)}, u32[]{:S(2)}) collective-permute-start(f32[520,128]{1,0:T(8,128)S(1)} %get-tuple-element.34.sent_ref), channel_id=1, source_target_pairs={{0,1},{1,0},{2,3},{3,2},{4,5},{5,4},{6,7},{7,6},{8,9},{9,8},{10,11... | collective-permute-start | bytes 798728 | tf_op jit(solution)/shard_map/ppermute | solution.py:28
  20.2 6.7 %collective-permute-start.8 = (f32[128,128]{1,0:T(8,128)S(1)}, f32[128,128]{1,0:T(8,128)S(1)}, u32[]{:S(2)}, u32[]{:S(2)}) collective-permute-start(f32[128,128]{1,0:T(8,128)S(1)} %get-tuple-element.37), channel_id=1, source_target_pairs={{0,16},{1,17},{2,18},{3,19},{4,20},{5,21},{6,22},{7,23},{8,24},{9,... | collective-permute-start | bytes 196616 | tf_op jit(solution)/shard_map/ppermute | solution.py:18
  22.4 4.8 %collective-permute-start.9 = (f32[136,128]{1,0:T(8,128)S(1)}, f32[136,128]{1,0:T(8,128)S(1)}, u32[]{:S(2)}, u32[]{:S(2)}) collective-permute-start(f32[136,128]{1,0:T(8,128)S(1)} %get-tuple-element.41), channel_id=1, source_target_pairs={{0,2},{1,3},{2,0},{3,1},{4,6},{5,7},{6,4},{7,5},{8,10},{9,11},{10,... | collective-permute-start | bytes 208904 | tf_op jit(solution)/shard_map/ppermute | solution.py:23
  22.9 4.3 %collective-permute-start.10 = (f32[136,128]{1,0:T(8,128)S(1)}, f32[136,128]{1,0:T(8,128)S(1)}, u32[]{:S(2)}, u32[]{:S(2)}) collective-permute-start(f32[136,128]{1,0:T(8,128)S(1)} %get-tuple-element.42), channel_id=1, source_target_pairs={{0,4},{1,5},{2,6},{3,7},{4,0},{5,1},{6,2},{7,3},{8,12},{9,13},{10,... | collective-permute-start | bytes 208904 | tf_op jit(solution)/shard_map/ppermute | solution.py:23
  24.5 5.2 %collective-permute-start.11 = (f32[136,128]{1,0:T(8,128)S(1)}, f32[136,128]{1,0:T(8,128)S(1)}, u32[]{:S(2)}, u32[]{:S(2)}) collective-permute-start(f32[136,128]{1,0:T(8,128)S(1)} %get-tuple-element.43), channel_id=1, source_target_pairs={{0,6},{1,7},{2,4},{3,5},{4,2},{5,3},{6,0},{7,1},{8,14},{9,15},{10,... | collective-permute-start | bytes 208904 | tf_op jit(solution)/shard_map/ppermute | solution.py:23
  29.8 6.2 %collective-permute-start.12 = (f32[136,128]{1,0:T(8,128)S(1)}, f32[136,128]{1,0:T(8,128)S(1)}, u32[]{:S(2)}, u32[]{:S(2)}) collective-permute-start(f32[136,128]{1,0:T(8,128)S(1)} %get-tuple-element.46), channel_id=1, source_target_pairs={{0,8},{1,9},{2,10},{3,11},{4,12},{5,13},{6,14},{7,15},{8,16},{9,17... | collective-permute-start | bytes 208904 | tf_op jit(solution)/shard_map/ppermute | solution.py:18
  31.5 4.6 %collective-permute-start.14 = (f32[8,128]{1,0:T(8,128)S(1)}, f32[8,128]{1,0:T(8,128)S(1)}, u32[]{:S(2)}, u32[]{:S(2)}) collective-permute-start(f32[8,128]{1,0:T(8,128)S(1)} %get-tuple-element.45.sums_ref), channel_id=1, source_target_pairs={{0,16},{1,17},{2,18},{3,19},{4,20},{5,21},{6,22},{7,23},{8,24},{9,... | collective-permute-start | bytes 12296 | tf_op jit(solution)/shard_map/ppermute | solution.py:18
  32.9 4.3 %collective-permute-start.13 = (f32[136,128]{1,0:T(8,128)S(1)}, f32[136,128]{1,0:T(8,128)S(1)}, u32[]{:S(2)}, u32[]{:S(2)}) collective-permute-start(f32[136,128]{1,0:T(8,128)S(1)} %get-tuple-element.49), channel_id=1, source_target_pairs={{0,24},{1,25},{2,26},{3,27},{4,28},{5,29},{6,30},{7,31},{8,0},{9,1... | collective-permute-start | bytes 208904 | tf_op jit(solution)/shard_map/ppermute | solution.py:18

commit v15 on v14

--- a/solution.py
+++ b/solution.py
@@ -39,14 +39,17 @@
     return (place // 2) & (chips - 1), place & 1
 
 
-def prepare_kernel(own_ref, tiles_ref, own_out, straight_ref, turned_ref):
-    own_out[...] = own_ref[...]
+def keep_kernel(block_ref, out_ref):
+    out_ref[...] = block_ref[...]
+
+
+def split_kernel(tiles_ref, straight_ref, turned_ref):
     slots, rows, cols = tiles_ref.shape
 
     def visit(t):
         tile = tiles_ref[t]
-        straight_ref[t, :rows, :], straight_ref[t, rows:, :] = split_two(tile)
-        turned_ref[t, :cols, :], turned_ref[t, cols:, :] = split_two(tile.T)
+        straight_ref[t, :, :cols], straight_ref[t, :, cols:] = split_two(tile)
+        turned_ref[t, :, :rows], turned_ref[t, :, rows:] = split_two(tile.T)
 
     if slots <= 32:
         for t in range(slots):
@@ -90,18 +93,22 @@
     chip, core = place_of(place_ref, chips)
     spare = jnp.where(core == 0, 1, window - 1)
 
+    def put_parts(place, high, low):
+        parts[place, :rows, :cols] = high
+        parts[place, :rows, cols:] = low
+        parts[place, rows:, :cols] = high
+        parts[place, rows:, cols:] = jnp.zeros_like(low)
+
     def put(place, values):
         whole[place] = values
-        high, low = split_two(values)
-        parts[place, :, :cols] = high
-        parts[place, :, cols:] = low
+        put_parts(place, *split_two(values))
 
     put(0, own_ref[...])
     for k in (1, planes - 1):
         put(window - 1 + k, far[k - 1][...])
     for k in range(2, planes - 1):
         whole[window - 1 + k] = far[k - 1][...]
-        parts[window - 1 + k] = middle_ref[k - 2]
+        put_parts(window - 1 + k, middle_ref[k - 2, :, :cols], middle_ref[k - 2, :, cols:])
     for m in range(1, chips):
         ahead = 2 * steps_ahead(chip, m, chips)
         put(ahead, even[m - 1][...])
@@ -112,9 +119,8 @@
     slots = straight_ref.shape[0]
 
     def product(split_ref, t, place):
-        high = jnp.dot(split_ref[t, :rows], parts[place], preferred_element_type=jnp.float32)
-        low = jnp.dot(split_ref[t, rows:], parts[place, :, :cols], preferred_element_type=jnp.float32)
-        return high[:, :cols] + (high[:, cols:] + low)
+        both = jnp.dot(split_ref[t], parts[place], preferred_element_type=jnp.float32)
+        return both[:, :cols] + both[:, cols:]
 
     def visit(t, mirrored):
         row_place, col_place = pairs_ref[0, t], pairs_ref[1, t]
@@ -221,11 +227,14 @@
     where = place[None]
     single, half = jnp.float32, jnp.bfloat16
 
-    own, straight, turned = call(
-        prepare_kernel,
+    block, marked, extra = ((rows, cols), single), ((rows + EXTRA, cols), single), ((EXTRA, cols), single)
+    (own,) = call(keep_kernel, (), (right_side,), [block])
+    straight, turned = call(
+        split_kernel,
         (),
-        (right_side, kernel_tiles[0]),
-        [((rows, cols), single), ((slots, 2 * rows, cols), half), ((slots, 2 * cols, rows), half)],
+        (kernel_tiles[0],),
+        [((slots, rows, 2 * cols), half), ((slots, cols, 2 * rows), half)],
+        cost=BESIDE,
     )
     far = {k: shifted(right_side, -k * window) for k in (planes - 1, *range(1, planes - 1))}
     own, far[planes - 1], far[1] = lax.optimization_barrier((own, far[planes - 1], far[1]))
@@ -238,7 +247,6 @@
     sent, middle_parts = lax.optimization_barrier((sent, middle_parts))
     odd = core_partner(sent)
 
-    block, marked, extra = ((rows, cols), single), ((rows + EXTRA, cols), single), ((EXTRA, cols), single)
     sent, kept, *far_out = call(
         functools.partial(product_kernel, planes, chips),
         (route_pairs.T, where),
@@ -246,7 +254,7 @@
         [((chips * rows + EXTRA, cols), single), ((chips + 1, rows, cols), single)] + [block] * (planes - 2),
         (
             pltpu.VMEM((cover_len, rows, cols), single),
-            pltpu.VMEM((cover_len, rows, 2 * cols), half),
+            pltpu.VMEM((cover_len, 2 * rows, 2 * cols), half),
             pltpu.VMEM((cover_len, rows, cols), single),
         ),
     )

time: 38 us -> 37.9 us (level)
  local copies, waits for them, and re-layouts: 2.09 us -> 0.88 us
  waiting for transfers between devices: 12 us -> 13.1 us
    unnamed x6, local copies, waits for them, and re-layouts: 2.09 us -> 0.88 us
    ppermute x6, waiting for transfers between devices: 6.55 us -> 7.47 us  [chip_partner(): lax.ppermute(value, 'blk', [(source, source ^ 2 * mask) for source in ran...]
    ppermute x7, waiting for transfers between devices: 3.94 us -> 4.51 us  [shifted(): return lax.ppermute(value, 'blk', pairs)]
    ppermute x2, waiting for transfers between devices: 1.52 us -> 1.1 us  [core_partner(): lax.ppermute(value, 'blk', [(source, source ^ 1) for source in range(coun...]
    pallas_call x8 -> x9, Pallas kernels: 2.99 us -> 2.88 us  [call(): pl.pallas_call(kernel, in_specs=[pl.BlockSpec(memory_space=pltpu.SMEM)] *...]
  transfers between devices with their start and end apart: 15 -> 15, of which waited for: 10 -> 11; matrix products, arithmetic and copies ran while one was open for 0% -> 0% of each run, Pallas kernels for 1% -> 1%
where the time goes in v15:
time: 37.9 us; the launch traced here: 37.7 us
  starting transfers between devices  20.1 us (53%)
  waiting for transfers between devices  13.1 us (35%)
  Pallas kernels  2.88 us (8%)
  local copies, waits for them, and re-layouts  0.88 us (2%)
  between operations  0.7 us (2%)
    ppermute x7, starting transfers between devices, shifted(): return lax.ppermute(value, 'blk', pairs)  12.7 us
    ppermute x6, waiting for transfers between devices, chip_partner(): lax.ppermute(value, 'blk', [(source, source ^ 2 * mask) for source in ran...  7.47 us
    ppermute x6, starting transfers between devices, chip_partner(): lax.ppermute(value, 'blk', [(source, source ^ 2 * mask) for source in ran...  7.11 us
    ppermute x7, waiting for transfers between devices, shifted(): return lax.ppermute(value, 'blk', pairs)  4.51 us
    pallas_call x9, Pallas kernels, call(): pl.pallas_call(kernel, in_specs=[pl.BlockSpec(memory_space=pltpu.SMEM)] *...  2.88 us
    ppermute x2, waiting for transfers between devices, core_partner(): lax.ppermute(value, 'blk', [(source, source ^ 1) for source in range(coun...  1.1 us
    unnamed x6, local copies, waits for them, and re-layouts  0.88 us
  transfers between devices with their start and end apart: 15, of which 11 were waited for; matrix products, arithmetic and copies ran while one was open for 0% of the time, Pallas kernels for 1%

profile of v15, /device:TPU:0, one launch (start us, length us, event | category | flops | bytes accessed | tf_op | source)
XLA Modules:
  0.0 37.7 jit_solution(10969412960934905143)
XLA Ops:
  0.6 3.1 %collective-permute-start = (f32[128,128]{1,0:T(8,128)}, f32[128,128]{1,0:T(8,128)S(1)}, u32[]{:S(2)}, u32[]{:S(2)}) collective-permute-start(f32[128,128]{1,0:T(8,128)} %block_ref.1), channel_id=1, source_target_pairs={{0,8},{1,9},{2,10},{3,11},{4,12},{5,13},{6,14},{7,15},{8,16},{9,17... | collective-permute-start | bytes 196616 | tf_op jit(solution)/shard_map/ppermute | solution.py:18
  3.7 2.1 %collective-permute-start.1 = (f32[128,128]{1,0:T(8,128)}, f32[128,128]{1,0:T(8,128)S(1)}, u32[]{:S(2)}, u32[]{:S(2)}) collective-permute-start(f32[128,128]{1,0:T(8,128)} %block_ref.1), channel_id=1, source_target_pairs={{0,24},{1,25},{2,26},{3,27},{4,28},{5,29},{6,30},{7,31},{8,0},{9,1... | collective-permute-start | bytes 196616 | tf_op jit(solution)/shard_map/ppermute | solution.py:18
  5.8 0.9 %collective-permute-start.2 = (f32[128,128]{1,0:T(8,128)}, f32[128,128]{1,0:T(8,128)S(1)}, u32[]{:S(2)}, u32[]{:S(2)}) collective-permute-start(f32[128,128]{1,0:T(8,128)} %block_ref.1), channel_id=1, source_target_pairs={{0,16},{1,17},{2,18},{3,19},{4,20},{5,21},{6,22},{7,23},{8,24},{9,... | collective-permute-start | bytes 196616 | tf_op jit(solution)/shard_map/ppermute | solution.py:18
  6.7 0.0 copy-start
  6.7 0.9 %copy-done = f32[128,128]{1,0:T(8,128)S(1)} copy-done((f32[128,128]{1,0:T(8,128)S(1)}, f32[128,128]{1,0:T(8,128)}, u32[]{:S(2)}) %copy-start) | copy-done | bytes 65560
  7.6 0.7 %collective-permute-done.refs_2_ = f32[128,128]{1,0:T(8,128)S(1)} collective-permute-done((f32[128,128]{1,0:T(8,128)}, f32[128,128]{1,0:T(8,128)S(1)}, u32[]{:S(2)}, u32[]{:S(2)}) %collective-permute-start) | collective-permute-done | bytes 65568 | tf_op jit(solution)/shard_map/ppermute | solution.py:18
  8.3 0.5 %collective-permute-done.1.refs_0_ = f32[128,128]{1,0:T(8,128)S(1)} collective-permute-done((f32[128,128]{1,0:T(8,128)}, f32[128,128]{1,0:T(8,128)S(1)}, u32[]{:S(2)}, u32[]{:S(2)}) %collective-permute-start.1) | collective-permute-done | bytes 65568 | tf_op jit(solution)/shard_map/ppermute | solution.py:18
  8.9 2.5 %collective-permute-start.5 = (f32[128,128]{1,0:T(8,128)S(1)}, f32[128,128]{1,0:T(8,128)S(1)}, u32[]{:S(2)}, u32[]{:S(2)}) collective-permute-start(f32[128,128]{1,0:T(8,128)S(1)} %get-tuple-element.49), channel_id=1, source_target_pairs={{0,6},{1,7},{2,4},{3,5},{4,2},{5,3},{6,0},{7,1},{8,14},{9,15},{10,... | collective-permute-start | bytes 196616 | tf_op jit(solution)/shard_map/ppermute | solution.py:23
  11.4 0.5 %collective-permute-start.4 = (f32[128,128]{1,0:T(8,128)S(1)}, f32[128,128]{1,0:T(8,128)S(1)}, u32[]{:S(2)}, u32[]{:S(2)}) collective-permute-start(f32[128,128]{1,0:T(8,128)S(1)} %get-tuple-element.50), channel_id=1, source_target_pairs={{0,4},{1,5},{2,6},{3,7},{4,0},{5,1},{6,2},{7,3},{8,12},{9,13},{10,... | collective-permute-start | bytes 196616 | tf_op jit(solution)/shard_map/ppermute | solution.py:23
  11.9 0.0 copy-start.2
  11.9 0.5 %collective-permute-start.3 = (f32[128,128]{1,0:T(8,128)S(1)}, f32[128,128]{1,0:T(8,128)S(1)}, u32[]{:S(2)}, u32[]{:S(2)}) collective-permute-start(f32[128,128]{1,0:T(8,128)S(1)} %get-tuple-element.51), channel_id=1, source_target_pairs={{0,2},{1,3},{2,0},{3,1},{4,6},{5,7},{6,4},{7,5},{8,10},{9,11},{10,... | collective-permute-start | bytes 196616 | tf_op jit(solution)/shard_map/ppermute | solution.py:23
  12.5 0.0 collective-permute-done.2.refs_0_.refs_1_
  12.5 2.2 %collective-permute-done.5.refs_5_ = f32[128,128]{1,0:T(8,128)S(1)} collective-permute-done((f32[128,128]{1,0:T(8,128)S(1)}, f32[128,128]{1,0:T(8,128)S(1)}, u32[]{:S(2)}, u32[]{:S(2)}) %collective-permute-start.5) | collective-permute-done | bytes 65568 | tf_op jit(solution)/shard_map/ppermute | solution.py:23
  14.7 1.0 %collective-permute-done.4.refs_4_ = f32[128,128]{1,0:T(8,128)S(1)} collective-permute-done((f32[128,128]{1,0:T(8,128)S(1)}, f32[128,128]{1,0:T(8,128)S(1)}, u32[]{:S(2)}, u32[]{:S(2)}) %collective-permute-start.4) | collective-permute-done | bytes 65568 | tf_op jit(solution)/shard_map/ppermute | solution.py:23
  15.7 0.5 %collective-permute-done.3.refs_3_ = f32[128,128]{1,0:T(8,128)S(1)} collective-permute-done((f32[128,128]{1,0:T(8,128)S(1)}, f32[128,128]{1,0:T(8,128)S(1)}, u32[]{:S(2)}, u32[]{:S(2)}) %collective-permute-start.3) | collective-permute-done | bytes 65568 | tf_op jit(solution)/shard_map/ppermute | solution.py:23
  16.2 0.1 collective-permute-start.6
  16.3 0.0 copy-done.2
  16.3 0.0 copy-start.1
  16.3 0.4 %shard_map.52 = (bf16[17,128,256]{2,1,0:T(8,128)(2,1)S(1)}, bf16[17,128,256]{2,1,0:T(8,128)(2,1)S(1)}) custom-call(f32[17,128,128]{2,1,0:T(8,128)S(1)} %bitcast.12), custom_call_target="tpu_custom_call" | custom-call | flops 10000000000 | tf_op jit(solution)/shard_map/pallas_call | solution.py:207
  16.7 1.1 %collective-permute-done.6.refs_6_ = f32[4,128,128]{2,1,0:T(8,128)S(1)} collective-permute-done((f32[4,128,128]{2,1,0:T(8,128)S(1)}, f32[4,128,128]{2,1,0:T(8,128)S(1)}, u32[]{:S(2)}, u32[]{:S(2)}) %collective-permute-start.6) | collective-permute-done | bytes 262176 | tf_op jit(solution)/shard_map/ppermute | solution.py:28
  17.8 0.0 copy-done.1
  17.8 1.7 %shard_map.53 = (f32[520,128]{1,0:T(8,128)S(1)}, f32[5,128,128]{2,1,0:T(8,128)S(1)}, f32[128,128]{1,0:T(8,128)S(1)}, f32[128,128]{1,0:T(8,128)S(1)}) custom-call(s32[2,17]{1,0:T(2,128)S(1)} %bitcast.11, s32[1]{0:T(128)} %bitcast.place_ref, f32[128,128]{1,0:T(8,128)S(1)} %shard_map.50.own_ref.right_ref, f32[128,128]{1,0:T(8,128)S(1)} %collective-permute-done.1.refs_0_, ...), custom_call_target="tpu_custom_call" | custom-call | tf_op jit(solution)/shard_map/pallas_call | solution.py:207
  19.5 0.2 collective-permute-start.7
  19.7 2.2 %collective-permute-start.8 = (f32[128,128]{1,0:T(8,128)S(1)}, f32[128,128]{1,0:T(8,128)S(1)}, u32[]{:S(2)}, u32[]{:S(2)}) collective-permute-start(f32[128,128]{1,0:T(8,128)S(1)} %get-tuple-element.35), channel_id=1, source_target_pairs={{0,16},{1,17},{2,18},{3,19},{4,20},{5,21},{6,22},{7,23},{8,24},{9,... | collective-permute-start | bytes 196616 | tf_op jit(solution)/shard_map/ppermute | solution.py:18
  21.9 0.0 collective-permute-done.7.got_ref
  22.0 0.4 %collective-permute-start.9 = (f32[136,128]{1,0:T(8,128)S(1)}, f32[136,128]{1,0:T(8,128)S(1)}, u32[]{:S(2)}, u32[]{:S(2)}) collective-permute-start(f32[136,128]{1,0:T(8,128)S(1)} %get-tuple-element.39), channel_id=1, source_target_pairs={{0,2},{1,3},{2,0},{3,1},{4,6},{5,7},{6,4},{7,5},{8,10},{9,11},{10,... | collective-permute-start | bytes 208904 | tf_op jit(solution)/shard_map/ppermute | solution.py:23
  22.4 1.7 %collective-permute-start.10 = (f32[136,128]{1,0:T(8,128)S(1)}, f32[136,128]{1,0:T(8,128)S(1)}, u32[]{:S(2)}, u32[]{:S(2)}) collective-permute-start(f32[136,128]{1,0:T(8,128)S(1)} %get-tuple-element.40), channel_id=1, source_target_pairs={{0,4},{1,5},{2,6},{3,7},{4,0},{5,1},{6,2},{7,3},{8,12},{9,13},{10,... | collective-permute-start | bytes 208904 | tf_op jit(solution)/shard_map/ppermute | solution.py:23
  24.1 1.4 %collective-permute-start.11 = (f32[136,128]{1,0:T(8,128)S(1)}, f32[136,128]{1,0:T(8,128)S(1)}, u32[]{:S(2)}, u32[]{:S(2)}) collective-permute-start(f32[136,128]{1,0:T(8,128)S(1)} %get-tuple-element.41), channel_id=1, source_target_pairs={{0,6},{1,7},{2,4},{3,5},{4,2},{5,3},{6,0},{7,1},{8,14},{9,15},{10,... | collective-permute-start | bytes 208904 | tf_op jit(solution)/shard_map/ppermute | solution.py:23
  25.5 0.0 collective-permute-done.8.refs_0_
  25.5 1.3 %collective-permute-done.9.refs_0_ = f32[136,128]{1,0:T(8,128)S(1)} collective-permute-done((f32[136,128]{1,0:T(8,128)S(1)}, f32[136,128]{1,0:T(8,128)S(1)}, u32[]{:S(2)}, u32[]{:S(2)}) %collective-permute-start.9) | collective-permute-done | bytes 69664 | tf_op jit(solution)/shard_map/ppermute | solution.py:23
  26.8 0.0 collective-permute-done.10.refs_1_
  26.8 2.5 %collective-permute-done.11.refs_2_ = f32[136,128]{1,0:T(8,128)S(1)} collective-permute-done((f32[136,128]{1,0:T(8,128)S(1)}, f32[136,128]{1,0:T(8,128)S(1)}, u32[]{:S(2)}, u32[]{:S(2)}) %collective-permute-start.11) | collective-permute-done | bytes 69664 | tf_op jit(solution)/shard_map/ppermute | solution.py:23
  29.3 2.0 %collective-permute-start.12 = (f32[136,128]{1,0:T(8,128)S(1)}, f32[136,128]{1,0:T(8,128)S(1)}, u32[]{:S(2)}, u32[]{:S(2)}) collective-permute-start(f32[136,128]{1,0:T(8,128)S(1)} %get-tuple-element.44), channel_id=1, source_target_pairs={{0,8},{1,9},{2,10},{3,11},{4,12},{5,13},{6,14},{7,15},{8,16},{9,17... | collective-permute-start | bytes 208904 | tf_op jit(solution)/shard_map/ppermute | solution.py:18
  31.3 1.4 %collective-permute-start.14 = (f32[8,128]{1,0:T(8,128)S(1)}, f32[8,128]{1,0:T(8,128)S(1)}, u32[]{:S(2)}, u32[]{:S(2)}) collective-permute-start(f32[8,128]{1,0:T(8,128)S(1)} %get-tuple-element.43.sums_ref), channel_id=1, source_target_pairs={{0,16},{1,17},{2,18},{3,19},{4,20},{5,21},{6,22},{7,23},{8,24},{9,... | collective-permute-start | bytes 12296 | tf_op jit(solution)/shard_map/ppermute | solution.py:18
  32.7 1.1 %collective-permute-start.13 = (f32[136,128]{1,0:T(8,128)S(1)}, f32[136,128]{1,0:T(8,128)S(1)}, u32[]{:S(2)}, u32[]{:S(2)}) collective-permute-start(f32[136,128]{1,0:T(8,128)S(1)} %get-tuple-element.47), channel_id=1, source_target_pairs={{0,24},{1,25},{2,26},{3,27},{4,28},{5,29},{6,30},{7,31},{8,0},{9,1... | collective-permute-start | bytes 208904 | tf_op jit(solution)/shard_map/ppermute | solution.py:18
  33.8 2.0 %collective-permute-done.12.next_ref = f32[136,128]{1,0:T(8,128)S(1)} collective-permute-done((f32[136,128]{1,0:T(8,128)S(1)}, f32[136,128]{1,0:T(8,128)S(1)}, u32[]{:S(2)}, u32[]{:S(2)}) %collective-permute-start.12) | collective-permute-done | bytes 69664 | tf_op jit(solution)/shard_map/ppermute | solution.py:18
  35.8 0.1 collective-permute-done.14.refs_0_
  35.9 1.2 %collective-permute-done.13.last_ref = f32[136,128]{1,0:T(8,128)S(1)} collective-permute-done((f32[136,128]{1,0:T(8,128)S(1)}, f32[136,128]{1,0:T(8,128)S(1)}, u32[]{:S(2)}, u32[]{:S(2)}) %collective-permute-start.13) | collective-permute-done | bytes 69664 | tf_op jit(solution)/shard_map/ppermute | solution.py:18
  37.0 0.7 %shard_map.58 = (f32[128,128]{1,0:T(8,128)}, f32[128,128]{1,0:T(8,128)}) custom-call(f32[128,128]{1,0:T(8,128)S(1)} %shard_map.50.own_ref.right_ref, f32[128,128]{1,0:T(8,128)S(1)} %get-tuple-element.45.near_ref, f32[8,128]{1,0:T(8,128)S(1)} %get-tuple-element.46.sums_ref, f32[136,128]{1,0:T(8,128)S(1)} %collective-permute-done.13.last_ref, ...), custom_call_target="tpu_custom_call" | custom-call | tf_op jit(solution)/shard_map/pallas_call | solution.py:207
  (8 shorter events, 0.2 us)
Async XLA Ops:
  0.6 7.7 %collective-permute-start = (f32[128,128]{1,0:T(8,128)}, f32[128,128]{1,0:T(8,128)S(1)}, u32[]{:S(2)}, u32[]{:S(2)}) collective-permute-start(f32[128,128]{1,0:T(8,128)} %block_ref.1), channel_id=1, source_target_pairs={{0,8},{1,9},{2,10},{3,11},{4,12},{5,13},{6,14},{7,15},{8,16},{9,17... | collective-permute-start | bytes 196616 | tf_op jit(solution)/shard_map/ppermute | solution.py:18
  3.7 5.2 %collective-permute-start.1 = (f32[128,128]{1,0:T(8,128)}, f32[128,128]{1,0:T(8,128)S(1)}, u32[]{:S(2)}, u32[]{:S(2)}) collective-permute-start(f32[128,128]{1,0:T(8,128)} %block_ref.1), channel_id=1, source_target_pairs={{0,24},{1,25},{2,26},{3,27},{4,28},{5,29},{6,30},{7,31},{8,0},{9,1... | collective-permute-start | bytes 196616 | tf_op jit(solution)/shard_map/ppermute | solution.py:18
  5.8 6.7 %collective-permute-start.2 = (f32[128,128]{1,0:T(8,128)}, f32[128,128]{1,0:T(8,128)S(1)}, u32[]{:S(2)}, u32[]{:S(2)}) collective-permute-start(f32[128,128]{1,0:T(8,128)} %block_ref.1), channel_id=1, source_target_pairs={{0,16},{1,17},{2,18},{3,19},{4,20},{5,21},{6,22},{7,23},{8,24},{9,... | collective-permute-start | bytes 196616 | tf_op jit(solution)/shard_map/ppermute | solution.py:18
  6.7 0.9 %copy-start = (f32[128,128]{1,0:T(8,128)S(1)}, f32[128,128]{1,0:T(8,128)}, u32[]{:S(2)}) copy-start(f32[128,128]{1,0:T(8,128)} %block_ref.1) | copy-start | bytes 196612
  8.9 5.8 %collective-permute-start.5 = (f32[128,128]{1,0:T(8,128)S(1)}, f32[128,128]{1,0:T(8,128)S(1)}, u32[]{:S(2)}, u32[]{:S(2)}) collective-permute-start(f32[128,128]{1,0:T(8,128)S(1)} %get-tuple-element.49), channel_id=1, source_target_pairs={{0,6},{1,7},{2,4},{3,5},{4,2},{5,3},{6,0},{7,1},{8,14},{9,15},{10,... | collective-permute-start | bytes 196616 | tf_op jit(solution)/shard_map/ppermute | solution.py:23
  11.4 4.3 %collective-permute-start.4 = (f32[128,128]{1,0:T(8,128)S(1)}, f32[128,128]{1,0:T(8,128)S(1)}, u32[]{:S(2)}, u32[]{:S(2)}) collective-permute-start(f32[128,128]{1,0:T(8,128)S(1)} %get-tuple-element.50), channel_id=1, source_target_pairs={{0,4},{1,5},{2,6},{3,7},{4,0},{5,1},{6,2},{7,3},{8,12},{9,13},{10,... | collective-permute-start | bytes 196616 | tf_op jit(solution)/shard_map/ppermute | solution.py:23
  11.9 4.4 %copy-start.2 = (f32[1,17,128,128]{3,2,1,0:T(8,128)S(1)}, f32[1,17,128,128]{3,2,1,0:T(8,128)}, u32[]{:S(2)}) copy-start(f32[1,17,128,128]{3,2,1,0:T(8,128)} %param.4) | copy-start | bytes 3342340
  11.9 4.3 %collective-permute-start.3 = (f32[128,128]{1,0:T(8,128)S(1)}, f32[128,128]{1,0:T(8,128)S(1)}, u32[]{:S(2)}, u32[]{:S(2)}) collective-permute-start(f32[128,128]{1,0:T(8,128)S(1)} %get-tuple-element.51), channel_id=1, source_target_pairs={{0,2},{1,3},{2,0},{3,1},{4,6},{5,7},{6,4},{7,5},{8,10},{9,11},{10,... | collective-permute-start | bytes 196616 | tf_op jit(solution)/shard_map/ppermute | solution.py:23
  16.2 1.6 %collective-permute-start.6 = (f32[4,128,128]{2,1,0:T(8,128)S(1)}, f32[4,128,128]{2,1,0:T(8,128)S(1)}, u32[]{:S(2)}, u32[]{:S(2)}) collective-permute-start(f32[4,128,128]{2,1,0:T(8,128)S(1)} %pad_maximum_fusion), channel_id=1, source_target_pairs={{0,1},{1,0},{2,3},{3,2},{4,5},{5,4},{6,7},{7,6},{8,9},{9,8},{10,11... | collective-permute-start | bytes 786440 | tf_op jit(solution)/shard_map/ppermute | solution.py:28
  16.3 1.5 %copy-start.1 = (s32[17,2]{0,1:T(2,128)S(1)}, s32[17,2]{0,1:T(2,128)}, u32[]{:S(2)}) copy-start(s32[17,2]{0,1:T(2,128)} %param.5) | copy-start | bytes 412
  19.5 2.4 %collective-permute-start.7 = (f32[520,128]{1,0:T(8,128)S(1)}, f32[520,128]{1,0:T(8,128)S(1)}, u32[]{:S(2)}, u32[]{:S(2)}) collective-permute-start(f32[520,128]{1,0:T(8,128)S(1)} %get-tuple-element.32.sent_ref), channel_id=1, source_target_pairs={{0,1},{1,0},{2,3},{3,2},{4,5},{5,4},{6,7},{7,6},{8,9},{9,8},{10,11... | collective-permute-start | bytes 798728 | tf_op jit(solution)/shard_map/ppermute | solution.py:28
  19.7 5.8 %collective-permute-start.8 = (f32[128,128]{1,0:T(8,128)S(1)}, f32[128,128]{1,0:T(8,128)S(1)}, u32[]{:S(2)}, u32[]{:S(2)}) collective-permute-start(f32[128,128]{1,0:T(8,128)S(1)} %get-tuple-element.35), channel_id=1, source_target_pairs={{0,16},{1,17},{2,18},{3,19},{4,20},{5,21},{6,22},{7,23},{8,24},{9,... | collective-permute-start | bytes 196616 | tf_op jit(solution)/shard_map/ppermute | solution.py:18
  22.0 4.8 %collective-permute-start.9 = (f32[136,128]{1,0:T(8,128)S(1)}, f32[136,128]{1,0:T(8,128)S(1)}, u32[]{:S(2)}, u32[]{:S(2)}) collective-permute-start(f32[136,128]{1,0:T(8,128)S(1)} %get-tuple-element.39), channel_id=1, source_target_pairs={{0,2},{1,3},{2,0},{3,1},{4,6},{5,7},{6,4},{7,5},{8,10},{9,11},{10,... | collective-permute-start | bytes 208904 | tf_op jit(solution)/shard_map/ppermute | solution.py:23
  22.4 4.5 %collective-permute-start.10 = (f32[136,128]{1,0:T(8,128)S(1)}, f32[136,128]{1,0:T(8,128)S(1)}, u32[]{:S(2)}, u32[]{:S(2)}) collective-permute-start(f32[136,128]{1,0:T(8,128)S(1)} %get-tuple-element.40), channel_id=1, source_target_pairs={{0,4},{1,5},{2,6},{3,7},{4,0},{5,1},{6,2},{7,3},{8,12},{9,13},{10,... | collective-permute-start | bytes 208904 | tf_op jit(solution)/shard_map/ppermute | solution.py:23
  24.1 5.2 %collective-permute-start.11 = (f32[136,128]{1,0:T(8,128)S(1)}, f32[136,128]{1,0:T(8,128)S(1)}, u32[]{:S(2)}, u32[]{:S(2)}) collective-permute-start(f32[136,128]{1,0:T(8,128)S(1)} %get-tuple-element.41), channel_id=1, source_target_pairs={{0,6},{1,7},{2,4},{3,5},{4,2},{5,3},{6,0},{7,1},{8,14},{9,15},{10,... | collective-permute-start | bytes 208904 | tf_op jit(solution)/shard_map/ppermute | solution.py:23
  29.3 6.4 %collective-permute-start.12 = (f32[136,128]{1,0:T(8,128)S(1)}, f32[136,128]{1,0:T(8,128)S(1)}, u32[]{:S(2)}, u32[]{:S(2)}) collective-permute-start(f32[136,128]{1,0:T(8,128)S(1)} %get-tuple-element.44), channel_id=1, source_target_pairs={{0,8},{1,9},{2,10},{3,11},{4,12},{5,13},{6,14},{7,15},{8,16},{9,17... | collective-permute-start | bytes 208904 | tf_op jit(solution)/shard_map/ppermute | solution.py:18
  31.3 4.5 %collective-permute-start.14 = (f32[8,128]{1,0:T(8,128)S(1)}, f32[8,128]{1,0:T(8,128)S(1)}, u32[]{:S(2)}, u32[]{:S(2)}) collective-permute-start(f32[8,128]{1,0:T(8,128)S(1)} %get-tuple-element.43.sums_ref), channel_id=1, source_target_pairs={{0,16},{1,17},{2,18},{3,19},{4,20},{5,21},{6,22},{7,23},{8,24},{9,... | collective-permute-start | bytes 12296 | tf_op jit(solution)/shard_map/ppermute | solution.py:18
  32.7 4.3 %collective-permute-start.13 = (f32[136,128]{1,0:T(8,128)S(1)}, f32[136,128]{1,0:T(8,128)S(1)}, u32[]{:S(2)}, u32[]{:S(2)}) collective-permute-start(f32[136,128]{1,0:T(8,128)S(1)} %get-tuple-element.47), channel_id=1, source_target_pairs={{0,24},{1,25},{2,26},{3,27},{4,28},{5,29},{6,30},{7,31},{8,0},{9,1... | collective-permute-start | bytes 208904 | tf_op jit(solution)/shard_map/ppermute | solution.py:18

commit v16 on v15

--- a/solution.py
+++ b/solution.py
@@ -82,13 +82,15 @@
     return ((chip ^ mask) - chip) & (chips - 1)
 
 
-def product_kernel(planes, chips, pairs_ref, place_ref, own_ref, *refs):
+def product_kernel(planes, chips, place_ref, table_ref, own_ref, *refs):
     window = 2 * chips
     far = refs[: planes - 1]
     even = refs[planes - 1 : planes + chips - 2]
     odd_ref, middle_ref, straight_ref, turned_ref, message_ref, kept_ref = refs[planes + chips - 2 : planes + chips + 4]
-    far_out = refs[planes + chips + 4 : -3]
-    whole, parts, total = refs[-3:]
+    far_out = refs[planes + chips + 4 : -4]
+    parts, total, pairs_ref, fetched = refs[-4:]
+    fetch = pltpu.make_async_copy(table_ref, pairs_ref, fetched)
+    fetch.start()
     rows, cols = own_ref.shape
     chip, core = place_of(place_ref, chips)
     spare = jnp.where(core == 0, 1, window - 1)
@@ -99,23 +101,26 @@
         parts[place, rows:, :cols] = high
         parts[place, rows:, cols:] = jnp.zeros_like(low)
 
-    def put(place, values):
-        whole[place] = values
-        put_parts(place, *split_two(values))
-
-    put(0, own_ref[...])
+    blocks = []
+
+    def put(place, block_ref):
+        blocks.append((place, block_ref))
+        put_parts(place, *split_two(block_ref[...]))
+
+    put(0, own_ref)
     for k in (1, planes - 1):
-        put(window - 1 + k, far[k - 1][...])
+        put(window - 1 + k, far[k - 1])
     for k in range(2, planes - 1):
-        whole[window - 1 + k] = far[k - 1][...]
+        blocks.append((window - 1 + k, far[k - 1]))
         put_parts(window - 1 + k, middle_ref[k - 2, :, :cols], middle_ref[k - 2, :, cols:])
     for m in range(1, chips):
         ahead = 2 * steps_ahead(chip, m, chips)
-        put(ahead, even[m - 1][...])
-        put(ahead + 1 - 2 * core, odd_ref[m])
-    put(spare, odd_ref[0])
+        put(ahead, even[m - 1])
+        put(ahead + 1 - 2 * core, odd_ref.at[m])
+    put(spare, odd_ref.at[0])
 
     total[...] = jnp.zeros_like(total)
+    fetch.wait()
     slots = straight_ref.shape[0]
 
     def product(split_ref, t, place):
@@ -137,8 +142,8 @@
     visit(slots - 1, False)
 
     dots = jnp.zeros((1, cols), jnp.float32)
-    for place in range(whole.shape[0]):
-        dots = dots + jnp.sum(whole[place] * total[place], axis=0, keepdims=True)
+    for place, block_ref in blocks:
+        dots = dots + jnp.sum(block_ref[...] * total[place], axis=0, keepdims=True)
     own = own_ref[...]
     norm = jnp.sum(own * own, axis=0, keepdims=True)
     sums = jnp.concatenate([norm, dots, jnp.zeros((EXTRA - 2, cols), jnp.float32)], axis=0)
@@ -249,13 +254,14 @@
 
     sent, kept, *far_out = call(
         functools.partial(product_kernel, planes, chips),
-        (route_pairs.T, where),
-        (own, *[far[k] for k in range(1, planes)], *even, odd, middle_parts, straight, turned),
+        (where,),
+        (route_pairs.T, own, *[far[k] for k in range(1, planes)], *even, odd, middle_parts, straight, turned),
         [((chips * rows + EXTRA, cols), single), ((chips + 1, rows, cols), single)] + [block] * (planes - 2),
         (
-            pltpu.VMEM((cover_len, rows, cols), single),
             pltpu.VMEM((cover_len, 2 * rows, 2 * cols), half),
             pltpu.VMEM((cover_len, rows, cols), single),
+            pltpu.SMEM((2, slots), jnp.int32),
+            pltpu.SemaphoreType.DMA,
         ),
     )
     got = core_partner(sent)

time: 37.9 us -> 37.7 us (level)
  no operation moved by 1% of the time
where the time goes in v16:
time: 37.7 us; the launch traced here: 37.5 us
  starting transfers between devices  20.1 us (53%)
  waiting for transfers between devices  13.1 us (35%)
  Pallas kernels  2.7 us (7%)
  local copies, waits for them, and re-layouts  0.88 us (2%)
  between operations  0.7 us (2%)
    ppermute x7, starting transfers between devices, shifted(): return lax.ppermute(value, 'blk', pairs)  12.7 us
    ppermute x6, waiting for transfers between devices, chip_partner(): lax.ppermute(value, 'blk', [(source, source ^ 2 * mask) for source in ran...  7.47 us
    ppermute x6, starting transfers between devices, chip_partner(): lax.ppermute(value, 'blk', [(source, source ^ 2 * mask) for source in ran...  7.11 us
    ppermute x7, waiting for transfers between devices, shifted(): return lax.ppermute(value, 'blk', pairs)  4.5 us
    pallas_call x9, Pallas kernels, call(): pl.pallas_call(kernel, in_specs=[pl.BlockSpec(memory_space=pltpu.SMEM)] *...  2.7 us
    ppermute x2, waiting for transfers between devices, core_partner(): lax.ppermute(value, 'blk', [(source, source ^ 1) for source in range(coun...  1.1 us
    unnamed x6, local copies, waits for them, and re-layouts  0.88 us
  transfers between devices with their start and end apart: 15, of which 11 were waited for; matrix products, arithmetic and copies ran while one was open for 0% of the time, Pallas kernels for 1%

profile of v16, /device:TPU:0, one launch (start us, length us, event | category | flops | bytes accessed | tf_op | source)
XLA Modules:
  0.0 37.5 jit_solution(15984236463668608541)
XLA Ops:
  0.6 3.1 %collective-permute-start = (f32[128,128]{1,0:T(8,128)}, f32[128,128]{1,0:T(8,128)S(1)}, u32[]{:S(2)}, u32[]{:S(2)}) collective-permute-start(f32[128,128]{1,0:T(8,128)} %block_ref.1), channel_id=1, source_target_pairs={{0,8},{1,9},{2,10},{3,11},{4,12},{5,13},{6,14},{7,15},{8,16},{9,17... | collective-permute-start | bytes 196616 | tf_op jit(solution)/shard_map/ppermute | solution.py:18
  3.7 2.1 %collective-permute-start.1 = (f32[128,128]{1,0:T(8,128)}, f32[128,128]{1,0:T(8,128)S(1)}, u32[]{:S(2)}, u32[]{:S(2)}) collective-permute-start(f32[128,128]{1,0:T(8,128)} %block_ref.1), channel_id=1, source_target_pairs={{0,24},{1,25},{2,26},{3,27},{4,28},{5,29},{6,30},{7,31},{8,0},{9,1... | collective-permute-start | bytes 196616 | tf_op jit(solution)/shard_map/ppermute | solution.py:18
  5.8 0.9 %collective-permute-start.2 = (f32[128,128]{1,0:T(8,128)}, f32[128,128]{1,0:T(8,128)S(1)}, u32[]{:S(2)}, u32[]{:S(2)}) collective-permute-start(f32[128,128]{1,0:T(8,128)} %block_ref.1), channel_id=1, source_target_pairs={{0,16},{1,17},{2,18},{3,19},{4,20},{5,21},{6,22},{7,23},{8,24},{9,... | collective-permute-start | bytes 196616 | tf_op jit(solution)/shard_map/ppermute | solution.py:18
  6.7 0.0 copy-start
  6.7 0.9 %copy-done = f32[128,128]{1,0:T(8,128)S(1)} copy-done((f32[128,128]{1,0:T(8,128)S(1)}, f32[128,128]{1,0:T(8,128)}, u32[]{:S(2)}) %copy-start) | copy-done | bytes 65560
  7.6 0.7 %collective-permute-done.refs_2_ = f32[128,128]{1,0:T(8,128)S(1)} collective-permute-done((f32[128,128]{1,0:T(8,128)}, f32[128,128]{1,0:T(8,128)S(1)}, u32[]{:S(2)}, u32[]{:S(2)}) %collective-permute-start) | collective-permute-done | bytes 65568 | tf_op jit(solution)/shard_map/ppermute | solution.py:18
  8.3 0.5 %collective-permute-done.1.refs_0_ = f32[128,128]{1,0:T(8,128)S(1)} collective-permute-done((f32[128,128]{1,0:T(8,128)}, f32[128,128]{1,0:T(8,128)S(1)}, u32[]{:S(2)}, u32[]{:S(2)}) %collective-permute-start.1) | collective-permute-done | bytes 65568 | tf_op jit(solution)/shard_map/ppermute | solution.py:18
  8.9 2.5 %collective-permute-start.5 = (f32[128,128]{1,0:T(8,128)S(1)}, f32[128,128]{1,0:T(8,128)S(1)}, u32[]{:S(2)}, u32[]{:S(2)}) collective-permute-start(f32[128,128]{1,0:T(8,128)S(1)} %get-tuple-element.49), channel_id=1, source_target_pairs={{0,6},{1,7},{2,4},{3,5},{4,2},{5,3},{6,0},{7,1},{8,14},{9,15},{10,... | collective-permute-start | bytes 196616 | tf_op jit(solution)/shard_map/ppermute | solution.py:23
  11.4 0.5 %collective-permute-start.4 = (f32[128,128]{1,0:T(8,128)S(1)}, f32[128,128]{1,0:T(8,128)S(1)}, u32[]{:S(2)}, u32[]{:S(2)}) collective-permute-start(f32[128,128]{1,0:T(8,128)S(1)} %get-tuple-element.50), channel_id=1, source_target_pairs={{0,4},{1,5},{2,6},{3,7},{4,0},{5,1},{6,2},{7,3},{8,12},{9,13},{10,... | collective-permute-start | bytes 196616 | tf_op jit(solution)/shard_map/ppermute | solution.py:23
  11.9 0.0 copy-start.2
  11.9 0.5 %collective-permute-start.3 = (f32[128,128]{1,0:T(8,128)S(1)}, f32[128,128]{1,0:T(8,128)S(1)}, u32[]{:S(2)}, u32[]{:S(2)}) collective-permute-start(f32[128,128]{1,0:T(8,128)S(1)} %get-tuple-element.51), channel_id=1, source_target_pairs={{0,2},{1,3},{2,0},{3,1},{4,6},{5,7},{6,4},{7,5},{8,10},{9,11},{10,... | collective-permute-start | bytes 196616 | tf_op jit(solution)/shard_map/ppermute | solution.py:23
  12.5 0.0 collective-permute-done.2.refs_0_.refs_1_
  12.5 2.2 %collective-permute-done.5.refs_5_ = f32[128,128]{1,0:T(8,128)S(1)} collective-permute-done((f32[128,128]{1,0:T(8,128)S(1)}, f32[128,128]{1,0:T(8,128)S(1)}, u32[]{:S(2)}, u32[]{:S(2)}) %collective-permute-start.5) | collective-permute-done | bytes 65568 | tf_op jit(solution)/shard_map/ppermute | solution.py:23
  14.7 1.0 %collective-permute-done.4.refs_4_ = f32[128,128]{1,0:T(8,128)S(1)} collective-permute-done((f32[128,128]{1,0:T(8,128)S(1)}, f32[128,128]{1,0:T(8,128)S(1)}, u32[]{:S(2)}, u32[]{:S(2)}) %collective-permute-start.4) | collective-permute-done | bytes 65568 | tf_op jit(solution)/shard_map/ppermute | solution.py:23
  15.7 0.5 %collective-permute-done.3.refs_3_ = f32[128,128]{1,0:T(8,128)S(1)} collective-permute-done((f32[128,128]{1,0:T(8,128)S(1)}, f32[128,128]{1,0:T(8,128)S(1)}, u32[]{:S(2)}, u32[]{:S(2)}) %collective-permute-start.3) | collective-permute-done | bytes 65568 | tf_op jit(solution)/shard_map/ppermute | solution.py:23
  16.2 0.1 collective-permute-start.6
  16.3 0.0 copy-done.2
  16.3 0.0 copy-start.1
  16.3 0.4 %shard_map.52 = (bf16[17,128,256]{2,1,0:T(8,128)(2,1)S(1)}, bf16[17,128,256]{2,1,0:T(8,128)(2,1)S(1)}) custom-call(f32[17,128,128]{2,1,0:T(8,128)S(1)} %bitcast.12), custom_call_target="tpu_custom_call" | custom-call | flops 10000000000 | tf_op jit(solution)/shard_map/pallas_call | solution.py:212
  16.7 1.1 %collective-permute-done.6.refs_6_ = f32[4,128,128]{2,1,0:T(8,128)S(1)} collective-permute-done((f32[4,128,128]{2,1,0:T(8,128)S(1)}, f32[4,128,128]{2,1,0:T(8,128)S(1)}, u32[]{:S(2)}, u32[]{:S(2)}) %collective-permute-start.6) | collective-permute-done | bytes 262176 | tf_op jit(solution)/shard_map/ppermute | solution.py:28
  17.8 0.0 copy-done.1
  17.8 1.5 %shard_map.53 = (f32[520,128]{1,0:T(8,128)S(1)}, f32[5,128,128]{2,1,0:T(8,128)S(1)}, f32[128,128]{1,0:T(8,128)S(1)}, f32[128,128]{1,0:T(8,128)S(1)}) custom-call(s32[1]{0:T(128)} %bitcast.place_ref, s32[2,17]{1,0:T(2,128)S(1)} %bitcast.11, f32[128,128]{1,0:T(8,128)S(1)} %shard_map.50.own_ref.right_ref, f32[128,128]{1,0:T(8,128)S(1)} %collective-permute-done.1.refs_0_, ...), custom_call_target="tpu_custom_call" | custom-call | tf_op jit(solution)/shard_map/pallas_call | solution.py:212
  19.3 0.2 collective-permute-start.7
  19.5 2.2 %collective-permute-start.8 = (f32[128,128]{1,0:T(8,128)S(1)}, f32[128,128]{1,0:T(8,128)S(1)}, u32[]{:S(2)}, u32[]{:S(2)}) collective-permute-start(f32[128,128]{1,0:T(8,128)S(1)} %get-tuple-element.35), channel_id=1, source_target_pairs={{0,16},{1,17},{2,18},{3,19},{4,20},{5,21},{6,22},{7,23},{8,24},{9,... | collective-permute-start | bytes 196616 | tf_op jit(solution)/shard_map/ppermute | solution.py:18
  21.7 0.0 collective-permute-done.7.got_ref
  21.8 0.4 %collective-permute-start.9 = (f32[136,128]{1,0:T(8,128)S(1)}, f32[136,128]{1,0:T(8,128)S(1)}, u32[]{:S(2)}, u32[]{:S(2)}) collective-permute-start(f32[136,128]{1,0:T(8,128)S(1)} %get-tuple-element.39), channel_id=1, source_target_pairs={{0,2},{1,3},{2,0},{3,1},{4,6},{5,7},{6,4},{7,5},{8,10},{9,11},{10,... | collective-permute-start | bytes 208904 | tf_op jit(solution)/shard_map/ppermute | solution.py:23
  22.2 1.7 %collective-permute-start.10 = (f32[136,128]{1,0:T(8,128)S(1)}, f32[136,128]{1,0:T(8,128)S(1)}, u32[]{:S(2)}, u32[]{:S(2)}) collective-permute-start(f32[136,128]{1,0:T(8,128)S(1)} %get-tuple-element.40), channel_id=1, source_target_pairs={{0,4},{1,5},{2,6},{3,7},{4,0},{5,1},{6,2},{7,3},{8,12},{9,13},{10,... | collective-permute-start | bytes 208904 | tf_op jit(solution)/shard_map/ppermute | solution.py:23
  23.9 1.4 %collective-permute-start.11 = (f32[136,128]{1,0:T(8,128)S(1)}, f32[136,128]{1,0:T(8,128)S(1)}, u32[]{:S(2)}, u32[]{:S(2)}) collective-permute-start(f32[136,128]{1,0:T(8,128)S(1)} %get-tuple-element.41), channel_id=1, source_target_pairs={{0,6},{1,7},{2,4},{3,5},{4,2},{5,3},{6,0},{7,1},{8,14},{9,15},{10,... | collective-permute-start | bytes 208904 | tf_op jit(solution)/shard_map/ppermute | solution.py:23
  25.3 0.0 collective-permute-done.8.refs_0_
  25.4 1.3 %collective-permute-done.9.refs_0_ = f32[136,128]{1,0:T(8,128)S(1)} collective-permute-done((f32[136,128]{1,0:T(8,128)S(1)}, f32[136,128]{1,0:T(8,128)S(1)}, u32[]{:S(2)}, u32[]{:S(2)}) %collective-permute-start.9) | collective-permute-done | bytes 69664 | tf_op jit(solution)/shard_map/ppermute | solution.py:23
  26.6 0.0 collective-permute-done.10.refs_1_
  26.6 2.5 %collective-permute-done.11.refs_2_ = f32[136,128]{1,0:T(8,128)S(1)} collective-permute-done((f32[136,128]{1,0:T(8,128)S(1)}, f32[136,128]{1,0:T(8,128)S(1)}, u32[]{:S(2)}, u32[]{:S(2)}) %collective-permute-start.11) | collective-permute-done | bytes 69664 | tf_op jit(solution)/shard_map/ppermute | solution.py:23
  29.2 2.0 %collective-permute-start.12 = (f32[136,128]{1,0:T(8,128)S(1)}, f32[136,128]{1,0:T(8,128)S(1)}, u32[]{:S(2)}, u32[]{:S(2)}) collective-permute-start(f32[136,128]{1,0:T(8,128)S(1)} %get-tuple-element.44), channel_id=1, source_target_pairs={{0,8},{1,9},{2,10},{3,11},{4,12},{5,13},{6,14},{7,15},{8,16},{9,17... | collective-permute-start | bytes 208904 | tf_op jit(solution)/shard_map/ppermute | solution.py:18
  31.2 1.4 %collective-permute-start.14 = (f32[8,128]{1,0:T(8,128)S(1)}, f32[8,128]{1,0:T(8,128)S(1)}, u32[]{:S(2)}, u32[]{:S(2)}) collective-permute-start(f32[8,128]{1,0:T(8,128)S(1)} %get-tuple-element.43.sums_ref), channel_id=1, source_target_pairs={{0,16},{1,17},{2,18},{3,19},{4,20},{5,21},{6,22},{7,23},{8,24},{9,... | collective-permute-start | bytes 12296 | tf_op jit(solution)/shard_map/ppermute | solution.py:18
  32.5 1.1 %collective-permute-start.13 = (f32[136,128]{1,0:T(8,128)S(1)}, f32[136,128]{1,0:T(8,128)S(1)}, u32[]{:S(2)}, u32[]{:S(2)}) collective-permute-start(f32[136,128]{1,0:T(8,128)S(1)} %get-tuple-element.47), channel_id=1, source_target_pairs={{0,24},{1,25},{2,26},{3,27},{4,28},{5,29},{6,30},{7,31},{8,0},{9,1... | collective-permute-start | bytes 208904 | tf_op jit(solution)/shard_map/ppermute | solution.py:18
  33.6 2.0 %collective-permute-done.12.next_ref = f32[136,128]{1,0:T(8,128)S(1)} collective-permute-done((f32[136,128]{1,0:T(8,128)S(1)}, f32[136,128]{1,0:T(8,128)S(1)}, u32[]{:S(2)}, u32[]{:S(2)}) %collective-permute-start.12) | collective-permute-done | bytes 69664 | tf_op jit(solution)/shard_map/ppermute | solution.py:18
  35.6 0.1 collective-permute-done.14.refs_0_
  35.7 1.2 %collective-permute-done.13.last_ref = f32[136,128]{1,0:T(8,128)S(1)} collective-permute-done((f32[136,128]{1,0:T(8,128)S(1)}, f32[136,128]{1,0:T(8,128)S(1)}, u32[]{:S(2)}, u32[]{:S(2)}) %collective-permute-start.13) | collective-permute-done | bytes 69664 | tf_op jit(solution)/shard_map/ppermute | solution.py:18
  36.8 0.7 %shard_map.58 = (f32[128,128]{1,0:T(8,128)}, f32[128,128]{1,0:T(8,128)}) custom-call(f32[128,128]{1,0:T(8,128)S(1)} %shard_map.50.own_ref.right_ref, f32[128,128]{1,0:T(8,128)S(1)} %get-tuple-element.45.near_ref, f32[8,128]{1,0:T(8,128)S(1)} %get-tuple-element.46.sums_ref, f32[136,128]{1,0:T(8,128)S(1)} %collective-permute-done.13.last_ref, ...), custom_call_target="tpu_custom_call" | custom-call | tf_op jit(solution)/shard_map/pallas_call | solution.py:212
  (8 shorter events, 0.2 us)
Async XLA Ops:
  0.6 7.7 %collective-permute-start = (f32[128,128]{1,0:T(8,128)}, f32[128,128]{1,0:T(8,128)S(1)}, u32[]{:S(2)}, u32[]{:S(2)}) collective-permute-start(f32[128,128]{1,0:T(8,128)} %block_ref.1), channel_id=1, source_target_pairs={{0,8},{1,9},{2,10},{3,11},{4,12},{5,13},{6,14},{7,15},{8,16},{9,17... | collective-permute-start | bytes 196616 | tf_op jit(solution)/shard_map/ppermute | solution.py:18
  3.7 5.2 %collective-permute-start.1 = (f32[128,128]{1,0:T(8,128)}, f32[128,128]{1,0:T(8,128)S(1)}, u32[]{:S(2)}, u32[]{:S(2)}) collective-permute-start(f32[128,128]{1,0:T(8,128)} %block_ref.1), channel_id=1, source_target_pairs={{0,24},{1,25},{2,26},{3,27},{4,28},{5,29},{6,30},{7,31},{8,0},{9,1... | collective-permute-start | bytes 196616 | tf_op jit(solution)/shard_map/ppermute | solution.py:18
  5.8 6.7 %collective-permute-start.2 = (f32[128,128]{1,0:T(8,128)}, f32[128,128]{1,0:T(8,128)S(1)}, u32[]{:S(2)}, u32[]{:S(2)}) collective-permute-start(f32[128,128]{1,0:T(8,128)} %block_ref.1), channel_id=1, source_target_pairs={{0,16},{1,17},{2,18},{3,19},{4,20},{5,21},{6,22},{7,23},{8,24},{9,... | collective-permute-start | bytes 196616 | tf_op jit(solution)/shard_map/ppermute | solution.py:18
  6.7 0.9 %copy-start = (f32[128,128]{1,0:T(8,128)S(1)}, f32[128,128]{1,0:T(8,128)}, u32[]{:S(2)}) copy-start(f32[128,128]{1,0:T(8,128)} %block_ref.1) | copy-start | bytes 196612
  8.9 5.8 %collective-permute-start.5 = (f32[128,128]{1,0:T(8,128)S(1)}, f32[128,128]{1,0:T(8,128)S(1)}, u32[]{:S(2)}, u32[]{:S(2)}) collective-permute-start(f32[128,128]{1,0:T(8,128)S(1)} %get-tuple-element.49), channel_id=1, source_target_pairs={{0,6},{1,7},{2,4},{3,5},{4,2},{5,3},{6,0},{7,1},{8,14},{9,15},{10,... | collective-permute-start | bytes 196616 | tf_op jit(solution)/shard_map/ppermute | solution.py:23
  11.4 4.3 %collective-permute-start.4 = (f32[128,128]{1,0:T(8,128)S(1)}, f32[128,128]{1,0:T(8,128)S(1)}, u32[]{:S(2)}, u32[]{:S(2)}) collective-permute-start(f32[128,128]{1,0:T(8,128)S(1)} %get-tuple-element.50), channel_id=1, source_target_pairs={{0,4},{1,5},{2,6},{3,7},{4,0},{5,1},{6,2},{7,3},{8,12},{9,13},{10,... | collective-permute-start | bytes 196616 | tf_op jit(solution)/shard_map/ppermute | solution.py:23
  11.9 4.4 %copy-start.2 = (f32[1,17,128,128]{3,2,1,0:T(8,128)S(1)}, f32[1,17,128,128]{3,2,1,0:T(8,128)}, u32[]{:S(2)}) copy-start(f32[1,17,128,128]{3,2,1,0:T(8,128)} %param.4) | copy-start | bytes 3342340
  11.9 4.3 %collective-permute-start.3 = (f32[128,128]{1,0:T(8,128)S(1)}, f32[128,128]{1,0:T(8,128)S(1)}, u32[]{:S(2)}, u32[]{:S(2)}) collective-permute-start(f32[128,128]{1,0:T(8,128)S(1)} %get-tuple-element.51), channel_id=1, source_target_pairs={{0,2},{1,3},{2,0},{3,1},{4,6},{5,7},{6,4},{7,5},{8,10},{9,11},{10,... | collective-permute-start | bytes 196616 | tf_op jit(solution)/shard_map/ppermute | solution.py:23
  16.2 1.6 %collective-permute-start.6 = (f32[4,128,128]{2,1,0:T(8,128)S(1)}, f32[4,128,128]{2,1,0:T(8,128)S(1)}, u32[]{:S(2)}, u32[]{:S(2)}) collective-permute-start(f32[4,128,128]{2,1,0:T(8,128)S(1)} %pad_maximum_fusion), channel_id=1, source_target_pairs={{0,1},{1,0},{2,3},{3,2},{4,5},{5,4},{6,7},{7,6},{8,9},{9,8},{10,11... | collective-permute-start | bytes 786440 | tf_op jit(solution)/shard_map/ppermute | solution.py:28
  16.3 1.5 %copy-start.1 = (s32[17,2]{0,1:T(2,128)S(1)}, s32[17,2]{0,1:T(2,128)}, u32[]{:S(2)}) copy-start(s32[17,2]{0,1:T(2,128)} %param.5) | copy-start | bytes 412
  19.3 2.4 %collective-permute-start.7 = (f32[520,128]{1,0:T(8,128)S(1)}, f32[520,128]{1,0:T(8,128)S(1)}, u32[]{:S(2)}, u32[]{:S(2)}) collective-permute-start(f32[520,128]{1,0:T(8,128)S(1)} %get-tuple-element.32.sent_ref), channel_id=1, source_target_pairs={{0,1},{1,0},{2,3},{3,2},{4,5},{5,4},{6,7},{7,6},{8,9},{9,8},{10,11... | collective-permute-start | bytes 798728 | tf_op jit(solution)/shard_map/ppermute | solution.py:28
  19.5 5.8 %collective-permute-start.8 = (f32[128,128]{1,0:T(8,128)S(1)}, f32[128,128]{1,0:T(8,128)S(1)}, u32[]{:S(2)}, u32[]{:S(2)}) collective-permute-start(f32[128,128]{1,0:T(8,128)S(1)} %get-tuple-element.35), channel_id=1, source_target_pairs={{0,16},{1,17},{2,18},{3,19},{4,20},{5,21},{6,22},{7,23},{8,24},{9,... | collective-permute-start | bytes 196616 | tf_op jit(solution)/shard_map/ppermute | solution.py:18
  21.8 4.8 %collective-permute-start.9 = (f32[136,128]{1,0:T(8,128)S(1)}, f32[136,128]{1,0:T(8,128)S(1)}, u32[]{:S(2)}, u32[]{:S(2)}) collective-permute-start(f32[136,128]{1,0:T(8,128)S(1)} %get-tuple-element.39), channel_id=1, source_target_pairs={{0,2},{1,3},{2,0},{3,1},{4,6},{5,7},{6,4},{7,5},{8,10},{9,11},{10,... | collective-permute-start | bytes 208904 | tf_op jit(solution)/shard_map/ppermute | solution.py:23
  22.2 4.4 %collective-permute-start.10 = (f32[136,128]{1,0:T(8,128)S(1)}, f32[136,128]{1,0:T(8,128)S(1)}, u32[]{:S(2)}, u32[]{:S(2)}) collective-permute-start(f32[136,128]{1,0:T(8,128)S(1)} %get-tuple-element.40), channel_id=1, source_target_pairs={{0,4},{1,5},{2,6},{3,7},{4,0},{5,1},{6,2},{7,3},{8,12},{9,13},{10,... | collective-permute-start | bytes 208904 | tf_op jit(solution)/shard_map/ppermute | solution.py:23
  23.9 5.2 %collective-permute-start.11 = (f32[136,128]{1,0:T(8,128)S(1)}, f32[136,128]{1,0:T(8,128)S(1)}, u32[]{:S(2)}, u32[]{:S(2)}) collective-permute-start(f32[136,128]{1,0:T(8,128)S(1)} %get-tuple-element.41), channel_id=1, source_target_pairs={{0,6},{1,7},{2,4},{3,5},{4,2},{5,3},{6,0},{7,1},{8,14},{9,15},{10,... | collective-permute-start | bytes 208904 | tf_op jit(solution)/shard_map/ppermute | solution.py:23
  29.2 6.4 %collective-permute-start.12 = (f32[136,128]{1,0:T(8,128)S(1)}, f32[136,128]{1,0:T(8,128)S(1)}, u32[]{:S(2)}, u32[]{:S(2)}) collective-permute-start(f32[136,128]{1,0:T(8,128)S(1)} %get-tuple-element.44), channel_id=1, source_target_pairs={{0,8},{1,9},{2,10},{3,11},{4,12},{5,13},{6,14},{7,15},{8,16},{9,17... | collective-permute-start | bytes 208904 | tf_op jit(solution)/shard_map/ppermute | solution.py:18
  31.2 4.5 %collective-permute-start.14 = (f32[8,128]{1,0:T(8,128)S(1)}, f32[8,128]{1,0:T(8,128)S(1)}, u32[]{:S(2)}, u32[]{:S(2)}) collective-permute-start(f32[8,128]{1,0:T(8,128)S(1)} %get-tuple-element.43.sums_ref), channel_id=1, source_target_pairs={{0,16},{1,17},{2,18},{3,19},{4,20},{5,21},{6,22},{7,23},{8,24},{9,... | collective-permute-start | bytes 12296 | tf_op jit(solution)/shard_map/ppermute | solution.py:18
  32.5 4.3 %collective-permute-start.13 = (f32[136,128]{1,0:T(8,128)S(1)}, f32[136,128]{1,0:T(8,128)S(1)}, u32[]{:S(2)}, u32[]{:S(2)}) collective-permute-start(f32[136,128]{1,0:T(8,128)S(1)} %get-tuple-element.47), channel_id=1, source_target_pairs={{0,24},{1,25},{2,26},{3,27},{4,28},{5,29},{6,30},{7,31},{8,0},{9,1... | collective-permute-start | bytes 208904 | tf_op jit(solution)/shard_map/ppermute | solution.py:18

commit v17 on v16

--- a/solution.py
+++ b/solution.py
@@ -9,6 +9,8 @@
 
 EXTRA = 8
 VMEM_BYTES = 48 * 1024 * 1024
+STEP = pl.CostEstimate(flops=4 * 10**7, bytes_accessed=0, transcendentals=0)
+AFTER = pl.CostEstimate(flops=73 * 10**7, bytes_accessed=0, transcendentals=0)
 BESIDE = pl.CostEstimate(flops=10**10, bytes_accessed=0, transcendentals=0)
 
 
@@ -174,12 +176,12 @@
     sums_ref[...] = sums
 
 
-def plane_kernel(chips, place_ref, near_ref, middle_ref, next_ref, sums_ref, last_ref, *refs):
+def plane_kernel(chips, place_ref, near_ref, next_ref, sums_ref, last_ref, *refs):
     got = refs[: chips - 1]
     next_out, last_out, near_out, sums_out = refs[chips - 1 :]
     rows = near_ref.shape[0]
     chip = place_of(place_ref, chips)[0]
-    near, ahead, sums = near_ref[...] + middle_ref[...], next_ref[...], sums_ref[...]
+    near, ahead, sums = near_ref[...], next_ref[...], sums_ref[...]
     for m in range(1, chips):
         block = got[m - 1][:rows, :]
         same = (chip ^ m) < chip
@@ -194,10 +196,10 @@
         message[rows:, :] = sums
 
 
-def final_kernel(right_ref, near_ref, sums_ref, last_ref, *refs):
+def final_kernel(right_ref, near_ref, middle_ref, sums_ref, last_ref, *refs):
     solution_ref, residual_ref = refs[-2:]
     rows = near_ref.shape[0]
-    image = near_ref[...] + last_ref[:rows, :]
+    image = near_ref[...] + middle_ref[...] + last_ref[:rows, :]
     sums = sums_ref[...] + last_ref[rows:, :]
     for more in refs[:-2]:
         sums = sums + more[...]
@@ -270,18 +272,18 @@
     )
     middle_got = [shifted(far_out[k - 2], k * window) for k in middle]
     got = [chip_partner(value, m) for m, value in enumerate(messages, 1)]
-    (middle_sum,) = call(add_kernel, (), middle_got, [block], cost=BESIDE)
+    (middle_sum,) = call(add_kernel, (), middle_got, [block], cost=AFTER)
     ahead, last, near, sums = call(
         functools.partial(plane_kernel, chips),
         (where,),
-        (near, middle_sum, ahead, sums, far_out[-1], *got),
+        (near, ahead, sums, far_out[-1], *got),
         [marked, marked, block, extra],
     )
     got = shifted(ahead, window)
     more = [shifted(sums, k * window) for k in middle]
     last = shifted(last, (planes - 1) * window)
-    near, sums = call(near_kernel, (), (near, sums, got), [block, extra], cost=BESIDE)
-    return call(final_kernel, (), (own, near, sums, last, *more), [block, block])
+    near, sums = call(near_kernel, (), (near, sums, got), [block, extra], cost=STEP)
+    return call(final_kernel, (), (own, near, middle_sum, sums, last, *more), [block, block])
 
 
 def solution(mesh):

time: 37.7 us -> 37.7 us (level)
  waiting for transfers between devices: 13.1 us -> 12.3 us
  starting transfers between devices: 20.1 us -> 20.9 us
    ppermute x6, waiting for transfers between devices: 7.47 us -> 5.29 us  [chip_partner(): lax.ppermute(value, 'blk', [(source, source ^ 2 * mask) for source in ran...]
    ppermute x2, waiting for transfers between devices: 1.1 us -> 2.5 us  [core_partner(): lax.ppermute(value, 'blk', [(source, source ^ 1) for source in range(coun...]
    ppermute x7, starting transfers between devices: 12.7 us -> 13.5 us  [shifted(): return lax.ppermute(value, 'blk', pairs)]
where the time goes in v17:
time: 37.7 us; the launch traced here: 37.5 us
  starting transfers between devices  20.9 us (55%)
  waiting for transfers between devices  12.3 us (33%)
  Pallas kernels  2.7 us (7%)
  local copies, waits for them, and re-layouts  0.88 us (2%)
  between operations  0.7 us (2%)
    ppermute x7, starting transfers between devices, shifted(): return lax.ppermute(value, 'blk', pairs)  13.5 us
    ppermute x6, starting transfers between devices, chip_partner(): lax.ppermute(value, 'blk', [(source, source ^ 2 * mask) for source in ran...  7.11 us
    ppermute x6, waiting for transfers between devices, chip_partner(): lax.ppermute(value, 'blk', [(source, source ^ 2 * mask) for source in ran...  5.29 us
    ppermute x7, waiting for transfers between devices, shifted(): return lax.ppermute(value, 'blk', pairs)  4.55 us
    pallas_call x9, Pallas kernels, call(): pl.pallas_call(kernel, in_specs=[pl.BlockSpec(memory_space=pltpu.SMEM)] *...  2.7 us
    ppermute x2, waiting for transfers between devices, core_partner(): lax.ppermute(value, 'blk', [(source, source ^ 1) for source in range(coun...  2.5 us
    unnamed x6, local copies, waits for them, and re-layouts  0.88 us
  transfers between devices with their start and end apart: 15, of which 11 were waited for; matrix products, arithmetic and copies ran while one was open for 0% of the time, Pallas kernels for 1%

profile of v17, /device:TPU:0, one launch (start us, length us, event | category | flops | bytes accessed | tf_op | source)
XLA Modules:
  0.0 37.5 jit_solution(12316444769697540808)
XLA Ops:
  0.6 3.1 %collective-permute-start = (f32[128,128]{1,0:T(8,128)}, f32[128,128]{1,0:T(8,128)S(1)}, u32[]{:S(2)}, u32[]{:S(2)}) collective-permute-start(f32[128,128]{1,0:T(8,128)} %block_ref.1), channel_id=1, source_target_pairs={{0,8},{1,9},{2,10},{3,11},{4,12},{5,13},{6,14},{7,15},{8,16},{9,17... | collective-permute-start | bytes 196616 | tf_op jit(solution)/shard_map/ppermute | solution.py:20
  3.7 2.1 %collective-permute-start.1 = (f32[128,128]{1,0:T(8,128)}, f32[128,128]{1,0:T(8,128)S(1)}, u32[]{:S(2)}, u32[]{:S(2)}) collective-permute-start(f32[128,128]{1,0:T(8,128)} %block_ref.1), channel_id=1, source_target_pairs={{0,24},{1,25},{2,26},{3,27},{4,28},{5,29},{6,30},{7,31},{8,0},{9,1... | collective-permute-start | bytes 196616 | tf_op jit(solution)/shard_map/ppermute | solution.py:20
  5.8 0.9 %collective-permute-start.2 = (f32[128,128]{1,0:T(8,128)}, f32[128,128]{1,0:T(8,128)S(1)}, u32[]{:S(2)}, u32[]{:S(2)}) collective-permute-start(f32[128,128]{1,0:T(8,128)} %block_ref.1), channel_id=1, source_target_pairs={{0,16},{1,17},{2,18},{3,19},{4,20},{5,21},{6,22},{7,23},{8,24},{9,... | collective-permute-start | bytes 196616 | tf_op jit(solution)/shard_map/ppermute | solution.py:20
  6.7 0.0 copy-start
  6.7 0.9 %copy-done = f32[128,128]{1,0:T(8,128)S(1)} copy-done((f32[128,128]{1,0:T(8,128)S(1)}, f32[128,128]{1,0:T(8,128)}, u32[]{:S(2)}) %copy-start) | copy-done | bytes 65560
  7.6 0.7 %collective-permute-done.refs_2_ = f32[128,128]{1,0:T(8,128)S(1)} collective-permute-done((f32[128,128]{1,0:T(8,128)}, f32[128,128]{1,0:T(8,128)S(1)}, u32[]{:S(2)}, u32[]{:S(2)}) %collective-permute-start) | collective-permute-done | bytes 65568 | tf_op jit(solution)/shard_map/ppermute | solution.py:20
  8.3 0.5 %collective-permute-done.1.refs_0_ = f32[128,128]{1,0:T(8,128)S(1)} collective-permute-done((f32[128,128]{1,0:T(8,128)}, f32[128,128]{1,0:T(8,128)S(1)}, u32[]{:S(2)}, u32[]{:S(2)}) %collective-permute-start.1) | collective-permute-done | bytes 65568 | tf_op jit(solution)/shard_map/ppermute | solution.py:20
  8.9 2.5 %collective-permute-start.5 = (f32[128,128]{1,0:T(8,128)S(1)}, f32[128,128]{1,0:T(8,128)S(1)}, u32[]{:S(2)}, u32[]{:S(2)}) collective-permute-start(f32[128,128]{1,0:T(8,128)S(1)} %get-tuple-element.49), channel_id=1, source_target_pairs={{0,6},{1,7},{2,4},{3,5},{4,2},{5,3},{6,0},{7,1},{8,14},{9,15},{10,... | collective-permute-start | bytes 196616 | tf_op jit(solution)/shard_map/ppermute | solution.py:25
  11.4 0.5 %collective-permute-start.4 = (f32[128,128]{1,0:T(8,128)S(1)}, f32[128,128]{1,0:T(8,128)S(1)}, u32[]{:S(2)}, u32[]{:S(2)}) collective-permute-start(f32[128,128]{1,0:T(8,128)S(1)} %get-tuple-element.50), channel_id=1, source_target_pairs={{0,4},{1,5},{2,6},{3,7},{4,0},{5,1},{6,2},{7,3},{8,12},{9,13},{10,... | collective-permute-start | bytes 196616 | tf_op jit(solution)/shard_map/ppermute | solution.py:25
  11.9 0.0 copy-start.2
  11.9 0.5 %collective-permute-start.3 = (f32[128,128]{1,0:T(8,128)S(1)}, f32[128,128]{1,0:T(8,128)S(1)}, u32[]{:S(2)}, u32[]{:S(2)}) collective-permute-start(f32[128,128]{1,0:T(8,128)S(1)} %get-tuple-element.51), channel_id=1, source_target_pairs={{0,2},{1,3},{2,0},{3,1},{4,6},{5,7},{6,4},{7,5},{8,10},{9,11},{10,... | collective-permute-start | bytes 196616 | tf_op jit(solution)/shard_map/ppermute | solution.py:25
  12.5 0.0 collective-permute-done.2.refs_0_.refs_1_
  12.5 2.2 %collective-permute-done.5.refs_5_ = f32[128,128]{1,0:T(8,128)S(1)} collective-permute-done((f32[128,128]{1,0:T(8,128)S(1)}, f32[128,128]{1,0:T(8,128)S(1)}, u32[]{:S(2)}, u32[]{:S(2)}) %collective-permute-start.5) | collective-permute-done | bytes 65568 | tf_op jit(solution)/shard_map/ppermute | solution.py:25
  14.7 1.0 %collective-permute-done.4.refs_4_ = f32[128,128]{1,0:T(8,128)S(1)} collective-permute-done((f32[128,128]{1,0:T(8,128)S(1)}, f32[128,128]{1,0:T(8,128)S(1)}, u32[]{:S(2)}, u32[]{:S(2)}) %collective-permute-start.4) | collective-permute-done | bytes 65568 | tf_op jit(solution)/shard_map/ppermute | solution.py:25
  15.7 0.5 %collective-permute-done.3.refs_3_ = f32[128,128]{1,0:T(8,128)S(1)} collective-permute-done((f32[128,128]{1,0:T(8,128)S(1)}, f32[128,128]{1,0:T(8,128)S(1)}, u32[]{:S(2)}, u32[]{:S(2)}) %collective-permute-start.3) | collective-permute-done | bytes 65568 | tf_op jit(solution)/shard_map/ppermute | solution.py:25
  16.2 0.1 collective-permute-start.6
  16.3 0.0 copy-done.2
  16.3 0.0 copy-start.1
  16.3 0.4 %shard_map.52 = (bf16[17,128,256]{2,1,0:T(8,128)(2,1)S(1)}, bf16[17,128,256]{2,1,0:T(8,128)(2,1)S(1)}) custom-call(f32[17,128,128]{2,1,0:T(8,128)S(1)} %bitcast.12), custom_call_target="tpu_custom_call" | custom-call | flops 10000000000 | tf_op jit(solution)/shard_map/pallas_call | solution.py:214
  16.7 1.1 %collective-permute-done.6.refs_6_ = f32[4,128,128]{2,1,0:T(8,128)S(1)} collective-permute-done((f32[4,128,128]{2,1,0:T(8,128)S(1)}, f32[4,128,128]{2,1,0:T(8,128)S(1)}, u32[]{:S(2)}, u32[]{:S(2)}) %collective-permute-start.6) | collective-permute-done | bytes 262176 | tf_op jit(solution)/shard_map/ppermute | solution.py:30
  17.8 0.0 copy-done.1
  17.8 1.5 %shard_map.53 = (f32[520,128]{1,0:T(8,128)S(1)}, f32[5,128,128]{2,1,0:T(8,128)S(1)}, f32[128,128]{1,0:T(8,128)S(1)}, f32[128,128]{1,0:T(8,128)S(1)}) custom-call(s32[1]{0:T(128)} %bitcast.place_ref, s32[2,17]{1,0:T(2,128)S(1)} %bitcast.11, f32[128,128]{1,0:T(8,128)S(1)} %shard_map.50.own_ref.right_ref, f32[128,128]{1,0:T(8,128)S(1)} %collective-permute-done.1.refs_0_, ...), custom_call_target="tpu_custom_call" | custom-call | tf_op jit(solution)/shard_map/pallas_call | solution.py:214
  19.3 0.2 collective-permute-start.7
  19.5 1.4 %collective-permute-done.7.got_ref = f32[520,128]{1,0:T(8,128)S(1)} collective-permute-done((f32[520,128]{1,0:T(8,128)S(1)}, f32[520,128]{1,0:T(8,128)S(1)}, u32[]{:S(2)}, u32[]{:S(2)}) %collective-permute-start.7) | collective-permute-done | bytes 266272 | tf_op jit(solution)/shard_map/ppermute | solution.py:30
  21.0 0.6 %collective-permute-start.8 = (f32[136,128]{1,0:T(8,128)S(1)}, f32[136,128]{1,0:T(8,128)S(1)}, u32[]{:S(2)}, u32[]{:S(2)}) collective-permute-start(f32[136,128]{1,0:T(8,128)S(1)} %get-tuple-element.38), channel_id=1, source_target_pairs={{0,2},{1,3},{2,0},{3,1},{4,6},{5,7},{6,4},{7,5},{8,10},{9,11},{10,... | collective-permute-start | bytes 208904 | tf_op jit(solution)/shard_map/ppermute | solution.py:25
  21.6 1.5 %collective-permute-start.9 = (f32[136,128]{1,0:T(8,128)S(1)}, f32[136,128]{1,0:T(8,128)S(1)}, u32[]{:S(2)}, u32[]{:S(2)}) collective-permute-start(f32[136,128]{1,0:T(8,128)S(1)} %get-tuple-element.39), channel_id=1, source_target_pairs={{0,4},{1,5},{2,6},{3,7},{4,0},{5,1},{6,2},{7,3},{8,12},{9,13},{10,... | collective-permute-start | bytes 208904 | tf_op jit(solution)/shard_map/ppermute | solution.py:25
  23.1 1.4 %collective-permute-start.10 = (f32[136,128]{1,0:T(8,128)S(1)}, f32[136,128]{1,0:T(8,128)S(1)}, u32[]{:S(2)}, u32[]{:S(2)}) collective-permute-start(f32[136,128]{1,0:T(8,128)S(1)} %get-tuple-element.40), channel_id=1, source_target_pairs={{0,6},{1,7},{2,4},{3,5},{4,2},{5,3},{6,0},{7,1},{8,14},{9,15},{10,... | collective-permute-start | bytes 208904 | tf_op jit(solution)/shard_map/ppermute | solution.py:25
  24.5 2.2 %collective-permute-start.12 = (f32[128,128]{1,0:T(8,128)S(1)}, f32[128,128]{1,0:T(8,128)S(1)}, u32[]{:S(2)}, u32[]{:S(2)}) collective-permute-start(f32[128,128]{1,0:T(8,128)S(1)} %get-tuple-element.45), channel_id=1, source_target_pairs={{0,16},{1,17},{2,18},{3,19},{4,20},{5,21},{6,22},{7,23},{8,24},{9,... | collective-permute-start | bytes 196616 | tf_op jit(solution)/shard_map/ppermute | solution.py:20
  26.7 0.0 collective-permute-done.8.refs_0_
  26.7 0.0 collective-permute-done.9.refs_1_
  26.7 1.6 %collective-permute-done.10.refs_2_ = f32[136,128]{1,0:T(8,128)S(1)} collective-permute-done((f32[136,128]{1,0:T(8,128)S(1)}, f32[136,128]{1,0:T(8,128)S(1)}, u32[]{:S(2)}, u32[]{:S(2)}) %collective-permute-start.10) | collective-permute-done | bytes 69664 | tf_op jit(solution)/shard_map/ppermute | solution.py:25
  28.4 2.3 %collective-permute-start.11 = (f32[136,128]{1,0:T(8,128)S(1)}, f32[136,128]{1,0:T(8,128)S(1)}, u32[]{:S(2)}, u32[]{:S(2)}) collective-permute-start(f32[136,128]{1,0:T(8,128)S(1)} %get-tuple-element.43), channel_id=1, source_target_pairs={{0,8},{1,9},{2,10},{3,11},{4,12},{5,13},{6,14},{7,15},{8,16},{9,17... | collective-permute-start | bytes 208904 | tf_op jit(solution)/shard_map/ppermute | solution.py:20
  30.6 1.9 %collective-permute-start.14 = (f32[8,128]{1,0:T(8,128)S(1)}, f32[8,128]{1,0:T(8,128)S(1)}, u32[]{:S(2)}, u32[]{:S(2)}) collective-permute-start(f32[8,128]{1,0:T(8,128)S(1)} %get-tuple-element.42.sums_ref), channel_id=1, source_target_pairs={{0,16},{1,17},{2,18},{3,19},{4,20},{5,21},{6,22},{7,23},{8,24},{9,... | collective-permute-start | bytes 12296 | tf_op jit(solution)/shard_map/ppermute | solution.py:20
  32.5 1.0 %collective-permute-start.13 = (f32[136,128]{1,0:T(8,128)S(1)}, f32[136,128]{1,0:T(8,128)S(1)}, u32[]{:S(2)}, u32[]{:S(2)}) collective-permute-start(f32[136,128]{1,0:T(8,128)S(1)} %get-tuple-element.47), channel_id=1, source_target_pairs={{0,24},{1,25},{2,26},{3,27},{4,28},{5,29},{6,30},{7,31},{8,0},{9,1... | collective-permute-start | bytes 208904 | tf_op jit(solution)/shard_map/ppermute | solution.py:20
  33.5 0.0 collective-permute-done.12.refs_0_
  33.5 1.6 %collective-permute-done.11.next_ref = f32[136,128]{1,0:T(8,128)S(1)} collective-permute-done((f32[136,128]{1,0:T(8,128)S(1)}, f32[136,128]{1,0:T(8,128)S(1)}, u32[]{:S(2)}, u32[]{:S(2)}) %collective-permute-start.11) | collective-permute-done | bytes 69664 | tf_op jit(solution)/shard_map/ppermute | solution.py:20
  35.2 0.1 collective-permute-done.14.refs_0_
  35.2 1.6 %collective-permute-done.13.last_ref = f32[136,128]{1,0:T(8,128)S(1)} collective-permute-done((f32[136,128]{1,0:T(8,128)S(1)}, f32[136,128]{1,0:T(8,128)S(1)}, u32[]{:S(2)}, u32[]{:S(2)}) %collective-permute-start.13) | collective-permute-done | bytes 69664 | tf_op jit(solution)/shard_map/ppermute | solution.py:20
  36.8 0.7 %shard_map.58 = (f32[128,128]{1,0:T(8,128)}, f32[128,128]{1,0:T(8,128)}) custom-call(f32[128,128]{1,0:T(8,128)S(1)} %shard_map.50.own_ref.right_ref, f32[128,128]{1,0:T(8,128)S(1)} %get-tuple-element.44.near_ref, f32[128,128]{1,0:T(8,128)S(1)} %shard_map.57.middle_ref, f32[8,128]{1,0:T(8,128)S(1)} %get-tuple-element.46.sums_ref, ...), custom_call_target="tpu_custom_call" | custom-call | tf_op jit(solution)/shard_map/pallas_call | solution.py:214
  (8 shorter events, 0.2 us)
Async XLA Ops:
  0.6 7.7 %collective-permute-start = (f32[128,128]{1,0:T(8,128)}, f32[128,128]{1,0:T(8,128)S(1)}, u32[]{:S(2)}, u32[]{:S(2)}) collective-permute-start(f32[128,128]{1,0:T(8,128)} %block_ref.1), channel_id=1, source_target_pairs={{0,8},{1,9},{2,10},{3,11},{4,12},{5,13},{6,14},{7,15},{8,16},{9,17... | collective-permute-start | bytes 196616 | tf_op jit(solution)/shard_map/ppermute | solution.py:20
  3.7 5.2 %collective-permute-start.1 = (f32[128,128]{1,0:T(8,128)}, f32[128,128]{1,0:T(8,128)S(1)}, u32[]{:S(2)}, u32[]{:S(2)}) collective-permute-start(f32[128,128]{1,0:T(8,128)} %block_ref.1), channel_id=1, source_target_pairs={{0,24},{1,25},{2,26},{3,27},{4,28},{5,29},{6,30},{7,31},{8,0},{9,1... | collective-permute-start | bytes 196616 | tf_op jit(solution)/shard_map/ppermute | solution.py:20
  5.8 6.7 %collective-permute-start.2 = (f32[128,128]{1,0:T(8,128)}, f32[128,128]{1,0:T(8,128)S(1)}, u32[]{:S(2)}, u32[]{:S(2)}) collective-permute-start(f32[128,128]{1,0:T(8,128)} %block_ref.1), channel_id=1, source_target_pairs={{0,16},{1,17},{2,18},{3,19},{4,20},{5,21},{6,22},{7,23},{8,24},{9,... | collective-permute-start | bytes 196616 | tf_op jit(solution)/shard_map/ppermute | solution.py:20
  6.7 0.9 %copy-start = (f32[128,128]{1,0:T(8,128)S(1)}, f32[128,128]{1,0:T(8,128)}, u32[]{:S(2)}) copy-start(f32[128,128]{1,0:T(8,128)} %block_ref.1) | copy-start | bytes 196612
  8.9 5.8 %collective-permute-start.5 = (f32[128,128]{1,0:T(8,128)S(1)}, f32[128,128]{1,0:T(8,128)S(1)}, u32[]{:S(2)}, u32[]{:S(2)}) collective-permute-start(f32[128,128]{1,0:T(8,128)S(1)} %get-tuple-element.49), channel_id=1, source_target_pairs={{0,6},{1,7},{2,4},{3,5},{4,2},{5,3},{6,0},{7,1},{8,14},{9,15},{10,... | collective-permute-start | bytes 196616 | tf_op jit(solution)/shard_map/ppermute | solution.py:25
  11.4 4.3 %collective-permute-start.4 = (f32[128,128]{1,0:T(8,128)S(1)}, f32[128,128]{1,0:T(8,128)S(1)}, u32[]{:S(2)}, u32[]{:S(2)}) collective-permute-start(f32[128,128]{1,0:T(8,128)S(1)} %get-tuple-element.50), channel_id=1, source_target_pairs={{0,4},{1,5},{2,6},{3,7},{4,0},{5,1},{6,2},{7,3},{8,12},{9,13},{10,... | collective-permute-start | bytes 196616 | tf_op jit(solution)/shard_map/ppermute | solution.py:25
  11.9 4.4 %copy-start.2 = (f32[1,17,128,128]{3,2,1,0:T(8,128)S(1)}, f32[1,17,128,128]{3,2,1,0:T(8,128)}, u32[]{:S(2)}) copy-start(f32[1,17,128,128]{3,2,1,0:T(8,128)} %param.4) | copy-start | bytes 3342340
  11.9 4.3 %collective-permute-start.3 = (f32[128,128]{1,0:T(8,128)S(1)}, f32[128,128]{1,0:T(8,128)S(1)}, u32[]{:S(2)}, u32[]{:S(2)}) collective-permute-start(f32[128,128]{1,0:T(8,128)S(1)} %get-tuple-element.51), channel_id=1, source_target_pairs={{0,2},{1,3},{2,0},{3,1},{4,6},{5,7},{6,4},{7,5},{8,10},{9,11},{10,... | collective-permute-start | bytes 196616 | tf_op jit(solution)/shard_map/ppermute | solution.py:25
  16.2 1.6 %collective-permute-start.6 = (f32[4,128,128]{2,1,0:T(8,128)S(1)}, f32[4,128,128]{2,1,0:T(8,128)S(1)}, u32[]{:S(2)}, u32[]{:S(2)}) collective-permute-start(f32[4,128,128]{2,1,0:T(8,128)S(1)} %pad_maximum_fusion), channel_id=1, source_target_pairs={{0,1},{1,0},{2,3},{3,2},{4,5},{5,4},{6,7},{7,6},{8,9},{9,8},{10,11... | collective-permute-start | bytes 786440 | tf_op jit(solution)/shard_map/ppermute | solution.py:30
  16.3 1.5 %copy-start.1 = (s32[17,2]{0,1:T(2,128)S(1)}, s32[17,2]{0,1:T(2,128)}, u32[]{:S(2)}) copy-start(s32[17,2]{0,1:T(2,128)} %param.5) | copy-start | bytes 412
  19.3 1.6 %collective-permute-start.7 = (f32[520,128]{1,0:T(8,128)S(1)}, f32[520,128]{1,0:T(8,128)S(1)}, u32[]{:S(2)}, u32[]{:S(2)}) collective-permute-start(f32[520,128]{1,0:T(8,128)S(1)} %get-tuple-element.32.sent_ref), channel_id=1, source_target_pairs={{0,1},{1,0},{2,3},{3,2},{4,5},{5,4},{6,7},{7,6},{8,9},{9,8},{10,11... | collective-permute-start | bytes 798728 | tf_op jit(solution)/shard_map/ppermute | solution.py:30
  21.0 5.8 %collective-permute-start.8 = (f32[136,128]{1,0:T(8,128)S(1)}, f32[136,128]{1,0:T(8,128)S(1)}, u32[]{:S(2)}, u32[]{:S(2)}) collective-permute-start(f32[136,128]{1,0:T(8,128)S(1)} %get-tuple-element.38), channel_id=1, source_target_pairs={{0,2},{1,3},{2,0},{3,1},{4,6},{5,7},{6,4},{7,5},{8,10},{9,11},{10,... | collective-permute-start | bytes 208904 | tf_op jit(solution)/shard_map/ppermute | solution.py:25
  21.6 5.2 %collective-permute-start.9 = (f32[136,128]{1,0:T(8,128)S(1)}, f32[136,128]{1,0:T(8,128)S(1)}, u32[]{:S(2)}, u32[]{:S(2)}) collective-permute-start(f32[136,128]{1,0:T(8,128)S(1)} %get-tuple-element.39), channel_id=1, source_target_pairs={{0,4},{1,5},{2,6},{3,7},{4,0},{5,1},{6,2},{7,3},{8,12},{9,13},{10,... | collective-permute-start | bytes 208904 | tf_op jit(solution)/shard_map/ppermute | solution.py:25
  23.1 5.2 %collective-permute-start.10 = (f32[136,128]{1,0:T(8,128)S(1)}, f32[136,128]{1,0:T(8,128)S(1)}, u32[]{:S(2)}, u32[]{:S(2)}) collective-permute-start(f32[136,128]{1,0:T(8,128)S(1)} %get-tuple-element.40), channel_id=1, source_target_pairs={{0,6},{1,7},{2,4},{3,5},{4,2},{5,3},{6,0},{7,1},{8,14},{9,15},{10,... | collective-permute-start | bytes 208904 | tf_op jit(solution)/shard_map/ppermute | solution.py:25
  24.5 9.0 %collective-permute-start.12 = (f32[128,128]{1,0:T(8,128)S(1)}, f32[128,128]{1,0:T(8,128)S(1)}, u32[]{:S(2)}, u32[]{:S(2)}) collective-permute-start(f32[128,128]{1,0:T(8,128)S(1)} %get-tuple-element.45), channel_id=1, source_target_pairs={{0,16},{1,17},{2,18},{3,19},{4,20},{5,21},{6,22},{7,23},{8,24},{9,... | collective-permute-start | bytes 196616 | tf_op jit(solution)/shard_map/ppermute | solution.py:20
  28.4 6.8 %collective-permute-start.11 = (f32[136,128]{1,0:T(8,128)S(1)}, f32[136,128]{1,0:T(8,128)S(1)}, u32[]{:S(2)}, u32[]{:S(2)}) collective-permute-start(f32[136,128]{1,0:T(8,128)S(1)} %get-tuple-element.43), channel_id=1, source_target_pairs={{0,8},{1,9},{2,10},{3,11},{4,12},{5,13},{6,14},{7,15},{8,16},{9,17... | collective-permute-start | bytes 208904 | tf_op jit(solution)/shard_map/ppermute | solution.py:20
  30.6 4.6 %collective-permute-start.14 = (f32[8,128]{1,0:T(8,128)S(1)}, f32[8,128]{1,0:T(8,128)S(1)}, u32[]{:S(2)}, u32[]{:S(2)}) collective-permute-start(f32[8,128]{1,0:T(8,128)S(1)} %get-tuple-element.42.sums_ref), channel_id=1, source_target_pairs={{0,16},{1,17},{2,18},{3,19},{4,20},{5,21},{6,22},{7,23},{8,24},{9,... | collective-permute-start | bytes 12296 | tf_op jit(solution)/shard_map/ppermute | solution.py:20
  32.5 4.3 %collective-permute-start.13 = (f32[136,128]{1,0:T(8,128)S(1)}, f32[136,128]{1,0:T(8,128)S(1)}, u32[]{:S(2)}, u32[]{:S(2)}) collective-permute-start(f32[136,128]{1,0:T(8,128)S(1)} %get-tuple-element.47), channel_id=1, source_target_pairs={{0,24},{1,25},{2,26},{3,27},{4,28},{5,29},{6,30},{7,31},{8,0},{9,1... | collective-permute-start | bytes 208904 | tf_op jit(solution)/shard_map/ppermute | solution.py:20

commit v18 on v16

--- a/solution.py
+++ b/solution.py
@@ -175,7 +175,7 @@
 
 
 def plane_kernel(chips, place_ref, near_ref, middle_ref, next_ref, sums_ref, last_ref, *refs):
-    got = refs[: chips - 1]
+    got = refs[: chips - 1][::-1]
     next_out, last_out, near_out, sums_out = refs[chips - 1 :]
     rows = near_ref.shape[0]
     chip = place_of(place_ref, chips)[0]
@@ -274,7 +274,7 @@
     ahead, last, near, sums = call(
         functools.partial(plane_kernel, chips),
         (where,),
-        (near, middle_sum, ahead, sums, far_out[-1], *got),
+        (near, middle_sum, ahead, sums, far_out[-1], *got[::-1]),
         [marked, marked, block, extra],
     )
     got = shifted(ahead, window)

time: 37.7 us -> 37.2 us (0.987)
  waiting for transfers between devices: 13.1 us -> 12.5 us
    ppermute x6, waiting for transfers between devices: 7.47 us -> 6.82 us  [chip_partner(): lax.ppermute(value, 'blk', [(source, source ^ 2 * mask) for source in ran...]
  transfers between devices with their start and end apart: 15 -> 15, of which waited for: 11 -> 12; matrix products, arithmetic and copies ran while one was open for 0% -> 0% of each run, Pallas kernels for 1% -> 1%
where the time goes in v18:
time: 37.2 us; the launch traced here: 37 us
  starting transfers between devices  20.2 us (54%)
  waiting for transfers between devices  12.5 us (34%)
  Pallas kernels  2.7 us (7%)
  local copies, waits for them, and re-layouts  0.88 us (2%)
  between operations  0.7 us (2%)
    ppermute x7, starting transfers between devices, shifted(): return lax.ppermute(value, 'blk', pairs)  12.8 us
    ppermute x6, starting transfers between devices, chip_partner(): lax.ppermute(value, 'blk', [(source, source ^ 2 * mask) for source in ran...  7.11 us
    ppermute x6, waiting for transfers between devices, chip_partner(): lax.ppermute(value, 'blk', [(source, source ^ 2 * mask) for source in ran...  6.82 us
    ppermute x7, waiting for transfers between devices, shifted(): return lax.ppermute(value, 'blk', pairs)  4.6 us
    pallas_call x9, Pallas kernels, call(): pl.pallas_call(kernel, in_specs=[pl.BlockSpec(memory_space=pltpu.SMEM)] *...  2.7 us
    ppermute x2, waiting for transfers between devices, core_partner(): lax.ppermute(value, 'blk', [(source, source ^ 1) for source in range(coun...  1.1 us
    unnamed x6, local copies, waits for them, and re-layouts  0.88 us
  transfers between devices with their start and end apart: 15, of which 12 were waited for; matrix products, arithmetic and copies ran while one was open for 0% of the time, Pallas kernels for 1%

profile of v18, /device:TPU:0, one launch (start us, length us, event | category | flops | bytes accessed | tf_op | source)
XLA Modules:
  0.0 37.0 jit_solution(10673611699082827236)
XLA Ops:
  0.6 3.1 %collective-permute-start = (f32[128,128]{1,0:T(8,128)}, f32[128,128]{1,0:T(8,128)S(1)}, u32[]{:S(2)}, u32[]{:S(2)}) collective-permute-start(f32[128,128]{1,0:T(8,128)} %block_ref.1), channel_id=1, source_target_pairs={{0,8},{1,9},{2,10},{3,11},{4,12},{5,13},{6,14},{7,15},{8,16},{9,17... | collective-permute-start | bytes 196616 | tf_op jit(solution)/shard_map/ppermute | solution.py:18
  3.7 2.1 %collective-permute-start.1 = (f32[128,128]{1,0:T(8,128)}, f32[128,128]{1,0:T(8,128)S(1)}, u32[]{:S(2)}, u32[]{:S(2)}) collective-permute-start(f32[128,128]{1,0:T(8,128)} %block_ref.1), channel_id=1, source_target_pairs={{0,24},{1,25},{2,26},{3,27},{4,28},{5,29},{6,30},{7,31},{8,0},{9,1... | collective-permute-start | bytes 196616 | tf_op jit(solution)/shard_map/ppermute | solution.py:18
  5.8 0.9 %collective-permute-start.2 = (f32[128,128]{1,0:T(8,128)}, f32[128,128]{1,0:T(8,128)S(1)}, u32[]{:S(2)}, u32[]{:S(2)}) collective-permute-start(f32[128,128]{1,0:T(8,128)} %block_ref.1), channel_id=1, source_target_pairs={{0,16},{1,17},{2,18},{3,19},{4,20},{5,21},{6,22},{7,23},{8,24},{9,... | collective-permute-start | bytes 196616 | tf_op jit(solution)/shard_map/ppermute | solution.py:18
  6.7 0.0 copy-start
  6.7 0.9 %copy-done = f32[128,128]{1,0:T(8,128)S(1)} copy-done((f32[128,128]{1,0:T(8,128)S(1)}, f32[128,128]{1,0:T(8,128)}, u32[]{:S(2)}) %copy-start) | copy-done | bytes 65560
  7.6 0.7 %collective-permute-done.refs_2_ = f32[128,128]{1,0:T(8,128)S(1)} collective-permute-done((f32[128,128]{1,0:T(8,128)}, f32[128,128]{1,0:T(8,128)S(1)}, u32[]{:S(2)}, u32[]{:S(2)}) %collective-permute-start) | collective-permute-done | bytes 65568 | tf_op jit(solution)/shard_map/ppermute | solution.py:18
  8.3 0.5 %collective-permute-done.1.refs_0_ = f32[128,128]{1,0:T(8,128)S(1)} collective-permute-done((f32[128,128]{1,0:T(8,128)}, f32[128,128]{1,0:T(8,128)S(1)}, u32[]{:S(2)}, u32[]{:S(2)}) %collective-permute-start.1) | collective-permute-done | bytes 65568 | tf_op jit(solution)/shard_map/ppermute | solution.py:18
  8.9 2.5 %collective-permute-start.5 = (f32[128,128]{1,0:T(8,128)S(1)}, f32[128,128]{1,0:T(8,128)S(1)}, u32[]{:S(2)}, u32[]{:S(2)}) collective-permute-start(f32[128,128]{1,0:T(8,128)S(1)} %get-tuple-element.49), channel_id=1, source_target_pairs={{0,6},{1,7},{2,4},{3,5},{4,2},{5,3},{6,0},{7,1},{8,14},{9,15},{10,... | collective-permute-start | bytes 196616 | tf_op jit(solution)/shard_map/ppermute | solution.py:23
  11.4 0.5 %collective-permute-start.4 = (f32[128,128]{1,0:T(8,128)S(1)}, f32[128,128]{1,0:T(8,128)S(1)}, u32[]{:S(2)}, u32[]{:S(2)}) collective-permute-start(f32[128,128]{1,0:T(8,128)S(1)} %get-tuple-element.50), channel_id=1, source_target_pairs={{0,4},{1,5},{2,6},{3,7},{4,0},{5,1},{6,2},{7,3},{8,12},{9,13},{10,... | collective-permute-start | bytes 196616 | tf_op jit(solution)/shard_map/ppermute | solution.py:23
  11.9 0.0 copy-start.2
  11.9 0.5 %collective-permute-start.3 = (f32[128,128]{1,0:T(8,128)S(1)}, f32[128,128]{1,0:T(8,128)S(1)}, u32[]{:S(2)}, u32[]{:S(2)}) collective-permute-start(f32[128,128]{1,0:T(8,128)S(1)} %get-tuple-element.51), channel_id=1, source_target_pairs={{0,2},{1,3},{2,0},{3,1},{4,6},{5,7},{6,4},{7,5},{8,10},{9,11},{10,... | collective-permute-start | bytes 196616 | tf_op jit(solution)/shard_map/ppermute | solution.py:23
  12.5 0.0 collective-permute-done.2.refs_0_.refs_1_
  12.5 2.2 %collective-permute-done.5.refs_5_ = f32[128,128]{1,0:T(8,128)S(1)} collective-permute-done((f32[128,128]{1,0:T(8,128)S(1)}, f32[128,128]{1,0:T(8,128)S(1)}, u32[]{:S(2)}, u32[]{:S(2)}) %collective-permute-start.5) | collective-permute-done | bytes 65568 | tf_op jit(solution)/shard_map/ppermute | solution.py:23
  14.7 1.0 %collective-permute-done.4.refs_4_ = f32[128,128]{1,0:T(8,128)S(1)} collective-permute-done((f32[128,128]{1,0:T(8,128)S(1)}, f32[128,128]{1,0:T(8,128)S(1)}, u32[]{:S(2)}, u32[]{:S(2)}) %collective-permute-start.4) | collective-permute-done | bytes 65568 | tf_op jit(solution)/shard_map/ppermute | solution.py:23
  15.7 0.5 %collective-permute-done.3.refs_3_ = f32[128,128]{1,0:T(8,128)S(1)} collective-permute-done((f32[128,128]{1,0:T(8,128)S(1)}, f32[128,128]{1,0:T(8,128)S(1)}, u32[]{:S(2)}, u32[]{:S(2)}) %collective-permute-start.3) | collective-permute-done | bytes 65568 | tf_op jit(solution)/shard_map/ppermute | solution.py:23
  16.2 0.1 collective-permute-start.6
  16.3 0.0 copy-done.2
  16.3 0.0 copy-start.1
  16.3 0.4 %shard_map.52 = (bf16[17,128,256]{2,1,0:T(8,128)(2,1)S(1)}, bf16[17,128,256]{2,1,0:T(8,128)(2,1)S(1)}) custom-call(f32[17,128,128]{2,1,0:T(8,128)S(1)} %bitcast.12), custom_call_target="tpu_custom_call" | custom-call | flops 10000000000 | tf_op jit(solution)/shard_map/pallas_call | solution.py:212
  16.7 1.1 %collective-permute-done.6.refs_6_ = f32[4,128,128]{2,1,0:T(8,128)S(1)} collective-permute-done((f32[4,128,128]{2,1,0:T(8,128)S(1)}, f32[4,128,128]{2,1,0:T(8,128)S(1)}, u32[]{:S(2)}, u32[]{:S(2)}) %collective-permute-start.6) | collective-permute-done | bytes 262176 | tf_op jit(solution)/shard_map/ppermute | solution.py:28
  17.8 0.0 copy-done.1
  17.8 1.5 %shard_map.53 = (f32[520,128]{1,0:T(8,128)S(1)}, f32[5,128,128]{2,1,0:T(8,128)S(1)}, f32[128,128]{1,0:T(8,128)S(1)}, f32[128,128]{1,0:T(8,128)S(1)}) custom-call(s32[1]{0:T(128)} %bitcast.place_ref, s32[2,17]{1,0:T(2,128)S(1)} %bitcast.11, f32[128,128]{1,0:T(8,128)S(1)} %shard_map.50.own_ref.right_ref, f32[128,128]{1,0:T(8,128)S(1)} %collective-permute-done.1.refs_0_, ...), custom_call_target="tpu_custom_call" | custom-call | tf_op jit(solution)/shard_map/pallas_call | solution.py:212
  19.3 0.2 collective-permute-start.7
  19.5 2.2 %collective-permute-start.8 = (f32[128,128]{1,0:T(8,128)S(1)}, f32[128,128]{1,0:T(8,128)S(1)}, u32[]{:S(2)}, u32[]{:S(2)}) collective-permute-start(f32[128,128]{1,0:T(8,128)S(1)} %get-tuple-element.35), channel_id=1, source_target_pairs={{0,16},{1,17},{2,18},{3,19},{4,20},{5,21},{6,22},{7,23},{8,24},{9,... | collective-permute-start | bytes 196616 | tf_op jit(solution)/shard_map/ppermute | solution.py:18
  21.7 0.0 collective-permute-done.7.got_ref
  21.8 1.6 %collective-permute-start.9 = (f32[136,128]{1,0:T(8,128)S(1)}, f32[136,128]{1,0:T(8,128)S(1)}, u32[]{:S(2)}, u32[]{:S(2)}) collective-permute-start(f32[136,128]{1,0:T(8,128)S(1)} %get-tuple-element.39), channel_id=1, source_target_pairs={{0,6},{1,7},{2,4},{3,5},{4,2},{5,3},{6,0},{7,1},{8,14},{9,15},{10,... | collective-permute-start | bytes 208904 | tf_op jit(solution)/shard_map/ppermute | solution.py:23
  23.3 0.3 collective-permute-start.10
  23.6 1.7 %collective-permute-start.11 = (f32[136,128]{1,0:T(8,128)S(1)}, f32[136,128]{1,0:T(8,128)S(1)}, u32[]{:S(2)}, u32[]{:S(2)}) collective-permute-start(f32[136,128]{1,0:T(8,128)S(1)} %get-tuple-element.41), channel_id=1, source_target_pairs={{0,2},{1,3},{2,0},{3,1},{4,6},{5,7},{6,4},{7,5},{8,10},{9,11},{10,... | collective-permute-start | bytes 208904 | tf_op jit(solution)/shard_map/ppermute | solution.py:23
  25.3 0.0 collective-permute-done.8.refs_0_
  25.4 1.9 %collective-permute-done.9.refs_0_ = f32[136,128]{1,0:T(8,128)S(1)} collective-permute-done((f32[136,128]{1,0:T(8,128)S(1)}, f32[136,128]{1,0:T(8,128)S(1)}, u32[]{:S(2)}, u32[]{:S(2)}) %collective-permute-start.9) | collective-permute-done | bytes 69664 | tf_op jit(solution)/shard_map/ppermute | solution.py:23
  27.3 1.1 %collective-permute-done.10.refs_1_ = f32[136,128]{1,0:T(8,128)S(1)} collective-permute-done((f32[136,128]{1,0:T(8,128)S(1)}, f32[136,128]{1,0:T(8,128)S(1)}, u32[]{:S(2)}, u32[]{:S(2)}) %collective-permute-start.10) | collective-permute-done | bytes 69664 | tf_op jit(solution)/shard_map/ppermute | solution.py:23
  28.4 0.1 collective-permute-done.11.refs_2_
  28.5 0.1 shard_map.56
  28.5 2.0 %collective-permute-start.12 = (f32[136,128]{1,0:T(8,128)S(1)}, f32[136,128]{1,0:T(8,128)S(1)}, u32[]{:S(2)}, u32[]{:S(2)}) collective-permute-start(f32[136,128]{1,0:T(8,128)S(1)} %get-tuple-element.44), channel_id=1, source_target_pairs={{0,8},{1,9},{2,10},{3,11},{4,12},{5,13},{6,14},{7,15},{8,16},{9,17... | collective-permute-start | bytes 208904 | tf_op jit(solution)/shard_map/ppermute | solution.py:18
  30.5 1.5 %collective-permute-start.14 = (f32[8,128]{1,0:T(8,128)S(1)}, f32[8,128]{1,0:T(8,128)S(1)}, u32[]{:S(2)}, u32[]{:S(2)}) collective-permute-start(f32[8,128]{1,0:T(8,128)S(1)} %get-tuple-element.43.sums_ref), channel_id=1, source_target_pairs={{0,16},{1,17},{2,18},{3,19},{4,20},{5,21},{6,22},{7,23},{8,24},{9,... | collective-permute-start | bytes 12296 | tf_op jit(solution)/shard_map/ppermute | solution.py:18
  32.0 1.0 %collective-permute-start.13 = (f32[136,128]{1,0:T(8,128)S(1)}, f32[136,128]{1,0:T(8,128)S(1)}, u32[]{:S(2)}, u32[]{:S(2)}) collective-permute-start(f32[136,128]{1,0:T(8,128)S(1)} %get-tuple-element.47), channel_id=1, source_target_pairs={{0,24},{1,25},{2,26},{3,27},{4,28},{5,29},{6,30},{7,31},{8,0},{9,1... | collective-permute-start | bytes 208904 | tf_op jit(solution)/shard_map/ppermute | solution.py:18
  33.0 1.8 %collective-permute-done.12.next_ref = f32[136,128]{1,0:T(8,128)S(1)} collective-permute-done((f32[136,128]{1,0:T(8,128)S(1)}, f32[136,128]{1,0:T(8,128)S(1)}, u32[]{:S(2)}, u32[]{:S(2)}) %collective-permute-start.12) | collective-permute-done | bytes 69664 | tf_op jit(solution)/shard_map/ppermute | solution.py:18
  34.8 0.3 collective-permute-done.14.refs_0_
  35.1 1.2 %collective-permute-done.13.last_ref = f32[136,128]{1,0:T(8,128)S(1)} collective-permute-done((f32[136,128]{1,0:T(8,128)S(1)}, f32[136,128]{1,0:T(8,128)S(1)}, u32[]{:S(2)}, u32[]{:S(2)}) %collective-permute-start.13) | collective-permute-done | bytes 69664 | tf_op jit(solution)/shard_map/ppermute | solution.py:18
  36.3 0.7 %shard_map.58 = (f32[128,128]{1,0:T(8,128)}, f32[128,128]{1,0:T(8,128)}) custom-call(f32[128,128]{1,0:T(8,128)S(1)} %shard_map.50.own_ref.right_ref, f32[128,128]{1,0:T(8,128)S(1)} %get-tuple-element.45.near_ref, f32[8,128]{1,0:T(8,128)S(1)} %get-tuple-element.46.sums_ref, f32[136,128]{1,0:T(8,128)S(1)} %collective-permute-done.13.last_ref, ...), custom_call_target="tpu_custom_call" | custom-call | tf_op jit(solution)/shard_map/pallas_call | solution.py:212
  (7 shorter events, 0.1 us)
Async XLA Ops:
  0.6 7.7 %collective-permute-start = (f32[128,128]{1,0:T(8,128)}, f32[128,128]{1,0:T(8,128)S(1)}, u32[]{:S(2)}, u32[]{:S(2)}) collective-permute-start(f32[128,128]{1,0:T(8,128)} %block_ref.1), channel_id=1, source_target_pairs={{0,8},{1,9},{2,10},{3,11},{4,12},{5,13},{6,14},{7,15},{8,16},{9,17... | collective-permute-start | bytes 196616 | tf_op jit(solution)/shard_map/ppermute | solution.py:18
  3.7 5.2 %collective-permute-start.1 = (f32[128,128]{1,0:T(8,128)}, f32[128,128]{1,0:T(8,128)S(1)}, u32[]{:S(2)}, u32[]{:S(2)}) collective-permute-start(f32[128,128]{1,0:T(8,128)} %block_ref.1), channel_id=1, source_target_pairs={{0,24},{1,25},{2,26},{3,27},{4,28},{5,29},{6,30},{7,31},{8,0},{9,1... | collective-permute-start | bytes 196616 | tf_op jit(solution)/shard_map/ppermute | solution.py:18
  5.8 6.7 %collective-permute-start.2 = (f32[128,128]{1,0:T(8,128)}, f32[128,128]{1,0:T(8,128)S(1)}, u32[]{:S(2)}, u32[]{:S(2)}) collective-permute-start(f32[128,128]{1,0:T(8,128)} %block_ref.1), channel_id=1, source_target_pairs={{0,16},{1,17},{2,18},{3,19},{4,20},{5,21},{6,22},{7,23},{8,24},{9,... | collective-permute-start | bytes 196616 | tf_op jit(solution)/shard_map/ppermute | solution.py:18
  6.7 0.9 %copy-start = (f32[128,128]{1,0:T(8,128)S(1)}, f32[128,128]{1,0:T(8,128)}, u32[]{:S(2)}) copy-start(f32[128,128]{1,0:T(8,128)} %block_ref.1) | copy-start | bytes 196612
  8.9 5.8 %collective-permute-start.5 = (f32[128,128]{1,0:T(8,128)S(1)}, f32[128,128]{1,0:T(8,128)S(1)}, u32[]{:S(2)}, u32[]{:S(2)}) collective-permute-start(f32[128,128]{1,0:T(8,128)S(1)} %get-tuple-element.49), channel_id=1, source_target_pairs={{0,6},{1,7},{2,4},{3,5},{4,2},{5,3},{6,0},{7,1},{8,14},{9,15},{10,... | collective-permute-start | bytes 196616 | tf_op jit(solution)/shard_map/ppermute | solution.py:23
  11.4 4.3 %collective-permute-start.4 = (f32[128,128]{1,0:T(8,128)S(1)}, f32[128,128]{1,0:T(8,128)S(1)}, u32[]{:S(2)}, u32[]{:S(2)}) collective-permute-start(f32[128,128]{1,0:T(8,128)S(1)} %get-tuple-element.50), channel_id=1, source_target_pairs={{0,4},{1,5},{2,6},{3,7},{4,0},{5,1},{6,2},{7,3},{8,12},{9,13},{10,... | collective-permute-start | bytes 196616 | tf_op jit(solution)/shard_map/ppermute | solution.py:23
  11.9 4.4 %copy-start.2 = (f32[1,17,128,128]{3,2,1,0:T(8,128)S(1)}, f32[1,17,128,128]{3,2,1,0:T(8,128)}, u32[]{:S(2)}) copy-start(f32[1,17,128,128]{3,2,1,0:T(8,128)} %param.4) | copy-start | bytes 3342340
  11.9 4.3 %collective-permute-start.3 = (f32[128,128]{1,0:T(8,128)S(1)}, f32[128,128]{1,0:T(8,128)S(1)}, u32[]{:S(2)}, u32[]{:S(2)}) collective-permute-start(f32[128,128]{1,0:T(8,128)S(1)} %get-tuple-element.51), channel_id=1, source_target_pairs={{0,2},{1,3},{2,0},{3,1},{4,6},{5,7},{6,4},{7,5},{8,10},{9,11},{10,... | collective-permute-start | bytes 196616 | tf_op jit(solution)/shard_map/ppermute | solution.py:23
  16.2 1.6 %collective-permute-start.6 = (f32[4,128,128]{2,1,0:T(8,128)S(1)}, f32[4,128,128]{2,1,0:T(8,128)S(1)}, u32[]{:S(2)}, u32[]{:S(2)}) collective-permute-start(f32[4,128,128]{2,1,0:T(8,128)S(1)} %pad_maximum_fusion), channel_id=1, source_target_pairs={{0,1},{1,0},{2,3},{3,2},{4,5},{5,4},{6,7},{7,6},{8,9},{9,8},{10,11... | collective-permute-start | bytes 786440 | tf_op jit(solution)/shard_map/ppermute | solution.py:28
  16.3 1.5 %copy-start.1 = (s32[17,2]{0,1:T(2,128)S(1)}, s32[17,2]{0,1:T(2,128)}, u32[]{:S(2)}) copy-start(s32[17,2]{0,1:T(2,128)} %param.5) | copy-start | bytes 412
  19.3 2.4 %collective-permute-start.7 = (f32[520,128]{1,0:T(8,128)S(1)}, f32[520,128]{1,0:T(8,128)S(1)}, u32[]{:S(2)}, u32[]{:S(2)}) collective-permute-start(f32[520,128]{1,0:T(8,128)S(1)} %get-tuple-element.32.sent_ref), channel_id=1, source_target_pairs={{0,1},{1,0},{2,3},{3,2},{4,5},{5,4},{6,7},{7,6},{8,9},{9,8},{10,11... | collective-permute-start | bytes 798728 | tf_op jit(solution)/shard_map/ppermute | solution.py:28
  19.5 5.8 %collective-permute-start.8 = (f32[128,128]{1,0:T(8,128)S(1)}, f32[128,128]{1,0:T(8,128)S(1)}, u32[]{:S(2)}, u32[]{:S(2)}) collective-permute-start(f32[128,128]{1,0:T(8,128)S(1)} %get-tuple-element.35), channel_id=1, source_target_pairs={{0,16},{1,17},{2,18},{3,19},{4,20},{5,21},{6,22},{7,23},{8,24},{9,... | collective-permute-start | bytes 196616 | tf_op jit(solution)/shard_map/ppermute | solution.py:18
  21.8 5.5 %collective-permute-start.9 = (f32[136,128]{1,0:T(8,128)S(1)}, f32[136,128]{1,0:T(8,128)S(1)}, u32[]{:S(2)}, u32[]{:S(2)}) collective-permute-start(f32[136,128]{1,0:T(8,128)S(1)} %get-tuple-element.39), channel_id=1, source_target_pairs={{0,6},{1,7},{2,4},{3,5},{4,2},{5,3},{6,0},{7,1},{8,14},{9,15},{10,... | collective-permute-start | bytes 208904 | tf_op jit(solution)/shard_map/ppermute | solution.py:23
  23.3 5.1 %collective-permute-start.10 = (f32[136,128]{1,0:T(8,128)S(1)}, f32[136,128]{1,0:T(8,128)S(1)}, u32[]{:S(2)}, u32[]{:S(2)}) collective-permute-start(f32[136,128]{1,0:T(8,128)S(1)} %get-tuple-element.40), channel_id=1, source_target_pairs={{0,4},{1,5},{2,6},{3,7},{4,0},{5,1},{6,2},{7,3},{8,12},{9,13},{10,... | collective-permute-start | bytes 208904 | tf_op jit(solution)/shard_map/ppermute | solution.py:23
  23.6 4.8 %collective-permute-start.11 = (f32[136,128]{1,0:T(8,128)S(1)}, f32[136,128]{1,0:T(8,128)S(1)}, u32[]{:S(2)}, u32[]{:S(2)}) collective-permute-start(f32[136,128]{1,0:T(8,128)S(1)} %get-tuple-element.41), channel_id=1, source_target_pairs={{0,2},{1,3},{2,0},{3,1},{4,6},{5,7},{6,4},{7,5},{8,10},{9,11},{10,... | collective-permute-start | bytes 208904 | tf_op jit(solution)/shard_map/ppermute | solution.py:23
  28.5 6.3 %collective-permute-start.12 = (f32[136,128]{1,0:T(8,128)S(1)}, f32[136,128]{1,0:T(8,128)S(1)}, u32[]{:S(2)}, u32[]{:S(2)}) collective-permute-start(f32[136,128]{1,0:T(8,128)S(1)} %get-tuple-element.44), channel_id=1, source_target_pairs={{0,8},{1,9},{2,10},{3,11},{4,12},{5,13},{6,14},{7,15},{8,16},{9,17... | collective-permute-start | bytes 208904 | tf_op jit(solution)/shard_map/ppermute | solution.py:18
  30.5 4.6 %collective-permute-start.14 = (f32[8,128]{1,0:T(8,128)S(1)}, f32[8,128]{1,0:T(8,128)S(1)}, u32[]{:S(2)}, u32[]{:S(2)}) collective-permute-start(f32[8,128]{1,0:T(8,128)S(1)} %get-tuple-element.43.sums_ref), channel_id=1, source_target_pairs={{0,16},{1,17},{2,18},{3,19},{4,20},{5,21},{6,22},{7,23},{8,24},{9,... | collective-permute-start | bytes 12296 | tf_op jit(solution)/shard_map/ppermute | solution.py:18
  32.0 4.3 %collective-permute-start.13 = (f32[136,128]{1,0:T(8,128)S(1)}, f32[136,128]{1,0:T(8,128)S(1)}, u32[]{:S(2)}, u32[]{:S(2)}) collective-permute-start(f32[136,128]{1,0:T(8,128)S(1)} %get-tuple-element.47), channel_id=1, source_target_pairs={{0,24},{1,25},{2,26},{3,27},{4,28},{5,29},{6,30},{7,31},{8,0},{9,1... | collective-permute-start | bytes 208904 | tf_op jit(solution)/shard_map/ppermute | solution.py:18

commit v19 on v17

--- a/solution.py
+++ b/solution.py
@@ -177,7 +177,7 @@
 
 
 def plane_kernel(chips, place_ref, near_ref, next_ref, sums_ref, last_ref, *refs):
-    got = refs[: chips - 1]
+    got = refs[: chips - 1][::-1]
     next_out, last_out, near_out, sums_out = refs[chips - 1 :]
     rows = near_ref.shape[0]
     chip = place_of(place_ref, chips)[0]
@@ -276,7 +276,7 @@
     ahead, last, near, sums = call(
         functools.partial(plane_kernel, chips),
         (where,),
-        (near, ahead, sums, far_out[-1], *got),
+        (near, ahead, sums, far_out[-1], *got[::-1]),
         [marked, marked, block, extra],
     )
     got = shifted(ahead, window)

time: 37.7 us -> 37.1 us (0.984)
  waiting for transfers between devices: 12.3 us -> 11.7 us
    ppermute x6, waiting for transfers between devices: 5.29 us -> 4.69 us  [chip_partner(): lax.ppermute(value, 'blk', [(source, source ^ 2 * mask) for source in ran...]
  transfers between devices with their start and end apart: 15 -> 15, of which waited for: 11 -> 12; matrix products, arithmetic and copies ran while one was open for 0% -> 0% of each run, Pallas kernels for 1% -> 1%
where the time goes in v19:
time: 37.1 us; the launch traced here: 36.9 us
  starting transfers between devices  20.9 us (56%)
  waiting for transfers between devices  11.7 us (32%)
  Pallas kernels  2.7 us (7%)
  local copies, waits for them, and re-layouts  0.88 us (2%)
  between operations  0.7 us (2%)
    ppermute x7, starting transfers between devices, shifted(): return lax.ppermute(value, 'blk', pairs)  13.5 us
    ppermute x6, starting transfers between devices, chip_partner(): lax.ppermute(value, 'blk', [(source, source ^ 2 * mask) for source in ran...  7.11 us
    ppermute x6, waiting for transfers between devices, chip_partner(): lax.ppermute(value, 'blk', [(source, source ^ 2 * mask) for source in ran...  4.69 us
    ppermute x7, waiting for transfers between devices, shifted(): return lax.ppermute(value, 'blk', pairs)  4.55 us
    pallas_call x9, Pallas kernels, call(): pl.pallas_call(kernel, in_specs=[pl.BlockSpec(memory_space=pltpu.SMEM)] *...  2.7 us
    ppermute x2, waiting for transfers between devices, core_partner(): lax.ppermute(value, 'blk', [(source, source ^ 1) for source in range(coun...  2.5 us
    unnamed x6, local copies, waits for them, and re-layouts  0.88 us
  transfers between devices with their start and end apart: 15, of which 12 were waited for; matrix products, arithmetic and copies ran while one was open for 0% of the time, Pallas kernels for 1%

profile of v19, /device:TPU:0, one launch (start us, length us, event | category | flops | bytes accessed | tf_op | source)
XLA Modules:
  0.0 36.9 jit_solution(2564965864588127590)
XLA Ops:
  0.6 3.1 %collective-permute-start = (f32[128,128]{1,0:T(8,128)}, f32[128,128]{1,0:T(8,128)S(1)}, u32[]{:S(2)}, u32[]{:S(2)}) collective-permute-start(f32[128,128]{1,0:T(8,128)} %block_ref.1), channel_id=1, source_target_pairs={{0,8},{1,9},{2,10},{3,11},{4,12},{5,13},{6,14},{7,15},{8,16},{9,17... | collective-permute-start | bytes 196616 | tf_op jit(solution)/shard_map/ppermute | solution.py:20
  3.7 2.1 %collective-permute-start.1 = (f32[128,128]{1,0:T(8,128)}, f32[128,128]{1,0:T(8,128)S(1)}, u32[]{:S(2)}, u32[]{:S(2)}) collective-permute-start(f32[128,128]{1,0:T(8,128)} %block_ref.1), channel_id=1, source_target_pairs={{0,24},{1,25},{2,26},{3,27},{4,28},{5,29},{6,30},{7,31},{8,0},{9,1... | collective-permute-start | bytes 196616 | tf_op jit(solution)/shard_map/ppermute | solution.py:20
  5.8 0.9 %collective-permute-start.2 = (f32[128,128]{1,0:T(8,128)}, f32[128,128]{1,0:T(8,128)S(1)}, u32[]{:S(2)}, u32[]{:S(2)}) collective-permute-start(f32[128,128]{1,0:T(8,128)} %block_ref.1), channel_id=1, source_target_pairs={{0,16},{1,17},{2,18},{3,19},{4,20},{5,21},{6,22},{7,23},{8,24},{9,... | collective-permute-start | bytes 196616 | tf_op jit(solution)/shard_map/ppermute | solution.py:20
  6.7 0.0 copy-start
  6.7 0.9 %copy-done = f32[128,128]{1,0:T(8,128)S(1)} copy-done((f32[128,128]{1,0:T(8,128)S(1)}, f32[128,128]{1,0:T(8,128)}, u32[]{:S(2)}) %copy-start) | copy-done | bytes 65560
  7.6 0.7 %collective-permute-done.refs_2_ = f32[128,128]{1,0:T(8,128)S(1)} collective-permute-done((f32[128,128]{1,0:T(8,128)}, f32[128,128]{1,0:T(8,128)S(1)}, u32[]{:S(2)}, u32[]{:S(2)}) %collective-permute-start) | collective-permute-done | bytes 65568 | tf_op jit(solution)/shard_map/ppermute | solution.py:20
  8.3 0.5 %collective-permute-done.1.refs_0_ = f32[128,128]{1,0:T(8,128)S(1)} collective-permute-done((f32[128,128]{1,0:T(8,128)}, f32[128,128]{1,0:T(8,128)S(1)}, u32[]{:S(2)}, u32[]{:S(2)}) %collective-permute-start.1) | collective-permute-done | bytes 65568 | tf_op jit(solution)/shard_map/ppermute | solution.py:20
  8.9 2.5 %collective-permute-start.5 = (f32[128,128]{1,0:T(8,128)S(1)}, f32[128,128]{1,0:T(8,128)S(1)}, u32[]{:S(2)}, u32[]{:S(2)}) collective-permute-start(f32[128,128]{1,0:T(8,128)S(1)} %get-tuple-element.49), channel_id=1, source_target_pairs={{0,6},{1,7},{2,4},{3,5},{4,2},{5,3},{6,0},{7,1},{8,14},{9,15},{10,... | collective-permute-start | bytes 196616 | tf_op jit(solution)/shard_map/ppermute | solution.py:25
  11.4 0.5 %collective-permute-start.4 = (f32[128,128]{1,0:T(8,128)S(1)}, f32[128,128]{1,0:T(8,128)S(1)}, u32[]{:S(2)}, u32[]{:S(2)}) collective-permute-start(f32[128,128]{1,0:T(8,128)S(1)} %get-tuple-element.50), channel_id=1, source_target_pairs={{0,4},{1,5},{2,6},{3,7},{4,0},{5,1},{6,2},{7,3},{8,12},{9,13},{10,... | collective-permute-start | bytes 196616 | tf_op jit(solution)/shard_map/ppermute | solution.py:25
  11.9 0.0 copy-start.2
  11.9 0.5 %collective-permute-start.3 = (f32[128,128]{1,0:T(8,128)S(1)}, f32[128,128]{1,0:T(8,128)S(1)}, u32[]{:S(2)}, u32[]{:S(2)}) collective-permute-start(f32[128,128]{1,0:T(8,128)S(1)} %get-tuple-element.51), channel_id=1, source_target_pairs={{0,2},{1,3},{2,0},{3,1},{4,6},{5,7},{6,4},{7,5},{8,10},{9,11},{10,... | collective-permute-start | bytes 196616 | tf_op jit(solution)/shard_map/ppermute | solution.py:25
  12.5 0.0 collective-permute-done.2.refs_0_.refs_1_
  12.5 2.2 %collective-permute-done.5.refs_5_ = f32[128,128]{1,0:T(8,128)S(1)} collective-permute-done((f32[128,128]{1,0:T(8,128)S(1)}, f32[128,128]{1,0:T(8,128)S(1)}, u32[]{:S(2)}, u32[]{:S(2)}) %collective-permute-start.5) | collective-permute-done | bytes 65568 | tf_op jit(solution)/shard_map/ppermute | solution.py:25
  14.7 1.0 %collective-permute-done.4.refs_4_ = f32[128,128]{1,0:T(8,128)S(1)} collective-permute-done((f32[128,128]{1,0:T(8,128)S(1)}, f32[128,128]{1,0:T(8,128)S(1)}, u32[]{:S(2)}, u32[]{:S(2)}) %collective-permute-start.4) | collective-permute-done | bytes 65568 | tf_op jit(solution)/shard_map/ppermute | solution.py:25
  15.7 0.5 %collective-permute-done.3.refs_3_ = f32[128,128]{1,0:T(8,128)S(1)} collective-permute-done((f32[128,128]{1,0:T(8,128)S(1)}, f32[128,128]{1,0:T(8,128)S(1)}, u32[]{:S(2)}, u32[]{:S(2)}) %collective-permute-start.3) | collective-permute-done | bytes 65568 | tf_op jit(solution)/shard_map/ppermute | solution.py:25
  16.2 0.1 collective-permute-start.6
  16.3 0.0 copy-done.2
  16.3 0.0 copy-start.1
  16.3 0.4 %shard_map.52 = (bf16[17,128,256]{2,1,0:T(8,128)(2,1)S(1)}, bf16[17,128,256]{2,1,0:T(8,128)(2,1)S(1)}) custom-call(f32[17,128,128]{2,1,0:T(8,128)S(1)} %bitcast.12), custom_call_target="tpu_custom_call" | custom-call | flops 10000000000 | tf_op jit(solution)/shard_map/pallas_call | solution.py:214
  16.7 1.1 %collective-permute-done.6.refs_6_ = f32[4,128,128]{2,1,0:T(8,128)S(1)} collective-permute-done((f32[4,128,128]{2,1,0:T(8,128)S(1)}, f32[4,128,128]{2,1,0:T(8,128)S(1)}, u32[]{:S(2)}, u32[]{:S(2)}) %collective-permute-start.6) | collective-permute-done | bytes 262176 | tf_op jit(solution)/shard_map/ppermute | solution.py:30
  17.8 0.0 copy-done.1
  17.8 1.5 %shard_map.53 = (f32[520,128]{1,0:T(8,128)S(1)}, f32[5,128,128]{2,1,0:T(8,128)S(1)}, f32[128,128]{1,0:T(8,128)S(1)}, f32[128,128]{1,0:T(8,128)S(1)}) custom-call(s32[1]{0:T(128)} %bitcast.place_ref, s32[2,17]{1,0:T(2,128)S(1)} %bitcast.11, f32[128,128]{1,0:T(8,128)S(1)} %shard_map.50.own_ref.right_ref, f32[128,128]{1,0:T(8,128)S(1)} %collective-permute-done.1.refs_0_, ...), custom_call_target="tpu_custom_call" | custom-call | tf_op jit(solution)/shard_map/pallas_call | solution.py:214
  19.3 0.2 collective-permute-start.7
  19.5 1.4 %collective-permute-done.7.got_ref = f32[520,128]{1,0:T(8,128)S(1)} collective-permute-done((f32[520,128]{1,0:T(8,128)S(1)}, f32[520,128]{1,0:T(8,128)S(1)}, u32[]{:S(2)}, u32[]{:S(2)}) %collective-permute-start.7) | collective-permute-done | bytes 266272 | tf_op jit(solution)/shard_map/ppermute | solution.py:30
  21.0 1.6 %collective-permute-start.8 = (f32[136,128]{1,0:T(8,128)S(1)}, f32[136,128]{1,0:T(8,128)S(1)}, u32[]{:S(2)}, u32[]{:S(2)}) collective-permute-start(f32[136,128]{1,0:T(8,128)S(1)} %get-tuple-element.38), channel_id=1, source_target_pairs={{0,6},{1,7},{2,4},{3,5},{4,2},{5,3},{6,0},{7,1},{8,14},{9,15},{10,... | collective-permute-start | bytes 208904 | tf_op jit(solution)/shard_map/ppermute | solution.py:25
  22.5 0.5 %collective-permute-start.9 = (f32[136,128]{1,0:T(8,128)S(1)}, f32[136,128]{1,0:T(8,128)S(1)}, u32[]{:S(2)}, u32[]{:S(2)}) collective-permute-start(f32[136,128]{1,0:T(8,128)S(1)} %get-tuple-element.39), channel_id=1, source_target_pairs={{0,4},{1,5},{2,6},{3,7},{4,0},{5,1},{6,2},{7,3},{8,12},{9,13},{10,... | collective-permute-start | bytes 208904 | tf_op jit(solution)/shard_map/ppermute | solution.py:25
  23.1 1.5 %collective-permute-start.10 = (f32[136,128]{1,0:T(8,128)S(1)}, f32[136,128]{1,0:T(8,128)S(1)}, u32[]{:S(2)}, u32[]{:S(2)}) collective-permute-start(f32[136,128]{1,0:T(8,128)S(1)} %get-tuple-element.40), channel_id=1, source_target_pairs={{0,2},{1,3},{2,0},{3,1},{4,6},{5,7},{6,4},{7,5},{8,10},{9,11},{10,... | collective-permute-start | bytes 208904 | tf_op jit(solution)/shard_map/ppermute | solution.py:25
  24.5 2.2 %collective-permute-start.12 = (f32[128,128]{1,0:T(8,128)S(1)}, f32[128,128]{1,0:T(8,128)S(1)}, u32[]{:S(2)}, u32[]{:S(2)}) collective-permute-start(f32[128,128]{1,0:T(8,128)S(1)} %get-tuple-element.45), channel_id=1, source_target_pairs={{0,16},{1,17},{2,18},{3,19},{4,20},{5,21},{6,22},{7,23},{8,24},{9,... | collective-permute-start | bytes 196616 | tf_op jit(solution)/shard_map/ppermute | solution.py:20
  26.7 0.0 collective-permute-done.8.refs_0_
  26.7 0.9 %collective-permute-done.9.refs_1_ = f32[136,128]{1,0:T(8,128)S(1)} collective-permute-done((f32[136,128]{1,0:T(8,128)S(1)}, f32[136,128]{1,0:T(8,128)S(1)}, u32[]{:S(2)}, u32[]{:S(2)}) %collective-permute-start.9) | collective-permute-done | bytes 69664 | tf_op jit(solution)/shard_map/ppermute | solution.py:25
  27.7 0.1 collective-permute-done.10.refs_2_
  27.8 2.7 %collective-permute-start.11 = (f32[136,128]{1,0:T(8,128)S(1)}, f32[136,128]{1,0:T(8,128)S(1)}, u32[]{:S(2)}, u32[]{:S(2)}) collective-permute-start(f32[136,128]{1,0:T(8,128)S(1)} %get-tuple-element.43), channel_id=1, source_target_pairs={{0,8},{1,9},{2,10},{3,11},{4,12},{5,13},{6,14},{7,15},{8,16},{9,17... | collective-permute-start | bytes 208904 | tf_op jit(solution)/shard_map/ppermute | solution.py:20
  30.4 1.5 %collective-permute-start.14 = (f32[8,128]{1,0:T(8,128)S(1)}, f32[8,128]{1,0:T(8,128)S(1)}, u32[]{:S(2)}, u32[]{:S(2)}) collective-permute-start(f32[8,128]{1,0:T(8,128)S(1)} %get-tuple-element.42.sums_ref), channel_id=1, source_target_pairs={{0,16},{1,17},{2,18},{3,19},{4,20},{5,21},{6,22},{7,23},{8,24},{9,... | collective-permute-start | bytes 12296 | tf_op jit(solution)/shard_map/ppermute | solution.py:20
  31.9 1.0 %collective-permute-start.13 = (f32[136,128]{1,0:T(8,128)S(1)}, f32[136,128]{1,0:T(8,128)S(1)}, u32[]{:S(2)}, u32[]{:S(2)}) collective-permute-start(f32[136,128]{1,0:T(8,128)S(1)} %get-tuple-element.47), channel_id=1, source_target_pairs={{0,24},{1,25},{2,26},{3,27},{4,28},{5,29},{6,30},{7,31},{8,0},{9,1... | collective-permute-start | bytes 208904 | tf_op jit(solution)/shard_map/ppermute | solution.py:20
  32.9 0.0 collective-permute-done.12.refs_0_
  32.9 1.2 %collective-permute-done.11.next_ref = f32[136,128]{1,0:T(8,128)S(1)} collective-permute-done((f32[136,128]{1,0:T(8,128)S(1)}, f32[136,128]{1,0:T(8,128)S(1)}, u32[]{:S(2)}, u32[]{:S(2)}) %collective-permute-start.11) | collective-permute-done | bytes 69664 | tf_op jit(solution)/shard_map/ppermute | solution.py:20
  34.1 0.8 %collective-permute-done.14.refs_0_ = f32[8,128]{1,0:T(8,128)S(1)} collective-permute-done((f32[8,128]{1,0:T(8,128)S(1)}, f32[8,128]{1,0:T(8,128)S(1)}, u32[]{:S(2)}, u32[]{:S(2)}) %collective-permute-start.14) | collective-permute-done | bytes 4128 | tf_op jit(solution)/shard_map/ppermute | solution.py:20
  34.9 1.3 %collective-permute-done.13.last_ref = f32[136,128]{1,0:T(8,128)S(1)} collective-permute-done((f32[136,128]{1,0:T(8,128)S(1)}, f32[136,128]{1,0:T(8,128)S(1)}, u32[]{:S(2)}, u32[]{:S(2)}) %collective-permute-start.13) | collective-permute-done | bytes 69664 | tf_op jit(solution)/shard_map/ppermute | solution.py:20
  36.2 0.7 %shard_map.58 = (f32[128,128]{1,0:T(8,128)}, f32[128,128]{1,0:T(8,128)}) custom-call(f32[128,128]{1,0:T(8,128)S(1)} %shard_map.50.own_ref.right_ref, f32[128,128]{1,0:T(8,128)S(1)} %get-tuple-element.44.near_ref, f32[128,128]{1,0:T(8,128)S(1)} %shard_map.57.middle_ref, f32[8,128]{1,0:T(8,128)S(1)} %get-tuple-element.46.sums_ref, ...), custom_call_target="tpu_custom_call" | custom-call | tf_op jit(solution)/shard_map/pallas_call | solution.py:214
  (8 shorter events, 0.2 us)
Async XLA Ops:
  0.6 7.7 %collective-permute-start = (f32[128,128]{1,0:T(8,128)}, f32[128,128]{1,0:T(8,128)S(1)}, u32[]{:S(2)}, u32[]{:S(2)}) collective-permute-start(f32[128,128]{1,0:T(8,128)} %block_ref.1), channel_id=1, source_target_pairs={{0,8},{1,9},{2,10},{3,11},{4,12},{5,13},{6,14},{7,15},{8,16},{9,17... | collective-permute-start | bytes 196616 | tf_op jit(solution)/shard_map/ppermute | solution.py:20
  3.7 5.2 %collective-permute-start.1 = (f32[128,128]{1,0:T(8,128)}, f32[128,128]{1,0:T(8,128)S(1)}, u32[]{:S(2)}, u32[]{:S(2)}) collective-permute-start(f32[128,128]{1,0:T(8,128)} %block_ref.1), channel_id=1, source_target_pairs={{0,24},{1,25},{2,26},{3,27},{4,28},{5,29},{6,30},{7,31},{8,0},{9,1... | collective-permute-start | bytes 196616 | tf_op jit(solution)/shard_map/ppermute | solution.py:20
  5.8 6.7 %collective-permute-start.2 = (f32[128,128]{1,0:T(8,128)}, f32[128,128]{1,0:T(8,128)S(1)}, u32[]{:S(2)}, u32[]{:S(2)}) collective-permute-start(f32[128,128]{1,0:T(8,128)} %block_ref.1), channel_id=1, source_target_pairs={{0,16},{1,17},{2,18},{3,19},{4,20},{5,21},{6,22},{7,23},{8,24},{9,... | collective-permute-start | bytes 196616 | tf_op jit(solution)/shard_map/ppermute | solution.py:20
  6.7 0.9 %copy-start = (f32[128,128]{1,0:T(8,128)S(1)}, f32[128,128]{1,0:T(8,128)}, u32[]{:S(2)}) copy-start(f32[128,128]{1,0:T(8,128)} %block_ref.1) | copy-start | bytes 196612
  8.9 5.8 %collective-permute-start.5 = (f32[128,128]{1,0:T(8,128)S(1)}, f32[128,128]{1,0:T(8,128)S(1)}, u32[]{:S(2)}, u32[]{:S(2)}) collective-permute-start(f32[128,128]{1,0:T(8,128)S(1)} %get-tuple-element.49), channel_id=1, source_target_pairs={{0,6},{1,7},{2,4},{3,5},{4,2},{5,3},{6,0},{7,1},{8,14},{9,15},{10,... | collective-permute-start | bytes 196616 | tf_op jit(solution)/shard_map/ppermute | solution.py:25
  11.4 4.3 %collective-permute-start.4 = (f32[128,128]{1,0:T(8,128)S(1)}, f32[128,128]{1,0:T(8,128)S(1)}, u32[]{:S(2)}, u32[]{:S(2)}) collective-permute-start(f32[128,128]{1,0:T(8,128)S(1)} %get-tuple-element.50), channel_id=1, source_target_pairs={{0,4},{1,5},{2,6},{3,7},{4,0},{5,1},{6,2},{7,3},{8,12},{9,13},{10,... | collective-permute-start | bytes 196616 | tf_op jit(solution)/shard_map/ppermute | solution.py:25
  11.9 4.4 %copy-start.2 = (f32[1,17,128,128]{3,2,1,0:T(8,128)S(1)}, f32[1,17,128,128]{3,2,1,0:T(8,128)}, u32[]{:S(2)}) copy-start(f32[1,17,128,128]{3,2,1,0:T(8,128)} %param.4) | copy-start | bytes 3342340
  11.9 4.3 %collective-permute-start.3 = (f32[128,128]{1,0:T(8,128)S(1)}, f32[128,128]{1,0:T(8,128)S(1)}, u32[]{:S(2)}, u32[]{:S(2)}) collective-permute-start(f32[128,128]{1,0:T(8,128)S(1)} %get-tuple-element.51), channel_id=1, source_target_pairs={{0,2},{1,3},{2,0},{3,1},{4,6},{5,7},{6,4},{7,5},{8,10},{9,11},{10,... | collective-permute-start | bytes 196616 | tf_op jit(solution)/shard_map/ppermute | solution.py:25
  16.2 1.6 %collective-permute-start.6 = (f32[4,128,128]{2,1,0:T(8,128)S(1)}, f32[4,128,128]{2,1,0:T(8,128)S(1)}, u32[]{:S(2)}, u32[]{:S(2)}) collective-permute-start(f32[4,128,128]{2,1,0:T(8,128)S(1)} %pad_maximum_fusion), channel_id=1, source_target_pairs={{0,1},{1,0},{2,3},{3,2},{4,5},{5,4},{6,7},{7,6},{8,9},{9,8},{10,11... | collective-permute-start | bytes 786440 | tf_op jit(solution)/shard_map/ppermute | solution.py:30
  16.3 1.5 %copy-start.1 = (s32[17,2]{0,1:T(2,128)S(1)}, s32[17,2]{0,1:T(2,128)}, u32[]{:S(2)}) copy-start(s32[17,2]{0,1:T(2,128)} %param.5) | copy-start | bytes 412
  19.3 1.6 %collective-permute-start.7 = (f32[520,128]{1,0:T(8,128)S(1)}, f32[520,128]{1,0:T(8,128)S(1)}, u32[]{:S(2)}, u32[]{:S(2)}) collective-permute-start(f32[520,128]{1,0:T(8,128)S(1)} %get-tuple-element.32.sent_ref), channel_id=1, source_target_pairs={{0,1},{1,0},{2,3},{3,2},{4,5},{5,4},{6,7},{7,6},{8,9},{9,8},{10,11... | collective-permute-start | bytes 798728 | tf_op jit(solution)/shard_map/ppermute | solution.py:30
  21.0 5.8 %collective-permute-start.8 = (f32[136,128]{1,0:T(8,128)S(1)}, f32[136,128]{1,0:T(8,128)S(1)}, u32[]{:S(2)}, u32[]{:S(2)}) collective-permute-start(f32[136,128]{1,0:T(8,128)S(1)} %get-tuple-element.38), channel_id=1, source_target_pairs={{0,6},{1,7},{2,4},{3,5},{4,2},{5,3},{6,0},{7,1},{8,14},{9,15},{10,... | collective-permute-start | bytes 208904 | tf_op jit(solution)/shard_map/ppermute | solution.py:25
  22.5 5.1 %collective-permute-start.9 = (f32[136,128]{1,0:T(8,128)S(1)}, f32[136,128]{1,0:T(8,128)S(1)}, u32[]{:S(2)}, u32[]{:S(2)}) collective-permute-start(f32[136,128]{1,0:T(8,128)S(1)} %get-tuple-element.39), channel_id=1, source_target_pairs={{0,4},{1,5},{2,6},{3,7},{4,0},{5,1},{6,2},{7,3},{8,12},{9,13},{10,... | collective-permute-start | bytes 208904 | tf_op jit(solution)/shard_map/ppermute | solution.py:25
  23.1 4.7 %collective-permute-start.10 = (f32[136,128]{1,0:T(8,128)S(1)}, f32[136,128]{1,0:T(8,128)S(1)}, u32[]{:S(2)}, u32[]{:S(2)}) collective-permute-start(f32[136,128]{1,0:T(8,128)S(1)} %get-tuple-element.40), channel_id=1, source_target_pairs={{0,2},{1,3},{2,0},{3,1},{4,6},{5,7},{6,4},{7,5},{8,10},{9,11},{10,... | collective-permute-start | bytes 208904 | tf_op jit(solution)/shard_map/ppermute | solution.py:25
  24.5 8.4 %collective-permute-start.12 = (f32[128,128]{1,0:T(8,128)S(1)}, f32[128,128]{1,0:T(8,128)S(1)}, u32[]{:S(2)}, u32[]{:S(2)}) collective-permute-start(f32[128,128]{1,0:T(8,128)S(1)} %get-tuple-element.45), channel_id=1, source_target_pairs={{0,16},{1,17},{2,18},{3,19},{4,20},{5,21},{6,22},{7,23},{8,24},{9,... | collective-permute-start | bytes 196616 | tf_op jit(solution)/shard_map/ppermute | solution.py:20
  27.8 6.4 %collective-permute-start.11 = (f32[136,128]{1,0:T(8,128)S(1)}, f32[136,128]{1,0:T(8,128)S(1)}, u32[]{:S(2)}, u32[]{:S(2)}) collective-permute-start(f32[136,128]{1,0:T(8,128)S(1)} %get-tuple-element.43), channel_id=1, source_target_pairs={{0,8},{1,9},{2,10},{3,11},{4,12},{5,13},{6,14},{7,15},{8,16},{9,17... | collective-permute-start | bytes 208904 | tf_op jit(solution)/shard_map/ppermute | solution.py:20
  30.4 4.5 %collective-permute-start.14 = (f32[8,128]{1,0:T(8,128)S(1)}, f32[8,128]{1,0:T(8,128)S(1)}, u32[]{:S(2)}, u32[]{:S(2)}) collective-permute-start(f32[8,128]{1,0:T(8,128)S(1)} %get-tuple-element.42.sums_ref), channel_id=1, source_target_pairs={{0,16},{1,17},{2,18},{3,19},{4,20},{5,21},{6,22},{7,23},{8,24},{9,... | collective-permute-start | bytes 12296 | tf_op jit(solution)/shard_map/ppermute | solution.py:20
  31.9 4.3 %collective-permute-start.13 = (f32[136,128]{1,0:T(8,128)S(1)}, f32[136,128]{1,0:T(8,128)S(1)}, u32[]{:S(2)}, u32[]{:S(2)}) collective-permute-start(f32[136,128]{1,0:T(8,128)S(1)} %get-tuple-element.47), channel_id=1, source_target_pairs={{0,24},{1,25},{2,26},{3,27},{4,28},{5,29},{6,30},{7,31},{8,0},{9,1... | collective-permute-start | bytes 208904 | tf_op jit(solution)/shard_map/ppermute | solution.py:20
